TPU v7x, 32 devices: a whole 2x2x4 slice. The times are simulated.
32 devices in a mesh: groups: 2 (over y), seq: 4 (over z), tp: 2 (over x), kv: 2 (over core).
Axes of the slice: x: 2, y: 2, z: 4, core: 2. Of those that a mesh axis runs over, the one named last changes fastest.
Arguments:
- events: bfloat16 [8, 512, 2048], P('groups', 'seq', ('tp', 'kv')), parts along dimension 0, may hold values from -6 to 6
- history_cache: bfloat16 [2, 8, 512, 1024], P(None, ('groups', 'seq'), None, ('tp', 'kv')), parts along dimension 1, may hold values from -6 to 6
- block_counts: int32 [8], P(('groups', 'seq')), parts along dimension 0, may hold values from 1 to 4
- semantic_ids: int32 [4, 128], P(None, ('groups', 'seq')), parts along dimension 1, may hold values from 0 to 4095
- beam_parents: int32 [3, 128], P(None, ('groups', 'seq')), parts along dimension 1, may hold values from 0 to 15
- query_weight: bfloat16 [2048, 2048], P('seq', ('tp', 'kv')), may hold values from -0.125 to 0.125
- keyval_weight: bfloat16 [2, 2048, 1024], P(None, 'seq', ('tp', 'kv')), may hold values from -0.125 to 0.125
- out_weight: bfloat16 [2048, 2048], P('seq', ('tp', 'kv')), may hold values from -0.125 to 0.125
- cross_weight: bfloat16 [2, 2048, 1024], P(None, 'seq', ('tp', 'kv')), may hold values from -0.125 to 0.125
- decoder_query: bfloat16 [2048, 2048], P(None, ('tp', 'kv')), may hold values from -0.125 to 0.125
- decoder_out: bfloat16 [2048, 2048], P(None, ('tp', 'kv')), may hold values from -0.125 to 0.125
- code_table: bfloat16 [4096, 2048], P(('tp', 'kv')), may hold values from -6 to 6
- encoder_gain: float32 [2048], replicated, may hold values from 0.25 to 1.75
- cross_gain: float32 [2048], replicated, may hold values from 0.25 to 1.75
- decoder_gain: float32 [2048], replicated, may hold values from 0.25 to 1.75
Outputs:
- encoded: bfloat16 [8, 512, 2048], P(('groups', 'seq'), ('tp', 'kv')), parts along dimension 0
- beam_state: bfloat16 [128, 2048], P(('groups', 'seq'), ('tp', 'kv')), parts along dimension 0
There are 2 independent parts, one for each index of `groups`. A program takes and returns all parts, laid end to end along the dimension named above; an argument that names none is the same for every part. Nothing has to cross between parts.
Inputs may be any that keep to these rules, and one draw needn't show every extreme that they name: A user's first 128 * block_counts new events are real; the rest are padding. `semantic_ids`: the codebook entry decoded for each beam row. `beam_parents`: the beam of the previous step that each beam row continues, counted among its user's 16 beams.
All inputs are finite; a program needn't handle non-finite values.
Results may differ from a plain program's by a relative error of at most 0.014.
Values may be sent and summed in bfloat16 or wider, within the bound.
No kernel may reach another device: no remote copies, remote signals or barrier semaphores. Data moves between devices by JAX's collectives and lax.ppermute only.
A program may use at most 64 MiB of HBM per device.

v0:
```python
import jax
import jax.numpy as jnp
from jax import lax
from jax.sharding import PartitionSpec as P

H = 16
DH = 128
KVH = 8
BLK = 128
STEPS = 4


eps = 1e-06


def root_norm(values, scale_gain):
    mean_square = jnp.mean(values * values, axis=-1, keepdims=True)
    return values * lax.rsqrt(mean_square + eps) * scale_gain


def shards(
    events,
    history_cache,
    block_counts,
    semantic_ids,
    beam_parents,
    query_weight,
    keyval_weight,
    out_weight,
    cross_weight,
    decoder_query,
    decoder_out,
    code_table,
    encoder_gain,
    cross_gain,
    decoder_gain,
):
    head_size = DH
    group_ratio = H // KVH
    relayed = lax.all_to_all(events, "seq", split_axis=0, concat_axis=1, tiled=True)
    whole = lax.all_gather(relayed, ("tp", "kv"), axis=2, tiled=True)
    users = whole.shape[0]
    length = whole.shape[1]
    width = whole.shape[2]
    source = whole.reshape(users * length, width).astype(jnp.float32)
    normed = root_norm(source, encoder_gain).astype(jnp.bfloat16)
    query_cols = query_weight.shape[1]
    key_cols = keyval_weight.shape[2]
    joined = jnp.concatenate([query_weight, keyval_weight[0], keyval_weight[1]], axis=1)
    projected = jnp.dot(
        normed,
        lax.all_gather(joined, "seq", axis=0, tiled=True),
        preferred_element_type=jnp.float32,
    )
    queries = projected[:, :query_cols].astype(jnp.bfloat16)
    keys_new = projected[:, query_cols : query_cols + key_cols].astype(jnp.bfloat16)
    values_new = projected[:, query_cols + key_cols :].astype(jnp.bfloat16)
    out_full, cross_full = (
        lax.all_gather(out_weight, "seq", axis=0, tiled=True),
        lax.all_gather(cross_weight, "seq", axis=1, tiled=True),
    )
    key_groups = key_cols // head_size
    history_len = history_cache.shape[2]
    query_heads = queries.reshape(users, length, key_groups, group_ratio, head_size)
    key_heads = jnp.concatenate(
        [history_cache[0], keys_new.reshape(users, length, key_cols)], axis=1
    )
    key_heads = key_heads.reshape(users, history_len + length, key_groups, head_size)
    value_heads = jnp.concatenate(
        [history_cache[1], values_new.reshape(users, length, key_cols)], axis=1
    )
    value_heads = value_heads.reshape(users, history_len + length, key_groups, head_size)
    scores = jnp.einsum(
        "uigad,ujgd->ugaij", query_heads, key_heads, preferred_element_type=jnp.float32
    ) * head_size ** (-0.5)
    query_index = lax.broadcasted_iota(jnp.int32, (length, history_len + length), 0)
    key_index = lax.broadcasted_iota(jnp.int32, (length, history_len + length), 1) - history_len
    live_limit = (block_counts * BLK)[:, None, None, None, None]
    visible = (key_index < 0)[None, None, None] | (key_index <= query_index)[None, None, None] & (
        key_index[None, None, None] < live_limit
    )
    raised = jnp.where(visible, jnp.exp(scores), jnp.float32(0.0))
    denominator = jnp.sum(raised, axis=-1, keepdims=True)
    softened = (raised / denominator).astype(jnp.bfloat16)
    attended = jnp.einsum(
        "ugaij,ujgd->uigad", softened, value_heads, preferred_element_type=jnp.float32
    )
    attended = attended.astype(jnp.bfloat16).reshape(users * length, query_cols)
    group = lax.axis_index(("tp", "kv"))
    groups = lax.axis_size(("tp", "kv"))
    share = users * length // groups
    group_term = lax.dot_general(
        attended, out_full, (((1,), (1,)), ((), ())), preferred_element_type=jnp.float32
    ).astype(jnp.bfloat16)
    mixed = lax.psum(group_term, ("tp", "kv")).astype(jnp.float32)
    encoded_all = source + mixed
    cross_all = root_norm(encoded_all, cross_gain).astype(jnp.bfloat16)
    encoded_rows = lax.dynamic_slice_in_dim(encoded_all, group * share, share, 0)
    encoded_out = encoded_rows.astype(jnp.bfloat16).reshape(users, share // users, width)
    cross_keys = jnp.dot(cross_all, cross_full[0], preferred_element_type=jnp.float32).astype(
        jnp.bfloat16
    )
    cross_values = jnp.dot(cross_all, cross_full[1], preferred_element_type=jnp.float32).astype(
        jnp.bfloat16
    )
    cross_key_heads = cross_keys.reshape(users, length, key_groups, head_size)
    cross_value_heads = cross_values.reshape(users, length, key_groups, head_size)
    live_events = (
        lax.broadcasted_iota(jnp.int32, (users, length), 1) < (block_counts * BLK)[:, None]
    )
    live_mask = live_events[:, None, None, None, :]
    beam_rows = semantic_ids.shape[1]
    per_user = beam_rows // users
    vocab_rows = code_table.shape[0]
    vocab_ids = group * vocab_rows + lax.broadcasted_iota(jnp.int32, (1, vocab_rows), 1)

    def lookup(id_values):
        onehot = (id_values[:, None] == vocab_ids).astype(jnp.bfloat16)
        return jnp.dot(onehot, code_table, preferred_element_type=jnp.float32)

    def attend(beam_hidden):
        normed_beams = root_norm(beam_hidden, decoder_gain).astype(jnp.bfloat16)
        beam_queries = jnp.dot(
            normed_beams, decoder_query, preferred_element_type=jnp.float32
        ).astype(jnp.bfloat16)
        beam_queries = beam_queries.reshape(users, per_user, key_groups, group_ratio, head_size)
        beam_scores = jnp.einsum(
            "ubgad,ujgd->ugabj", beam_queries, cross_key_heads, preferred_element_type=jnp.float32
        ) * head_size ** (-0.5)
        beam_raised = jnp.where(live_mask, jnp.exp(beam_scores), jnp.float32(0.0))
        beam_total = jnp.sum(beam_raised, axis=-1, keepdims=True)
        beam_soft = (beam_raised / beam_total).astype(jnp.bfloat16)
        beam_attended = jnp.einsum(
            "ugabj,ujgd->ubgad", beam_soft, cross_value_heads, preferred_element_type=jnp.float32
        )
        beam_attended = beam_attended.astype(jnp.bfloat16).reshape(beam_rows, query_cols)
        return lax.dot_general(
            beam_attended, decoder_out, (((1,), (1,)), ((), ())), preferred_element_type=jnp.float32
        )

    def combine(beam_terms):
        return lax.psum(beam_terms.astype(jnp.bfloat16), ("tp", "kv")).astype(jnp.float32)

    local_rows = lax.broadcasted_iota(jnp.int32, (beam_rows,), 0)
    beam_hidden = combine(lookup(semantic_ids[0]))
    mixed_state = attend(beam_hidden)
    for level in range(1, STEPS):
        source_rows = local_rows // per_user * per_user + beam_parents[level - 1]
        moved = jnp.take(mixed_state, source_rows, axis=0) + lookup(semantic_ids[level])
        beam_hidden = jnp.take(beam_hidden, source_rows, axis=0) + combine(moved)
        mixed_state = attend(beam_hidden)
    finished = (beam_hidden + combine(mixed_state)).astype(jnp.bfloat16)
    width_share = width // groups
    beam_out = lax.dynamic_slice_in_dim(finished, group * width_share, width_share, 1)
    return (encoded_out, beam_out)


def solution(mesh):
    in_specs = (
        P("groups", "seq", ("tp", "kv")),
        P(None, ("groups", "seq"), None, ("tp", "kv")),
        P(("groups", "seq")),
        P(None, ("groups", "seq")),
        P(None, ("groups", "seq")),
        P("seq", ("tp", "kv")),
        P(None, "seq", ("tp", "kv")),
        P("seq", ("tp", "kv")),
        P(None, "seq", ("tp", "kv")),
        P(None, ("tp", "kv")),
        P(None, ("tp", "kv")),
        P(("tp", "kv"), None),
        P(),
        P(),
        P(),
    )
    out_specs = (P(("groups", "seq"), ("tp", "kv"), None), P(("groups", "seq"), ("tp", "kv")))
    return jax.shard_map(shards, mesh=mesh, in_specs=in_specs, out_specs=out_specs, check_vma=False)
```

profile of v0, /device:TPU:0, one launch (start us, length us, event | category | flops | bytes accessed | tf_op | source)
XLA Modules:
  0.0 446.0 jit_solution(481606835040528028)
XLA Ops:
  7.2 21.1 %all_to_all.12 = bf16[4,128,512]{2,1,0:T(8,128)(2,1)} all-to-all(bf16[4,128,512]{2,1,0:T(8,128)(2,1)} %param.17), channel_id=1, replica_groups=mesh['groups'=2,'seq'=4,'tp'=2,'kv'=2] {'seq'}, dimensions={0} | all-to-all | bytes 1048576 | tf_op jit(solution)/shard_map/all_to_all | solution.py:40
  28.4 1.1 slice_bitcast_fusion.5
  29.5 1.2 pad_maximum_fusion
  30.8 0.7 all-gather.9.cloned.1.call-update
  32.2 0.1 copy.85
  32.4 0.9 copy.37
  33.2 0.8 copy.34
  34.1 1.6 fusion.15
  35.7 3.5 convolution_convert_fusion.2
  39.2 11.0 %all-gather.5.cloned.1.call-done = bf16[1,512,2048]{2,1,0:T(8,128)(2,1)} async-done(((bf16[1,512,512]{2,1,0:T(8,128)(2,1)}), bf16[1,512,2048]{2,1,0:T(8,128)(2,1)}) %all-gather.5.cloned.1.call-update) | async-done | bytes 2097168 | tf_op jit(solution)/shard_map/all_gather | solution.py:41
  50.2 2.1 fusion.1
  52.3 80.3 %all-gather.7.cloned.1.call-done = bf16[2048,1024]{1,0:T(8,128)(2,1)} async-done(((bf16[512,1024]{1,0:T(8,128)(2,1)}), bf16[2048,1024]{1,0:T(8,128)(2,1)}) %all-gather.7.cloned.1.call-update) | async-done | bytes 4194320 | tf_op jit(solution)/shard_map/all_gather | solution.py:52
  132.6 5.2 %fusion.16 = bf16[512,1024]{1,0:T(8,128)(2,1)S(1)} fusion(bf16[2048,1024]{1,0:T(8,128)(2,1)} %all-gather.7.cloned.1.call-done, bf16[1,512,2048]{2,1,0:T(8,128)(2,1)} %all-gather.5.cloned.1.call-done, f32[2048]{0:T(1024)S(1)} %copy-done.13, f32[512]{0:T(512)S(1)} %add_rsqrt_fusion.1), kind=kOutput, calls=%fused_computation.35 | convolution fusion | flops 2152202240 | bytes 7350272 | tf_op jit(solution)/shard_map/dot_general | solution.py:50
  137.9 0.8 copy.38
  138.7 0.9 reshape.294
  139.6 0.1 copy.68
  139.8 3.6 fusion
  143.4 2.4 fusion.19
  145.8 32.8 %all-gather.9.cloned.1.call-done = bf16[2048,512]{1,0:T(8,128)(2,1)} async-done(((bf16[512,512]{1,0:T(8,128)(2,1)}), bf16[2048,512]{1,0:T(8,128)(2,1)}) %all-gather.9.cloned.1.call-update) | async-done | bytes 2097168 | tf_op jit(solution)/shard_map/all_gather | solution.py:59
  178.6 4.2 convolution_convert_fusion
  182.9 0.5 all-gather.11.cloned.1.call-update
  183.5 0.2 all-reduce.7.cloned.1.call-start
  183.8 50.6 %all-reduce.15.cloned.1.call-done = (bf16[512,2048]{1,0:T(8,128)(2,1)}, bf16[16,2048]{1,0:T(8,128)(2,1)}) async-done(((bf16[512,2048]{1,0:T(8,128)(2,1)}, bf16[16,2048]{1,0:T(8,128)(2,1)}), (bf16[512,2048]{1,0:T(8,128)(2,1)}, bf16[16,2048]{1,0:T(8,128)(2,1)})) %all-reduce.15.cloned.1.call-update) | async-done | bytes 2162704 | tf_op jit(solution)/shard_map/psum | solution.py:95
  234.4 1.0 multiply_reduce_fusion.4
  235.4 2.1 convolution_convert_fusion.12
  237.5 3.0 multiply_reduce_fusion
  240.5 41.5 %all-gather.11.cloned.1.call-done = bf16[2,2048,256]{2,1,0:T(8,128)(2,1)} async-done(((bf16[2,512,256]{2,1,0:T(8,128)(2,1)}), bf16[2,2048,256]{2,1,0:T(8,128)(2,1)}) %all-gather.11.cloned.1.call-update) | async-done | bytes 2097168 | tf_op jit(solution)/shard_map/all_gather | solution.py:60
  282.0 3.8 convolution_convert_fusion.3
  285.7 0.2 fusion.88
  286.0 0.4 copy-done.12
  286.4 1.2 convolution_convert_fusion.4
  287.6 0.2 fusion.38
  287.8 0.6 fusion.92
  288.5 0.6 gather_fusion.1
  289.1 3.5 fusion.6
  292.8 0.6 gather_fusion
  293.4 29.2 %all-reduce.7.cloned.1.call-done = bf16[16,2048]{1,0:T(8,128)(2,1)} async-done(((bf16[16,2048]{1,0:T(8,128)(2,1)}), bf16[16,2048]{1,0:T(8,128)(2,1)}) %all-reduce.7.cloned.1.call-update) | async-done | bytes 65552 | tf_op jit(solution)/shard_map/psum | solution.py:142
  322.6 1.0 multiply_reduce_fusion.3
  323.7 2.0 convolution_convert_fusion.10
  325.7 0.2 fusion.89
  326.0 0.2 fusion.39
  326.3 0.6 fusion.93
  326.9 0.6 gather_fusion.3
  327.5 3.5 fusion.7
  331.1 0.6 gather_fusion.2
  331.7 30.6 %all-reduce.9.cloned.1.call-done = bf16[16,2048]{1,0:T(8,128)(2,1)} async-done(((bf16[16,2048]{1,0:T(8,128)(2,1)}), bf16[16,2048]{1,0:T(8,128)(2,1)}) %all-reduce.9.cloned.1.call-update) | async-done | bytes 65552 | tf_op jit(solution)/shard_map/psum | solution.py:142
  362.3 1.0 multiply_reduce_fusion.2
  363.4 2.0 convolution_convert_fusion.8
  365.4 0.2 fusion.90
  365.6 0.2 fusion.40
  365.9 0.6 fusion.94
  366.6 0.6 gather_fusion.5
  367.2 3.5 fusion.8
  370.8 4.4 convert_add_fusion
  375.2 0.6 gather_fusion.4
  375.9 26.1 %all-reduce.11.cloned.1.call-done = bf16[16,2048]{1,0:T(8,128)(2,1)} async-done(((bf16[16,2048]{1,0:T(8,128)(2,1)}), bf16[16,2048]{1,0:T(8,128)(2,1)}) %all-reduce.11.cloned.1.call-update) | async-done | bytes 65552 | tf_op jit(solution)/shard_map/psum | solution.py:142
  402.0 1.0 multiply_reduce_fusion.1
  403.0 2.0 convolution_convert_fusion.6
  405.0 0.2 fusion.91
  405.3 0.2 fusion.41
  405.6 1.3 convolution_convert_fusion.1
  406.9 1.9 fusion.42
  408.8 29.3 %all-reduce.13.cloned.1.call-done = bf16[16,2048]{1,0:T(8,128)(2,1)} async-done(((bf16[16,2048]{1,0:T(8,128)(2,1)}), bf16[16,2048]{1,0:T(8,128)(2,1)}) %all-reduce.13.cloned.1.call-update) | async-done | bytes 65552 | tf_op jit(solution)/shard_map/psum | solution.py:142
  438.1 1.3 fusion.66
  (76 shorter events, 1.1 us)
Async XLA Ops:
  7.2 280.7 %copy-start = (bf16[2048,512]{1,0:T(8,128)(2,1)S(1)}, bf16[2048,512]{1,0:T(8,128)(2,1)}, u32[]{:S(2)}) copy-start(bf16[2048,512]{1,0:T(8,128)(2,1)} %param.27) | copy-start | bytes 6291460
  7.2 22.3 %copy-start.6 = (bf16[512,512]{1,0:T(8,128)(2,1)S(1)}, bf16[512,512]{1,0:T(8,128)(2,1)}, u32[]{:S(2)}) copy-start(bf16[512,512]{1,0:T(8,128)(2,1)} %param.22) | copy-start | bytes 1572868
  7.2 43.0 %all-gather.5.cloned.1.call-start = ((), (), s32[]{:S(2)}) async-start(), calls=%async_computation.1 | async-start | bytes 2621440 | tf_op jit(solution)/shard_map/all_gather | solution.py:41
  28.3 104.2 %all-gather.7.cloned.1.call-start = ((), (), s32[]{:S(2)}) async-start(), calls=%async_computation.2 | async-start | bytes 5242880 | tf_op jit(solution)/shard_map/all_gather | solution.py:52
  29.4 2.7 copy-start.4
  30.7 3.4 copy-start.10
  30.7 147.9 %all-gather.9.cloned.1.call-start = ((), (), s32[]{:S(2)}) async-start(), calls=%async_computation.3 | async-start | bytes 2621440 | tf_op jit(solution)/shard_map/all_gather | solution.py:59
  31.4 203.0 %all-reduce.15.cloned.1.call-start = ((), (), s32[]{:S(2)}) async-start(), calls=%async_computation.9 | async-start | bytes 4325376 | tf_op jit(solution)/shard_map/psum | solution.py:95
  39.2 93.4 %copy-start.13 = (f32[2048]{0:T(1024)S(1)}, f32[2048]{0:T(1024)}, u32[]{:S(2)}) copy-start(f32[2048]{0:T(1024)} %param.29) | copy-start | bytes 24580
  137.9 1.9 copy-start.8
  139.8 3.6 copy-start.5
  139.8 3.6 copy-start.7
  182.9 0.9 copy-start.11
  182.9 52.5 %copy-start.9 = (f32[2048]{0:T(1024)S(1)}, f32[2048]{0:T(1024)}, u32[]{:S(2)}) copy-start(f32[2048]{0:T(1024)} %param.31) | copy-start | bytes 24580
  182.9 99.1 %all-gather.11.cloned.1.call-start = ((), (), s32[]{:S(2)}) async-start(), calls=%async_computation.4 | async-start | bytes 2621440 | tf_op jit(solution)/shard_map/all_gather | solution.py:60
  183.5 139.2 %all-reduce.7.cloned.1.call-start = ((), (), s32[]{:S(2)}) async-start(), calls=%async_computation.5 | async-start | bytes 131072 | tf_op jit(solution)/shard_map/psum | solution.py:142
  237.5 44.5 %copy-start.14 = (f32[2048]{0:T(1024)S(1)}, f32[2048]{0:T(1024)}, u32[]{:S(2)}) copy-start(f32[2048]{0:T(1024)} %param.30) | copy-start | bytes 24580
  282.0 4.0 copy-start.1
  282.0 4.0 copy-start.2
  282.0 4.4 copy-start.12
  289.1 3.6 copy-start.3
  292.7 69.6 %all-reduce.9.cloned.1.call-start = ((), (), s32[]{:S(2)}) async-start(), calls=%async_computation.6 | async-start | bytes 131072 | tf_op jit(solution)/shard_map/psum | solution.py:142
  331.1 70.9 %all-reduce.11.cloned.1.call-start = ((), (), s32[]{:S(2)}) async-start(), calls=%async_computation.7 | async-start | bytes 131072 | tf_op jit(solution)/shard_map/psum | solution.py:142
  370.8 67.4 %all-reduce.13.cloned.1.call-start = ((), (), s32[]{:S(2)}) async-start(), calls=%async_computation.8 | async-start | bytes 131072 | tf_op jit(solution)/shard_map/psum | solution.py:142
Sparse Core Ops, SparseCore 0:
  28.4 21.7 all-gather.4
  51.8 80.7 all-gather.6
  134.1 44.4 all-gather.8
  183.0 51.3 all-reduce.14
  235.9 46.0 all-gather.10
  292.8 29.7 all-reduce.6
  331.2 31.0 all-reduce.8
  370.9 31.0 all-reduce.10
  407.0 31.0 all-reduce.12
where the time goes:
time: 447 us; the launch traced here: 446 us
  waiting for transfers between devices  333 us (74%)
  matrix products  47.6 us (11%)
  blocking collectives  21.1 us (5%)
  other arithmetic  17.9 us (4%)
  between operations  14.9 us (3%)
  local copies, waits for them, and re-layouts  11.2 us (3%)
    psum x4, waiting for transfers between devices, combine(): lax.psum(beam_terms.astype(jnp.bfloat16), ('tp', 'kv')).astype(jnp.float32)  115 us
    all_gather x1, waiting for transfers between devices, shards(): lax.all_gather(joined, 'seq', axis=0, tiled=True)  80.3 us
    psum x1, waiting for transfers between devices, shards(): mixed = lax.psum(group_term, ('tp', 'kv')).astype(jnp.float32)  50.6 us
    all_gather x1, waiting for transfers between devices, shards(): lax.all_gather(cross_weight, 'seq', axis=1, tiled=True)  41.5 us
    all_gather x1, waiting for transfers between devices, shards(): lax.all_gather(out_weight, 'seq', axis=0, tiled=True)  32.8 us
    all_to_all x1, blocking collectives, shards(): lax.all_to_all(events, 'seq', split_axis=0, concat_axis=1, tiled=True)  21.1 us
    dot_general x4, matrix products, lookup(): return jnp.dot(onehot, code_table, preferred_element_type=jnp.float32)  14.1 us
    all_gather x1, waiting for transfers between devices, shards(): whole = lax.all_gather(relayed, ('tp', 'kv'), axis=2, tiled=True)  11 us
  transfers between devices with their start and end apart: 9, of which 9 were waited for; matrix products, arithmetic and copies ran while one was open for 9% of the time, Pallas kernels for 0%

commit v1 on v0

v1 whole, which is shorter than its diff:
```python
import functools

import jax
import jax.numpy as jnp
from jax import lax
from jax.experimental import pallas as pl
from jax.experimental.pallas import tpu as pltpu
from jax.sharding import PartitionSpec as P

H = 16
DH = 128
KVH = 8
BLK = 128
STEPS = 4
RING_LIMIT = 8
VMEM_BYTES = 56 * 1024 * 1024

eps = 1e-06

VM = pl.BlockSpec(memory_space=pltpu.VMEM)
SM = pl.BlockSpec(memory_space=pltpu.SMEM)
HB = pl.BlockSpec(memory_space=pl.ANY)


def params():
    return pltpu.CompilerParams(vmem_limit_bytes=VMEM_BYTES)


def partner(index, step, size):
    if size & (size - 1) == 0:
        return index ^ step
    return (index + step) % size


def origin(index, step, size):
    if size & (size - 1) == 0:
        return index ^ step
    return (index - step) % size


def exchange(value, axis, step):
    size = lax.axis_size(axis)
    return lax.ppermute(value, axis, [(i, partner(i, step, size)) for i in range(size)])


def shift(value, axis, step):
    size = lax.axis_size(axis)
    return lax.ppermute(value, axis, [(i, (i + step) % size) for i in range(size)])


def after(value, *others):
    return lax.optimization_barrier((value, *others))[0]


def gather_rows(value):
    size = lax.axis_size("seq")
    rows = value.shape[0]
    here = lax.axis_index("seq")
    if size > RING_LIMIT:
        return [(lax.all_gather(value, "seq", axis=0, tiled=True), jnp.int32(0))], []
    twins = lax.axis_size("groups")
    share = twins == 2 and rows % 32 == 0
    twin = lax.axis_index("groups")
    half = rows // 2
    moving = lax.dynamic_slice_in_dim(value, twin * half, half, 0) if share else value
    pieces = [(value, here * rows)]
    arrivals = []
    for step in range(1, size):
        moving = shift(moving, "seq", 1)
        arrivals.append(moving)
        first = (here - step) % size * rows
        if share:
            pieces.append((moving, first + twin * half))
            pieces.append((exchange(moving, "groups", 1), first + (1 - twin) * half))
        else:
            pieces.append((moving, first))
    return pieces, arrivals


def gather_heads(value):
    tp, kv = lax.axis_size("tp"), lax.axis_size("kv")
    my_tp, my_kv = lax.axis_index("tp"), lax.axis_index("kv")
    along = [(value, my_tp)]
    for step in range(1, tp):
        along.append((exchange(value, "tp", step), origin(my_tp, step, tp)))
    pieces = []
    for piece, where in along:
        pieces.append((piece, where * kv + my_kv))
    for piece, where in along:
        for step in range(1, kv):
            pieces.append((exchange(piece, "kv", step), where * kv + origin(my_kv, step, kv)))
    return pieces


def collect_events(events):
    size = lax.axis_size("seq")
    here = lax.axis_index("seq")
    rows = events.shape[1]
    if size > RING_LIMIT:
        mine = lax.all_to_all(events, "seq", split_axis=0, concat_axis=1, tiled=True)[0]
        return gather_heads(mine), [jnp.int32(0)]
    blocks = [lax.dynamic_index_in_dim(events, here, 0, False)]
    firsts = [here * rows]
    for step in range(1, size):
        block = lax.dynamic_index_in_dim(events, (here + step) % size, 0, False)
        blocks.append(shift(block, "seq", step))
        firsts.append((here - step) % size * rows)
    return gather_heads(jnp.concatenate(blocks, axis=0)), firsts


def norm_kernel(count, blocks, col_ref, row_ref, gain_ref, *refs):
    pieces, (normed_ref, source_ref) = refs[:count], refs[count:]
    width = normed_ref.shape[1]
    cols = pieces[0].shape[1]
    rows = pieces[0].shape[0] // blocks
    for block in range(blocks):
        first = pl.multiple_of(row_ref[block], rows)
        parts = [p[block * rows : (block + 1) * rows, :].astype(jnp.float32) for p in pieces]
        square = sum(jnp.sum(v * v, axis=-1, keepdims=True) for v in parts)
        scale = lax.rsqrt(square / width + eps)
        for index in range(count):
            col = pl.ds(pl.multiple_of(col_ref[index], cols), cols)
            source_ref[pl.ds(first, rows), col] = parts[index].astype(jnp.bfloat16)
            normed_ref[pl.ds(first, rows), col] = (
                parts[index] * scale * gain_ref[:, col]
            ).astype(jnp.bfloat16)


def norm_events(pieces, firsts, gain):
    cols = pieces[0][0].shape[1]
    length = pieces[0][0].shape[0]
    width = gain.shape[0]
    shape = jax.ShapeDtypeStruct((length, width), jnp.bfloat16)
    return pl.pallas_call(
        functools.partial(norm_kernel, len(pieces), len(firsts)),
        out_shape=(shape, shape),
        in_specs=[SM, SM] + [VM] * (1 + len(pieces)),
        out_specs=(VM, VM),
        compiler_params=params(),
        name="norm_events",
    )(
        jnp.stack([where * cols for _, where in pieces]),
        jnp.stack(firsts),
        gain[None, :],
        *[piece for piece, _ in pieces],
    )


def load_pieces(pieces, first_ref, base, whole, columns, sems):
    copies = []
    for index, piece in enumerate(pieces):
        rows = piece.shape[0]
        first = pl.multiple_of(first_ref[base + index], rows)
        copy = pltpu.make_async_copy(
            piece, whole.at[pl.ds(first, rows), columns], sems.at[base + index]
        )
        copy.start()
        copies.append(copy)
    return copies


def encoder_kernel(
    counts, ratio, first_ref, live_ref, normed_ref, history_ref, *refs
):
    query_count, keyval_count = counts
    total = query_count + keyval_count
    pieces, (out_ref, whole, projected, sems) = refs[:total], refs[total:]
    length = normed_ref.shape[0]
    heads = out_ref.shape[1] // DH
    kv_heads = heads // ratio
    query_cols = heads * DH
    key_cols = kv_heads * DH
    past = history_ref.shape[1]
    copies = load_pieces(
        pieces[:query_count], first_ref, 0, whole, pl.ds(0, query_cols), sems
    ) + load_pieces(
        pieces[query_count:], first_ref, query_count, whole, pl.ds(query_cols, 2 * key_cols), sems
    )
    for copy in copies:
        copy.wait()
    tile = min(256, length)
    for row in range(0, length, tile):
        projected[row : row + tile, :] = jnp.dot(
            normed_ref[row : row + tile, :], whole[...], preferred_element_type=jnp.float32
        ).astype(jnp.bfloat16)
    live = live_ref[0] * BLK
    contract = (((1,), (1,)), ((), ()))
    for group in range(kv_heads):
        keys = slice(query_cols + group * DH, query_cols + (group + 1) * DH)
        values = slice(query_cols + key_cols + group * DH, query_cols + key_cols + (group + 1) * DH)
        cached = slice(group * DH, (group + 1) * DH)
        for row in range(0, length, tile):
            reach = row + tile
            for head in range(group * ratio, (group + 1) * ratio):
                query = projected[row:reach, head * DH : (head + 1) * DH]
                old = lax.dot_general(
                    query, history_ref[0, :, cached], contract, preferred_element_type=jnp.float32
                )
                new = lax.dot_general(
                    query, projected[:reach, keys], contract, preferred_element_type=jnp.float32
                )
                query_index = row + lax.broadcasted_iota(jnp.int32, (tile, reach), 0)
                key_index = lax.broadcasted_iota(jnp.int32, (tile, reach), 1)
                new = jnp.where((key_index <= query_index) & (key_index < live), new, -1e30)
                top = jnp.maximum(
                    jnp.max(old, axis=-1, keepdims=True), jnp.max(new, axis=-1, keepdims=True)
                )
                scale = DH ** (-0.5)
                old = jnp.exp((old - top) * scale)
                new = jnp.exp((new - top) * scale)
                total_weight = jnp.sum(old, axis=-1, keepdims=True) + jnp.sum(
                    new, axis=-1, keepdims=True
                )
                mixed = jnp.dot(
                    old.astype(jnp.bfloat16),
                    history_ref[1, :, cached],
                    preferred_element_type=jnp.float32,
                ) + jnp.dot(
                    new.astype(jnp.bfloat16),
                    projected[:reach, values],
                    preferred_element_type=jnp.float32,
                )
                out_ref[row:reach, head * DH : (head + 1) * DH] = (mixed / total_weight).astype(
                    jnp.bfloat16
                )


def encoder_attention(normed, history, block_counts, query_pieces, keyval_pieces):
    length, width = normed.shape
    key_cols = history.shape[2]
    query_cols = query_pieces[0][0].shape[1]
    counts = (len(query_pieces), len(keyval_pieces))
    pieces = query_pieces + keyval_pieces
    joined = query_cols + 2 * key_cols
    return pl.pallas_call(
        functools.partial(encoder_kernel, counts, query_cols // key_cols),
        out_shape=jax.ShapeDtypeStruct((length, query_cols), jnp.bfloat16),
        in_specs=[SM, SM, VM, VM] + [HB] * len(pieces),
        out_specs=VM,
        scratch_shapes=[
            pltpu.VMEM((width, joined), jnp.bfloat16),
            pltpu.VMEM((length, joined), jnp.bfloat16),
            pltpu.SemaphoreType.DMA((len(pieces),)),
        ],
        compiler_params=params(),
        name="encoder_attention",
    )(
        jnp.stack([first for _, first in pieces]),
        block_counts,
        normed,
        history,
        *[piece for piece, _ in pieces],
    )


def project_kernel(count, groups, first_ref, share_ref, attended_ref, *refs):
    pieces, outs, (whole, sems) = refs[:count], refs[count:-2], refs[-2:]
    copies = load_pieces(pieces, first_ref, 0, whole, slice(None), sems)
    share = outs[0].shape[0] // groups
    for copy in copies:
        copy.wait()
    for index, out_ref in enumerate(outs):
        parts = []
        for group in range(groups):
            first = pl.multiple_of(share_ref[index * groups + group] * share, share)
            parts.append(attended_ref[pl.ds(first, share), :])
        rows = jnp.concatenate(parts, axis=0)
        out_ref[...] = lax.dot_general(
            rows, whole[...], (((1,), (1,)), ((), ())), preferred_element_type=jnp.float32
        ).astype(jnp.bfloat16)


def project_out(attended, pieces, orders):
    length, cols = attended.shape
    groups = lax.axis_size("tp")
    share = length // (groups * len(orders))
    width = sum(piece.shape[0] for piece, _ in pieces)
    shape = jax.ShapeDtypeStruct((groups * share, width), jnp.bfloat16)
    return pl.pallas_call(
        functools.partial(project_kernel, len(pieces), groups),
        out_shape=tuple([shape] * len(orders)),
        in_specs=[SM, SM, VM] + [HB] * len(pieces),
        out_specs=tuple([VM] * len(orders)),
        scratch_shapes=[
            pltpu.VMEM((width, cols), jnp.bfloat16),
            pltpu.SemaphoreType.DMA((len(pieces),)),
        ],
        compiler_params=params(),
        name="project_out",
    )(
        jnp.stack([first for _, first in pieces]),
        jnp.stack([where for order in orders for where in order]),
        attended,
        *[piece for piece, _ in pieces],
    )


def merge_kernel(count, place_ref, gain_ref, source_ref, *refs):
    terms, (encoded_ref, crossed_ref) = refs[:count], refs[count:]
    rows = encoded_ref.shape[0]
    first = pl.multiple_of(place_ref[0], rows)
    total = source_ref[pl.ds(first, rows), :].astype(jnp.float32)
    for term in terms:
        total = total + term[...].astype(jnp.float32)
    encoded_ref[...] = total.astype(jnp.bfloat16)
    square = jnp.mean(total * total, axis=-1, keepdims=True)
    crossed_ref[...] = (total * lax.rsqrt(square + eps) * gain_ref[...]).astype(jnp.bfloat16)


def merge_terms(source, terms, place, gain):
    shape = jax.ShapeDtypeStruct(terms[0].shape, jnp.bfloat16)
    return pl.pallas_call(
        functools.partial(merge_kernel, len(terms)),
        out_shape=(shape, shape),
        in_specs=[SM] + [VM] * (2 + len(terms)),
        out_specs=(VM, VM),
        compiler_params=params(),
        name="merge_terms",
    )(place[None], gain[None, :], source, *terms)


def cross_kernel(row_count, count, first_ref, place_ref, *refs):
    rows_refs, pieces = refs[:row_count], refs[row_count : row_count + count]
    out_ref, whole, sems = refs[row_count + count :]
    copies = load_pieces(pieces, first_ref, 0, whole, slice(None), sems)
    for copy in copies:
        copy.wait()
    rows = rows_refs[0].shape[0]
    for index, rows_ref in enumerate(rows_refs):
        first = pl.multiple_of(place_ref[index] * rows, rows)
        out_ref[pl.ds(first, rows), :] = jnp.dot(
            rows_ref[...], whole[...], preferred_element_type=jnp.float32
        ).astype(jnp.bfloat16)


def cross_project(row_pieces, pieces):
    width = row_pieces[0][0].shape[1]
    rows = row_pieces[0][0].shape[0]
    cols = pieces[0][0].shape[1]
    return pl.pallas_call(
        functools.partial(cross_kernel, len(row_pieces), len(pieces)),
        out_shape=jax.ShapeDtypeStruct((rows * len(row_pieces), cols), jnp.bfloat16),
        in_specs=[SM, SM] + [VM] * len(row_pieces) + [HB] * len(pieces),
        out_specs=VM,
        scratch_shapes=[
            pltpu.VMEM((width, cols), jnp.bfloat16),
            pltpu.SemaphoreType.DMA((len(pieces),)),
        ],
        compiler_params=params(),
        name="cross_project",
    )(
        jnp.stack([first for _, first in pieces]),
        jnp.stack([where for _, where in row_pieces]),
        *[rows for rows, _ in row_pieces],
        *[piece for piece, _ in pieces],
    )


def beam_kernel(
    level, count, last, ratio,
    live_ref, parent_ref, place_ref, gain_ref, query_ref, out_weight_ref, cross_ref, code_ref,
    *refs,
):
    inputs, outs, moved = refs[: count + 1 if level else 0], refs[count + 1 if level else 0 : -1], refs[-1]
    beams = code_ref.shape[0]
    code = code_ref[...].astype(jnp.float32)
    if level:
        total = inputs[0][...]
        for term in inputs[1:]:
            total = total + term[...].astype(jnp.float32)
        moved[...] = total
        rows = [moved[pl.ds(parent_ref[level - 1, row], 1), :] for row in range(beams)]
        hidden = jnp.concatenate(rows, axis=0) + code
    else:
        hidden = code
    square = jnp.mean(hidden * hidden, axis=-1, keepdims=True)
    normed = (hidden * lax.rsqrt(square + eps) * gain_ref[...]).astype(jnp.bfloat16)
    queries = jnp.dot(normed, query_ref[...], preferred_element_type=jnp.float32)
    queries = queries.astype(jnp.bfloat16)
    key_cols = cross_ref.shape[1] // 2
    events = cross_ref.shape[0]
    live = live_ref[0] * BLK
    attended = []
    for group in range(key_cols // DH):
        first = group * ratio
        stacked = jnp.concatenate(
            [queries[:, h * DH : (h + 1) * DH] for h in range(first, first + ratio)], axis=0
        )
        scores = lax.dot_general(
            stacked,
            cross_ref[:, group * DH : (group + 1) * DH],
            (((1,), (1,)), ((), ())),
            preferred_element_type=jnp.float32,
        )
        index = lax.broadcasted_iota(jnp.int32, scores.shape, 1)
        scores = jnp.where(index < live, scores, -1e30)
        top = jnp.max(scores, axis=-1, keepdims=True)
        raised = jnp.exp((scores - top) * DH ** (-0.5))
        weight = jnp.sum(raised, axis=-1, keepdims=True)
        mixed = jnp.dot(
            raised.astype(jnp.bfloat16),
            cross_ref[:, key_cols + group * DH : key_cols + (group + 1) * DH],
            preferred_element_type=jnp.float32,
        )
        mixed = (mixed / weight).astype(jnp.bfloat16)
        attended += [mixed[h * beams : (h + 1) * beams, :] for h in range(ratio)]
    terms = jnp.dot(
        jnp.concatenate(attended, axis=1), out_weight_ref[...], preferred_element_type=jnp.float32
    )
    if not last:
        outs[0][...] = hidden
        outs[1][...] = terms.astype(jnp.bfloat16)
    else:
        cols = outs[0].shape[1]
        moved[...] = terms
        for index in range(1, len(outs)):
            col = pl.ds(pl.multiple_of(place_ref[index] * cols, cols), cols)
            outs[index][...] = moved[:, col].astype(jnp.bfloat16)
        moved[...] = hidden + terms
        outs[0][...] = moved[:, pl.ds(pl.multiple_of(place_ref[0] * cols, cols), cols)]


def beam_step(level, live, parents, places, gain, query, out_weight, cross, code, inputs, last):
    beams, width = code.shape
    ratio = H // KVH
    if last:
        cols = width // len(places)
        outs = [jax.ShapeDtypeStruct((beams, cols), jnp.float32)] + [
            jax.ShapeDtypeStruct((beams, cols), jnp.bfloat16)
        ] * (len(places) - 1)
    else:
        outs = [
            jax.ShapeDtypeStruct((beams, width), jnp.float32),
            jax.ShapeDtypeStruct((beams, width), jnp.bfloat16),
        ]
    return pl.pallas_call(
        functools.partial(beam_kernel, level, max(len(inputs) - 1, 0), last, ratio),
        out_shape=tuple(outs),
        in_specs=[SM, SM, SM] + [VM] * (5 + len(inputs)),
        out_specs=tuple([VM] * len(outs)),
        scratch_shapes=[pltpu.VMEM((beams, width), jnp.float32)],
        compiler_params=params(),
        name=f"beam_step_{level}",
    )(live, parents, jnp.stack(places), gain[None, :], query, out_weight, cross, code, *inputs)


def shards(
    events,
    history_cache,
    block_counts,
    semantic_ids,
    beam_parents,
    query_weight,
    keyval_weight,
    out_weight,
    cross_weight,
    decoder_query,
    decoder_out,
    code_table,
    encoder_gain,
    cross_gain,
    decoder_gain,
):
    tp, kv = lax.axis_size("tp"), lax.axis_size("kv")
    my_tp, my_kv = lax.axis_index("tp"), lax.axis_index("kv")
    group, groups = my_tp * kv + my_kv, tp * kv

    keyval = jnp.concatenate([keyval_weight[0], keyval_weight[1]], axis=1)
    crossing = jnp.concatenate([cross_weight[0], cross_weight[1]], axis=1)
    query_pieces, query_steps = gather_rows(query_weight)
    keyval_pieces, keyval_steps = gather_rows(keyval)
    event_pieces, firsts = collect_events(events)
    normed, source = norm_events(event_pieces, firsts, encoder_gain)
    out_pieces, out_steps = gather_rows(after(out_weight, *query_steps[-1:]))
    cross_pieces, _ = gather_rows(after(crossing, *keyval_steps[-1:]))

    vocab_rows = code_table.shape[0]
    vocab_ids = group * vocab_rows + lax.broadcasted_iota(jnp.int32, (1, vocab_rows), 1)
    onehot = (semantic_ids.reshape(-1)[:, None] == vocab_ids).astype(jnp.bfloat16)
    codes = jnp.dot(onehot, code_table, preferred_element_type=jnp.float32).astype(jnp.bfloat16)
    for axis, size in (("kv", kv), ("tp", tp)):
        codes = sum([exchange(codes, axis, step) for step in range(1, size)], codes)
    steps, beams = semantic_ids.shape
    codes = codes.reshape(steps, beams, codes.shape[1])
    out_turned = decoder_out.T

    attended = encoder_attention(
        normed, history_cache[:, 0], block_counts, query_pieces, keyval_pieces
    )
    orders = [
        [partner(my_tp, d, tp) * kv + partner(my_kv, e, kv) for d in range(tp)] for e in range(kv)
    ]
    kept, *sent = project_out(attended, out_pieces, orders)
    arrived = [exchange(terms, "kv", e + 1) for e, terms in enumerate(sent)]
    share = attended.shape[0] // groups

    def summed(d):
        rows = slice(d * share, (d + 1) * share)
        return sum([a[rows].astype(jnp.float32) for a in arrived], kept[rows].astype(jnp.float32))

    terms = [exchange(summed(d).astype(jnp.bfloat16), "tp", d) for d in range(1, tp)]
    terms = [kept[:share]] + [a[:share] for a in arrived] + terms
    encoded, crossed = merge_terms(source, terms, group * share, cross_gain)
    cross = cross_project(gather_heads(crossed), cross_pieces)

    places = [group]
    moves = []
    for d in range(tp):
        for e in range(kv):
            if d or e:
                places.append(partner(my_tp, d, tp) * kv + partner(my_kv, e, kv))
                moves.append(
                    [
                        (a * kv + b, partner(a, d, tp) * kv + partner(b, e, kv))
                        for a in range(tp)
                        for b in range(kv)
                    ]
                )
    inputs = []
    for level in range(steps):
        last = level == steps - 1
        kept, *sent = beam_step(
            level, block_counts, beam_parents, places, decoder_gain, decoder_query, out_turned,
            cross, codes[level], inputs, last,
        )
        if not last:
            sent = sent * len(moves)
        arrived = [lax.ppermute(v, ("tp", "kv"), move) for v, move in zip(sent, moves)]
        inputs = [kept] + sent[:1] + arrived
    beam_out = sum([a.astype(jnp.float32) for a in arrived], kept).astype(jnp.bfloat16)
    return (encoded[None], beam_out)


def solution(mesh):
    in_specs = (
        P("groups", "seq", ("tp", "kv")),
        P(None, ("groups", "seq"), None, ("tp", "kv")),
        P(("groups", "seq")),
        P(None, ("groups", "seq")),
        P(None, ("groups", "seq")),
        P("seq", ("tp", "kv")),
        P(None, "seq", ("tp", "kv")),
        P("seq", ("tp", "kv")),
        P(None, "seq", ("tp", "kv")),
        P(None, ("tp", "kv")),
        P(None, ("tp", "kv")),
        P(("tp", "kv"), None),
        P(),
        P(),
        P(),
    )
    out_specs = (P(("groups", "seq"), ("tp", "kv"), None), P(("groups", "seq"), ("tp", "kv")))
    return jax.shard_map(shards, mesh=mesh, in_specs=in_specs, out_specs=out_specs, check_vma=False)
```

time: 447 us -> 215 us (0.48)
  waiting for transfers between devices: 333 us -> 112 us
  Pallas kernels: 0 us -> 46.9 us
  matrix products: 47.6 us -> 0.87 us
  starting transfers between devices: 0.55 us -> 34.1 us
  blocking collectives: 21.1 us -> 0 us
  between operations: 14.9 us -> 1.75 us
  other arithmetic: 17.9 us -> 6.61 us
    psum x5 -> x0, waiting for transfers between devices: 166 us -> none  [the longest x4 115 us: combine(): lax.psum(beam_terms.astype(jnp.bfloat16), ('tp', 'kv')).astype(jnp.float32)]
    all_gather x4 -> x0, waiting for transfers between devices: 166 us -> none  [the longest x1 80.3 us: shards(): lax.all_gather(joined, 'seq', axis=0, tiled=True)]
    ppermute x0 -> x49, waiting for transfers between devices: none -> 112 us  [the longest x15 62 us: shift(): lax.ppermute(value, axis, [(i, (i + step) % size) for i in range(size)])]
    pallas_call x0 -> x9, Pallas kernels: none -> 46.9 us  [the longest x4 18.2 us: beam_step(): pl.pallas_call(functools.partial(beam_kernel, level, max(len(inputs) - 1,...]
    dot_general x26 -> x1, matrix products: 47.6 us -> 0.87 us  [shards(): jnp.dot(onehot, code_table, preferred_element_type=jnp.float32)]
    ppermute x0 -> x49, starting transfers between devices: none -> 34.1 us  [the longest x22 18.6 us: exchange(): lax.ppermute(value, axis, [(i, partner(i, step, size)) for i in range(siz...]
    all_to_all x1 -> x0, blocking collectives: 21.1 us -> none  [shards(): lax.all_to_all(events, 'seq', split_axis=0, concat_axis=1, tiled=True)]
    reduce_sum x6 -> x0, other arithmetic: 9.15 us -> none  [root_norm(): mean_square = jnp.mean(values * values, axis=-1, keepdims=True)]
  transfers between devices with their start and end apart: 9 -> 49, of which waited for: 9 -> 28; matrix products, arithmetic and copies ran while one was open for 9% -> 6% of each run, Pallas kernels for 0% -> 9%
where the time goes in v1:
time: 215 us; the launch traced here: 214 us
  waiting for transfers between devices  112 us (52%)
  Pallas kernels  46.9 us (22%)
  starting transfers between devices  34.1 us (16%)
  local copies, waits for them, and re-layouts  12.2 us (6%)
  other arithmetic  6.61 us (3%)
    ppermute x15, waiting for transfers between devices, shift(): lax.ppermute(value, axis, [(i, (i + step) % size) for i in range(size)])  62 us
    ppermute x22, waiting for transfers between devices, exchange(): lax.ppermute(value, axis, [(i, partner(i, step, size)) for i in range(siz...  35.2 us
    ppermute x22, starting transfers between devices, exchange(): lax.ppermute(value, axis, [(i, partner(i, step, size)) for i in range(siz...  18.6 us
    pallas_call x4, Pallas kernels, beam_step(): pl.pallas_call(functools.partial(beam_kernel, level, max(len(inputs) - 1,...  18.2 us
    ppermute x12, waiting for transfers between devices, shards(): lax.ppermute(v, ('tp', 'kv'), move)  14.4 us
    pallas_call x1, Pallas kernels, encoder_attention(): pl.pallas_call(functools.partial(encoder_kernel, counts, query_cols // ke...  10.9 us
    ppermute x15, starting transfers between devices, shift(): lax.ppermute(value, axis, [(i, (i + step) % size) for i in range(size)])  8.07 us
    ppermute x12, starting transfers between devices, shards(): lax.ppermute(v, ('tp', 'kv'), move)  7.51 us
  transfers between devices with their start and end apart: 49, of which 28 were waited for; matrix products, arithmetic and copies ran while one was open for 6% of the time, Pallas kernels for 9%

profile of v1, /device:TPU:0, one launch (start us, length us, event | category | flops | bytes accessed | tf_op | source)
XLA Modules:
  0.0 214.1 jit_solution(8675648660443584358)
XLA Ops:
  0.6 1.0 constant_dynamic-slice_fusion.2
  1.7 3.1 %collective-permute-start.6 = (bf16[256,512]{1,0:T(8,128)(2,1)S(1)}, bf16[256,512]{1,0:T(8,128)(2,1)S(1)}, u32[]{:S(2)}, u32[]{:S(2)}) collective-permute-start(bf16[256,512]{1,0:T(8,128)(2,1)S(1)} %constant_dynamic-slice_fusion.2), channel_id=1, source_target_pairs={{0,4},{4,8},{8,12},{12,0},{1,5},{5,9},{9,13},{13,1},{2,6},{6,10},{... | collective-permute-start | bytes 786440 | tf_op jit(solution)/shard_map/ppermute | solution.py:48
  4.8 8.3 %collective-permute-done.6.refs_1_ = bf16[256,512]{1,0:T(8,128)(2,1)S(1)} collective-permute-done((bf16[256,512]{1,0:T(8,128)(2,1)S(1)}, bf16[256,512]{1,0:T(8,128)(2,1)S(1)}, u32[]{:S(2)}, u32[]{:S(2)}) %collective-permute-start.6) | collective-permute-done | bytes 262176 | tf_op jit(solution)/shard_map/ppermute | solution.py:48
  13.1 1.2 dynamic-slice_bitcast_fusion.3
  14.3 3.8 %collective-permute-start.2 = (bf16[128,512]{1,0:T(8,128)(2,1)S(1)}, bf16[128,512]{1,0:T(8,128)(2,1)S(1)}, u32[]{:S(2)}, u32[]{:S(2)}) collective-permute-start(bf16[128,512]{1,0:T(8,128)(2,1)S(1)} %get-tuple-element.44), channel_id=1, source_target_pairs={{0,12},{4,0},{8,4},{12,8},{1,13},{5,1},{9,5},{13,9},{2,14},{6,2},{... | collective-permute-start | bytes 393224 | tf_op jit(solution)/shard_map/ppermute | solution.py:48
  18.8 6.0 %collective-permute-done.2 = bf16[128,512]{1,0:T(8,128)(2,1)S(1)} collective-permute-done((bf16[128,512]{1,0:T(8,128)(2,1)S(1)}, bf16[128,512]{1,0:T(8,128)(2,1)S(1)}, u32[]{:S(2)}, u32[]{:S(2)}) %collective-permute-start.2) | collective-permute-done | bytes 131104 | tf_op jit(solution)/shard_map/ppermute | solution.py:48
  24.7 8.4 %collective-permute-done.1 = bf16[128,512]{1,0:T(8,128)(2,1)S(1)} collective-permute-done((bf16[128,512]{1,0:T(8,128)(2,1)S(1)}, bf16[128,512]{1,0:T(8,128)(2,1)S(1)}, u32[]{:S(2)}, u32[]{:S(2)}) %collective-permute-start.1) | collective-permute-done | bytes 131104 | tf_op jit(solution)/shard_map/ppermute | solution.py:48
  33.2 1.6 collective-permute-start.3
  35.0 1.6 collective-permute-start.7
  36.6 9.2 %collective-permute-done.10.refs_5_ = bf16[256,512]{1,0:T(8,128)(2,1)S(1)} collective-permute-done((bf16[256,512]{1,0:T(8,128)(2,1)S(1)}, bf16[256,512]{1,0:T(8,128)(2,1)S(1)}, u32[]{:S(2)}, u32[]{:S(2)}) %collective-permute-start.10) | collective-permute-done | bytes 262176 | tf_op jit(solution)/shard_map/ppermute | solution.py:48
  45.9 5.5 %collective-permute-done.12.refs_8_ = bf16[256,512]{1,0:T(8,128)(2,1)S(1)} collective-permute-done((bf16[256,512]{1,0:T(8,128)(2,1)S(1)}, bf16[256,512]{1,0:T(8,128)(2,1)S(1)}, u32[]{:S(2)}, u32[]{:S(2)}) %collective-permute-start.12) | collective-permute-done | bytes 262176 | tf_op jit(solution)/shard_map/ppermute | solution.py:48
  51.4 1.5 collective-permute-start.13
  53.0 3.8 %collective-permute-done.18.refs_1_ = bf16[256,512]{1,0:T(8,128)(2,1)S(1)} collective-permute-done((bf16[256,512]{1,0:T(8,128)(2,1)S(1)}, bf16[256,512]{1,0:T(8,128)(2,1)S(1)}, u32[]{:S(2)}, u32[]{:S(2)}) %collective-permute-start.18) | collective-permute-done | bytes 262176 | tf_op jit(solution)/shard_map/ppermute | solution.py:48
  56.8 1.9 collective-permute-done.13.refs_9_
  58.8 1.5 collective-permute-start.9
  60.3 3.6 %collective-permute-done.14.refs_10_ = bf16[256,512]{1,0:T(8,128)(2,1)} collective-permute-done((bf16[256,512]{1,0:T(8,128)(2,1)S(1)}, bf16[256,512]{1,0:T(8,128)(2,1)}, u32[]{:S(2)}, u32[]{:S(2)}) %collective-permute-start.14) | collective-permute-done | bytes 262176 | tf_op jit(solution)/shard_map/ppermute | solution.py:48
  63.9 0.8 collective-permute-start.15
  64.7 4.8 %collective-permute-done.20.refs_3_ = bf16[256,512]{1,0:T(8,128)(2,1)} collective-permute-done((bf16[256,512]{1,0:T(8,128)(2,1)S(1)}, bf16[256,512]{1,0:T(8,128)(2,1)}, u32[]{:S(2)}, u32[]{:S(2)}) %collective-permute-start.20) | collective-permute-done | bytes 262176 | tf_op jit(solution)/shard_map/ppermute | solution.py:48
  69.6 0.8 collective-permute-start.11
  70.4 4.8 %collective-permute-done.16.refs_12_ = bf16[256,512]{1,0:T(8,128)(2,1)} collective-permute-done((bf16[256,512]{1,0:T(8,128)(2,1)}, bf16[256,512]{1,0:T(8,128)(2,1)}, u32[]{:S(2)}, u32[]{:S(2)}) %collective-permute-start.16) | collective-permute-done | bytes 262176 | tf_op jit(solution)/shard_map/ppermute | solution.py:48
  75.2 0.7 collective-permute-start.17
  76.0 1.3 collective-permute-start.19
  77.3 0.7 collective-permute-start.21
  78.1 1.5 collective-permute-start.23
  82.8 0.8 pad_maximum_fusion.refs_7_
  83.6 4.3 %norm_events.1 = (bf16[512,2048]{1,0:T(8,128)(2,1)}, bf16[512,2048]{1,0:T(8,128)(2,1)}) custom-call(s32[4]{0:T(128)} %get-tuple-element.50.col_ref, s32[4]{0:T(128)} %get-tuple-element.51.row_ref, f32[1,2048]{1,0:T(1,128)} %bitcast.52, bf16[512,512]{1,0:T(8,128)(2,1)} %copy-done.3, bf16[512,512]{1,0:T(8,128)(2,1)} %copy-done.12, ...), custom_call_target="tpu_custom_call" | custom-call | tf_op jit(solution)/shard_map/norm_events/pallas_call | solution.py:134
  87.9 10.9 %encoder_attention.1.attended_ref = bf16[512,512]{1,0:T(8,128)(2,1)} custom-call(s32[14]{0:T(128)} %stack.144.first_ref, s32[1]{0:T(128)S(6)} %copy.18.live_ref, bf16[512,2048]{1,0:T(8,128)(2,1)} %get-tuple-element.21.normed_ref, bf16[2,512,256]{2,1,0:T(8,128)(2,1)} %bitcast.47, bf16[512,512]{1,0:T(8,128)(2,1)} %refs_0_.1, bf16[256,512]{1,0:T(8,128)(2,1)} %copy-done.15, ...), custom_call_target="tpu_custom_call" | custom-call | tf_op jit(solution)/shard_map/encoder_attention/pallas_call | solution.py:235
  98.9 5.0 %project_out.1 = (bf16[256,2048]{1,0:T(8,128)(2,1)}, bf16[256,2048]{1,0:T(8,128)(2,1)}) custom-call(s32[7]{0:T(128)} %stack.67.first_ref, s32[4]{0:T(128)} %add_add_fusion.share_ref.place_ref, bf16[512,512]{1,0:T(8,128)(2,1)} %encoder_attention.1.attended_ref, bf16[512,512]{1,0:T(8,128)(2,1)} %refs_0_.2, bf16[256,512]{1,0:T(8,128)(2,1)} %copy-done.18, ...), custom_call_target="tpu_custom_call" | custom-call | tf_op jit(solution)/shard_map/project_out/pallas_call | solution.py:279
  104.0 2.9 %collective-permute-done.24 = bf16[256,2048]{1,0:T(8,128)(2,1)S(1)} collective-permute-done((bf16[256,2048]{1,0:T(8,128)(2,1)}, bf16[256,2048]{1,0:T(8,128)(2,1)S(1)}, u32[]{:S(2)}, u32[]{:S(2)}) %collective-permute-start.24) | collective-permute-done | bytes 1048608 | tf_op jit(solution)/shard_map/ppermute | solution.py:43
  106.8 1.3 add_convert_fusion
  109.2 0.8 slice.42.refs_0_
  110.0 0.8 slice.52.refs_1_
  110.9 11.4 %collective-permute-done.25.refs_2_ = bf16[128,2048]{1,0:T(8,128)(2,1)} collective-permute-done((bf16[128,2048]{1,0:T(8,128)(2,1)S(1)}, bf16[128,2048]{1,0:T(8,128)(2,1)}, u32[]{:S(2)}, u32[]{:S(2)}) %collective-permute-start.25) | collective-permute-done | bytes 524320 | tf_op jit(solution)/shard_map/ppermute | solution.py:43
  122.2 3.3 %merge_terms.1 = (bf16[128,2048]{1,0:T(8,128)(2,1)}, bf16[128,2048]{1,0:T(8,128)(2,1)}) custom-call(s32[1]{0:T(128)} %bitcast.place_ref, f32[1,2048]{1,0:T(1,128)} %bitcast.53, bf16[512,2048]{1,0:T(8,128)(2,1)} %get-tuple-element.20.source_ref, bf16[128,2048]{1,0:T(8,128)(2,1)} %slice.42.refs_0_, bf16[128,2048]{1,0:T(8,128)(2,1)} %slice.52.refs_1_, ...), custom_call_target="tpu_custom_call" | custom-call | tf_op jit(solution)/shard_map/merge_terms/pallas_call | solution.py:312
  126.1 0.9 convolution_convert_fusion
  127.2 1.4 collective-permute-done.35
  128.7 1.6 collective-permute-start.36
  130.2 7.5 %collective-permute-done.31.refs_7_ = bf16[256,512]{1,0:T(8,128)(2,1)} collective-permute-done((bf16[256,512]{1,0:T(8,128)(2,1)S(1)}, bf16[256,512]{1,0:T(8,128)(2,1)}, u32[]{:S(2)}, u32[]{:S(2)}) %collective-permute-start.31) | collective-permute-done | bytes 262176 | tf_op jit(solution)/shard_map/ppermute | solution.py:48
  137.7 2.5 %copy.17 = bf16[2048,512]{0,1:T(8,128)(2,1)} copy(bf16[2048,512]{1,0:T(8,128)(2,1)S(1)} %copy-done.2) | data formatting | bytes 4194304 | tf_op args[10]
  141.4 3.3 %collective-permute-done.36 = bf16[64,2048]{1,0:T(8,128)(2,1)} collective-permute-done((bf16[64,2048]{1,0:T(8,128)(2,1)S(1)}, bf16[64,2048]{1,0:T(8,128)(2,1)}, u32[]{:S(2)}, u32[]{:S(2)}) %collective-permute-start.36) | collective-permute-done | bytes 262176 | tf_op jit(solution)/shard_map/ppermute | solution.py:43
  144.7 1.0 add.179
  145.7 1.6 collective-permute-start.30
  147.8 1.5 collective-permute-start.34
  149.3 0.7 fusion.4
  150.0 5.2 %collective-permute-done.30.refs_6_ = bf16[256,512]{1,0:T(8,128)(2,1)S(1)} collective-permute-done((bf16[256,512]{1,0:T(8,128)(2,1)}, bf16[256,512]{1,0:T(8,128)(2,1)S(1)}, u32[]{:S(2)}, u32[]{:S(2)}) %collective-permute-start.30) | collective-permute-done | bytes 262176 | tf_op jit(solution)/shard_map/ppermute | solution.py:43
  155.2 5.6 %collective-permute-done.32.refs_8_ = bf16[256,512]{1,0:T(8,128)(2,1)S(1)} collective-permute-done((bf16[256,512]{1,0:T(8,128)(2,1)}, bf16[256,512]{1,0:T(8,128)(2,1)S(1)}, u32[]{:S(2)}, u32[]{:S(2)}) %collective-permute-start.32) | collective-permute-done | bytes 262176 | tf_op jit(solution)/shard_map/ppermute | solution.py:43
  160.8 3.0 %collective-permute-done.34.refs_10_ = bf16[256,512]{1,0:T(8,128)(2,1)S(1)} collective-permute-done((bf16[256,512]{1,0:T(8,128)(2,1)}, bf16[256,512]{1,0:T(8,128)(2,1)S(1)}, u32[]{:S(2)}, u32[]{:S(2)}) %collective-permute-start.34) | collective-permute-done | bytes 262176 | tf_op jit(solution)/shard_map/ppermute | solution.py:43
  164.7 0.8 copy-done.9
  165.5 5.2 %cross_project.1.cross_ref = bf16[512,512]{1,0:T(8,128)(2,1)} custom-call(s32[7]{0:T(128)} %stack.67.first_ref, s32[4]{0:T(128)} %add_add_fusion.share_ref.place_ref, bf16[128,2048]{1,0:T(8,128)(2,1)} %get-tuple-element.26.refs_0_, bf16[128,2048]{1,0:T(8,128)(2,1)} %copy-done.7, bf16[128,2048]{1,0:T(8,128)(2,1)} %copy-done.8, bf16[128,2048]{1,0:T(8,128)(2,1)} %copy-done.9, ...), custom_call_target="tpu_custom_call" | custom-call | tf_op jit(solution)/shard_map/cross_project/pallas_call | solution.py:340
  170.7 4.4 %beam_step_0.1 = (f32[16,2048]{1,0:T(8,128)}, bf16[16,2048]{1,0:T(8,128)(2,1)}) custom-call(s32[1]{0:T(128)S(6)} %copy.18.live_ref, s32[3,16]{1,0:T(4,128)} %parent_ref.7, s32[4]{0:T(128)} %add_add_fusion.1.place_ref, f32[1,2048]{1,0:T(1,128)} %bitcast.48, bf16[2048,512]{1,0:T(8,128)(2,1)} %query_ref.7, bf16[512,2048]{1,0:T(8,128)(2,1)} %bitcast.43, ...), custom_call_target="tpu_custom_call" | custom-call | tf_op jit(solution)/shard_map/beam_step_0/pallas_call | solution.py:436
  175.6 1.3 collective-permute-start.39
  176.9 3.2 %collective-permute-done.38.refs_3_ = bf16[16,2048]{1,0:T(8,128)(2,1)S(1)} collective-permute-done((bf16[16,2048]{1,0:T(8,128)(2,1)}, bf16[16,2048]{1,0:T(8,128)(2,1)S(1)}, u32[]{:S(2)}, u32[]{:S(2)}) %collective-permute-start.38) | collective-permute-done | bytes 65568 | tf_op jit(solution)/shard_map/ppermute | solution.py:528
  181.4 4.6 %beam_step_1.1 = (f32[16,2048]{1,0:T(8,128)}, bf16[16,2048]{1,0:T(8,128)(2,1)}) custom-call(s32[1]{0:T(128)S(6)} %copy.18.live_ref, s32[3,16]{1,0:T(4,128)} %parent_ref.7, s32[4]{0:T(128)} %add_add_fusion.1.place_ref, f32[1,2048]{1,0:T(1,128)} %bitcast.49, bf16[2048,512]{1,0:T(8,128)(2,1)} %query_ref.7, bf16[512,2048]{1,0:T(8,128)(2,1)} %bitcast.44, ...), custom_call_target="tpu_custom_call" | custom-call | tf_op jit(solution)/shard_map/beam_step_1/pallas_call | solution.py:436
  186.8 1.1 collective-permute-start.42
  187.9 3.5 %collective-permute-done.41.refs_3_ = bf16[16,2048]{1,0:T(8,128)(2,1)S(1)} collective-permute-done((bf16[16,2048]{1,0:T(8,128)(2,1)}, bf16[16,2048]{1,0:T(8,128)(2,1)S(1)}, u32[]{:S(2)}, u32[]{:S(2)}) %collective-permute-start.41) | collective-permute-done | bytes 65568 | tf_op jit(solution)/shard_map/ppermute | solution.py:528
  192.2 4.6 %beam_step_2.1 = (f32[16,2048]{1,0:T(8,128)}, bf16[16,2048]{1,0:T(8,128)(2,1)}) custom-call(s32[1]{0:T(128)S(6)} %copy.18.live_ref, s32[3,16]{1,0:T(4,128)} %parent_ref.7, s32[4]{0:T(128)} %add_add_fusion.1.place_ref, f32[1,2048]{1,0:T(1,128)} %bitcast.50, bf16[2048,512]{1,0:T(8,128)(2,1)} %query_ref.7, bf16[512,2048]{1,0:T(8,128)(2,1)} %bitcast.45, ...), custom_call_target="tpu_custom_call" | custom-call | tf_op jit(solution)/shard_map/beam_step_2/pallas_call | solution.py:436
  197.2 0.8 collective-permute-start.44
  198.7 3.5 %collective-permute-done.44.refs_3_ = bf16[16,2048]{1,0:T(8,128)(2,1)S(1)} collective-permute-done((bf16[16,2048]{1,0:T(8,128)(2,1)}, bf16[16,2048]{1,0:T(8,128)(2,1)S(1)}, u32[]{:S(2)}, u32[]{:S(2)}) %collective-permute-start.44) | collective-permute-done | bytes 65568 | tf_op jit(solution)/shard_map/ppermute | solution.py:528
  203.3 4.6 %beam_step_3.1 = (f32[16,512]{1,0:T(8,128)}, bf16[16,512]{1,0:T(8,128)(2,1)}, bf16[16,512]{1,0:T(8,128)(2,1)}, bf16[16,512]{1,0:T(8,128)(2,1)}) custom-call(s32[1]{0:T(128)S(6)} %copy.18.live_ref, s32[3,16]{1,0:T(4,128)} %parent_ref.7, s32[4]{0:T(128)} %add_add_fusion.1.place_ref, f32[1,2048]{1,0:T(1,128)} %bitcast.51, bf16[2048,512]{1,0:T(8,128)(2,1)} %query_ref.7, ...), custom_call_target="tpu_custom_call" | custom-call | tf_op jit(solution)/shard_map/beam_step_3/pallas_call | solution.py:436
  207.9 0.9 collective-permute-start.48
  208.8 1.0 collective-permute-start.47
  209.8 1.4 collective-permute-done.48
  211.3 1.5 collective-permute-done.47
  212.7 1.4 add_convert_fusion.1
  (141 shorter events, 13.8 us)
Async XLA Ops:
  0.6 34.1 %copy-start.10 = (bf16[2,512,256]{2,1,0:T(8,128)(2,1)S(1)}, bf16[2,512,256]{2,1,0:T(8,128)(2,1)}, u32[]{:S(2)}) copy-start(bf16[2,512,256]{2,1,0:T(8,128)(2,1)} %param.21) | copy-start | bytes 1572868
  1.7 44.1 %copy-start.4 = (bf16[512,512]{1,0:T(8,128)(2,1)S(1)}, bf16[512,512]{1,0:T(8,128)(2,1)}, u32[]{:S(2)}) copy-start(bf16[512,512]{1,0:T(8,128)(2,1)} %refs_0_.2) | copy-start | bytes 1572868
  1.7 11.4 %collective-permute-start.6 = (bf16[256,512]{1,0:T(8,128)(2,1)S(1)}, bf16[256,512]{1,0:T(8,128)(2,1)S(1)}, u32[]{:S(2)}, u32[]{:S(2)}) collective-permute-start(bf16[256,512]{1,0:T(8,128)(2,1)S(1)} %constant_dynamic-slice_fusion.2), channel_id=1, source_target_pairs={{0,4},{4,8},{8,12},{12,0},{1,5},{5,9},{9,13},{13,1},{2,6},{6,10},{... | collective-permute-start | bytes 786440 | tf_op jit(solution)/shard_map/ppermute | solution.py:48
  13.1 32.7 %copy-start.15 = (bf16[256,512]{1,0:T(8,128)(2,1)}, bf16[256,512]{1,0:T(8,128)(2,1)S(1)}, u32[]{:S(2)}) copy-start(bf16[256,512]{1,0:T(8,128)(2,1)S(1)} %collective-permute-done.6.refs_1_) | copy-start | bytes 786436
  13.1 21.7 %collective-permute-start.8 = (bf16[256,512]{1,0:T(8,128)(2,1)S(1)}, bf16[256,512]{1,0:T(8,128)(2,1)S(1)}, u32[]{:S(2)}, u32[]{:S(2)}) collective-permute-start(bf16[256,512]{1,0:T(8,128)(2,1)S(1)} %collective-permute-done.6.refs_1_), channel_id=1, source_target_pairs={{0,4},{4,8},{8,12},{12,0},{1,5},{5,9},{9,13},{13,1},{2,6},{6,10},{... | collective-permute-start | bytes 786440 | tf_op jit(solution)/shard_map/ppermute | solution.py:48
  14.3 10.4 %collective-permute-start.2 = (bf16[128,512]{1,0:T(8,128)(2,1)S(1)}, bf16[128,512]{1,0:T(8,128)(2,1)S(1)}, u32[]{:S(2)}, u32[]{:S(2)}) collective-permute-start(bf16[128,512]{1,0:T(8,128)(2,1)S(1)} %get-tuple-element.44), channel_id=1, source_target_pairs={{0,12},{4,0},{8,4},{12,8},{1,13},{5,1},{9,5},{13,9},{2,14},{6,2},{... | collective-permute-start | bytes 393224 | tf_op jit(solution)/shard_map/ppermute | solution.py:48
  18.1 15.0 %collective-permute-start.1 = (bf16[128,512]{1,0:T(8,128)(2,1)S(1)}, bf16[128,512]{1,0:T(8,128)(2,1)S(1)}, u32[]{:S(2)}, u32[]{:S(2)}) collective-permute-start(bf16[128,512]{1,0:T(8,128)(2,1)S(1)} %get-tuple-element.45), channel_id=1, source_target_pairs={{0,8},{4,12},{8,0},{12,4},{1,9},{5,13},{9,1},{13,5},{2,10},{6,14},... | collective-permute-start | bytes 393224 | tf_op jit(solution)/shard_map/ppermute | solution.py:48
  18.1 15.0 %collective-permute-start = (bf16[128,512]{1,0:T(8,128)(2,1)S(1)}, bf16[128,512]{1,0:T(8,128)(2,1)S(1)}, u32[]{:S(2)}, u32[]{:S(2)}) collective-permute-start(bf16[128,512]{1,0:T(8,128)(2,1)S(1)} %get-tuple-element.43), channel_id=1, source_target_pairs={{0,4},{4,8},{8,12},{12,0},{1,5},{5,9},{9,13},{13,1},{2,6},{6,10},{... | collective-permute-start | bytes 393224 | tf_op jit(solution)/shard_map/ppermute | solution.py:48
  33.2 50.4 %copy-start.3 = (bf16[512,512]{1,0:T(8,128)(2,1)}, bf16[512,512]{1,0:T(8,128)(2,1)S(1)}, u32[]{:S(2)}) copy-start(bf16[512,512]{1,0:T(8,128)(2,1)S(1)} %pad_maximum_fusion.1.refs_0_) | copy-start | bytes 1572868
  33.2 19.8 %collective-permute-start.3 = (bf16[512,512]{1,0:T(8,128)(2,1)S(1)}, bf16[512,512]{1,0:T(8,128)(2,1)S(1)}, u32[]{:S(2)}, u32[]{:S(2)}) collective-permute-start(bf16[512,512]{1,0:T(8,128)(2,1)S(1)} %pad_maximum_fusion.1.refs_0_), channel_id=1, source_target_pairs={{0,2},{2,0},{1,3},{3,1},{4,6},{6,4},{5,7},{7,5},{8,10},{10,8},{9,1... | collective-permute-start | bytes 1572872 | tf_op jit(solution)/shard_map/ppermute | solution.py:43
  34.8 53.1 %copy-start.16 = (bf16[256,512]{1,0:T(8,128)(2,1)}, bf16[256,512]{1,0:T(8,128)(2,1)S(1)}, u32[]{:S(2)}) copy-start(bf16[256,512]{1,0:T(8,128)(2,1)S(1)} %collective-permute-done.8.refs_3_) | copy-start | bytes 786436
  34.8 11.0 %collective-permute-start.10 = (bf16[256,512]{1,0:T(8,128)(2,1)S(1)}, bf16[256,512]{1,0:T(8,128)(2,1)S(1)}, u32[]{:S(2)}, u32[]{:S(2)}) collective-permute-start(bf16[256,512]{1,0:T(8,128)(2,1)S(1)} %collective-permute-done.8.refs_3_), channel_id=1, source_target_pairs={{0,4},{4,8},{8,12},{12,0},{1,5},{5,9},{9,13},{13,1},{2,6},{6,10},{... | collective-permute-start | bytes 786440 | tf_op jit(solution)/shard_map/ppermute | solution.py:48
  34.9 16.6 %collective-permute-start.12 = (bf16[256,512]{1,0:T(8,128)(2,1)S(1)}, bf16[256,512]{1,0:T(8,128)(2,1)S(1)}, u32[]{:S(2)}, u32[]{:S(2)}) collective-permute-start(bf16[256,512]{1,0:T(8,128)(2,1)S(1)} %fusion), channel_id=1, source_target_pairs={{0,4},{4,8},{8,12},{12,0},{1,5},{5,9},{9,13},{13,1},{2,6},{6,10},{... | collective-permute-start | bytes 786440 | tf_op jit(solution)/shard_map/ppermute | solution.py:48
  35.0 28.9 %collective-permute-start.4 = (bf16[512,512]{1,0:T(8,128)(2,1)S(1)}, bf16[512,512]{1,0:T(8,128)(2,1)S(1)}, u32[]{:S(2)}, u32[]{:S(2)}) collective-permute-start(bf16[512,512]{1,0:T(8,128)(2,1)S(1)} %pad_maximum_fusion.1.refs_0_), channel_id=1, source_target_pairs={{0,1},{1,0},{2,3},{3,2},{4,5},{5,4},{6,7},{7,6},{8,9},{9,8},{10,11... | collective-permute-start | bytes 1572872 | tf_op jit(solution)/shard_map/ppermute | solution.py:43
  35.0 17.9 %collective-permute-start.7 = (bf16[256,512]{1,0:T(8,128)(2,1)S(1)}, bf16[256,512]{1,0:T(8,128)(2,1)S(1)}, u32[]{:S(2)}, u32[]{:S(2)}) collective-permute-start(bf16[256,512]{1,0:T(8,128)(2,1)S(1)} %collective-permute-done.6.refs_1_), channel_id=1, source_target_pairs={{0,16},{16,0},{1,17},{17,1},{2,18},{18,2},{3,19},{19,3},{4,20},{20... | collective-permute-start | bytes 786440 | tf_op jit(solution)/shard_map/ppermute | solution.py:43
  45.8 42.1 %copy-start.17 = (bf16[256,512]{1,0:T(8,128)(2,1)}, bf16[256,512]{1,0:T(8,128)(2,1)S(1)}, u32[]{:S(2)}) copy-start(bf16[256,512]{1,0:T(8,128)(2,1)S(1)} %collective-permute-done.10.refs_5_) | copy-start | bytes 786436
  45.8 11.0 %collective-permute-start.18 = (bf16[256,512]{1,0:T(8,128)(2,1)S(1)}, bf16[256,512]{1,0:T(8,128)(2,1)S(1)}, u32[]{:S(2)}, u32[]{:S(2)}) collective-permute-start(bf16[256,512]{1,0:T(8,128)(2,1)S(1)} %constant_dynamic-slice_fusion.1), channel_id=1, source_target_pairs={{0,4},{4,8},{8,12},{12,0},{1,5},{5,9},{9,13},{13,1},{2,6},{6,10},{... | collective-permute-start | bytes 786440 | tf_op jit(solution)/shard_map/ppermute | solution.py:48
  51.4 18.1 %copy-start.19 = (bf16[256,512]{1,0:T(8,128)(2,1)}, bf16[256,512]{1,0:T(8,128)(2,1)S(1)}, u32[]{:S(2)}) copy-start(bf16[256,512]{1,0:T(8,128)(2,1)S(1)} %collective-permute-done.12.refs_8_) | copy-start | bytes 786436
  51.4 7.3 %collective-permute-start.13 = (bf16[256,512]{1,0:T(8,128)(2,1)S(1)}, bf16[256,512]{1,0:T(8,128)(2,1)S(1)}, u32[]{:S(2)}, u32[]{:S(2)}) collective-permute-start(bf16[256,512]{1,0:T(8,128)(2,1)S(1)} %collective-permute-done.12.refs_8_), channel_id=1, source_target_pairs={{0,16},{16,0},{1,17},{17,1},{2,18},{18,2},{3,19},{19,3},{4,20},{20... | collective-permute-start | bytes 786440 | tf_op jit(solution)/shard_map/ppermute | solution.py:43
  52.9 16.6 %copy-start.20 = (bf16[256,512]{1,0:T(8,128)(2,1)}, bf16[256,512]{1,0:T(8,128)(2,1)S(1)}, u32[]{:S(2)}) copy-start(bf16[256,512]{1,0:T(8,128)(2,1)S(1)} %collective-permute-done.7.refs_2_) | copy-start | bytes 786436
  52.9 10.9 %collective-permute-start.14 = (bf16[256,512]{1,0:T(8,128)(2,1)S(1)}, bf16[256,512]{1,0:T(8,128)(2,1)}, u32[]{:S(2)}, u32[]{:S(2)}) collective-permute-start(bf16[256,512]{1,0:T(8,128)(2,1)S(1)} %collective-permute-done.12.refs_8_), channel_id=1, source_target_pairs={{0,4},{4,8},{8,12},{12,0},{1,5},{5,9},{9,13},{13,1},{2,6},{6,10},{... | collective-permute-start | bytes 786440 | tf_op jit(solution)/shard_map/ppermute | solution.py:48
  53.0 30.6 %copy-start.12 = (bf16[512,512]{1,0:T(8,128)(2,1)}, bf16[512,512]{1,0:T(8,128)(2,1)S(1)}, u32[]{:S(2)}) copy-start(bf16[512,512]{1,0:T(8,128)(2,1)S(1)} %collective-permute-done.3.refs_1_) | copy-start | bytes 1572868
  53.0 24.3 %collective-permute-start.5 = (bf16[512,512]{1,0:T(8,128)(2,1)S(1)}, bf16[512,512]{1,0:T(8,128)(2,1)S(1)}, u32[]{:S(2)}, u32[]{:S(2)}) collective-permute-start(bf16[512,512]{1,0:T(8,128)(2,1)S(1)} %collective-permute-done.3.refs_1_), channel_id=1, source_target_pairs={{0,1},{1,0},{2,3},{3,2},{4,5},{5,4},{6,7},{7,6},{8,9},{9,8},{10,11... | collective-permute-start | bytes 1572872 | tf_op jit(solution)/shard_map/ppermute | solution.py:43
  56.8 42.1 %copy-start.18 = (bf16[256,512]{1,0:T(8,128)(2,1)}, bf16[256,512]{1,0:T(8,128)(2,1)S(1)}, u32[]{:S(2)}) copy-start(bf16[256,512]{1,0:T(8,128)(2,1)S(1)} %collective-permute-done.18.refs_1_) | copy-start | bytes 786436
  56.8 12.7 %collective-permute-start.20 = (bf16[256,512]{1,0:T(8,128)(2,1)S(1)}, bf16[256,512]{1,0:T(8,128)(2,1)}, u32[]{:S(2)}, u32[]{:S(2)}) collective-permute-start(bf16[256,512]{1,0:T(8,128)(2,1)S(1)} %collective-permute-done.18.refs_1_), channel_id=1, source_target_pairs={{0,4},{4,8},{8,12},{12,0},{1,5},{5,9},{9,13},{13,1},{2,6},{6,10},{... | collective-permute-start | bytes 786440 | tf_op jit(solution)/shard_map/ppermute | solution.py:48
  58.8 10.8 %collective-permute-start.9 = (bf16[256,512]{1,0:T(8,128)(2,1)S(1)}, bf16[256,512]{1,0:T(8,128)(2,1)}, u32[]{:S(2)}, u32[]{:S(2)}) collective-permute-start(bf16[256,512]{1,0:T(8,128)(2,1)S(1)} %collective-permute-done.8.refs_3_), channel_id=1, source_target_pairs={{0,16},{16,0},{1,17},{17,1},{2,18},{18,2},{3,19},{19,3},{4,20},{20... | collective-permute-start | bytes 786440 | tf_op jit(solution)/shard_map/ppermute | solution.py:43
  63.9 11.4 %collective-permute-start.16 = (bf16[256,512]{1,0:T(8,128)(2,1)}, bf16[256,512]{1,0:T(8,128)(2,1)}, u32[]{:S(2)}, u32[]{:S(2)}) collective-permute-start(bf16[256,512]{1,0:T(8,128)(2,1)} %collective-permute-done.14.refs_10_), channel_id=1, source_target_pairs={{0,4},{4,8},{8,12},{12,0},{1,5},{5,9},{9,13},{13,1},{2,6},{6,10},{... | collective-permute-start | bytes 786440 | tf_op jit(solution)/shard_map/ppermute | solution.py:48
  63.9 19.7 %copy-start.13 = (bf16[512,512]{1,0:T(8,128)(2,1)}, bf16[512,512]{1,0:T(8,128)(2,1)S(1)}, u32[]{:S(2)}) copy-start(bf16[512,512]{1,0:T(8,128)(2,1)S(1)} %collective-permute-done.4.refs_2_) | copy-start | bytes 1572868
  63.9 12.1 %collective-permute-start.15 = (bf16[256,512]{1,0:T(8,128)(2,1)}, bf16[256,512]{1,0:T(8,128)(2,1)}, u32[]{:S(2)}, u32[]{:S(2)}) collective-permute-start(bf16[256,512]{1,0:T(8,128)(2,1)} %collective-permute-done.14.refs_10_), channel_id=1, source_target_pairs={{0,16},{16,0},{1,17},{17,1},{2,18},{18,2},{3,19},{19,3},{4,20},{20... | collective-permute-start | bytes 786440 | tf_op jit(solution)/shard_map/ppermute | solution.py:43
  69.5 8.6 %collective-permute-start.22 = (bf16[256,512]{1,0:T(8,128)(2,1)}, bf16[256,512]{1,0:T(8,128)(2,1)}, u32[]{:S(2)}, u32[]{:S(2)}) collective-permute-start(bf16[256,512]{1,0:T(8,128)(2,1)} %collective-permute-done.20.refs_3_), channel_id=1, source_target_pairs={{0,4},{4,8},{8,12},{12,0},{1,5},{5,9},{9,13},{13,1},{2,6},{6,10},{... | collective-permute-start | bytes 786440 | tf_op jit(solution)/shard_map/ppermute | solution.py:48
  69.6 18.3 %collective-permute-start.11 = (bf16[256,512]{1,0:T(8,128)(2,1)S(1)}, bf16[256,512]{1,0:T(8,128)(2,1)}, u32[]{:S(2)}, u32[]{:S(2)}) collective-permute-start(bf16[256,512]{1,0:T(8,128)(2,1)S(1)} %collective-permute-done.10.refs_5_), channel_id=1, source_target_pairs={{0,16},{16,0},{1,17},{17,1},{2,18},{18,2},{3,19},{19,3},{4,20},{20... | collective-permute-start | bytes 786440 | tf_op jit(solution)/shard_map/ppermute | solution.py:43
  75.2 12.7 %collective-permute-start.17 = (bf16[256,512]{1,0:T(8,128)(2,1)}, bf16[256,512]{1,0:T(8,128)(2,1)}, u32[]{:S(2)}, u32[]{:S(2)}) collective-permute-start(bf16[256,512]{1,0:T(8,128)(2,1)} %collective-permute-done.16.refs_12_), channel_id=1, source_target_pairs={{0,16},{16,0},{1,17},{17,1},{2,18},{18,2},{3,19},{19,3},{4,20},{20... | collective-permute-start | bytes 786440 | tf_op jit(solution)/shard_map/ppermute | solution.py:43
  76.0 22.9 %collective-permute-start.19 = (bf16[256,512]{1,0:T(8,128)(2,1)S(1)}, bf16[256,512]{1,0:T(8,128)(2,1)}, u32[]{:S(2)}, u32[]{:S(2)}) collective-permute-start(bf16[256,512]{1,0:T(8,128)(2,1)S(1)} %collective-permute-done.18.refs_1_), channel_id=1, source_target_pairs={{0,16},{16,0},{1,17},{17,1},{2,18},{18,2},{3,19},{19,3},{4,20},{20... | collective-permute-start | bytes 786440 | tf_op jit(solution)/shard_map/ppermute | solution.py:43
  77.3 21.6 %collective-permute-start.21 = (bf16[256,512]{1,0:T(8,128)(2,1)}, bf16[256,512]{1,0:T(8,128)(2,1)}, u32[]{:S(2)}, u32[]{:S(2)}) collective-permute-start(bf16[256,512]{1,0:T(8,128)(2,1)} %collective-permute-done.20.refs_3_), channel_id=1, source_target_pairs={{0,16},{16,0},{1,17},{17,1},{2,18},{18,2},{3,19},{19,3},{4,20},{20... | collective-permute-start | bytes 786440 | tf_op jit(solution)/shard_map/ppermute | solution.py:43
  78.1 20.8 %collective-permute-start.23 = (bf16[256,512]{1,0:T(8,128)(2,1)}, bf16[256,512]{1,0:T(8,128)(2,1)}, u32[]{:S(2)}, u32[]{:S(2)}) collective-permute-start(bf16[256,512]{1,0:T(8,128)(2,1)} %collective-permute-done.22.refs_5_), channel_id=1, source_target_pairs={{0,16},{16,0},{1,17},{17,1},{2,18},{18,2},{3,19},{19,3},{4,20},{20... | collective-permute-start | bytes 786440 | tf_op jit(solution)/shard_map/ppermute | solution.py:43
  103.9 2.9 %collective-permute-start.24 = (bf16[256,2048]{1,0:T(8,128)(2,1)}, bf16[256,2048]{1,0:T(8,128)(2,1)S(1)}, u32[]{:S(2)}, u32[]{:S(2)}) collective-permute-start(bf16[256,2048]{1,0:T(8,128)(2,1)} %get-tuple-element.24), channel_id=1, source_target_pairs={{0,1},{1,0},{2,3},{3,2},{4,5},{5,4},{6,7},{7,6},{8,9},{9,8},{10,11... | collective-permute-start | bytes 3145736 | tf_op jit(solution)/shard_map/ppermute | solution.py:43
  108.1 14.1 %collective-permute-start.25 = (bf16[128,2048]{1,0:T(8,128)(2,1)S(1)}, bf16[128,2048]{1,0:T(8,128)(2,1)}, u32[]{:S(2)}, u32[]{:S(2)}) collective-permute-start(bf16[128,2048]{1,0:T(8,128)(2,1)S(1)} %add_convert_fusion), channel_id=1, source_target_pairs={{0,2},{2,0},{1,3},{3,1},{4,6},{6,4},{5,7},{7,5},{8,10},{10,8},{9,1... | collective-permute-start | bytes 1572872 | tf_op jit(solution)/shard_map/ppermute | solution.py:43
  108.9 16.7 %copy-start.1 = (bf16[512,512]{1,0:T(8,128)(2,1)}, bf16[512,512]{1,0:T(8,128)(2,1)S(1)}, u32[]{:S(2)}) copy-start(bf16[512,512]{1,0:T(8,128)(2,1)S(1)} %pad_maximum_fusion.2.refs_4_) | copy-start | bytes 1572868
  108.9 18.2 %collective-permute-start.29 = (bf16[256,512]{1,0:T(8,128)(2,1)S(1)}, bf16[256,512]{1,0:T(8,128)(2,1)S(1)}, u32[]{:S(2)}, u32[]{:S(2)}) collective-permute-start(bf16[256,512]{1,0:T(8,128)(2,1)S(1)} %constant_dynamic-slice_fusion), channel_id=1, source_target_pairs={{0,4},{4,8},{8,12},{12,0},{1,5},{5,9},{9,13},{13,1},{2,6},{6,10},{... | collective-permute-start | bytes 786440 | tf_op jit(solution)/shard_map/ppermute | solution.py:48
  110.0 16.1 %copy-start = (bf16[1024,2048]{1,0:T(8,128)(2,1)S(1)}, bf16[1024,2048]{1,0:T(8,128)(2,1)}, u32[]{:S(2)}) copy-start(bf16[1024,2048]{1,0:T(8,128)(2,1)} %param.26) | copy-start | bytes 12582916
  125.6 12.1 %copy-start.2 = (bf16[2048,512]{1,0:T(8,128)(2,1)S(1)}, bf16[2048,512]{1,0:T(8,128)(2,1)}, u32[]{:S(2)}) copy-start(bf16[2048,512]{1,0:T(8,128)(2,1)} %param.25) | copy-start | bytes 6291460
  125.6 15.1 %collective-permute-start.26 = (bf16[128,2048]{1,0:T(8,128)(2,1)}, bf16[128,2048]{1,0:T(8,128)(2,1)S(1)}, u32[]{:S(2)}, u32[]{:S(2)}) collective-permute-start(bf16[128,2048]{1,0:T(8,128)(2,1)} %get-tuple-element.26.refs_0_), channel_id=1, source_target_pairs={{0,2},{2,0},{1,3},{3,1},{4,6},{6,4},{5,7},{7,5},{8,10},{10,8},{9,1... | collective-permute-start | bytes 1572872 | tf_op jit(solution)/shard_map/ppermute | solution.py:43
  127.0 1.6 collective-permute-start.35
  127.1 10.6 %collective-permute-start.31 = (bf16[256,512]{1,0:T(8,128)(2,1)S(1)}, bf16[256,512]{1,0:T(8,128)(2,1)}, u32[]{:S(2)}, u32[]{:S(2)}) collective-permute-start(bf16[256,512]{1,0:T(8,128)(2,1)S(1)} %collective-permute-done.29.refs_5_), channel_id=1, source_target_pairs={{0,4},{4,8},{8,12},{12,0},{1,5},{5,9},{9,13},{13,1},{2,6},{6,10},{... | collective-permute-start | bytes 786440 | tf_op jit(solution)/shard_map/ppermute | solution.py:48
  128.7 16.0 %collective-permute-start.36 = (bf16[64,2048]{1,0:T(8,128)(2,1)S(1)}, bf16[64,2048]{1,0:T(8,128)(2,1)}, u32[]{:S(2)}, u32[]{:S(2)}) collective-permute-start(bf16[64,2048]{1,0:T(8,128)(2,1)S(1)} %add.178), channel_id=1, source_target_pairs={{0,2},{2,0},{1,3},{3,1},{4,6},{6,4},{5,7},{7,5},{8,10},{10,8},{9,1... | collective-permute-start | bytes 786440 | tf_op jit(solution)/shard_map/ppermute | solution.py:43
  137.7 10.1 %collective-permute-start.33 = (bf16[256,512]{1,0:T(8,128)(2,1)}, bf16[256,512]{1,0:T(8,128)(2,1)}, u32[]{:S(2)}, u32[]{:S(2)}) collective-permute-start(bf16[256,512]{1,0:T(8,128)(2,1)} %collective-permute-done.31.refs_7_), channel_id=1, source_target_pairs={{0,4},{4,8},{8,12},{12,0},{1,5},{5,9},{9,13},{13,1},{2,6},{6,10},{... | collective-permute-start | bytes 786440 | tf_op jit(solution)/shard_map/ppermute | solution.py:48
  140.2 23.6 %collective-permute-start.27 = (bf16[128,2048]{1,0:T(8,128)(2,1)S(1)}, bf16[128,2048]{1,0:T(8,128)(2,1)S(1)}, u32[]{:S(2)}, u32[]{:S(2)}) collective-permute-start(bf16[128,2048]{1,0:T(8,128)(2,1)S(1)} %copy-done.6), channel_id=1, source_target_pairs={{0,1},{1,0},{2,3},{3,2},{4,5},{5,4},{6,7},{7,6},{8,9},{9,8},{10,11... | collective-permute-start | bytes 1572872 | tf_op jit(solution)/shard_map/ppermute | solution.py:43
  140.7 23.1 %copy-start.7 = (bf16[128,2048]{1,0:T(8,128)(2,1)}, bf16[128,2048]{1,0:T(8,128)(2,1)S(1)}, u32[]{:S(2)}) copy-start(bf16[128,2048]{1,0:T(8,128)(2,1)S(1)} %collective-permute-done.26.refs_1_) | copy-start | bytes 1572868
  140.7 23.1 %collective-permute-start.28 = (bf16[128,2048]{1,0:T(8,128)(2,1)S(1)}, bf16[128,2048]{1,0:T(8,128)(2,1)S(1)}, u32[]{:S(2)}, u32[]{:S(2)}) collective-permute-start(bf16[128,2048]{1,0:T(8,128)(2,1)S(1)} %collective-permute-done.26.refs_1_), channel_id=1, source_target_pairs={{0,1},{1,0},{2,3},{3,2},{4,5},{5,4},{6,7},{7,6},{8,9},{9,8},{10,11... | collective-permute-start | bytes 1572872 | tf_op jit(solution)/shard_map/ppermute | solution.py:43
  145.7 9.5 %collective-permute-start.30 = (bf16[256,512]{1,0:T(8,128)(2,1)}, bf16[256,512]{1,0:T(8,128)(2,1)S(1)}, u32[]{:S(2)}, u32[]{:S(2)}) collective-permute-start(bf16[256,512]{1,0:T(8,128)(2,1)} %copy-done.22), channel_id=1, source_target_pairs={{0,16},{16,0},{1,17},{17,1},{2,18},{18,2},{3,19},{19,3},{4,20},{20... | collective-permute-start | bytes 786440 | tf_op jit(solution)/shard_map/ppermute | solution.py:43
  147.2 13.6 %collective-permute-start.32 = (bf16[256,512]{1,0:T(8,128)(2,1)}, bf16[256,512]{1,0:T(8,128)(2,1)S(1)}, u32[]{:S(2)}, u32[]{:S(2)}) collective-permute-start(bf16[256,512]{1,0:T(8,128)(2,1)} %collective-permute-done.31.refs_7_), channel_id=1, source_target_pairs={{0,16},{16,0},{1,17},{17,1},{2,18},{18,2},{3,19},{19,3},{4,20},{20... | collective-permute-start | bytes 786440 | tf_op jit(solution)/shard_map/ppermute | solution.py:43
  147.8 16.0 %collective-permute-start.34 = (bf16[256,512]{1,0:T(8,128)(2,1)}, bf16[256,512]{1,0:T(8,128)(2,1)S(1)}, u32[]{:S(2)}, u32[]{:S(2)}) collective-permute-start(bf16[256,512]{1,0:T(8,128)(2,1)} %collective-permute-done.33.refs_9_), channel_id=1, source_target_pairs={{0,16},{16,0},{1,17},{17,1},{2,18},{18,2},{3,19},{19,3},{4,20},{20... | collective-permute-start | bytes 786440 | tf_op jit(solution)/shard_map/ppermute | solution.py:43
  175.1 1.9 collective-permute-start.37
  175.1 5.1 %collective-permute-start.38 = (bf16[16,2048]{1,0:T(8,128)(2,1)}, bf16[16,2048]{1,0:T(8,128)(2,1)S(1)}, u32[]{:S(2)}, u32[]{:S(2)}) collective-permute-start(bf16[16,2048]{1,0:T(8,128)(2,1)} %get-tuple-element.29.refs_1_), channel_id=1, source_target_pairs={{0,2},{1,3},{2,0},{3,1},{4,6},{5,7},{6,4},{7,5},{8,10},{9,11},{10,... | collective-permute-start | bytes 196616 | tf_op jit(solution)/shard_map/ppermute | solution.py:528
  175.6 5.2 %collective-permute-start.39 = (bf16[16,2048]{1,0:T(8,128)(2,1)}, bf16[16,2048]{1,0:T(8,128)(2,1)S(1)}, u32[]{:S(2)}, u32[]{:S(2)}) collective-permute-start(bf16[16,2048]{1,0:T(8,128)(2,1)} %get-tuple-element.29.refs_1_), channel_id=1, source_target_pairs={{0,3},{1,2},{2,1},{3,0},{4,7},{5,6},{6,5},{7,4},{8,11},{9,10},{10,... | collective-permute-start | bytes 196616 | tf_op jit(solution)/shard_map/ppermute | solution.py:528
  186.1 1.9 collective-permute-start.40
  186.3 5.1 %collective-permute-start.41 = (bf16[16,2048]{1,0:T(8,128)(2,1)}, bf16[16,2048]{1,0:T(8,128)(2,1)S(1)}, u32[]{:S(2)}, u32[]{:S(2)}) collective-permute-start(bf16[16,2048]{1,0:T(8,128)(2,1)} %get-tuple-element.31.refs_1_), channel_id=1, source_target_pairs={{0,2},{1,3},{2,0},{3,1},{4,6},{5,7},{6,4},{7,5},{8,10},{9,11},{10,... | collective-permute-start | bytes 196616 | tf_op jit(solution)/shard_map/ppermute | solution.py:528
  186.8 4.7 %collective-permute-start.42 = (bf16[16,2048]{1,0:T(8,128)(2,1)}, bf16[16,2048]{1,0:T(8,128)(2,1)S(1)}, u32[]{:S(2)}, u32[]{:S(2)}) collective-permute-start(bf16[16,2048]{1,0:T(8,128)(2,1)} %get-tuple-element.31.refs_1_), channel_id=1, source_target_pairs={{0,3},{1,2},{2,1},{3,0},{4,7},{5,6},{6,5},{7,4},{8,11},{9,10},{10,... | collective-permute-start | bytes 196616 | tf_op jit(solution)/shard_map/ppermute | solution.py:528
  196.8 1.9 collective-permute-start.43
  197.2 4.9 %collective-permute-start.44 = (bf16[16,2048]{1,0:T(8,128)(2,1)}, bf16[16,2048]{1,0:T(8,128)(2,1)S(1)}, u32[]{:S(2)}, u32[]{:S(2)}) collective-permute-start(bf16[16,2048]{1,0:T(8,128)(2,1)} %get-tuple-element.33.refs_1_), channel_id=1, source_target_pairs={{0,2},{1,3},{2,0},{3,1},{4,6},{5,7},{6,4},{7,5},{8,10},{9,11},{10,... | collective-permute-start | bytes 196616 | tf_op jit(solution)/shard_map/ppermute | solution.py:528
  198.0 4.6 %collective-permute-start.45 = (bf16[16,2048]{1,0:T(8,128)(2,1)}, bf16[16,2048]{1,0:T(8,128)(2,1)S(1)}, u32[]{:S(2)}, u32[]{:S(2)}) collective-permute-start(bf16[16,2048]{1,0:T(8,128)(2,1)} %get-tuple-element.33.refs_1_), channel_id=1, source_target_pairs={{0,3},{1,2},{2,1},{3,0},{4,7},{5,6},{6,5},{7,4},{8,11},{9,10},{10,... | collective-permute-start | bytes 196616 | tf_op jit(solution)/shard_map/ppermute | solution.py:528
  207.9 3.4 %collective-permute-start.48 = (bf16[16,512]{1,0:T(8,128)(2,1)}, bf16[16,512]{1,0:T(8,128)(2,1)S(1)}, u32[]{:S(2)}, u32[]{:S(2)}) collective-permute-start(bf16[16,512]{1,0:T(8,128)(2,1)} %get-tuple-element.37), channel_id=1, source_target_pairs={{0,3},{1,2},{2,1},{3,0},{4,7},{5,6},{6,5},{7,4},{8,11},{9,10},{10,... | collective-permute-start | bytes 49160 | tf_op jit(solution)/shard_map/ppermute | solution.py:528
  208.8 3.9 %collective-permute-start.47 = (bf16[16,512]{1,0:T(8,128)(2,1)}, bf16[16,512]{1,0:T(8,128)(2,1)S(1)}, u32[]{:S(2)}, u32[]{:S(2)}) collective-permute-start(bf16[16,512]{1,0:T(8,128)(2,1)} %get-tuple-element.36), channel_id=1, source_target_pairs={{0,2},{1,3},{2,0},{3,1},{4,6},{5,7},{6,4},{7,5},{8,10},{9,11},{10,... | collective-permute-start | bytes 49160 | tf_op jit(solution)/shard_map/ppermute | solution.py:528
  209.8 2.9 %collective-permute-start.46 = (bf16[16,512]{1,0:T(8,128)(2,1)}, bf16[16,512]{1,0:T(8,128)(2,1)S(1)}, u32[]{:S(2)}, u32[]{:S(2)}) collective-permute-start(bf16[16,512]{1,0:T(8,128)(2,1)} %get-tuple-element.35), channel_id=1, source_target_pairs={{0,1},{1,0},{2,3},{3,2},{4,5},{5,4},{6,7},{7,6},{8,9},{9,8},{10,11... | collective-permute-start | bytes 49160 | tf_op jit(solution)/shard_map/ppermute | solution.py:528
  (21 other events, 81.6 us)

commit v2 on v1

v2 whole, which is shorter than its diff:
```python
import functools

import jax
import jax.numpy as jnp
from jax import lax
from jax.experimental import pallas as pl
from jax.experimental.pallas import tpu as pltpu
from jax.sharding import PartitionSpec as P

H = 16
DH = 128
KVH = 8
BLK = 128
STEPS = 4
RING_LIMIT = 8
RING_WAYS = (1, -1)
VMEM_BYTES = 56 * 1024 * 1024

eps = 1e-06

VM = pl.BlockSpec(memory_space=pltpu.VMEM)
SM = pl.BlockSpec(memory_space=pltpu.SMEM)
HB = pl.BlockSpec(memory_space=pl.ANY)


def params():
    return pltpu.CompilerParams(vmem_limit_bytes=VMEM_BYTES)


def cost(micros):
    return pl.CostEstimate(flops=0, bytes_accessed=int(micros * 3.0e6), transcendentals=0)


def partner(index, step, size):
    if size & (size - 1) == 0:
        return index ^ step
    return (index + step) % size


def origin(index, step, size):
    if size & (size - 1) == 0:
        return index ^ step
    return (index - step) % size


def exchange(value, axis, step):
    size = lax.axis_size(axis)
    return lax.ppermute(value, axis, [(i, partner(i, step, size)) for i in range(size)])


def shift(value, axis, step):
    size = lax.axis_size(axis)
    return lax.ppermute(value, axis, [(i, (i + step) % size) for i in range(size)])


def after(value, *others):
    return lax.optimization_barrier((value, *others))[0]


def position():
    return jnp.stack([lax.axis_index(axis) for axis in ("seq", "groups", "tp", "kv")])


def gather_heads(value, beside=None):
    tp, kv = lax.axis_size("tp"), lax.axis_size("kv")
    along = [(value, lambda at: at[2])]
    for step in range(1, tp):
        along.append(
            (exchange(value, "tp", step), functools.partial(lambda d, at: origin(at[2], d, tp), step))
        )
    waits = beside() if beside else []
    if waits:
        along = along[:1] + [(after(piece, *waits), where) for piece, where in along[1:]]
    pieces = []
    for piece, where in along:
        pieces.append((piece, functools.partial(lambda f, at: f(at) * kv + at[3], where)))
    for piece, where in along:
        for step in range(1, kv):
            pieces.append(
                (
                    exchange(piece, "kv", step),
                    functools.partial(
                        lambda f, e, at: f(at) * kv + origin(at[3], e, kv), where, step
                    ),
                )
            )
    return pieces


class Rows:
    def __init__(self, value, *waits):
        self.size = lax.axis_size("seq")
        self.rows = value.shape[0]
        self.shared = lax.axis_size("groups") == 2 and self.rows % 32 == 0
        self.pieces = [(value, [functools.partial(lambda r, at: at[0] * r, self.rows)])]
        half = self.rows // 2
        if self.shared:
            value = lax.dynamic_slice_in_dim(value, lax.axis_index("groups") * half, half, 0)
        if waits:
            value = after(value, *waits)
        self.last = {1: value, -1: value}
        self.hops = {1: 0, -1: 0}
        self.fresh = []

    def hop(self, way, *waits):
        arrived = shift(after(self.last[way], *waits) if waits else self.last[way], "seq", way)
        self.last[way] = arrived
        self.hops[way] += 1
        self.fresh.append((arrived, way * self.hops[way]))

    def place(self, distance, twin):
        size, rows = self.size, self.rows

        def first(at):
            row = lax.rem(at[0] + size - distance, size) * rows
            return row + (at[1] ^ twin) * (rows // 2) if self.shared else row

        return [first]

    def keep(self):
        for arrived, distance in self.fresh:
            self.pieces.append((arrived, self.place(distance, 0)))
        self.fresh = []

    def swap(self, *waits):
        for arrived, distance in self.fresh:
            self.pieces.append((arrived, self.place(distance, 0)))
            if self.shared:
                other = exchange(after(arrived, *waits) if waits else arrived, "groups", 1)
                self.pieces.append((other, self.place(distance, 1)))
        self.fresh = []

    def direct(self, distance, *waits):
        if self.shared:
            half = self.rows // 2
            rest = 1 - lax.axis_index("groups")
            other = lax.dynamic_slice_in_dim(self.pieces[0][0], rest * half, half, 0)
            other = shift(after(other, *waits) if waits else other, "seq", distance)
            self.pieces.append((other, self.place(distance, 1)))

    def start(self, *waits):
        for way in RING_WAYS[: self.size - 1]:
            self.hop(way, *waits)

    def swapped(self):
        return self.pieces[-1][0]

    def end(self, *waits):
        for hop in range(len(RING_WAYS), self.size - 1):
            self.hop(RING_WAYS[hop % len(RING_WAYS)], *waits)

    def held(self, *waits):
        arrays = lax.optimization_barrier((*[piece for piece, _ in self.pieces], *waits))
        self.pieces = [(piece, places) for piece, (_, places) in zip(arrays, self.pieces)]
        return arrays[len(self.pieces) :]


def whole_rows(value):
    return [(lax.all_gather(value, "seq", axis=0, tiled=True), [lambda at: 0])]


def collect_events(events):
    size = lax.axis_size("seq")
    here = lax.axis_index("seq")
    rows = events.shape[1]
    if size > RING_LIMIT:
        return [lax.all_to_all(events, "seq", split_axis=0, concat_axis=1, tiled=True)[0]], [lambda at: 0]
    blocks = [lax.dynamic_index_in_dim(events, here, 0, False)]
    firsts = [lambda at: at[0] * rows]
    for step in range(1, size):
        block = lax.dynamic_index_in_dim(events, (here + step) % size, 0, False)
        blocks.append(shift(block, "seq", step))
        firsts.append(
            functools.partial(lambda d, at: lax.rem(at[0] + size - d, size) * rows, step)
        )
    return blocks, firsts


def norm_kernel(places, firsts, at_ref, gain_ref, *refs):
    count, blocks = len(places), len(firsts)
    pieces, (normed_ref, source_ref) = refs[:count], refs[count:]
    width = normed_ref.shape[1]
    cols = pieces[0].shape[1]
    rows = pieces[0].shape[0] // blocks
    for block in range(blocks):
        first = pl.multiple_of(firsts[block](at_ref), rows)
        parts = [p[block * rows : (block + 1) * rows, :].astype(jnp.float32) for p in pieces]
        square = sum(jnp.sum(v * v, axis=-1, keepdims=True) for v in parts)
        scale = lax.rsqrt(square / width + eps)
        for index in range(count):
            col = pl.ds(pl.multiple_of(places[index](at_ref) * cols, cols), cols)
            source_ref[pl.ds(first, rows), col] = parts[index].astype(jnp.bfloat16)
            normed_ref[pl.ds(first, rows), col] = (
                parts[index] * scale * gain_ref[:, col]
            ).astype(jnp.bfloat16)


def norm_events(at, pieces, firsts, gain):
    length = pieces[0][0].shape[0]
    width = gain.shape[0]
    shape = jax.ShapeDtypeStruct((length, width), jnp.bfloat16)
    return pl.pallas_call(
        functools.partial(norm_kernel, [where for _, where in pieces], firsts),
        out_shape=(shape, shape),
        in_specs=[SM] + [VM] * (1 + len(pieces)),
        out_specs=(VM, VM),
        compiler_params=params(),
        cost_estimate=cost(4),
        name="norm_events",
    )(
        at,
        gain[None, :],
        *[piece for piece, _ in pieces],
    )


def load_pieces(pieces, firsts, at_ref, base, whole, columns, sems):
    copies = []
    for piece, places in zip(pieces, firsts):
        rows = piece.shape[0] // len(places)
        for block, place in enumerate(places):
            first = pl.multiple_of(place(at_ref), rows)
            copy = pltpu.make_async_copy(
                piece.at[pl.ds(block * rows, rows)],
                whole.at[pl.ds(first, rows), columns],
                sems.at[base + len(copies)],
            )
            copy.start()
            copies.append(copy)
    return copies


def block_count(pieces):
    return sum(len(places) for _, places in pieces)


def encoder_kernel(
    firsts, ratio, at_ref, live_ref, normed_ref, history_ref, *refs
):
    pieces, (out_ref, whole, projected, sems) = refs[:-4], refs[-4:]
    length = normed_ref.shape[0]
    heads = out_ref.shape[1] // DH
    kv_heads = heads // ratio
    query_cols = heads * DH
    key_cols = kv_heads * DH
    past = history_ref.shape[1]
    copies = load_pieces(pieces, firsts, at_ref, 0, whole, slice(None), sems)
    for copy in copies:
        copy.wait()
    tile = min(256, length)
    for row in range(0, length, tile):
        projected[row : row + tile, :] = jnp.dot(
            normed_ref[row : row + tile, :], whole[...], preferred_element_type=jnp.float32
        ).astype(jnp.bfloat16)
    live = live_ref[0] * BLK
    contract = (((1,), (1,)), ((), ()))
    for group in range(kv_heads):
        keys = slice(query_cols + group * DH, query_cols + (group + 1) * DH)
        values = slice(query_cols + key_cols + group * DH, query_cols + key_cols + (group + 1) * DH)
        cached = slice(group * DH, (group + 1) * DH)
        for row in range(0, length, tile):
            reach = row + tile
            for head in range(group * ratio, (group + 1) * ratio):
                query = projected[row:reach, head * DH : (head + 1) * DH]
                old = lax.dot_general(
                    query, history_ref[0, :, cached], contract, preferred_element_type=jnp.float32
                )
                new = lax.dot_general(
                    query, projected[:reach, keys], contract, preferred_element_type=jnp.float32
                )
                query_index = row + lax.broadcasted_iota(jnp.int32, (tile, reach), 0)
                key_index = lax.broadcasted_iota(jnp.int32, (tile, reach), 1)
                new = jnp.where((key_index <= query_index) & (key_index < live), new, -1e30)
                top = jnp.maximum(
                    jnp.max(old, axis=-1, keepdims=True), jnp.max(new, axis=-1, keepdims=True)
                )
                scale = DH ** (-0.5)
                old = jnp.exp((old - top) * scale)
                new = jnp.exp((new - top) * scale)
                total_weight = jnp.sum(old, axis=-1, keepdims=True) + jnp.sum(
                    new, axis=-1, keepdims=True
                )
                mixed = jnp.dot(
                    old.astype(jnp.bfloat16),
                    history_ref[1, :, cached],
                    preferred_element_type=jnp.float32,
                ) + jnp.dot(
                    new.astype(jnp.bfloat16),
                    projected[:reach, values],
                    preferred_element_type=jnp.float32,
                )
                out_ref[row:reach, head * DH : (head + 1) * DH] = (mixed / total_weight).astype(
                    jnp.bfloat16
                )


def encoder_attention(at, normed, history, block_counts, pieces):
    length, width = normed.shape
    key_cols = history.shape[2]
    joined = pieces[0][0].shape[1]
    query_cols = joined - 2 * key_cols
    return pl.pallas_call(
        functools.partial(
            encoder_kernel, [places for _, places in pieces], query_cols // key_cols
        ),
        out_shape=jax.ShapeDtypeStruct((length, query_cols), jnp.bfloat16),
        in_specs=[SM, SM, VM, VM] + [HB] * len(pieces),
        out_specs=VM,
        scratch_shapes=[
            pltpu.VMEM((width, joined), jnp.bfloat16),
            pltpu.VMEM((length, joined), jnp.bfloat16),
            pltpu.SemaphoreType.DMA((block_count(pieces),)),
        ],
        compiler_params=params(),
        cost_estimate=cost(11),
        name="encoder_attention",
    )(
        at,
        block_counts,
        normed,
        history,
        *[piece for piece, _ in pieces],
    )


def project_kernel(firsts, orders, at_ref, attended_ref, *refs):
    count = len(firsts)
    pieces, outs, (whole, sems) = refs[:count], refs[count:-2], refs[-2:]
    copies = load_pieces(pieces, firsts, at_ref, 0, whole, slice(None), sems)
    share = outs[0].shape[0] // len(orders[0])
    for copy in copies:
        copy.wait()
    for index, out_ref in enumerate(outs):
        parts = []
        for where in orders[index]:
            first = pl.multiple_of(where(at_ref) * share, share)
            parts.append(attended_ref[pl.ds(first, share), :])
        rows = jnp.concatenate(parts, axis=0)
        out_ref[...] = lax.dot_general(
            rows, whole[...], (((1,), (1,)), ((), ())), preferred_element_type=jnp.float32
        ).astype(jnp.bfloat16)


def project_out(at, attended, pieces, orders):
    length, cols = attended.shape
    groups = lax.axis_size("tp")
    share = length // (groups * len(orders))
    width = sum(piece.shape[0] for piece, _ in pieces)
    shape = jax.ShapeDtypeStruct((groups * share, width), jnp.bfloat16)
    return pl.pallas_call(
        functools.partial(project_kernel, [first for _, first in pieces], orders),
        out_shape=tuple([shape] * len(orders)),
        in_specs=[SM, VM] + [HB] * len(pieces),
        out_specs=tuple([VM] * len(orders)),
        scratch_shapes=[
            pltpu.VMEM((width, cols), jnp.bfloat16),
            pltpu.SemaphoreType.DMA((block_count(pieces),)),
        ],
        compiler_params=params(),
        cost_estimate=cost(5),
        name="project_out",
    )(
        at,
        attended,
        *[piece for piece, _ in pieces],
    )


def merge_kernel(count, at_ref, gain_ref, source_ref, *refs):
    terms, (encoded_ref, crossed_ref) = refs[:count], refs[count:]
    rows = encoded_ref.shape[0]
    first = pl.multiple_of((at_ref[2] * lax.axis_size("kv") + at_ref[3]) * rows, rows)
    total = source_ref[pl.ds(first, rows), :].astype(jnp.float32)
    for term in terms:
        total = total + term[...].astype(jnp.float32)
    encoded_ref[...] = total.astype(jnp.bfloat16)
    square = jnp.mean(total * total, axis=-1, keepdims=True)
    crossed_ref[...] = (total * lax.rsqrt(square + eps) * gain_ref[...]).astype(jnp.bfloat16)


def merge_terms(at, source, terms, gain):
    shape = jax.ShapeDtypeStruct(terms[0].shape, jnp.bfloat16)
    return pl.pallas_call(
        functools.partial(merge_kernel, len(terms)),
        out_shape=(shape, shape),
        in_specs=[SM] + [VM] * (2 + len(terms)),
        out_specs=(VM, VM),
        compiler_params=params(),
        cost_estimate=cost(3),
        name="merge_terms",
    )(at, gain[None, :], source, *terms)


def cross_kernel(places, firsts, at_ref, *refs):
    row_count, count = len(places), len(firsts)
    rows_refs, pieces = refs[:row_count], refs[row_count : row_count + count]
    out_ref, whole, sems = refs[row_count + count :]
    copies = load_pieces(pieces, firsts, at_ref, 0, whole, slice(None), sems)
    for copy in copies:
        copy.wait()
    rows = rows_refs[0].shape[0]
    for index, rows_ref in enumerate(rows_refs):
        first = pl.multiple_of(places[index](at_ref) * rows, rows)
        out_ref[pl.ds(first, rows), :] = jnp.dot(
            rows_ref[...], whole[...], preferred_element_type=jnp.float32
        ).astype(jnp.bfloat16)


def cross_project(at, row_pieces, pieces):
    width = row_pieces[0][0].shape[1]
    rows = row_pieces[0][0].shape[0]
    cols = pieces[0][0].shape[1]
    return pl.pallas_call(
        functools.partial(
            cross_kernel, [where for _, where in row_pieces], [first for _, first in pieces]
        ),
        out_shape=jax.ShapeDtypeStruct((rows * len(row_pieces), cols), jnp.bfloat16),
        in_specs=[SM] + [VM] * len(row_pieces) + [HB] * len(pieces),
        out_specs=VM,
        scratch_shapes=[
            pltpu.VMEM((width, cols), jnp.bfloat16),
            pltpu.SemaphoreType.DMA((block_count(pieces),)),
        ],
        compiler_params=params(),
        cost_estimate=cost(5),
        name="cross_project",
    )(
        at,
        *[rows for rows, _ in row_pieces],
        *[piece for piece, _ in pieces],
    )


def beam_kernel(
    level, count, last, ratio, places,
    at_ref, live_ref, parent_ref, gain_ref, query_ref, out_weight_ref, cross_ref, code_ref,
    *refs,
):
    inputs, outs, moved = refs[: count + 1 if level else 0], refs[count + 1 if level else 0 : -1], refs[-1]
    beams = code_ref.shape[0]
    code = code_ref[...].astype(jnp.float32)
    if level:
        total = inputs[0][...]
        for term in inputs[1:]:
            total = total + term[...].astype(jnp.float32)
        moved[...] = total
        rows = [moved[pl.ds(parent_ref[level - 1, row], 1), :] for row in range(beams)]
        hidden = jnp.concatenate(rows, axis=0) + code
    else:
        hidden = code
    square = jnp.mean(hidden * hidden, axis=-1, keepdims=True)
    normed = (hidden * lax.rsqrt(square + eps) * gain_ref[...]).astype(jnp.bfloat16)
    queries = jnp.dot(normed, query_ref[...], preferred_element_type=jnp.float32)
    queries = queries.astype(jnp.bfloat16)
    key_cols = cross_ref.shape[1] // 2
    events = cross_ref.shape[0]
    live = live_ref[0] * BLK
    attended = []
    for group in range(key_cols // DH):
        first = group * ratio
        stacked = jnp.concatenate(
            [queries[:, h * DH : (h + 1) * DH] for h in range(first, first + ratio)], axis=0
        )
        scores = lax.dot_general(
            stacked,
            cross_ref[:, group * DH : (group + 1) * DH],
            (((1,), (1,)), ((), ())),
            preferred_element_type=jnp.float32,
        )
        index = lax.broadcasted_iota(jnp.int32, scores.shape, 1)
        scores = jnp.where(index < live, scores, -1e30)
        top = jnp.max(scores, axis=-1, keepdims=True)
        raised = jnp.exp((scores - top) * DH ** (-0.5))
        weight = jnp.sum(raised, axis=-1, keepdims=True)
        mixed = jnp.dot(
            raised.astype(jnp.bfloat16),
            cross_ref[:, key_cols + group * DH : key_cols + (group + 1) * DH],
            preferred_element_type=jnp.float32,
        )
        mixed = (mixed / weight).astype(jnp.bfloat16)
        attended += [mixed[h * beams : (h + 1) * beams, :] for h in range(ratio)]
    terms = jnp.dot(
        jnp.concatenate(attended, axis=1), out_weight_ref[...], preferred_element_type=jnp.float32
    )
    if not last:
        outs[0][...] = hidden
        outs[1][...] = terms.astype(jnp.bfloat16)
    else:
        cols = outs[0].shape[1]
        moved[...] = terms
        for index in range(1, len(outs)):
            col = pl.ds(pl.multiple_of(places[index](at_ref) * cols, cols), cols)
            outs[index][...] = moved[:, col].astype(jnp.bfloat16)
        moved[...] = hidden + terms
        outs[0][...] = moved[:, pl.ds(pl.multiple_of(places[0](at_ref) * cols, cols), cols)]


def beam_step(at, level, live, parents, places, gain, query, out_weight, cross, code, inputs, last):
    beams, width = code.shape
    ratio = H // KVH
    if last:
        cols = width // len(places)
        outs = [jax.ShapeDtypeStruct((beams, cols), jnp.float32)] + [
            jax.ShapeDtypeStruct((beams, cols), jnp.bfloat16)
        ] * (len(places) - 1)
    else:
        outs = [
            jax.ShapeDtypeStruct((beams, width), jnp.float32),
            jax.ShapeDtypeStruct((beams, width), jnp.bfloat16),
        ]
    return pl.pallas_call(
        functools.partial(beam_kernel, level, max(len(inputs) - 1, 0), last, ratio, places),
        out_shape=tuple(outs),
        in_specs=[SM, SM, SM] + [VM] * (5 + len(inputs)),
        out_specs=tuple([VM] * len(outs)),
        scratch_shapes=[pltpu.VMEM((beams, width), jnp.float32)],
        compiler_params=params(),
        cost_estimate=cost(4),
        name=f"beam_step_{level}",
    )(at, live, parents, gain[None, :], query, out_weight, cross, code, *inputs)


def shards(
    events,
    history_cache,
    block_counts,
    semantic_ids,
    beam_parents,
    query_weight,
    keyval_weight,
    out_weight,
    cross_weight,
    decoder_query,
    decoder_out,
    code_table,
    encoder_gain,
    cross_gain,
    decoder_gain,
):
    tp, kv = lax.axis_size("tp"), lax.axis_size("kv")
    my_tp, my_kv = lax.axis_index("tp"), lax.axis_index("kv")
    group, groups = my_tp * kv + my_kv, tp * kv

    at = position()
    joined = jnp.concatenate([query_weight, keyval_weight[0], keyval_weight[1]], axis=1)
    crossing = jnp.concatenate([cross_weight[0], cross_weight[1]], axis=1)
    ringed = lax.axis_size("seq") <= RING_LIMIT
    blocks, firsts = collect_events(events)

    def look_up(waits):
        vocab_rows = code_table.shape[0]
        vocab_ids = group * vocab_rows + lax.broadcasted_iota(jnp.int32, (1, vocab_rows), 1)
        onehot = (semantic_ids.reshape(-1)[:, None] == vocab_ids).astype(jnp.bfloat16)
        onehot = after(onehot, *waits)
        rows = jnp.dot(onehot, code_table, preferred_element_type=jnp.float32).astype(jnp.bfloat16)
        for axis, size in (("kv", kv), ("tp", tp)):
            rows = sum([exchange(rows, axis, step) for step in range(1, size)], rows)
        return rows

    if ringed:
        joined, out, cross = map(Rows, (joined, out_weight, crossing))
        ways = [RING_WAYS[hop % len(RING_WAYS)] for hop in range(lax.axis_size("seq") - 1)]
        joined.hop(ways[0])
        mine = jnp.concatenate(blocks, axis=0)
        mine, joined.last[1] = lax.optimization_barrier((mine, joined.last[1]))
        joined.fresh = [(joined.last[1], 1)]
        stage = [joined.last[1]]
        event_pieces = gather_heads(mine)
        codes, turned = look_up(stage), after(decoder_out, *stage).T
        normed, source = norm_events(at, event_pieces, firsts, encoder_gain)
        for way in ways[1:]:
            joined.swap()
            swapped = joined.swapped()
            joined.hop(way, *stage)
            stage = [joined.last[way], swapped]
        normed, codes, turned, *stage = lax.optimization_barrier((normed, codes, turned, *stage))
        joined.swap(normed)
        out.start(*stage)
        normed, *_ = joined.held(normed, *out.last.values())
        joined_pieces = joined.pieces
        far = [1 + hop // 2 if hop % 2 == 0 else -(1 + hop // 2) for hop in range(len(RING_WAYS), len(ways))]
        out.swap(normed)
        out.end()
        out.keep()
        for distance in far:
            out.direct(distance, normed)
        out_pieces = out.pieces
    else:
        joined_pieces, out_pieces, cross_pieces = map(whole_rows, (joined, out_weight, crossing))
        normed, source = norm_events(at, gather_heads(blocks[0]), firsts, encoder_gain)
        codes = look_up([])
        turned = decoder_out.T
    attended = encoder_attention(
        at, normed, history_cache[:, 0], block_counts, joined_pieces
    )
    steps, beams = semantic_ids.shape
    codes = codes.reshape(steps, beams, codes.shape[1])

    def place(d, e, at):
        return partner(at[2], d, tp) * kv + partner(at[3], e, kv)

    orders = [[functools.partial(place, d, e) for d in range(tp)] for e in range(kv)]
    kept, *sent = project_out(at, attended, out_pieces, orders)
    share = normed.shape[0] // groups
    arrived = [exchange(terms, "kv", e + 1) for e, terms in enumerate(sent)]
    late = []
    if ringed:
        cross.start(*arrived)
        for distance in far:
            cross.direct(distance, *arrived)
        late = list(cross.last.values())

    def summed(d):
        rows = slice(d * share, (d + 1) * share)
        return sum([a[rows].astype(jnp.float32) for a in arrived], kept[rows].astype(jnp.float32))

    terms = [exchange(summed(d).astype(jnp.bfloat16), "tp", d) for d in range(1, tp)]
    terms = [kept[:share]] + [a[:share] for a in arrived] + [after(t, *late) if late else t for t in terms]
    encoded, crossed = merge_terms(at, source, terms, cross_gain)


    def finish_cross():
        cross.swap(crossed)
        cross.end()
        cross.keep()
        return [piece for piece, _ in cross.pieces[1:]]

    crossed_pieces = gather_heads(crossed, finish_cross if ringed else None)
    keys_values = cross_project(at, crossed_pieces, cross.pieces if ringed else cross_pieces)

    places = [functools.partial(place, 0, 0)]
    moves = []
    for d in range(tp):
        for e in range(kv):
            if d or e:
                places.append(functools.partial(place, d, e))
                moves.append(
                    [
                        (a * kv + b, partner(a, d, tp) * kv + partner(b, e, kv))
                        for a in range(tp)
                        for b in range(kv)
                    ]
                )
    inputs = []
    for level in range(steps):
        last = level == steps - 1
        kept, *sent = beam_step(
            at, level, block_counts, beam_parents, places, decoder_gain, decoder_query, turned,
            keys_values, codes[level], inputs, last,
        )
        if not last:
            sent = sent * len(moves)
        arrived = [lax.ppermute(v, ("tp", "kv"), move) for v, move in zip(sent, moves)]
        inputs = [kept] + sent[:1] + arrived
    beam_out = sum([a.astype(jnp.float32) for a in arrived], kept).astype(jnp.bfloat16)
    return (encoded[None], beam_out)


def solution(mesh):
    in_specs = (
        P("groups", "seq", ("tp", "kv")),
        P(None, ("groups", "seq"), None, ("tp", "kv")),
        P(("groups", "seq")),
        P(None, ("groups", "seq")),
        P(None, ("groups", "seq")),
        P("seq", ("tp", "kv")),
        P(None, "seq", ("tp", "kv")),
        P("seq", ("tp", "kv")),
        P(None, "seq", ("tp", "kv")),
        P(None, ("tp", "kv")),
        P(None, ("tp", "kv")),
        P(("tp", "kv"), None),
        P(),
        P(),
        P(),
    )
    out_specs = (P(("groups", "seq"), ("tp", "kv"), None), P(("groups", "seq"), ("tp", "kv")))
    return jax.shard_map(shards, mesh=mesh, in_specs=in_specs, out_specs=out_specs, check_vma=False)
```

time: 215 us -> 200 us (0.930)
  waiting for transfers between devices: 112 us -> 84.4 us
  starting transfers between devices: 34.1 us -> 42.6 us
  local copies, waits for them, and re-layouts: 12.2 us -> 15.1 us
  matrix products: 0.87 us -> 3.03 us
    ppermute x22 -> x17, waiting for transfers between devices: 35.2 us -> 13.8 us  [exchange(): lax.ppermute(value, axis, [(i, partner(i, step, size)) for i in range(siz...]
    ppermute x15 -> x14, starting transfers between devices: 8.07 us -> 22.1 us  [shift(): lax.ppermute(value, axis, [(i, (i + step) % size) for i in range(size)])]
    ppermute x15 -> x14, waiting for transfers between devices: 62 us -> 55.7 us  [shift(): lax.ppermute(value, axis, [(i, (i + step) % size) for i in range(size)])]
    ppermute x22 -> x17, starting transfers between devices: 18.6 us -> 13.1 us  [exchange(): lax.ppermute(value, axis, [(i, partner(i, step, size)) for i in range(siz...]
    optimization_barrier x0 -> x1, local copies, waits for them, and re-layouts: none -> 3.97 us  [after(): return lax.optimization_barrier((value, *others))[0]]
    dot_general x1, matrix products: 0.87 us -> 3.03 us  [look_up(): jnp.dot(onehot, code_table, preferred_element_type=jnp.float32)]
    unnamed x73 -> x74, local copies, waits for them, and re-layouts: 6.15 us -> 6.44 us
  transfers between devices with their start and end apart: 49 -> 43, of which waited for: 28 -> 21; matrix products, arithmetic and copies ran while one was open for 6% -> 6% of each run, Pallas kernels for 9% -> 8%
where the time goes in v2:
time: 200 us; the launch traced here: 199 us
  waiting for transfers between devices  84.4 us (42%)
  Pallas kernels  46.6 us (23%)
  starting transfers between devices  42.6 us (21%)
  local copies, waits for them, and re-layouts  15.1 us (8%)
  other arithmetic  5.54 us (3%)
  matrix products  3.03 us (2%)
    ppermute x14, waiting for transfers between devices, shift(): lax.ppermute(value, axis, [(i, (i + step) % size) for i in range(size)])  55.7 us
    ppermute x14, starting transfers between devices, shift(): lax.ppermute(value, axis, [(i, (i + step) % size) for i in range(size)])  22.1 us
    pallas_call x4, Pallas kernels, beam_step(): pl.pallas_call(functools.partial(beam_kernel, level, max(len(inputs) - 1,...  18.2 us
    ppermute x12, waiting for transfers between devices, shards(): lax.ppermute(v, ('tp', 'kv'), move)  14.8 us
    ppermute x17, waiting for transfers between devices, exchange(): lax.ppermute(value, axis, [(i, partner(i, step, size)) for i in range(siz...  13.8 us
    ppermute x17, starting transfers between devices, exchange(): lax.ppermute(value, axis, [(i, partner(i, step, size)) for i in range(siz...  13.1 us
    pallas_call x1, Pallas kernels, encoder_attention(): pl.pallas_call(functools.partial(encoder_kernel, [places for _, places in...  10.8 us
    ppermute x12, starting transfers between devices, shards(): lax.ppermute(v, ('tp', 'kv'), move)  7.44 us
  transfers between devices with their start and end apart: 43, of which 21 were waited for; matrix products, arithmetic and copies ran while one was open for 6% of the time, Pallas kernels for 8%

profile of v2, /device:TPU:0, one launch (start us, length us, event | category | flops | bytes accessed | tf_op | source)
XLA Modules:
  0.0 199.1 jit_solution(18062906059033187464)
XLA Ops:
  0.6 1.1 slice_bitcast_fusion.3
  1.8 1.2 pad_maximum_fusion.refs_0_
  3.0 0.9 constant_dynamic-slice_fusion.2
  3.9 3.0 %collective-permute-start.3 = (bf16[256,1024]{1,0:T(8,128)(2,1)}, bf16[256,1024]{1,0:T(8,128)(2,1)}, u32[]{:S(2)}, u32[]{:S(2)}) collective-permute-start(bf16[256,1024]{1,0:T(8,128)(2,1)} %constant_dynamic-slice_fusion.2), channel_id=1, source_target_pairs={{0,4},{4,8},{8,12},{12,0},{1,5},{5,9},{9,13},{13,1},{2,6},{6,10},{... | collective-permute-start | bytes 1572872 | tf_op jit(solution)/shard_map/ppermute | solution.py:53
  7.0 2.1 %collective-permute-start.2 = (bf16[128,512]{1,0:T(8,128)(2,1)S(1)}, bf16[128,512]{1,0:T(8,128)(2,1)S(1)}, u32[]{:S(2)}, u32[]{:S(2)}) collective-permute-start(bf16[128,512]{1,0:T(8,128)(2,1)S(1)} %get-tuple-element.98), channel_id=1, source_target_pairs={{0,12},{4,0},{8,4},{12,8},{1,13},{5,1},{9,5},{13,9},{2,14},{6,2},{... | collective-permute-start | bytes 393224 | tf_op jit(solution)/shard_map/ppermute | solution.py:53
  9.0 1.0 collective-permute-start.1
  10.0 1.6 collective-permute-start
  11.7 11.5 %collective-permute-done.2 = bf16[128,512]{1,0:T(8,128)(2,1)S(1)} collective-permute-done((bf16[128,512]{1,0:T(8,128)(2,1)S(1)}, bf16[128,512]{1,0:T(8,128)(2,1)S(1)}, u32[]{:S(2)}, u32[]{:S(2)}) %collective-permute-start.2) | collective-permute-done | bytes 131104 | tf_op jit(solution)/shard_map/ppermute | solution.py:53
  23.2 9.1 %collective-permute-done.1 = bf16[128,512]{1,0:T(8,128)(2,1)S(1)} collective-permute-done((bf16[128,512]{1,0:T(8,128)(2,1)S(1)}, bf16[128,512]{1,0:T(8,128)(2,1)S(1)}, u32[]{:S(2)}, u32[]{:S(2)}) %collective-permute-start.1) | collective-permute-done | bytes 131104 | tf_op jit(solution)/shard_map/ppermute | solution.py:53
  32.4 1.6 collective-permute-start.7
  34.0 1.5 collective-permute-start.4
  35.5 3.0 %convolution_convert_fusion = bf16[64,2048]{1,0:T(8,128)(2,1)S(1)} fusion(bf16[64,1024]{1,0:T(8,128)(2,1)S(1)} %compare_convert_fusion, bf16[1024,2048]{1,0:T(8,128)(2,1)} %param.26), kind=kOutput, calls=%fused_computation | convolution fusion | flops 268566528 | bytes 4587520 | tf_op jit(solution)/shard_map/dot_general | solution.py:555
  39.2 8.3 %collective-permute-done.4.refs_1_ = bf16[512,512]{1,0:T(8,128)(2,1)S(1)} collective-permute-done((bf16[512,512]{1,0:T(8,128)(2,1)S(1)}, bf16[512,512]{1,0:T(8,128)(2,1)S(1)}, u32[]{:S(2)}, u32[]{:S(2)}) %collective-permute-start.4) | collective-permute-done | bytes 524320 | tf_op jit(solution)/shard_map/ppermute | solution.py:48
  47.5 1.5 collective-permute-done.8.refs_3_
  50.2 0.7 pad_add_fusion.at_ref
  50.9 4.0 %copy.17 = bf16[2048,512]{0,1:T(8,128)(2,1)} copy(bf16[2048,512]{1,0:T(8,128)(2,1)} %param.25) | data formatting | bytes 4194304 | tf_op jit(solution)/shard_map/optimization_barrier | solution.py:57
  54.9 2.2 %collective-permute-done.12 = bf16[64,2048]{1,0:T(8,128)(2,1)S(1)} collective-permute-done((bf16[64,2048]{1,0:T(8,128)(2,1)S(1)}, bf16[64,2048]{1,0:T(8,128)(2,1)S(1)}, u32[]{:S(2)}, u32[]{:S(2)}) %collective-permute-start.12) | collective-permute-done | bytes 262176 | tf_op jit(solution)/shard_map/ppermute | solution.py:48
  57.2 0.8 copy-done.6
  58.1 4.3 %norm_events.1 = (bf16[512,2048]{1,0:T(8,128)(2,1)}, bf16[512,2048]{1,0:T(8,128)(2,1)}) custom-call(s32[4]{0:T(128)} %pad_add_fusion.at_ref, f32[1,2048]{1,0:T(1,128)} %bitcast.37, bf16[512,512]{1,0:T(8,128)(2,1)} %copy-done.1, bf16[512,512]{1,0:T(8,128)(2,1)} %copy-done.4, bf16[512,512]{1,0:T(8,128)(2,1)} %copy-done.6, bf16[512,512]{1,0:T(8,128)(2,1)} %copy-done.7), custom_call_target="tpu_custom_call" | custom-call | bytes 12000000 | tf_op jit(solution)/shard_map/norm_events/pallas_call | solution.py:202
  62.4 1.9 collective-permute-done.10.refs_5_
  64.3 1.5 collective-permute-start.13
  65.9 3.8 %collective-permute-start.15 = (bf16[256,512]{1,0:T(8,128)(2,1)S(1)}, bf16[256,512]{1,0:T(8,128)(2,1)S(1)}, u32[]{:S(2)}, u32[]{:S(2)}) collective-permute-start(bf16[256,512]{1,0:T(8,128)(2,1)S(1)} %get-tuple-element.93), channel_id=1, source_target_pairs={{0,12},{4,0},{8,4},{12,8},{1,13},{5,1},{9,5},{13,9},{2,14},{6,2},{... | collective-permute-start | bytes 786440 | tf_op jit(solution)/shard_map/ppermute | solution.py:53
  69.7 7.4 %collective-permute-done.14.refs_1_ = bf16[256,512]{1,0:T(8,128)(2,1)S(1)} collective-permute-done((bf16[256,512]{1,0:T(8,128)(2,1)S(1)}, bf16[256,512]{1,0:T(8,128)(2,1)S(1)}, u32[]{:S(2)}, u32[]{:S(2)}) %collective-permute-start.14) | collective-permute-done | bytes 262176 | tf_op jit(solution)/shard_map/ppermute | solution.py:53
  77.1 1.9 collective-permute-done.15.refs_3_
  79.5 1.5 collective-permute-start.17
  81.0 4.2 %collective-permute-start.19 = (bf16[256,512]{1,0:T(8,128)(2,1)S(1)}, bf16[256,512]{1,0:T(8,128)(2,1)S(1)}, u32[]{:S(2)}, u32[]{:S(2)}) collective-permute-start(bf16[256,512]{1,0:T(8,128)(2,1)S(1)} %get-tuple-element.65), channel_id=1, source_target_pairs={{0,8},{4,12},{8,0},{12,4},{1,9},{5,13},{9,1},{13,5},{2,10},{6,14},... | collective-permute-start | bytes 786440 | tf_op jit(solution)/shard_map/ppermute | solution.py:53
  85.9 10.8 %encoder_attention.1.attended_ref = bf16[512,512]{1,0:T(8,128)(2,1)} custom-call(s32[4]{0:T(128)} %pad_add_fusion.at_ref, s32[1]{0:T(128)S(6)} %copy.18.live_ref, bf16[512,2048]{1,0:T(8,128)(2,1)} %get-tuple-element.55.normed_ref, bf16[2,512,256]{2,1,0:T(8,128)(2,1)} %bitcast.32, bf16[512,1024]{1,0:T(8,128)(2,1)} %copy-done, ...), custom_call_target="tpu_custom_call" | custom-call | bytes 33000000 | tf_op jit(solution)/shard_map/encoder_attention/pallas_call | solution.py:302
  97.6 0.7 copy-done.26
  98.3 4.9 %project_out.1 = (bf16[256,2048]{1,0:T(8,128)(2,1)}, bf16[256,2048]{1,0:T(8,128)(2,1)}) custom-call(s32[4]{0:T(128)} %pad_add_fusion.at_ref, bf16[512,512]{1,0:T(8,128)(2,1)} %encoder_attention.1.attended_ref, bf16[512,512]{1,0:T(8,128)(2,1)} %refs_0_.1, bf16[256,512]{1,0:T(8,128)(2,1)} %copy-done.21, bf16[256,512]{1,0:T(8,128)(2,1)} %copy-done.24, ...), custom_call_target="tpu_custom_call" | custom-call | bytes 15000000 | tf_op jit(solution)/shard_map/project_out/pallas_call | solution.py:350
  103.3 2.9 %collective-permute-done.20 = bf16[256,2048]{1,0:T(8,128)(2,1)S(1)} collective-permute-done((bf16[256,2048]{1,0:T(8,128)(2,1)}, bf16[256,2048]{1,0:T(8,128)(2,1)S(1)}, u32[]{:S(2)}, u32[]{:S(2)}) %collective-permute-start.20) | collective-permute-done | bytes 1048608 | tf_op jit(solution)/shard_map/ppermute | solution.py:48
  106.1 1.2 add_convert_fusion
  107.3 1.5 collective-permute-start.21
  109.0 3.8 %collective-permute-start.23 = (bf16[256,512]{1,0:T(8,128)(2,1)S(1)}, bf16[256,512]{1,0:T(8,128)(2,1)S(1)}, u32[]{:S(2)}, u32[]{:S(2)}) collective-permute-start(bf16[256,512]{1,0:T(8,128)(2,1)S(1)} %get-tuple-element.68), channel_id=1, source_target_pairs={{0,12},{4,0},{8,4},{12,8},{1,13},{5,1},{9,5},{13,9},{2,14},{6,2},{... | collective-permute-start | bytes 786440 | tf_op jit(solution)/shard_map/ppermute | solution.py:53
  112.8 0.9 slice.42.refs_0_
  113.7 0.9 slice.52.refs_1_
  114.5 5.4 %collective-permute-done.22.refs_6_ = bf16[256,512]{1,0:T(8,128)(2,1)S(1)} collective-permute-done((bf16[256,512]{1,0:T(8,128)(2,1)S(1)}, bf16[256,512]{1,0:T(8,128)(2,1)S(1)}, u32[]{:S(2)}, u32[]{:S(2)}) %collective-permute-start.22) | collective-permute-done | bytes 262176 | tf_op jit(solution)/shard_map/ppermute | solution.py:53
  120.0 2.9 %collective-permute-done.23.refs_8_ = bf16[256,512]{1,0:T(8,128)(2,1)S(1)} collective-permute-done((bf16[256,512]{1,0:T(8,128)(2,1)S(1)}, bf16[256,512]{1,0:T(8,128)(2,1)S(1)}, u32[]{:S(2)}, u32[]{:S(2)}) %collective-permute-start.23) | collective-permute-done | bytes 262176 | tf_op jit(solution)/shard_map/ppermute | solution.py:53
  122.9 0.8 copy-done.12
  123.7 3.4 %merge_terms.1 = (bf16[128,2048]{1,0:T(8,128)(2,1)}, bf16[128,2048]{1,0:T(8,128)(2,1)}) custom-call(s32[4]{0:T(128)} %pad_add_fusion.at_ref, f32[1,2048]{1,0:T(1,128)} %bitcast.38, bf16[512,2048]{1,0:T(8,128)(2,1)} %get-tuple-element.46.source_ref, bf16[128,2048]{1,0:T(8,128)(2,1)} %slice.42.refs_0_, bf16[128,2048]{1,0:T(8,128)(2,1)} %slice.52.refs_1_, ...), custom_call_target="tpu_custom_call" | custom-call | bytes 9000000 | tf_op jit(solution)/shard_map/merge_terms/pallas_call | solution.py:383
  127.7 2.2 %collective-permute-start.25 = (bf16[256,512]{1,0:T(8,128)(2,1)S(1)}, bf16[256,512]{1,0:T(8,128)(2,1)S(1)}, u32[]{:S(2)}, u32[]{:S(2)}) collective-permute-start(bf16[256,512]{1,0:T(8,128)(2,1)S(1)} %get-tuple-element.73), channel_id=1, source_target_pairs={{0,8},{4,12},{8,0},{12,4},{1,9},{5,13},{9,1},{13,5},{2,10},{6,14},... | collective-permute-start | bytes 786440 | tf_op jit(solution)/shard_map/ppermute | solution.py:53
  130.6 1.5 collective-permute-start.27
  132.1 14.1 %collective-permute-done.25.refs_5_ = bf16[256,512]{1,0:T(8,128)(2,1)S(1)} collective-permute-done((bf16[256,512]{1,0:T(8,128)(2,1)S(1)}, bf16[256,512]{1,0:T(8,128)(2,1)S(1)}, u32[]{:S(2)}, u32[]{:S(2)}) %collective-permute-start.25) | collective-permute-done | bytes 262176 | tf_op jit(solution)/shard_map/ppermute | solution.py:53
  146.9 0.9 pad_maximum_fusion.1.refs_4_
  147.8 0.7 fusion.2
  149.3 0.8 copy-done.9
  150.1 5.2 %cross_project.1.cross_ref = bf16[512,512]{1,0:T(8,128)(2,1)} custom-call(s32[4]{0:T(128)} %pad_add_fusion.at_ref, bf16[128,2048]{1,0:T(8,128)(2,1)} %get-tuple-element.72.refs_0_, bf16[128,2048]{1,0:T(8,128)(2,1)} %copy-done.5, bf16[128,2048]{1,0:T(8,128)(2,1)} %copy-done.8, bf16[128,2048]{1,0:T(8,128)(2,1)} %copy-done.9, ...), custom_call_target="tpu_custom_call" | custom-call | bytes 15000000 | tf_op jit(solution)/shard_map/cross_project/pallas_call | solution.py:413
  155.3 4.4 %beam_step_0.1 = (f32[16,2048]{1,0:T(8,128)}, bf16[16,2048]{1,0:T(8,128)(2,1)}) custom-call(s32[4]{0:T(128)} %pad_add_fusion.at_ref, s32[1]{0:T(128)S(6)} %copy.18.live_ref, s32[3,16]{1,0:T(4,128)} %parent_ref.7, f32[1,2048]{1,0:T(1,128)} %bitcast.33, bf16[2048,512]{1,0:T(8,128)(2,1)} %query_ref.7, bf16[512,2048]{1,0:T(8,128)(2,1)} %bitcast.28, ...), custom_call_target="tpu_custom_call" | custom-call | bytes 12000000 | tf_op jit(solution)/shard_map/beam_step_0/pallas_call | solution.py:511
  159.8 1.4 collective-permute-start.32
  161.5 2.9 %collective-permute-done.32.refs_3_ = bf16[16,2048]{1,0:T(8,128)(2,1)S(1)} collective-permute-done((bf16[16,2048]{1,0:T(8,128)(2,1)}, bf16[16,2048]{1,0:T(8,128)(2,1)S(1)}, u32[]{:S(2)}, u32[]{:S(2)}) %collective-permute-start.32) | collective-permute-done | bytes 65568 | tf_op jit(solution)/shard_map/ppermute | solution.py:653
  164.4 1.2 collective-permute-done.33.refs_4_
  166.2 4.6 %beam_step_1.1 = (f32[16,2048]{1,0:T(8,128)}, bf16[16,2048]{1,0:T(8,128)(2,1)}) custom-call(s32[4]{0:T(128)} %pad_add_fusion.at_ref, s32[1]{0:T(128)S(6)} %copy.18.live_ref, s32[3,16]{1,0:T(4,128)} %parent_ref.7, f32[1,2048]{1,0:T(1,128)} %bitcast.34, bf16[2048,512]{1,0:T(8,128)(2,1)} %query_ref.7, bf16[512,2048]{1,0:T(8,128)(2,1)} %bitcast.29, ...), custom_call_target="tpu_custom_call" | custom-call | bytes 12000000 | tf_op jit(solution)/shard_map/beam_step_1/pallas_call | solution.py:511
  170.9 1.3 collective-permute-start.35
  172.7 3.0 %collective-permute-done.35.refs_3_ = bf16[16,2048]{1,0:T(8,128)(2,1)S(1)} collective-permute-done((bf16[16,2048]{1,0:T(8,128)(2,1)}, bf16[16,2048]{1,0:T(8,128)(2,1)S(1)}, u32[]{:S(2)}, u32[]{:S(2)}) %collective-permute-start.35) | collective-permute-done | bytes 65568 | tf_op jit(solution)/shard_map/ppermute | solution.py:653
  175.7 1.1 collective-permute-done.36.refs_4_
  177.4 4.6 %beam_step_2.1 = (f32[16,2048]{1,0:T(8,128)}, bf16[16,2048]{1,0:T(8,128)(2,1)}) custom-call(s32[4]{0:T(128)} %pad_add_fusion.at_ref, s32[1]{0:T(128)S(6)} %copy.18.live_ref, s32[3,16]{1,0:T(4,128)} %parent_ref.7, f32[1,2048]{1,0:T(1,128)} %bitcast.35, bf16[2048,512]{1,0:T(8,128)(2,1)} %query_ref.7, bf16[512,2048]{1,0:T(8,128)(2,1)} %bitcast.30, ...), custom_call_target="tpu_custom_call" | custom-call | bytes 12000000 | tf_op jit(solution)/shard_map/beam_step_2/pallas_call | solution.py:511
  182.2 1.0 collective-permute-start.38
  183.2 0.7 collective-permute-start.39
  183.9 3.2 %collective-permute-done.38.refs_3_ = bf16[16,2048]{1,0:T(8,128)(2,1)S(1)} collective-permute-done((bf16[16,2048]{1,0:T(8,128)(2,1)}, bf16[16,2048]{1,0:T(8,128)(2,1)S(1)}, u32[]{:S(2)}, u32[]{:S(2)}) %collective-permute-start.38) | collective-permute-done | bytes 65568 | tf_op jit(solution)/shard_map/ppermute | solution.py:653
  188.4 4.6 %beam_step_3.1 = (f32[16,512]{1,0:T(8,128)}, bf16[16,512]{1,0:T(8,128)(2,1)}, bf16[16,512]{1,0:T(8,128)(2,1)}, bf16[16,512]{1,0:T(8,128)(2,1)}) custom-call(s32[4]{0:T(128)} %pad_add_fusion.at_ref, s32[1]{0:T(128)S(6)} %copy.18.live_ref, s32[3,16]{1,0:T(4,128)} %parent_ref.7, f32[1,2048]{1,0:T(1,128)} %bitcast.36, bf16[2048,512]{1,0:T(8,128)(2,1)} %query_ref.7, ...), custom_call_target="tpu_custom_call" | custom-call | bytes 12000000 | tf_op jit(solution)/shard_map/beam_step_3/pallas_call | solution.py:511
  193.0 0.7 collective-permute-start.42
  193.7 1.1 collective-permute-start.41
  194.9 1.5 collective-permute-done.42
  196.4 1.3 collective-permute-done.41
  197.7 1.4 add_convert_fusion.1
  (127 shorter events, 10.5 us)
Async XLA Ops:
  0.6 6.3 %copy-start.10 = (bf16[4,128,512]{2,1,0:T(8,128)(2,1)S(1)}, bf16[4,128,512]{2,1,0:T(8,128)(2,1)}, u32[]{:S(2)}) copy-start(bf16[4,128,512]{2,1,0:T(8,128)(2,1)} %param.15) | copy-start | bytes 1572868
  1.8 9.9 %copy-start.36 = (s32[4,16]{1,0:T(4,128)S(1)}, s32[4,16]{1,0:T(4,128)}, u32[]{:S(2)}) copy-start(s32[4,16]{1,0:T(4,128)} %param.18) | copy-start | bytes 772
  3.0 35.6 %copy-start = (bf16[512,1024]{1,0:T(8,128)(2,1)}, bf16[512,1024]{1,0:T(8,128)(2,1)S(1)}, u32[]{:S(2)}) copy-start(bf16[512,1024]{1,0:T(8,128)(2,1)S(1)} %pad_maximum_fusion.refs_0_) | copy-start | bytes 3145732
  3.9 28.5 %collective-permute-start.3 = (bf16[256,1024]{1,0:T(8,128)(2,1)}, bf16[256,1024]{1,0:T(8,128)(2,1)}, u32[]{:S(2)}, u32[]{:S(2)}) collective-permute-start(bf16[256,1024]{1,0:T(8,128)(2,1)} %constant_dynamic-slice_fusion.2), channel_id=1, source_target_pairs={{0,4},{4,8},{8,12},{12,0},{1,5},{5,9},{9,13},{13,1},{2,6},{6,10},{... | collective-permute-start | bytes 1572872 | tf_op jit(solution)/shard_map/ppermute | solution.py:53
  7.0 16.2 %collective-permute-start.2 = (bf16[128,512]{1,0:T(8,128)(2,1)S(1)}, bf16[128,512]{1,0:T(8,128)(2,1)S(1)}, u32[]{:S(2)}, u32[]{:S(2)}) collective-permute-start(bf16[128,512]{1,0:T(8,128)(2,1)S(1)} %get-tuple-element.98), channel_id=1, source_target_pairs={{0,12},{4,0},{8,4},{12,8},{1,13},{5,1},{9,5},{13,9},{2,14},{6,2},{... | collective-permute-start | bytes 393224 | tf_op jit(solution)/shard_map/ppermute | solution.py:53
  9.0 23.3 %collective-permute-start.1 = (bf16[128,512]{1,0:T(8,128)(2,1)S(1)}, bf16[128,512]{1,0:T(8,128)(2,1)S(1)}, u32[]{:S(2)}, u32[]{:S(2)}) collective-permute-start(bf16[128,512]{1,0:T(8,128)(2,1)S(1)} %get-tuple-element.99), channel_id=1, source_target_pairs={{0,8},{4,12},{8,0},{12,4},{1,9},{5,13},{9,1},{13,5},{2,10},{6,14},... | collective-permute-start | bytes 393224 | tf_op jit(solution)/shard_map/ppermute | solution.py:53
  10.0 22.3 %collective-permute-start = (bf16[128,512]{1,0:T(8,128)(2,1)S(1)}, bf16[128,512]{1,0:T(8,128)(2,1)S(1)}, u32[]{:S(2)}, u32[]{:S(2)}) collective-permute-start(bf16[128,512]{1,0:T(8,128)(2,1)S(1)} %get-tuple-element.97), channel_id=1, source_target_pairs={{0,4},{4,8},{8,12},{12,0},{1,5},{5,9},{9,13},{13,1},{2,6},{6,10},{... | collective-permute-start | bytes 393224 | tf_op jit(solution)/shard_map/ppermute | solution.py:53
  32.3 6.3 %copy-start.1 = (bf16[512,512]{1,0:T(8,128)(2,1)}, bf16[512,512]{1,0:T(8,128)(2,1)S(1)}, u32[]{:S(2)}) copy-start(bf16[512,512]{1,0:T(8,128)(2,1)S(1)} %pad_maximum_fusion.2.refs_0_) | copy-start | bytes 1572868
  32.4 15.2 %collective-permute-start.7 = (bf16[256,1024]{1,0:T(8,128)(2,1)}, bf16[256,1024]{1,0:T(8,128)(2,1)S(1)}, u32[]{:S(2)}, u32[]{:S(2)}) collective-permute-start(bf16[256,1024]{1,0:T(8,128)(2,1)} %collective-permute-done.3.refs_1_), channel_id=1, source_target_pairs={{0,16},{16,0},{1,17},{17,1},{2,18},{18,2},{3,19},{19,3},{4,20},{20... | collective-permute-start | bytes 1572872 | tf_op jit(solution)/shard_map/ppermute | solution.py:48
  34.0 13.6 %collective-permute-start.4 = (bf16[512,512]{1,0:T(8,128)(2,1)S(1)}, bf16[512,512]{1,0:T(8,128)(2,1)S(1)}, u32[]{:S(2)}, u32[]{:S(2)}) collective-permute-start(bf16[512,512]{1,0:T(8,128)(2,1)S(1)} %pad_maximum_fusion.2.refs_0_), channel_id=1, source_target_pairs={{0,2},{2,0},{1,3},{3,1},{4,6},{6,4},{5,7},{7,5},{8,10},{10,8},{9,1... | collective-permute-start | bytes 1572872 | tf_op jit(solution)/shard_map/ppermute | solution.py:48
  35.4 13.6 %collective-permute-start.8 = (bf16[256,1024]{1,0:T(8,128)(2,1)}, bf16[256,1024]{1,0:T(8,128)(2,1)}, u32[]{:S(2)}, u32[]{:S(2)}) collective-permute-start(bf16[256,1024]{1,0:T(8,128)(2,1)} %constant_dynamic-slice_fusion.2), channel_id=1, source_target_pairs={{0,12},{4,0},{8,4},{12,8},{1,13},{5,1},{9,5},{13,9},{2,14},{6,2},{... | collective-permute-start | bytes 1572872 | tf_op jit(solution)/shard_map/ppermute | solution.py:53
  38.6 11.0 %collective-permute-start.11 = (bf16[64,2048]{1,0:T(8,128)(2,1)S(1)}, bf16[64,2048]{1,0:T(8,128)(2,1)S(1)}, u32[]{:S(2)}, u32[]{:S(2)}) collective-permute-start(bf16[64,2048]{1,0:T(8,128)(2,1)S(1)} %convolution_convert_fusion), channel_id=1, source_target_pairs={{0,1},{1,0},{2,3},{3,2},{4,5},{5,4},{6,7},{7,6},{8,9},{9,8},{10,11... | collective-permute-start | bytes 786440 | tf_op jit(solution)/shard_map/ppermute | solution.py:48
  38.7 18.4 %collective-permute-start.5 = (bf16[512,512]{1,0:T(8,128)(2,1)S(1)}, bf16[512,512]{1,0:T(8,128)(2,1)S(1)}, u32[]{:S(2)}, u32[]{:S(2)}) collective-permute-start(bf16[512,512]{1,0:T(8,128)(2,1)S(1)} %pad_maximum_fusion.2.refs_0_), channel_id=1, source_target_pairs={{0,1},{1,0},{2,3},{3,2},{4,5},{5,4},{6,7},{7,6},{8,9},{9,8},{10,11... | collective-permute-start | bytes 1572872 | tf_op jit(solution)/shard_map/ppermute | solution.py:48
  47.5 7.4 %copy-start.4 = (bf16[512,512]{1,0:T(8,128)(2,1)}, bf16[512,512]{1,0:T(8,128)(2,1)S(1)}, u32[]{:S(2)}) copy-start(bf16[512,512]{1,0:T(8,128)(2,1)S(1)} %collective-permute-done.4.refs_1_) | copy-start | bytes 1572868
  47.5 9.6 %collective-permute-start.6 = (bf16[512,512]{1,0:T(8,128)(2,1)S(1)}, bf16[512,512]{1,0:T(8,128)(2,1)S(1)}, u32[]{:S(2)}, u32[]{:S(2)}) collective-permute-start(bf16[512,512]{1,0:T(8,128)(2,1)S(1)} %collective-permute-done.4.refs_1_), channel_id=1, source_target_pairs={{0,1},{1,0},{2,3},{3,2},{4,5},{5,4},{6,7},{7,6},{8,9},{9,8},{10,11... | collective-permute-start | bytes 1572872 | tf_op jit(solution)/shard_map/ppermute | solution.py:48
  49.0 13.3 %collective-permute-start.9 = (bf16[256,1024]{1,0:T(8,128)(2,1)}, bf16[256,1024]{1,0:T(8,128)(2,1)}, u32[]{:S(2)}, u32[]{:S(2)}) collective-permute-start(bf16[256,1024]{1,0:T(8,128)(2,1)} %collective-permute-done.8.refs_3_), channel_id=1, source_target_pairs={{0,16},{16,0},{1,17},{17,1},{2,18},{18,2},{3,19},{19,3},{4,20},{20... | collective-permute-start | bytes 1572872 | tf_op jit(solution)/shard_map/ppermute | solution.py:48
  49.6 14.7 %collective-permute-start.10 = (bf16[256,1024]{1,0:T(8,128)(2,1)}, bf16[256,1024]{1,0:T(8,128)(2,1)}, u32[]{:S(2)}, u32[]{:S(2)}) collective-permute-start(bf16[256,1024]{1,0:T(8,128)(2,1)} %collective-permute-done.3.refs_1_), channel_id=1, source_target_pairs={{0,4},{4,8},{8,12},{12,0},{1,5},{5,9},{9,13},{13,1},{2,6},{6,10},{... | collective-permute-start | bytes 1572872 | tf_op jit(solution)/shard_map/ppermute | solution.py:53
  49.6 7.4 %collective-permute-start.12 = (bf16[64,2048]{1,0:T(8,128)(2,1)S(1)}, bf16[64,2048]{1,0:T(8,128)(2,1)S(1)}, u32[]{:S(2)}, u32[]{:S(2)}) collective-permute-start(bf16[64,2048]{1,0:T(8,128)(2,1)S(1)} %add.87), channel_id=1, source_target_pairs={{0,2},{2,0},{1,3},{3,1},{4,6},{6,4},{5,7},{7,5},{8,10},{10,8},{9,1... | collective-permute-start | bytes 786440 | tf_op jit(solution)/shard_map/ppermute | solution.py:48
  54.9 10.9 %copy-start.2 = (bf16[512,512]{1,0:T(8,128)(2,1)S(1)}, bf16[512,512]{1,0:T(8,128)(2,1)}, u32[]{:S(2)}) copy-start(bf16[512,512]{1,0:T(8,128)(2,1)} %refs_0_.1) | copy-start | bytes 1572868
  64.3 14.7 %collective-permute-start.13 = (bf16[256,1024]{1,0:T(8,128)(2,1)}, bf16[256,1024]{1,0:T(8,128)(2,1)S(1)}, u32[]{:S(2)}, u32[]{:S(2)}) collective-permute-start(bf16[256,1024]{1,0:T(8,128)(2,1)} %collective-permute-done.10.refs_5_), channel_id=1, source_target_pairs={{0,16},{16,0},{1,17},{17,1},{2,18},{18,2},{3,19},{19,3},{4,20},{20... | collective-permute-start | bytes 1572872 | tf_op jit(solution)/shard_map/ppermute | solution.py:48
  65.8 11.2 %collective-permute-start.14 = (bf16[256,512]{1,0:T(8,128)(2,1)S(1)}, bf16[256,512]{1,0:T(8,128)(2,1)S(1)}, u32[]{:S(2)}, u32[]{:S(2)}) collective-permute-start(bf16[256,512]{1,0:T(8,128)(2,1)S(1)} %get-tuple-element.93), channel_id=1, source_target_pairs={{0,4},{4,8},{8,12},{12,0},{1,5},{5,9},{9,13},{13,1},{2,6},{6,10},{... | collective-permute-start | bytes 786440 | tf_op jit(solution)/shard_map/ppermute | solution.py:53
  65.9 13.0 %collective-permute-start.15 = (bf16[256,512]{1,0:T(8,128)(2,1)S(1)}, bf16[256,512]{1,0:T(8,128)(2,1)S(1)}, u32[]{:S(2)}, u32[]{:S(2)}) collective-permute-start(bf16[256,512]{1,0:T(8,128)(2,1)S(1)} %get-tuple-element.93), channel_id=1, source_target_pairs={{0,12},{4,0},{8,4},{12,8},{1,13},{5,1},{9,5},{13,9},{2,14},{6,2},{... | collective-permute-start | bytes 786440 | tf_op jit(solution)/shard_map/ppermute | solution.py:53
  77.1 19.7 %copy-start.21 = (bf16[256,512]{1,0:T(8,128)(2,1)}, bf16[256,512]{1,0:T(8,128)(2,1)S(1)}, u32[]{:S(2)}) copy-start(bf16[256,512]{1,0:T(8,128)(2,1)S(1)} %collective-permute-done.14.refs_1_) | copy-start | bytes 786436
  77.1 19.6 %collective-permute-start.18 = (bf16[256,512]{1,0:T(8,128)(2,1)S(1)}, bf16[256,512]{1,0:T(8,128)(2,1)S(1)}, u32[]{:S(2)}, u32[]{:S(2)}) collective-permute-start(bf16[256,512]{1,0:T(8,128)(2,1)S(1)} %collective-permute-done.14.refs_1_), channel_id=1, source_target_pairs={{0,4},{4,8},{8,12},{12,0},{1,5},{5,9},{9,13},{13,1},{2,6},{6,10},{... | collective-permute-start | bytes 786440 | tf_op jit(solution)/shard_map/ppermute | solution.py:53
  78.9 17.8 %copy-start.22 = (bf16[256,512]{1,0:T(8,128)(2,1)}, bf16[256,512]{1,0:T(8,128)(2,1)S(1)}, u32[]{:S(2)}) copy-start(bf16[256,512]{1,0:T(8,128)(2,1)S(1)} %collective-permute-done.15.refs_3_) | copy-start | bytes 786436
  79.0 7.0 %copy-start.14 = (bf16[256,1024]{1,0:T(8,128)(2,1)}, bf16[256,1024]{1,0:T(8,128)(2,1)S(1)}, u32[]{:S(2)}) copy-start(bf16[256,1024]{1,0:T(8,128)(2,1)S(1)} %collective-permute-done.13.refs_6_) | copy-start | bytes 1572868
  79.0 17.8 %collective-permute-start.16 = (bf16[256,512]{1,0:T(8,128)(2,1)S(1)}, bf16[256,512]{1,0:T(8,128)(2,1)S(1)}, u32[]{:S(2)}, u32[]{:S(2)}) collective-permute-start(bf16[256,512]{1,0:T(8,128)(2,1)S(1)} %collective-permute-done.14.refs_1_), channel_id=1, source_target_pairs={{0,16},{16,0},{1,17},{17,1},{2,18},{18,2},{3,19},{19,3},{4,20},{20... | collective-permute-start | bytes 786440 | tf_op jit(solution)/shard_map/ppermute | solution.py:48
  79.5 17.2 %collective-permute-start.17 = (bf16[256,512]{1,0:T(8,128)(2,1)S(1)}, bf16[256,512]{1,0:T(8,128)(2,1)S(1)}, u32[]{:S(2)}, u32[]{:S(2)}) collective-permute-start(bf16[256,512]{1,0:T(8,128)(2,1)S(1)} %collective-permute-done.15.refs_3_), channel_id=1, source_target_pairs={{0,16},{16,0},{1,17},{17,1},{2,18},{18,2},{3,19},{19,3},{4,20},{20... | collective-permute-start | bytes 786440 | tf_op jit(solution)/shard_map/ppermute | solution.py:48
  81.0 15.7 %collective-permute-start.19 = (bf16[256,512]{1,0:T(8,128)(2,1)S(1)}, bf16[256,512]{1,0:T(8,128)(2,1)S(1)}, u32[]{:S(2)}, u32[]{:S(2)}) collective-permute-start(bf16[256,512]{1,0:T(8,128)(2,1)S(1)} %get-tuple-element.65), channel_id=1, source_target_pairs={{0,8},{4,12},{8,0},{12,4},{1,9},{5,13},{9,1},{13,5},{2,10},{6,14},... | collective-permute-start | bytes 786440 | tf_op jit(solution)/shard_map/ppermute | solution.py:53
  96.7 12.1 %copy-start.11 = (bf16[2,512,256]{2,1,0:T(8,128)(2,1)S(1)}, bf16[2,512,256]{2,1,0:T(8,128)(2,1)}, u32[]{:S(2)}) copy-start(bf16[2,512,256]{2,1,0:T(8,128)(2,1)} %param.23) | copy-start | bytes 1572868
  103.2 9.6 %copy-start.3 = (bf16[256,2048]{1,0:T(8,128)(2,1)S(1)}, bf16[256,2048]{1,0:T(8,128)(2,1)}, u32[]{:S(2)}) copy-start(bf16[256,2048]{1,0:T(8,128)(2,1)} %get-tuple-element.66) | copy-start | bytes 3145732
  103.2 2.9 %collective-permute-start.20 = (bf16[256,2048]{1,0:T(8,128)(2,1)}, bf16[256,2048]{1,0:T(8,128)(2,1)S(1)}, u32[]{:S(2)}, u32[]{:S(2)}) collective-permute-start(bf16[256,2048]{1,0:T(8,128)(2,1)} %get-tuple-element.67), channel_id=1, source_target_pairs={{0,1},{1,0},{2,3},{3,2},{4,5},{5,4},{6,7},{7,6},{8,9},{9,8},{10,11... | collective-permute-start | bytes 3145736 | tf_op jit(solution)/shard_map/ppermute | solution.py:48
  107.3 15.6 %collective-permute-start.21 = (bf16[128,2048]{1,0:T(8,128)(2,1)S(1)}, bf16[128,2048]{1,0:T(8,128)(2,1)S(1)}, u32[]{:S(2)}, u32[]{:S(2)}) collective-permute-start(bf16[128,2048]{1,0:T(8,128)(2,1)S(1)} %add_convert_fusion), channel_id=1, source_target_pairs={{0,2},{2,0},{1,3},{3,1},{4,6},{6,4},{5,7},{7,5},{8,10},{10,8},{9,1... | collective-permute-start | bytes 1572872 | tf_op jit(solution)/shard_map/ppermute | solution.py:48
  108.9 11.0 %collective-permute-start.22 = (bf16[256,512]{1,0:T(8,128)(2,1)S(1)}, bf16[256,512]{1,0:T(8,128)(2,1)S(1)}, u32[]{:S(2)}, u32[]{:S(2)}) collective-permute-start(bf16[256,512]{1,0:T(8,128)(2,1)S(1)} %get-tuple-element.68), channel_id=1, source_target_pairs={{0,4},{4,8},{8,12},{12,0},{1,5},{5,9},{9,13},{13,1},{2,6},{6,10},{... | collective-permute-start | bytes 786440 | tf_op jit(solution)/shard_map/ppermute | solution.py:53
  109.0 13.9 %collective-permute-start.23 = (bf16[256,512]{1,0:T(8,128)(2,1)S(1)}, bf16[256,512]{1,0:T(8,128)(2,1)S(1)}, u32[]{:S(2)}, u32[]{:S(2)}) collective-permute-start(bf16[256,512]{1,0:T(8,128)(2,1)S(1)} %get-tuple-element.68), channel_id=1, source_target_pairs={{0,12},{4,0},{8,4},{12,8},{1,13},{5,1},{9,5},{13,9},{2,14},{6,2},{... | collective-permute-start | bytes 786440 | tf_op jit(solution)/shard_map/ppermute | solution.py:53
  120.0 29.0 %copy-start.15 = (bf16[256,512]{1,0:T(8,128)(2,1)}, bf16[256,512]{1,0:T(8,128)(2,1)S(1)}, u32[]{:S(2)}) copy-start(bf16[256,512]{1,0:T(8,128)(2,1)S(1)} %collective-permute-done.22.refs_6_) | copy-start | bytes 786436
  122.9 26.0 %copy-start.16 = (bf16[256,512]{1,0:T(8,128)(2,1)}, bf16[256,512]{1,0:T(8,128)(2,1)S(1)}, u32[]{:S(2)}) copy-start(bf16[256,512]{1,0:T(8,128)(2,1)S(1)} %collective-permute-done.23.refs_8_) | copy-start | bytes 786436
  127.1 19.2 %collective-permute-start.24 = (bf16[128,2048]{1,0:T(8,128)(2,1)}, bf16[128,2048]{1,0:T(8,128)(2,1)S(1)}, u32[]{:S(2)}, u32[]{:S(2)}) collective-permute-start(bf16[128,2048]{1,0:T(8,128)(2,1)} %get-tuple-element.72.refs_0_), channel_id=1, source_target_pairs={{0,2},{2,0},{1,3},{3,1},{4,6},{6,4},{5,7},{7,5},{8,10},{10,8},{9,1... | collective-permute-start | bytes 1572872 | tf_op jit(solution)/shard_map/ppermute | solution.py:48
  127.7 18.6 %collective-permute-start.25 = (bf16[256,512]{1,0:T(8,128)(2,1)S(1)}, bf16[256,512]{1,0:T(8,128)(2,1)S(1)}, u32[]{:S(2)}, u32[]{:S(2)}) collective-permute-start(bf16[256,512]{1,0:T(8,128)(2,1)S(1)} %get-tuple-element.73), channel_id=1, source_target_pairs={{0,8},{4,12},{8,0},{12,4},{1,9},{5,13},{9,1},{13,5},{2,10},{6,14},... | collective-permute-start | bytes 786440 | tf_op jit(solution)/shard_map/ppermute | solution.py:53
  129.9 16.4 %collective-permute-start.28 = (bf16[256,512]{1,0:T(8,128)(2,1)S(1)}, bf16[256,512]{1,0:T(8,128)(2,1)S(1)}, u32[]{:S(2)}, u32[]{:S(2)}) collective-permute-start(bf16[256,512]{1,0:T(8,128)(2,1)S(1)} %collective-permute-done.22.refs_6_), channel_id=1, source_target_pairs={{0,4},{4,8},{8,12},{12,0},{1,5},{5,9},{9,13},{13,1},{2,6},{6,10},{... | collective-permute-start | bytes 786440 | tf_op jit(solution)/shard_map/ppermute | solution.py:53
  130.1 16.2 %collective-permute-start.26 = (bf16[256,512]{1,0:T(8,128)(2,1)S(1)}, bf16[256,512]{1,0:T(8,128)(2,1)S(1)}, u32[]{:S(2)}, u32[]{:S(2)}) collective-permute-start(bf16[256,512]{1,0:T(8,128)(2,1)S(1)} %collective-permute-done.22.refs_6_), channel_id=1, source_target_pairs={{0,16},{16,0},{1,17},{17,1},{2,18},{18,2},{3,19},{19,3},{4,20},{20... | collective-permute-start | bytes 786440 | tf_op jit(solution)/shard_map/ppermute | solution.py:48
  130.6 15.7 %collective-permute-start.27 = (bf16[256,512]{1,0:T(8,128)(2,1)S(1)}, bf16[256,512]{1,0:T(8,128)(2,1)S(1)}, u32[]{:S(2)}, u32[]{:S(2)}) collective-permute-start(bf16[256,512]{1,0:T(8,128)(2,1)S(1)} %collective-permute-done.23.refs_8_), channel_id=1, source_target_pairs={{0,16},{16,0},{1,17},{17,1},{2,18},{18,2},{3,19},{19,3},{4,20},{20... | collective-permute-start | bytes 786440 | tf_op jit(solution)/shard_map/ppermute | solution.py:48
  146.3 2.7 %copy-start.17 = (bf16[256,512]{1,0:T(8,128)(2,1)}, bf16[256,512]{1,0:T(8,128)(2,1)S(1)}, u32[]{:S(2)}) copy-start(bf16[256,512]{1,0:T(8,128)(2,1)S(1)} %collective-permute-done.25.refs_5_) | copy-start | bytes 786436
  146.3 2.2 %collective-permute-start.29 = (bf16[128,2048]{1,0:T(8,128)(2,1)}, bf16[128,2048]{1,0:T(8,128)(2,1)S(1)}, u32[]{:S(2)}, u32[]{:S(2)}) collective-permute-start(bf16[128,2048]{1,0:T(8,128)(2,1)} %get-tuple-element.72.refs_0_), channel_id=1, source_target_pairs={{0,1},{1,0},{2,3},{3,2},{4,5},{5,4},{6,7},{7,6},{8,9},{9,8},{10,11... | collective-permute-start | bytes 1572872 | tf_op jit(solution)/shard_map/ppermute | solution.py:48
  146.3 2.7 %copy-start.18 = (bf16[256,512]{1,0:T(8,128)(2,1)}, bf16[256,512]{1,0:T(8,128)(2,1)S(1)}, u32[]{:S(2)}) copy-start(bf16[256,512]{1,0:T(8,128)(2,1)S(1)} %collective-permute-done.28.refs_10_) | copy-start | bytes 786436
  146.3 2.7 %copy-start.19 = (bf16[256,512]{1,0:T(8,128)(2,1)}, bf16[256,512]{1,0:T(8,128)(2,1)S(1)}, u32[]{:S(2)}) copy-start(bf16[256,512]{1,0:T(8,128)(2,1)S(1)} %collective-permute-done.26.refs_7_) | copy-start | bytes 786436
  146.3 2.6 %copy-start.20 = (bf16[256,512]{1,0:T(8,128)(2,1)}, bf16[256,512]{1,0:T(8,128)(2,1)S(1)}, u32[]{:S(2)}) copy-start(bf16[256,512]{1,0:T(8,128)(2,1)S(1)} %collective-permute-done.27.refs_9_) | copy-start | bytes 786436
  146.3 2.6 %copy-start.5 = (bf16[128,2048]{1,0:T(8,128)(2,1)}, bf16[128,2048]{1,0:T(8,128)(2,1)S(1)}, u32[]{:S(2)}) copy-start(bf16[128,2048]{1,0:T(8,128)(2,1)S(1)} %collective-permute-done.24.refs_1_) | copy-start | bytes 1572868
  146.4 2.6 %collective-permute-start.30 = (bf16[128,2048]{1,0:T(8,128)(2,1)S(1)}, bf16[128,2048]{1,0:T(8,128)(2,1)S(1)}, u32[]{:S(2)}, u32[]{:S(2)}) collective-permute-start(bf16[128,2048]{1,0:T(8,128)(2,1)S(1)} %collective-permute-done.24.refs_1_), channel_id=1, source_target_pairs={{0,1},{1,0},{2,3},{3,2},{4,5},{5,4},{6,7},{7,6},{8,9},{9,8},{10,11... | collective-permute-start | bytes 1572872 | tf_op jit(solution)/shard_map/ppermute | solution.py:48
  159.7 1.9 collective-permute-start.31
  159.8 4.6 %collective-permute-start.32 = (bf16[16,2048]{1,0:T(8,128)(2,1)}, bf16[16,2048]{1,0:T(8,128)(2,1)S(1)}, u32[]{:S(2)}, u32[]{:S(2)}) collective-permute-start(bf16[16,2048]{1,0:T(8,128)(2,1)} %get-tuple-element.79.refs_1_), channel_id=1, source_target_pairs={{0,2},{1,3},{2,0},{3,1},{4,6},{5,7},{6,4},{7,5},{8,10},{9,11},{10,... | collective-permute-start | bytes 196616 | tf_op jit(solution)/shard_map/ppermute | solution.py:653
  161.2 4.4 %collective-permute-start.33 = (bf16[16,2048]{1,0:T(8,128)(2,1)}, bf16[16,2048]{1,0:T(8,128)(2,1)S(1)}, u32[]{:S(2)}, u32[]{:S(2)}) collective-permute-start(bf16[16,2048]{1,0:T(8,128)(2,1)} %get-tuple-element.79.refs_1_), channel_id=1, source_target_pairs={{0,3},{1,2},{2,1},{3,0},{4,7},{5,6},{6,5},{7,4},{8,11},{9,10},{10,... | collective-permute-start | bytes 196616 | tf_op jit(solution)/shard_map/ppermute | solution.py:653
  161.5 4.1 %copy-start.30 = (bf16[16,2048]{1,0:T(8,128)(2,1)}, bf16[16,2048]{1,0:T(8,128)(2,1)S(1)}, u32[]{:S(2)}) copy-start(bf16[16,2048]{1,0:T(8,128)(2,1)S(1)} %collective-permute-done.31.refs_2_) | copy-start | bytes 196612
  170.8 1.9 collective-permute-start.34
  170.9 4.7 %collective-permute-start.35 = (bf16[16,2048]{1,0:T(8,128)(2,1)}, bf16[16,2048]{1,0:T(8,128)(2,1)S(1)}, u32[]{:S(2)}, u32[]{:S(2)}) collective-permute-start(bf16[16,2048]{1,0:T(8,128)(2,1)} %get-tuple-element.81.refs_1_), channel_id=1, source_target_pairs={{0,2},{1,3},{2,0},{3,1},{4,6},{5,7},{6,4},{7,5},{8,10},{9,11},{10,... | collective-permute-start | bytes 196616 | tf_op jit(solution)/shard_map/ppermute | solution.py:653
  172.3 4.6 %collective-permute-start.36 = (bf16[16,2048]{1,0:T(8,128)(2,1)}, bf16[16,2048]{1,0:T(8,128)(2,1)S(1)}, u32[]{:S(2)}, u32[]{:S(2)}) collective-permute-start(bf16[16,2048]{1,0:T(8,128)(2,1)} %get-tuple-element.81.refs_1_), channel_id=1, source_target_pairs={{0,3},{1,2},{2,1},{3,0},{4,7},{5,6},{6,5},{7,4},{8,11},{9,10},{10,... | collective-permute-start | bytes 196616 | tf_op jit(solution)/shard_map/ppermute | solution.py:653
  172.7 4.1 %copy-start.31 = (bf16[16,2048]{1,0:T(8,128)(2,1)}, bf16[16,2048]{1,0:T(8,128)(2,1)S(1)}, u32[]{:S(2)}) copy-start(bf16[16,2048]{1,0:T(8,128)(2,1)S(1)} %collective-permute-done.34.refs_2_) | copy-start | bytes 196612
  182.0 1.9 collective-permute-start.37
  182.2 5.0 %collective-permute-start.38 = (bf16[16,2048]{1,0:T(8,128)(2,1)}, bf16[16,2048]{1,0:T(8,128)(2,1)S(1)}, u32[]{:S(2)}, u32[]{:S(2)}) collective-permute-start(bf16[16,2048]{1,0:T(8,128)(2,1)} %get-tuple-element.83.refs_1_), channel_id=1, source_target_pairs={{0,2},{1,3},{2,0},{3,1},{4,6},{5,7},{6,4},{7,5},{8,10},{9,11},{10,... | collective-permute-start | bytes 196616 | tf_op jit(solution)/shard_map/ppermute | solution.py:653
  183.2 4.6 %collective-permute-start.39 = (bf16[16,2048]{1,0:T(8,128)(2,1)}, bf16[16,2048]{1,0:T(8,128)(2,1)S(1)}, u32[]{:S(2)}, u32[]{:S(2)}) collective-permute-start(bf16[16,2048]{1,0:T(8,128)(2,1)} %get-tuple-element.83.refs_1_), channel_id=1, source_target_pairs={{0,3},{1,2},{2,1},{3,0},{4,7},{5,6},{6,5},{7,4},{8,11},{9,10},{10,... | collective-permute-start | bytes 196616 | tf_op jit(solution)/shard_map/ppermute | solution.py:653
  183.9 3.9 %copy-start.27 = (bf16[16,2048]{1,0:T(8,128)(2,1)}, bf16[16,2048]{1,0:T(8,128)(2,1)S(1)}, u32[]{:S(2)}) copy-start(bf16[16,2048]{1,0:T(8,128)(2,1)S(1)} %collective-permute-done.37.refs_2_) | copy-start | bytes 196612
  193.0 3.4 %collective-permute-start.42 = (bf16[16,512]{1,0:T(8,128)(2,1)}, bf16[16,512]{1,0:T(8,128)(2,1)S(1)}, u32[]{:S(2)}, u32[]{:S(2)}) collective-permute-start(bf16[16,512]{1,0:T(8,128)(2,1)} %get-tuple-element.87), channel_id=1, source_target_pairs={{0,3},{1,2},{2,1},{3,0},{4,7},{5,6},{6,5},{7,4},{8,11},{9,10},{10,... | collective-permute-start | bytes 49160 | tf_op jit(solution)/shard_map/ppermute | solution.py:653
  193.7 4.0 %collective-permute-start.41 = (bf16[16,512]{1,0:T(8,128)(2,1)}, bf16[16,512]{1,0:T(8,128)(2,1)S(1)}, u32[]{:S(2)}, u32[]{:S(2)}) collective-permute-start(bf16[16,512]{1,0:T(8,128)(2,1)} %get-tuple-element.86), channel_id=1, source_target_pairs={{0,2},{1,3},{2,0},{3,1},{4,6},{5,7},{6,4},{7,5},{8,10},{9,11},{10,... | collective-permute-start | bytes 49160 | tf_op jit(solution)/shard_map/ppermute | solution.py:653
  194.9 2.8 %collective-permute-start.40 = (bf16[16,512]{1,0:T(8,128)(2,1)}, bf16[16,512]{1,0:T(8,128)(2,1)S(1)}, u32[]{:S(2)}, u32[]{:S(2)}) collective-permute-start(bf16[16,512]{1,0:T(8,128)(2,1)} %get-tuple-element.85), channel_id=1, source_target_pairs={{0,1},{1,0},{2,3},{3,2},{4,5},{5,4},{6,7},{7,6},{8,9},{9,8},{10,11... | collective-permute-start | bytes 49160 | tf_op jit(solution)/shard_map/ppermute | solution.py:653
  (16 other events, 14.3 us)

commit v3 on v2

--- a/solution.py
+++ b/solution.py
@@ -14,7 +14,7 @@
 STEPS = 4
 RING_LIMIT = 8
 RING_WAYS = (1, -1)
-VMEM_BYTES = 56 * 1024 * 1024
+VMEM_BYTES = 16 * 1024 * 1024
 
 eps = 1e-06
 

time: 200 us -> 176 us (0.88)
  Pallas kernels: 46.6 us -> 25 us
  local copies, waits for them, and re-layouts: 15.1 us -> 11.8 us
  waiting for transfers between devices: 84.4 us -> 86.5 us
    pallas_call x4, Pallas kernels: 18.2 us -> 8.12 us  [beam_step(): pl.pallas_call(functools.partial(beam_kernel, level, max(len(inputs) - 1,...]
    ppermute x17, waiting for transfers between devices: 13.8 us -> 17.3 us  [exchange(): lax.ppermute(value, axis, [(i, partner(i, step, size)) for i in range(siz...]
    pallas_call x1, Pallas kernels: 5.17 us -> 2.07 us  [cross_project(): pl.pallas_call(functools.partial(cross_kernel, [where for _, where in row...]
    pallas_call x1, Pallas kernels: 4.87 us -> 2.11 us  [project_out(): pl.pallas_call(functools.partial(project_kernel, [first for _, first in p...]
    pallas_call x1, Pallas kernels: 10.8 us -> 8.46 us  [encoder_attention(): pl.pallas_call(functools.partial(encoder_kernel, [places for _, places in...]
    unnamed x74 -> x34, local copies, waits for them, and re-layouts: 6.44 us -> 6.39 us
  transfers between devices with their start and end apart: 43 -> 43, of which waited for: 21 -> 22; matrix products, arithmetic and copies ran while one was open for 6% -> 6% of each run, Pallas kernels for 8% -> 6%
where the time goes in v3:
time: 176 us
  waiting for transfers between devices  86.5 us (49%)
  starting transfers between devices  42.9 us (24%)
  Pallas kernels  25 us (14%)
  local copies, waits for them, and re-layouts  11.8 us (7%)
  other arithmetic  4.8 us (3%)
  matrix products  3.03 us (2%)
    ppermute x14, waiting for transfers between devices, shift(): lax.ppermute(value, axis, [(i, (i + step) % size) for i in range(size)])  55.3 us
    ppermute x14, starting transfers between devices, shift(): lax.ppermute(value, axis, [(i, (i + step) % size) for i in range(size)])  22.3 us
    ppermute x17, waiting for transfers between devices, exchange(): lax.ppermute(value, axis, [(i, partner(i, step, size)) for i in range(siz...  17.3 us
    ppermute x12, waiting for transfers between devices, shards(): lax.ppermute(v, ('tp', 'kv'), move)  14 us
    ppermute x17, starting transfers between devices, exchange(): lax.ppermute(value, axis, [(i, partner(i, step, size)) for i in range(siz...  13 us
    pallas_call x1, Pallas kernels, encoder_attention(): pl.pallas_call(functools.partial(encoder_kernel, [places for _, places in...  8.46 us
    pallas_call x4, Pallas kernels, beam_step(): pl.pallas_call(functools.partial(beam_kernel, level, max(len(inputs) - 1,...  8.12 us
    ppermute x12, starting transfers between devices, shards(): lax.ppermute(v, ('tp', 'kv'), move)  7.54 us
  transfers between devices with their start and end apart: 43, of which 22 were waited for; matrix products, arithmetic and copies ran while one was open for 6% of the time, Pallas kernels for 6%

profile of v3, /device:TPU:0, one launch (start us, length us, event | category | flops | bytes accessed | tf_op | source)
XLA Modules:
  0.0 175.8 jit_solution(15358917607849137743)
XLA Ops:
  0.6 1.1 slice_bitcast_fusion.3
  1.8 1.2 pad_maximum_fusion.refs_0_
  3.0 3.1 %collective-permute-start.3 = (bf16[256,1024]{1,0:T(8,128)(2,1)S(1)}, bf16[256,1024]{1,0:T(8,128)(2,1)}, u32[]{:S(2)}, u32[]{:S(2)}) collective-permute-start(bf16[256,1024]{1,0:T(8,128)(2,1)S(1)} %constant_dynamic-slice_fusion.2), channel_id=1, source_target_pairs={{0,4},{4,8},{8,12},{12,0},{1,5},{5,9},{9,13},{13,1},{2,6},{6,10},{... | collective-permute-start | bytes 1572872 | tf_op jit(solution)/shard_map/ppermute | solution.py:53
  6.1 2.2 %collective-permute-start.2 = (bf16[128,512]{1,0:T(8,128)(2,1)S(1)}, bf16[128,512]{1,0:T(8,128)(2,1)S(1)}, u32[]{:S(2)}, u32[]{:S(2)}) collective-permute-start(bf16[128,512]{1,0:T(8,128)(2,1)S(1)} %get-tuple-element.98), channel_id=1, source_target_pairs={{0,12},{4,0},{8,4},{12,8},{1,13},{5,1},{9,5},{13,9},{2,14},{6,2},{... | collective-permute-start | bytes 393224 | tf_op jit(solution)/shard_map/ppermute | solution.py:53
  8.3 0.9 collective-permute-start.1
  9.2 1.6 collective-permute-start
  10.9 11.5 %collective-permute-done.2 = bf16[128,512]{1,0:T(8,128)(2,1)S(1)} collective-permute-done((bf16[128,512]{1,0:T(8,128)(2,1)S(1)}, bf16[128,512]{1,0:T(8,128)(2,1)S(1)}, u32[]{:S(2)}, u32[]{:S(2)}) %collective-permute-start.2) | collective-permute-done | bytes 131104 | tf_op jit(solution)/shard_map/ppermute | solution.py:53
  22.4 8.9 %collective-permute-done.1 = bf16[128,512]{1,0:T(8,128)(2,1)S(1)} collective-permute-done((bf16[128,512]{1,0:T(8,128)(2,1)S(1)}, bf16[128,512]{1,0:T(8,128)(2,1)S(1)}, u32[]{:S(2)}, u32[]{:S(2)}) %collective-permute-start.1) | collective-permute-done | bytes 131104 | tf_op jit(solution)/shard_map/ppermute | solution.py:53
  31.3 0.8 pad_maximum_fusion.2.refs_0_
  32.1 1.5 collective-permute-start.7
  33.6 1.5 collective-permute-start.4
  35.2 3.0 %convolution_convert_fusion = bf16[64,2048]{1,0:T(8,128)(2,1)S(1)} fusion(bf16[64,1024]{1,0:T(8,128)(2,1)S(1)} %compare_convert_fusion, bf16[1024,2048]{1,0:T(8,128)(2,1)} %param.26), kind=kOutput, calls=%fused_computation | convolution fusion | flops 268566528 | bytes 4587520 | tf_op jit(solution)/shard_map/dot_general | solution.py:555
  38.9 8.7 %collective-permute-done.4.refs_1_ = bf16[512,512]{1,0:T(8,128)(2,1)} collective-permute-done((bf16[512,512]{1,0:T(8,128)(2,1)}, bf16[512,512]{1,0:T(8,128)(2,1)}, u32[]{:S(2)}, u32[]{:S(2)}) %collective-permute-start.4) | collective-permute-done | bytes 524320 | tf_op jit(solution)/shard_map/ppermute | solution.py:48
  47.5 1.0 collective-permute-done.8.refs_3_
  49.1 0.6 collective-permute-start.12
  49.8 2.9 %copy.17 = bf16[2048,512]{0,1:T(8,128)(2,1)S(1)} copy(bf16[2048,512]{1,0:T(8,128)(2,1)} %param.25) | data formatting | bytes 4194304 | tf_op jit(solution)/shard_map/optimization_barrier | solution.py:57
  52.8 4.0 %collective-permute-done.12 = bf16[64,2048]{1,0:T(8,128)(2,1)} collective-permute-done((bf16[64,2048]{1,0:T(8,128)(2,1)S(1)}, bf16[64,2048]{1,0:T(8,128)(2,1)}, u32[]{:S(2)}, u32[]{:S(2)}) %collective-permute-start.12) | collective-permute-done | bytes 262176 | tf_op jit(solution)/shard_map/ppermute | solution.py:48
  56.8 1.7 add.88
  58.5 2.6 %norm_events.1 = (bf16[512,2048]{1,0:T(8,128)(2,1)S(1)}, bf16[512,2048]{1,0:T(8,128)(2,1)S(1)}) custom-call(s32[4]{0:T(128)S(1)} %pad_add_fusion.at_ref, f32[1,2048]{1,0:T(1,128)S(1)} %bitcast.37, bf16[512,512]{1,0:T(8,128)(2,1)} %pad_maximum_fusion.2.refs_0_, bf16[512,512]{1,0:T(8,128)(2,1)} %collective-permute-done.4.refs_1_, ...), custom_call_target="tpu_custom_call" | custom-call | bytes 12000000 | tf_op jit(solution)/shard_map/norm_events/pallas_call | solution.py:202
  61.1 1.3 copy-done.1
  62.5 1.3 copy-done.4
  64.3 1.5 collective-permute-start.13
  65.8 1.1 constant_dynamic-slice_fusion
  66.9 3.8 %collective-permute-start.15 = (bf16[256,512]{1,0:T(8,128)(2,1)S(1)}, bf16[256,512]{1,0:T(8,128)(2,1)S(1)}, u32[]{:S(2)}, u32[]{:S(2)}) collective-permute-start(bf16[256,512]{1,0:T(8,128)(2,1)S(1)} %get-tuple-element.93), channel_id=1, source_target_pairs={{0,12},{4,0},{8,4},{12,8},{1,13},{5,1},{9,5},{13,9},{2,14},{6,2},{... | collective-permute-start | bytes 786440 | tf_op jit(solution)/shard_map/ppermute | solution.py:53
  70.7 7.2 %collective-permute-done.14.refs_1_ = bf16[256,512]{1,0:T(8,128)(2,1)S(1)} collective-permute-done((bf16[256,512]{1,0:T(8,128)(2,1)S(1)}, bf16[256,512]{1,0:T(8,128)(2,1)S(1)}, u32[]{:S(2)}, u32[]{:S(2)}) %collective-permute-start.14) | collective-permute-done | bytes 262176 | tf_op jit(solution)/shard_map/ppermute | solution.py:53
  78.0 2.0 %collective-permute-done.15.refs_3_ = bf16[256,512]{1,0:T(8,128)(2,1)S(1)} collective-permute-done((bf16[256,512]{1,0:T(8,128)(2,1)S(1)}, bf16[256,512]{1,0:T(8,128)(2,1)S(1)}, u32[]{:S(2)}, u32[]{:S(2)}) %collective-permute-start.15) | collective-permute-done | bytes 262176 | tf_op jit(solution)/shard_map/ppermute | solution.py:53
  80.5 1.5 collective-permute-start.17
  82.1 4.0 %collective-permute-start.19 = (bf16[256,512]{1,0:T(8,128)(2,1)S(1)}, bf16[256,512]{1,0:T(8,128)(2,1)S(1)}, u32[]{:S(2)}, u32[]{:S(2)}) collective-permute-start(bf16[256,512]{1,0:T(8,128)(2,1)S(1)} %get-tuple-element.65), channel_id=1, source_target_pairs={{0,8},{4,12},{8,0},{12,4},{1,9},{5,13},{9,1},{13,5},{2,10},{6,14},... | collective-permute-start | bytes 786440 | tf_op jit(solution)/shard_map/ppermute | solution.py:53
  86.8 1.6 copy-done.5
  88.3 1.0 copy-done.6
  89.4 1.0 copy-done.8
  90.4 8.5 %encoder_attention.1.attended_ref = bf16[512,512]{1,0:T(8,128)(2,1)S(1)} custom-call(s32[4]{0:T(128)S(1)} %pad_add_fusion.at_ref, s32[1]{0:T(128)S(6)} %copy.18.live_ref, bf16[512,2048]{1,0:T(8,128)(2,1)S(1)} %copy-done.5, bf16[2,512,256]{2,1,0:T(8,128)(2,1)S(1)} %bitcast.32, bf16[512,1024]{1,0:T(8,128)(2,1)S(1)} %pad_maximum_fusion.refs_0_, ...), custom_call_target="tpu_custom_call" | custom-call | bytes 33000000 | tf_op jit(solution)/shard_map/encoder_attention/pallas_call | solution.py:302
  99.0 2.1 %project_out.1 = (bf16[256,2048]{1,0:T(8,128)(2,1)S(1)}, bf16[256,2048]{1,0:T(8,128)(2,1)S(1)}) custom-call(s32[4]{0:T(128)S(1)} %pad_add_fusion.at_ref, bf16[512,512]{1,0:T(8,128)(2,1)S(1)} %encoder_attention.1.attended_ref, bf16[512,512]{1,0:T(8,128)(2,1)S(1)} %copy-done.3, bf16[256,512]{1,0:T(8,128)(2,1)S(1)} %collective-permute-done.14.refs_1_, ...), custom_call_target="tpu_custom_call" | custom-call | bytes 15000000 | tf_op jit(solution)/shard_map/project_out/pallas_call | solution.py:350
  101.2 2.6 %collective-permute-done.20 = bf16[256,2048]{1,0:T(8,128)(2,1)S(1)} collective-permute-done((bf16[256,2048]{1,0:T(8,128)(2,1)S(1)}, bf16[256,2048]{1,0:T(8,128)(2,1)S(1)}, u32[]{:S(2)}, u32[]{:S(2)}) %collective-permute-start.20) | collective-permute-done | bytes 1048608 | tf_op jit(solution)/shard_map/ppermute | solution.py:48
  104.0 1.6 collective-permute-start.21
  106.0 3.8 %collective-permute-start.23 = (bf16[256,512]{1,0:T(8,128)(2,1)S(1)}, bf16[256,512]{1,0:T(8,128)(2,1)S(1)}, u32[]{:S(2)}, u32[]{:S(2)}) collective-permute-start(bf16[256,512]{1,0:T(8,128)(2,1)S(1)} %get-tuple-element.68), channel_id=1, source_target_pairs={{0,12},{4,0},{8,4},{12,8},{1,13},{5,1},{9,5},{13,9},{2,14},{6,2},{... | collective-permute-start | bytes 786440 | tf_op jit(solution)/shard_map/ppermute | solution.py:53
  109.8 7.1 %collective-permute-done.22.refs_6_ = bf16[256,512]{1,0:T(8,128)(2,1)S(1)} collective-permute-done((bf16[256,512]{1,0:T(8,128)(2,1)S(1)}, bf16[256,512]{1,0:T(8,128)(2,1)S(1)}, u32[]{:S(2)}, u32[]{:S(2)}) %collective-permute-start.22) | collective-permute-done | bytes 262176 | tf_op jit(solution)/shard_map/ppermute | solution.py:53
  116.9 2.8 %collective-permute-done.23.refs_8_ = bf16[256,512]{1,0:T(8,128)(2,1)S(1)} collective-permute-done((bf16[256,512]{1,0:T(8,128)(2,1)S(1)}, bf16[256,512]{1,0:T(8,128)(2,1)S(1)}, u32[]{:S(2)}, u32[]{:S(2)}) %collective-permute-start.23) | collective-permute-done | bytes 262176 | tf_op jit(solution)/shard_map/ppermute | solution.py:53
  119.7 1.7 merge_terms.1
  121.8 2.3 %collective-permute-start.25 = (bf16[256,512]{1,0:T(8,128)(2,1)S(1)}, bf16[256,512]{1,0:T(8,128)(2,1)S(1)}, u32[]{:S(2)}, u32[]{:S(2)}) collective-permute-start(bf16[256,512]{1,0:T(8,128)(2,1)S(1)} %get-tuple-element.73), channel_id=1, source_target_pairs={{0,8},{4,12},{8,0},{12,4},{1,9},{5,13},{9,1},{13,5},{2,10},{6,14},... | collective-permute-start | bytes 786440 | tf_op jit(solution)/shard_map/ppermute | solution.py:53
  124.9 1.5 collective-permute-start.27
  126.5 14.3 %collective-permute-done.25.refs_5_ = bf16[256,512]{1,0:T(8,128)(2,1)S(1)} collective-permute-done((bf16[256,512]{1,0:T(8,128)(2,1)S(1)}, bf16[256,512]{1,0:T(8,128)(2,1)S(1)}, u32[]{:S(2)}, u32[]{:S(2)}) %collective-permute-start.25) | collective-permute-done | bytes 262176 | tf_op jit(solution)/shard_map/ppermute | solution.py:53
  141.5 1.2 collective-permute-done.29.refs_2_
  142.7 0.7 collective-permute-done.30.refs_3_
  143.4 2.1 %cross_project.1.cross_ref = bf16[512,512]{1,0:T(8,128)(2,1)S(1)} custom-call(s32[4]{0:T(128)S(1)} %pad_add_fusion.at_ref, bf16[128,2048]{1,0:T(8,128)(2,1)S(1)} %get-tuple-element.72.refs_0_, bf16[128,2048]{1,0:T(8,128)(2,1)S(1)} %collective-permute-done.24.refs_1_, bf16[128,2048]{1,0:T(8,128)(2,1)S(1)} %collective-permute-done.29.refs_2_, ...), custom_call_target="tpu_custom_call" | custom-call | bytes 15000000 | tf_op jit(solution)/shard_map/cross_project/pallas_call | solution.py:413
  145.5 1.9 %beam_step_0.1 = (f32[16,2048]{1,0:T(8,128)S(1)}, bf16[16,2048]{1,0:T(8,128)(2,1)S(1)}) custom-call(s32[4]{0:T(128)S(1)} %pad_add_fusion.at_ref, s32[1]{0:T(128)S(6)} %copy.18.live_ref, s32[3,16]{1,0:T(4,128)S(1)} %copy-done.10, f32[1,2048]{1,0:T(1,128)S(1)} %bitcast.33, bf16[2048,512]{1,0:T(8,128)(2,1)S(1)} %copy-done, bf16[512,2048]{1,0:T(8,128)(2,1)S(1)} %bitcast.28, ...), custom_call_target="tpu_custom_call" | custom-call | bytes 12000000 | tf_op jit(solution)/shard_map/beam_step_0/pallas_call | solution.py:511
  147.6 1.4 collective-permute-start.32
  149.3 2.7 %collective-permute-done.32.refs_3_ = bf16[16,2048]{1,0:T(8,128)(2,1)S(1)} collective-permute-done((bf16[16,2048]{1,0:T(8,128)(2,1)S(1)}, bf16[16,2048]{1,0:T(8,128)(2,1)S(1)}, u32[]{:S(2)}, u32[]{:S(2)}) %collective-permute-start.32) | collective-permute-done | bytes 65568 | tf_op jit(solution)/shard_map/ppermute | solution.py:653
  152.0 1.1 collective-permute-done.33.refs_4_
  153.1 2.1 %beam_step_1.1 = (f32[16,2048]{1,0:T(8,128)S(1)}, bf16[16,2048]{1,0:T(8,128)(2,1)S(1)}) custom-call(s32[4]{0:T(128)S(1)} %pad_add_fusion.at_ref, s32[1]{0:T(128)S(6)} %copy.18.live_ref, s32[3,16]{1,0:T(4,128)S(1)} %copy-done.10, f32[1,2048]{1,0:T(1,128)S(1)} %bitcast.34, bf16[2048,512]{1,0:T(8,128)(2,1)S(1)} %copy-done, bf16[512,2048]{1,0:T(8,128)(2,1)S(1)} %bitcast.29, ...), custom_call_target="tpu_custom_call" | custom-call | bytes 12000000 | tf_op jit(solution)/shard_map/beam_step_1/pallas_call | solution.py:511
  155.3 1.3 collective-permute-start.35
  157.1 2.8 %collective-permute-done.35.refs_3_ = bf16[16,2048]{1,0:T(8,128)(2,1)S(1)} collective-permute-done((bf16[16,2048]{1,0:T(8,128)(2,1)S(1)}, bf16[16,2048]{1,0:T(8,128)(2,1)S(1)}, u32[]{:S(2)}, u32[]{:S(2)}) %collective-permute-start.35) | collective-permute-done | bytes 65568 | tf_op jit(solution)/shard_map/ppermute | solution.py:653
  159.9 1.1 collective-permute-done.36.refs_4_
  161.0 2.1 %beam_step_2.1 = (f32[16,2048]{1,0:T(8,128)S(1)}, bf16[16,2048]{1,0:T(8,128)(2,1)S(1)}) custom-call(s32[4]{0:T(128)S(1)} %pad_add_fusion.at_ref, s32[1]{0:T(128)S(6)} %copy.18.live_ref, s32[3,16]{1,0:T(4,128)S(1)} %copy-done.10, f32[1,2048]{1,0:T(1,128)S(1)} %bitcast.35, bf16[2048,512]{1,0:T(8,128)(2,1)S(1)} %copy-done, bf16[512,2048]{1,0:T(8,128)(2,1)S(1)} %bitcast.30, ...), custom_call_target="tpu_custom_call" | custom-call | bytes 12000000 | tf_op jit(solution)/shard_map/beam_step_2/pallas_call | solution.py:511
  163.2 1.0 collective-permute-start.38
  164.2 0.7 collective-permute-start.39
  164.9 3.0 %collective-permute-done.38.refs_3_ = bf16[16,2048]{1,0:T(8,128)(2,1)S(1)} collective-permute-done((bf16[16,2048]{1,0:T(8,128)(2,1)S(1)}, bf16[16,2048]{1,0:T(8,128)(2,1)S(1)}, u32[]{:S(2)}, u32[]{:S(2)}) %collective-permute-start.38) | collective-permute-done | bytes 65568 | tf_op jit(solution)/shard_map/ppermute | solution.py:653
  167.9 0.7 collective-permute-done.39.refs_4_
  168.6 2.1 %beam_step_3.1 = (f32[16,512]{1,0:T(8,128)S(1)}, bf16[16,512]{1,0:T(8,128)(2,1)S(1)}, bf16[16,512]{1,0:T(8,128)(2,1)S(1)}, bf16[16,512]{1,0:T(8,128)(2,1)S(1)}) custom-call(s32[4]{0:T(128)S(1)} %pad_add_fusion.at_ref, s32[1]{0:T(128)S(6)} %copy.18.live_ref, s32[3,16]{1,0:T(4,128)S(1)} %copy-done.10, f32[1,2048]{1,0:T(1,128)S(1)} %bitcast.36, ...), custom_call_target="tpu_custom_call" | custom-call | bytes 12000000 | tf_op jit(solution)/shard_map/beam_step_3/pallas_call | solution.py:511
  170.7 0.8 collective-permute-start.42
  171.4 1.1 collective-permute-start.41
  172.6 1.3 collective-permute-done.42
  173.9 1.3 collective-permute-done.41
  175.2 0.6 add_convert_fusion.1
  (87 shorter events, 6.4 us)
Async XLA Ops:
  0.6 5.5 %copy-start.14 = (bf16[4,128,512]{2,1,0:T(8,128)(2,1)S(1)}, bf16[4,128,512]{2,1,0:T(8,128)(2,1)}, u32[]{:S(2)}) copy-start(bf16[4,128,512]{2,1,0:T(8,128)(2,1)} %param.15) | copy-start | bytes 1572868
  1.8 9.0 %copy-start.16 = (s32[4,16]{1,0:T(4,128)S(1)}, s32[4,16]{1,0:T(4,128)}, u32[]{:S(2)}) copy-start(s32[4,16]{1,0:T(4,128)} %param.18) | copy-start | bytes 772
  3.0 29.1 %collective-permute-start.3 = (bf16[256,1024]{1,0:T(8,128)(2,1)S(1)}, bf16[256,1024]{1,0:T(8,128)(2,1)}, u32[]{:S(2)}, u32[]{:S(2)}) collective-permute-start(bf16[256,1024]{1,0:T(8,128)(2,1)S(1)} %constant_dynamic-slice_fusion.2), channel_id=1, source_target_pairs={{0,4},{4,8},{8,12},{12,0},{1,5},{5,9},{9,13},{13,1},{2,6},{6,10},{... | collective-permute-start | bytes 1572872 | tf_op jit(solution)/shard_map/ppermute | solution.py:53
  6.1 16.2 %collective-permute-start.2 = (bf16[128,512]{1,0:T(8,128)(2,1)S(1)}, bf16[128,512]{1,0:T(8,128)(2,1)S(1)}, u32[]{:S(2)}, u32[]{:S(2)}) collective-permute-start(bf16[128,512]{1,0:T(8,128)(2,1)S(1)} %get-tuple-element.98), channel_id=1, source_target_pairs={{0,12},{4,0},{8,4},{12,8},{1,13},{5,1},{9,5},{13,9},{2,14},{6,2},{... | collective-permute-start | bytes 393224 | tf_op jit(solution)/shard_map/ppermute | solution.py:53
  8.3 23.0 %collective-permute-start.1 = (bf16[128,512]{1,0:T(8,128)(2,1)S(1)}, bf16[128,512]{1,0:T(8,128)(2,1)S(1)}, u32[]{:S(2)}, u32[]{:S(2)}) collective-permute-start(bf16[128,512]{1,0:T(8,128)(2,1)S(1)} %get-tuple-element.99), channel_id=1, source_target_pairs={{0,8},{4,12},{8,0},{12,4},{1,9},{5,13},{9,1},{13,5},{2,10},{6,14},... | collective-permute-start | bytes 393224 | tf_op jit(solution)/shard_map/ppermute | solution.py:53
  9.2 22.1 %collective-permute-start = (bf16[128,512]{1,0:T(8,128)(2,1)S(1)}, bf16[128,512]{1,0:T(8,128)(2,1)S(1)}, u32[]{:S(2)}, u32[]{:S(2)}) collective-permute-start(bf16[128,512]{1,0:T(8,128)(2,1)S(1)} %get-tuple-element.97), channel_id=1, source_target_pairs={{0,4},{4,8},{8,12},{12,0},{1,5},{5,9},{9,13},{13,1},{2,6},{6,10},{... | collective-permute-start | bytes 393224 | tf_op jit(solution)/shard_map/ppermute | solution.py:53
  32.1 15.4 %collective-permute-start.7 = (bf16[256,1024]{1,0:T(8,128)(2,1)}, bf16[256,1024]{1,0:T(8,128)(2,1)S(1)}, u32[]{:S(2)}, u32[]{:S(2)}) collective-permute-start(bf16[256,1024]{1,0:T(8,128)(2,1)} %collective-permute-done.3.refs_1_), channel_id=1, source_target_pairs={{0,16},{16,0},{1,17},{17,1},{2,18},{18,2},{3,19},{19,3},{4,20},{20... | collective-permute-start | bytes 1572872 | tf_op jit(solution)/shard_map/ppermute | solution.py:48
  33.6 13.9 %collective-permute-start.4 = (bf16[512,512]{1,0:T(8,128)(2,1)}, bf16[512,512]{1,0:T(8,128)(2,1)}, u32[]{:S(2)}, u32[]{:S(2)}) collective-permute-start(bf16[512,512]{1,0:T(8,128)(2,1)} %pad_maximum_fusion.2.refs_0_), channel_id=1, source_target_pairs={{0,2},{2,0},{1,3},{3,1},{4,6},{6,4},{5,7},{7,5},{8,10},{10,8},{9,1... | collective-permute-start | bytes 1572872 | tf_op jit(solution)/shard_map/ppermute | solution.py:48
  35.1 13.4 %collective-permute-start.8 = (bf16[256,1024]{1,0:T(8,128)(2,1)S(1)}, bf16[256,1024]{1,0:T(8,128)(2,1)}, u32[]{:S(2)}, u32[]{:S(2)}) collective-permute-start(bf16[256,1024]{1,0:T(8,128)(2,1)S(1)} %constant_dynamic-slice_fusion.2), channel_id=1, source_target_pairs={{0,12},{4,0},{8,4},{12,8},{1,13},{5,1},{9,5},{13,9},{2,14},{6,2},{... | collective-permute-start | bytes 1572872 | tf_op jit(solution)/shard_map/ppermute | solution.py:53
  38.3 10.8 %collective-permute-start.11 = (bf16[64,2048]{1,0:T(8,128)(2,1)S(1)}, bf16[64,2048]{1,0:T(8,128)(2,1)S(1)}, u32[]{:S(2)}, u32[]{:S(2)}) collective-permute-start(bf16[64,2048]{1,0:T(8,128)(2,1)S(1)} %convolution_convert_fusion), channel_id=1, source_target_pairs={{0,1},{1,0},{2,3},{3,2},{4,5},{5,4},{6,7},{7,6},{8,9},{9,8},{10,11... | collective-permute-start | bytes 786440 | tf_op jit(solution)/shard_map/ppermute | solution.py:48
  38.4 20.2 %collective-permute-start.5 = (bf16[512,512]{1,0:T(8,128)(2,1)}, bf16[512,512]{1,0:T(8,128)(2,1)}, u32[]{:S(2)}, u32[]{:S(2)}) collective-permute-start(bf16[512,512]{1,0:T(8,128)(2,1)} %pad_maximum_fusion.2.refs_0_), channel_id=1, source_target_pairs={{0,1},{1,0},{2,3},{3,2},{4,5},{5,4},{6,7},{7,6},{8,9},{9,8},{10,11... | collective-permute-start | bytes 1572872 | tf_op jit(solution)/shard_map/ppermute | solution.py:48
  47.5 11.0 %collective-permute-start.6 = (bf16[512,512]{1,0:T(8,128)(2,1)}, bf16[512,512]{1,0:T(8,128)(2,1)}, u32[]{:S(2)}, u32[]{:S(2)}) collective-permute-start(bf16[512,512]{1,0:T(8,128)(2,1)} %collective-permute-done.4.refs_1_), channel_id=1, source_target_pairs={{0,1},{1,0},{2,3},{3,2},{4,5},{5,4},{6,7},{7,6},{8,9},{9,8},{10,11... | collective-permute-start | bytes 1572872 | tf_op jit(solution)/shard_map/ppermute | solution.py:48
  47.5 2.2 %copy-start.7 = (bf16[256,1024]{1,0:T(8,128)(2,1)}, bf16[256,1024]{1,0:T(8,128)(2,1)S(1)}, u32[]{:S(2)}) copy-start(bf16[256,1024]{1,0:T(8,128)(2,1)S(1)} %collective-permute-done.7.refs_2_) | copy-start | bytes 1572868
  48.5 15.3 %collective-permute-start.9 = (bf16[256,1024]{1,0:T(8,128)(2,1)}, bf16[256,1024]{1,0:T(8,128)(2,1)}, u32[]{:S(2)}, u32[]{:S(2)}) collective-permute-start(bf16[256,1024]{1,0:T(8,128)(2,1)} %collective-permute-done.8.refs_3_), channel_id=1, source_target_pairs={{0,16},{16,0},{1,17},{17,1},{2,18},{18,2},{3,19},{19,3},{4,20},{20... | collective-permute-start | bytes 1572872 | tf_op jit(solution)/shard_map/ppermute | solution.py:48
  49.0 15.2 %collective-permute-start.10 = (bf16[256,1024]{1,0:T(8,128)(2,1)}, bf16[256,1024]{1,0:T(8,128)(2,1)}, u32[]{:S(2)}, u32[]{:S(2)}) collective-permute-start(bf16[256,1024]{1,0:T(8,128)(2,1)} %collective-permute-done.3.refs_1_), channel_id=1, source_target_pairs={{0,4},{4,8},{8,12},{12,0},{1,5},{5,9},{9,13},{13,1},{2,6},{6,10},{... | collective-permute-start | bytes 1572872 | tf_op jit(solution)/shard_map/ppermute | solution.py:53
  49.1 7.7 %collective-permute-start.12 = (bf16[64,2048]{1,0:T(8,128)(2,1)S(1)}, bf16[64,2048]{1,0:T(8,128)(2,1)}, u32[]{:S(2)}, u32[]{:S(2)}) collective-permute-start(bf16[64,2048]{1,0:T(8,128)(2,1)S(1)} %add.87), channel_id=1, source_target_pairs={{0,2},{2,0},{1,3},{3,1},{4,6},{6,4},{5,7},{7,5},{8,10},{10,8},{9,1... | collective-permute-start | bytes 786440 | tf_op jit(solution)/shard_map/ppermute | solution.py:48
  49.8 8.7 %copy-start.11 = (f32[2048]{0:T(1024)S(1)}, f32[2048]{0:T(1024)}, u32[]{:S(2)}) copy-start(f32[2048]{0:T(1024)} %param.27) | copy-start | bytes 24580
  61.1 1.3 copy-start.1
  62.5 1.3 copy-start.4
  64.3 15.7 %collective-permute-start.13 = (bf16[256,1024]{1,0:T(8,128)(2,1)}, bf16[256,1024]{1,0:T(8,128)(2,1)}, u32[]{:S(2)}, u32[]{:S(2)}) collective-permute-start(bf16[256,1024]{1,0:T(8,128)(2,1)} %collective-permute-done.10.refs_5_), channel_id=1, source_target_pairs={{0,16},{16,0},{1,17},{17,1},{2,18},{18,2},{3,19},{19,3},{4,20},{20... | collective-permute-start | bytes 1572872 | tf_op jit(solution)/shard_map/ppermute | solution.py:48
  66.9 11.1 %collective-permute-start.14 = (bf16[256,512]{1,0:T(8,128)(2,1)S(1)}, bf16[256,512]{1,0:T(8,128)(2,1)S(1)}, u32[]{:S(2)}, u32[]{:S(2)}) collective-permute-start(bf16[256,512]{1,0:T(8,128)(2,1)S(1)} %get-tuple-element.93), channel_id=1, source_target_pairs={{0,4},{4,8},{8,12},{12,0},{1,5},{5,9},{9,13},{13,1},{2,6},{6,10},{... | collective-permute-start | bytes 786440 | tf_op jit(solution)/shard_map/ppermute | solution.py:53
  66.9 13.1 %collective-permute-start.15 = (bf16[256,512]{1,0:T(8,128)(2,1)S(1)}, bf16[256,512]{1,0:T(8,128)(2,1)S(1)}, u32[]{:S(2)}, u32[]{:S(2)}) collective-permute-start(bf16[256,512]{1,0:T(8,128)(2,1)S(1)} %get-tuple-element.93), channel_id=1, source_target_pairs={{0,12},{4,0},{8,4},{12,8},{1,13},{5,1},{9,5},{13,9},{2,14},{6,2},{... | collective-permute-start | bytes 786440 | tf_op jit(solution)/shard_map/ppermute | solution.py:53
  78.0 20.9 %collective-permute-start.18 = (bf16[256,512]{1,0:T(8,128)(2,1)S(1)}, bf16[256,512]{1,0:T(8,128)(2,1)S(1)}, u32[]{:S(2)}, u32[]{:S(2)}) collective-permute-start(bf16[256,512]{1,0:T(8,128)(2,1)S(1)} %collective-permute-done.14.refs_1_), channel_id=1, source_target_pairs={{0,4},{4,8},{8,12},{12,0},{1,5},{5,9},{9,13},{13,1},{2,6},{6,10},{... | collective-permute-start | bytes 786440 | tf_op jit(solution)/shard_map/ppermute | solution.py:53
  80.0 18.9 %collective-permute-start.16 = (bf16[256,512]{1,0:T(8,128)(2,1)S(1)}, bf16[256,512]{1,0:T(8,128)(2,1)S(1)}, u32[]{:S(2)}, u32[]{:S(2)}) collective-permute-start(bf16[256,512]{1,0:T(8,128)(2,1)S(1)} %collective-permute-done.14.refs_1_), channel_id=1, source_target_pairs={{0,16},{16,0},{1,17},{17,1},{2,18},{18,2},{3,19},{19,3},{4,20},{20... | collective-permute-start | bytes 786440 | tf_op jit(solution)/shard_map/ppermute | solution.py:48
  80.5 18.4 %collective-permute-start.17 = (bf16[256,512]{1,0:T(8,128)(2,1)S(1)}, bf16[256,512]{1,0:T(8,128)(2,1)S(1)}, u32[]{:S(2)}, u32[]{:S(2)}) collective-permute-start(bf16[256,512]{1,0:T(8,128)(2,1)S(1)} %collective-permute-done.15.refs_3_), channel_id=1, source_target_pairs={{0,16},{16,0},{1,17},{17,1},{2,18},{18,2},{3,19},{19,3},{4,20},{20... | collective-permute-start | bytes 786440 | tf_op jit(solution)/shard_map/ppermute | solution.py:48
  82.1 16.9 %collective-permute-start.19 = (bf16[256,512]{1,0:T(8,128)(2,1)S(1)}, bf16[256,512]{1,0:T(8,128)(2,1)S(1)}, u32[]{:S(2)}, u32[]{:S(2)}) collective-permute-start(bf16[256,512]{1,0:T(8,128)(2,1)S(1)} %get-tuple-element.65), channel_id=1, source_target_pairs={{0,8},{4,12},{8,0},{12,4},{1,9},{5,13},{9,1},{13,5},{2,10},{6,14},... | collective-permute-start | bytes 786440 | tf_op jit(solution)/shard_map/ppermute | solution.py:53
  86.7 1.6 copy-start.5
  88.3 1.0 copy-start.6
  89.4 1.0 copy-start.8
  90.4 8.5 %copy-start.3 = (bf16[512,512]{1,0:T(8,128)(2,1)S(1)}, bf16[512,512]{1,0:T(8,128)(2,1)}, u32[]{:S(2)}) copy-start(bf16[512,512]{1,0:T(8,128)(2,1)} %refs_0_.1) | copy-start | bytes 1572868
  98.9 6.7 %copy-start.15 = (bf16[2,512,256]{2,1,0:T(8,128)(2,1)S(1)}, bf16[2,512,256]{2,1,0:T(8,128)(2,1)}, u32[]{:S(2)}) copy-start(bf16[2,512,256]{2,1,0:T(8,128)(2,1)} %param.23) | copy-start | bytes 1572868
  101.1 2.7 %collective-permute-start.20 = (bf16[256,2048]{1,0:T(8,128)(2,1)S(1)}, bf16[256,2048]{1,0:T(8,128)(2,1)S(1)}, u32[]{:S(2)}, u32[]{:S(2)}) collective-permute-start(bf16[256,2048]{1,0:T(8,128)(2,1)S(1)} %get-tuple-element.67), channel_id=1, source_target_pairs={{0,1},{1,0},{2,3},{3,2},{4,5},{5,4},{6,7},{7,6},{8,9},{9,8},{10,11... | collective-permute-start | bytes 3145736 | tf_op jit(solution)/shard_map/ppermute | solution.py:48
  103.9 15.7 %copy-start.2 = (bf16[512,2048]{1,0:T(8,128)(2,1)S(1)}, bf16[512,2048]{1,0:T(8,128)(2,1)}, u32[]{:S(2)}) copy-start(bf16[512,2048]{1,0:T(8,128)(2,1)} %copy-done.1) | copy-start | bytes 6291460
  103.9 15.7 %copy-start.12 = (f32[2048]{0:T(1024)S(1)}, f32[2048]{0:T(1024)}, u32[]{:S(2)}) copy-start(f32[2048]{0:T(1024)} %param.28) | copy-start | bytes 24580
  104.0 15.7 %collective-permute-start.21 = (bf16[128,2048]{1,0:T(8,128)(2,1)S(1)}, bf16[128,2048]{1,0:T(8,128)(2,1)S(1)}, u32[]{:S(2)}, u32[]{:S(2)}) collective-permute-start(bf16[128,2048]{1,0:T(8,128)(2,1)S(1)} %add_convert_fusion), channel_id=1, source_target_pairs={{0,2},{2,0},{1,3},{3,1},{4,6},{6,4},{5,7},{7,5},{8,10},{10,8},{9,1... | collective-permute-start | bytes 1572872 | tf_op jit(solution)/shard_map/ppermute | solution.py:48
  105.7 11.2 %collective-permute-start.22 = (bf16[256,512]{1,0:T(8,128)(2,1)S(1)}, bf16[256,512]{1,0:T(8,128)(2,1)S(1)}, u32[]{:S(2)}, u32[]{:S(2)}) collective-permute-start(bf16[256,512]{1,0:T(8,128)(2,1)S(1)} %get-tuple-element.68), channel_id=1, source_target_pairs={{0,4},{4,8},{8,12},{12,0},{1,5},{5,9},{9,13},{13,1},{2,6},{6,10},{... | collective-permute-start | bytes 786440 | tf_op jit(solution)/shard_map/ppermute | solution.py:53
  106.0 13.7 %collective-permute-start.23 = (bf16[256,512]{1,0:T(8,128)(2,1)S(1)}, bf16[256,512]{1,0:T(8,128)(2,1)S(1)}, u32[]{:S(2)}, u32[]{:S(2)}) collective-permute-start(bf16[256,512]{1,0:T(8,128)(2,1)S(1)} %get-tuple-element.68), channel_id=1, source_target_pairs={{0,12},{4,0},{8,4},{12,8},{1,13},{5,1},{9,5},{13,9},{2,14},{6,2},{... | collective-permute-start | bytes 786440 | tf_op jit(solution)/shard_map/ppermute | solution.py:53
  119.7 21.7 %copy-start.13 = (bf16[64,2048]{1,0:T(8,128)(2,1)S(1)}, bf16[64,2048]{1,0:T(8,128)(2,1)}, u32[]{:S(2)}) copy-start(bf16[64,2048]{1,0:T(8,128)(2,1)} %add.88) | copy-start | bytes 786436
  121.4 19.4 %collective-permute-start.24 = (bf16[128,2048]{1,0:T(8,128)(2,1)S(1)}, bf16[128,2048]{1,0:T(8,128)(2,1)S(1)}, u32[]{:S(2)}, u32[]{:S(2)}) collective-permute-start(bf16[128,2048]{1,0:T(8,128)(2,1)S(1)} %get-tuple-element.72.refs_0_), channel_id=1, source_target_pairs={{0,2},{2,0},{1,3},{3,1},{4,6},{6,4},{5,7},{7,5},{8,10},{10,8},{9,1... | collective-permute-start | bytes 1572872 | tf_op jit(solution)/shard_map/ppermute | solution.py:48
  121.8 18.9 %collective-permute-start.25 = (bf16[256,512]{1,0:T(8,128)(2,1)S(1)}, bf16[256,512]{1,0:T(8,128)(2,1)S(1)}, u32[]{:S(2)}, u32[]{:S(2)}) collective-permute-start(bf16[256,512]{1,0:T(8,128)(2,1)S(1)} %get-tuple-element.73), channel_id=1, source_target_pairs={{0,8},{4,12},{8,0},{12,4},{1,9},{5,13},{9,1},{13,5},{2,10},{6,14},... | collective-permute-start | bytes 786440 | tf_op jit(solution)/shard_map/ppermute | solution.py:53
  124.2 16.6 %collective-permute-start.28 = (bf16[256,512]{1,0:T(8,128)(2,1)S(1)}, bf16[256,512]{1,0:T(8,128)(2,1)S(1)}, u32[]{:S(2)}, u32[]{:S(2)}) collective-permute-start(bf16[256,512]{1,0:T(8,128)(2,1)S(1)} %collective-permute-done.22.refs_6_), channel_id=1, source_target_pairs={{0,4},{4,8},{8,12},{12,0},{1,5},{5,9},{9,13},{13,1},{2,6},{6,10},{... | collective-permute-start | bytes 786440 | tf_op jit(solution)/shard_map/ppermute | solution.py:53
  124.4 16.4 %collective-permute-start.26 = (bf16[256,512]{1,0:T(8,128)(2,1)S(1)}, bf16[256,512]{1,0:T(8,128)(2,1)S(1)}, u32[]{:S(2)}, u32[]{:S(2)}) collective-permute-start(bf16[256,512]{1,0:T(8,128)(2,1)S(1)} %collective-permute-done.22.refs_6_), channel_id=1, source_target_pairs={{0,16},{16,0},{1,17},{17,1},{2,18},{18,2},{3,19},{19,3},{4,20},{20... | collective-permute-start | bytes 786440 | tf_op jit(solution)/shard_map/ppermute | solution.py:48
  124.9 15.8 %collective-permute-start.27 = (bf16[256,512]{1,0:T(8,128)(2,1)S(1)}, bf16[256,512]{1,0:T(8,128)(2,1)S(1)}, u32[]{:S(2)}, u32[]{:S(2)}) collective-permute-start(bf16[256,512]{1,0:T(8,128)(2,1)S(1)} %collective-permute-done.23.refs_8_), channel_id=1, source_target_pairs={{0,16},{16,0},{1,17},{17,1},{2,18},{18,2},{3,19},{19,3},{4,20},{20... | collective-permute-start | bytes 786440 | tf_op jit(solution)/shard_map/ppermute | solution.py:48
  140.8 1.9 %collective-permute-start.29 = (bf16[128,2048]{1,0:T(8,128)(2,1)S(1)}, bf16[128,2048]{1,0:T(8,128)(2,1)S(1)}, u32[]{:S(2)}, u32[]{:S(2)}) collective-permute-start(bf16[128,2048]{1,0:T(8,128)(2,1)S(1)} %get-tuple-element.72.refs_0_), channel_id=1, source_target_pairs={{0,1},{1,0},{2,3},{3,2},{4,5},{5,4},{6,7},{7,6},{8,9},{9,8},{10,11... | collective-permute-start | bytes 1572872 | tf_op jit(solution)/shard_map/ppermute | solution.py:48
  140.8 2.6 %collective-permute-start.30 = (bf16[128,2048]{1,0:T(8,128)(2,1)S(1)}, bf16[128,2048]{1,0:T(8,128)(2,1)S(1)}, u32[]{:S(2)}, u32[]{:S(2)}) collective-permute-start(bf16[128,2048]{1,0:T(8,128)(2,1)S(1)} %collective-permute-done.24.refs_1_), channel_id=1, source_target_pairs={{0,1},{1,0},{2,3},{3,2},{4,5},{5,4},{6,7},{7,6},{8,9},{9,8},{10,11... | collective-permute-start | bytes 1572872 | tf_op jit(solution)/shard_map/ppermute | solution.py:48
  141.4 4.1 %copy-start = (bf16[2048,512]{1,0:T(8,128)(2,1)S(1)}, bf16[2048,512]{1,0:T(8,128)(2,1)}, u32[]{:S(2)}) copy-start(bf16[2048,512]{1,0:T(8,128)(2,1)} %query_ref.7) | copy-start | bytes 6291460
  141.5 4.1 %copy-start.9 = (f32[2048]{0:T(1024)S(1)}, f32[2048]{0:T(1024)}, u32[]{:S(2)}) copy-start(f32[2048]{0:T(1024)} %param.29) | copy-start | bytes 24580
  141.5 4.1 %copy-start.10 = (s32[3,16]{1,0:T(4,128)S(1)}, s32[3,16]{1,0:T(4,128)}, u32[]{:S(2)}) copy-start(s32[3,16]{1,0:T(4,128)} %parent_ref.7) | copy-start | bytes 580
  147.5 1.9 %collective-permute-start.31 = (bf16[16,2048]{1,0:T(8,128)(2,1)S(1)}, bf16[16,2048]{1,0:T(8,128)(2,1)S(1)}, u32[]{:S(2)}, u32[]{:S(2)}) collective-permute-start(bf16[16,2048]{1,0:T(8,128)(2,1)S(1)} %get-tuple-element.79.refs_1_), channel_id=1, source_target_pairs={{0,1},{1,0},{2,3},{3,2},{4,5},{5,4},{6,7},{7,6},{8,9},{9,8},{10,11... | collective-permute-start | bytes 196616 | tf_op jit(solution)/shard_map/ppermute | solution.py:653
  147.6 4.4 %collective-permute-start.32 = (bf16[16,2048]{1,0:T(8,128)(2,1)S(1)}, bf16[16,2048]{1,0:T(8,128)(2,1)S(1)}, u32[]{:S(2)}, u32[]{:S(2)}) collective-permute-start(bf16[16,2048]{1,0:T(8,128)(2,1)S(1)} %get-tuple-element.79.refs_1_), channel_id=1, source_target_pairs={{0,2},{1,3},{2,0},{3,1},{4,6},{5,7},{6,4},{7,5},{8,10},{9,11},{10,... | collective-permute-start | bytes 196616 | tf_op jit(solution)/shard_map/ppermute | solution.py:653
  149.0 4.2 %collective-permute-start.33 = (bf16[16,2048]{1,0:T(8,128)(2,1)S(1)}, bf16[16,2048]{1,0:T(8,128)(2,1)S(1)}, u32[]{:S(2)}, u32[]{:S(2)}) collective-permute-start(bf16[16,2048]{1,0:T(8,128)(2,1)S(1)} %get-tuple-element.79.refs_1_), channel_id=1, source_target_pairs={{0,3},{1,2},{2,1},{3,0},{4,7},{5,6},{6,5},{7,4},{8,11},{9,10},{10,... | collective-permute-start | bytes 196616 | tf_op jit(solution)/shard_map/ppermute | solution.py:653
  155.2 1.9 %collective-permute-start.34 = (bf16[16,2048]{1,0:T(8,128)(2,1)S(1)}, bf16[16,2048]{1,0:T(8,128)(2,1)S(1)}, u32[]{:S(2)}, u32[]{:S(2)}) collective-permute-start(bf16[16,2048]{1,0:T(8,128)(2,1)S(1)} %get-tuple-element.81.refs_1_), channel_id=1, source_target_pairs={{0,1},{1,0},{2,3},{3,2},{4,5},{5,4},{6,7},{7,6},{8,9},{9,8},{10,11... | collective-permute-start | bytes 196616 | tf_op jit(solution)/shard_map/ppermute | solution.py:653
  155.3 4.5 %collective-permute-start.35 = (bf16[16,2048]{1,0:T(8,128)(2,1)S(1)}, bf16[16,2048]{1,0:T(8,128)(2,1)S(1)}, u32[]{:S(2)}, u32[]{:S(2)}) collective-permute-start(bf16[16,2048]{1,0:T(8,128)(2,1)S(1)} %get-tuple-element.81.refs_1_), channel_id=1, source_target_pairs={{0,2},{1,3},{2,0},{3,1},{4,6},{5,7},{6,4},{7,5},{8,10},{9,11},{10,... | collective-permute-start | bytes 196616 | tf_op jit(solution)/shard_map/ppermute | solution.py:653
  156.6 4.3 %collective-permute-start.36 = (bf16[16,2048]{1,0:T(8,128)(2,1)S(1)}, bf16[16,2048]{1,0:T(8,128)(2,1)S(1)}, u32[]{:S(2)}, u32[]{:S(2)}) collective-permute-start(bf16[16,2048]{1,0:T(8,128)(2,1)S(1)} %get-tuple-element.81.refs_1_), channel_id=1, source_target_pairs={{0,3},{1,2},{2,1},{3,0},{4,7},{5,6},{6,5},{7,4},{8,11},{9,10},{10,... | collective-permute-start | bytes 196616 | tf_op jit(solution)/shard_map/ppermute | solution.py:653
  163.0 1.9 %collective-permute-start.37 = (bf16[16,2048]{1,0:T(8,128)(2,1)S(1)}, bf16[16,2048]{1,0:T(8,128)(2,1)S(1)}, u32[]{:S(2)}, u32[]{:S(2)}) collective-permute-start(bf16[16,2048]{1,0:T(8,128)(2,1)S(1)} %get-tuple-element.83.refs_1_), channel_id=1, source_target_pairs={{0,1},{1,0},{2,3},{3,2},{4,5},{5,4},{6,7},{7,6},{8,9},{9,8},{10,11... | collective-permute-start | bytes 196616 | tf_op jit(solution)/shard_map/ppermute | solution.py:653
  163.2 4.8 %collective-permute-start.38 = (bf16[16,2048]{1,0:T(8,128)(2,1)S(1)}, bf16[16,2048]{1,0:T(8,128)(2,1)S(1)}, u32[]{:S(2)}, u32[]{:S(2)}) collective-permute-start(bf16[16,2048]{1,0:T(8,128)(2,1)S(1)} %get-tuple-element.83.refs_1_), channel_id=1, source_target_pairs={{0,2},{1,3},{2,0},{3,1},{4,6},{5,7},{6,4},{7,5},{8,10},{9,11},{10,... | collective-permute-start | bytes 196616 | tf_op jit(solution)/shard_map/ppermute | solution.py:653
  164.2 4.4 %collective-permute-start.39 = (bf16[16,2048]{1,0:T(8,128)(2,1)S(1)}, bf16[16,2048]{1,0:T(8,128)(2,1)S(1)}, u32[]{:S(2)}, u32[]{:S(2)}) collective-permute-start(bf16[16,2048]{1,0:T(8,128)(2,1)S(1)} %get-tuple-element.83.refs_1_), channel_id=1, source_target_pairs={{0,3},{1,2},{2,1},{3,0},{4,7},{5,6},{6,5},{7,4},{8,11},{9,10},{10,... | collective-permute-start | bytes 196616 | tf_op jit(solution)/shard_map/ppermute | solution.py:653
  170.7 3.2 %collective-permute-start.42 = (bf16[16,512]{1,0:T(8,128)(2,1)S(1)}, bf16[16,512]{1,0:T(8,128)(2,1)S(1)}, u32[]{:S(2)}, u32[]{:S(2)}) collective-permute-start(bf16[16,512]{1,0:T(8,128)(2,1)S(1)} %get-tuple-element.87), channel_id=1, source_target_pairs={{0,3},{1,2},{2,1},{3,0},{4,7},{5,6},{6,5},{7,4},{8,11},{9,10},{10,... | collective-permute-start | bytes 49160 | tf_op jit(solution)/shard_map/ppermute | solution.py:653
  171.4 3.8 %collective-permute-start.41 = (bf16[16,512]{1,0:T(8,128)(2,1)S(1)}, bf16[16,512]{1,0:T(8,128)(2,1)S(1)}, u32[]{:S(2)}, u32[]{:S(2)}) collective-permute-start(bf16[16,512]{1,0:T(8,128)(2,1)S(1)} %get-tuple-element.86), channel_id=1, source_target_pairs={{0,2},{1,3},{2,0},{3,1},{4,6},{5,7},{6,4},{7,5},{8,10},{9,11},{10,... | collective-permute-start | bytes 49160 | tf_op jit(solution)/shard_map/ppermute | solution.py:653
  172.6 2.6 %collective-permute-start.40 = (bf16[16,512]{1,0:T(8,128)(2,1)S(1)}, bf16[16,512]{1,0:T(8,128)(2,1)S(1)}, u32[]{:S(2)}, u32[]{:S(2)}) collective-permute-start(bf16[16,512]{1,0:T(8,128)(2,1)S(1)} %get-tuple-element.85), channel_id=1, source_target_pairs={{0,1},{1,0},{2,3},{3,2},{4,5},{5,4},{6,7},{7,6},{8,9},{9,8},{10,11... | collective-permute-start | bytes 49160 | tf_op jit(solution)/shard_map/ppermute | solution.py:653

commit v4 on v3

--- a/solution.py
+++ b/solution.py
@@ -61,14 +61,13 @@
     return jnp.stack([lax.axis_index(axis) for axis in ("seq", "groups", "tp", "kv")])
 
 
-def gather_heads(value, beside=None):
+def gather_heads(value, waits=()):
     tp, kv = lax.axis_size("tp"), lax.axis_size("kv")
     along = [(value, lambda at: at[2])]
     for step in range(1, tp):
         along.append(
             (exchange(value, "tp", step), functools.partial(lambda d, at: origin(at[2], d, tp), step))
         )
-    waits = beside() if beside else []
     if waits:
         along = along[:1] + [(after(piece, *waits), where) for piece, where in along[1:]]
     pieces = []
@@ -178,7 +177,7 @@
 
 def norm_kernel(places, firsts, at_ref, gain_ref, *refs):
     count, blocks = len(places), len(firsts)
-    pieces, (normed_ref, source_ref) = refs[:count], refs[count:]
+    pieces, (normed_ref, share_ref, source_ref) = refs[:count], refs[count:]
     width = normed_ref.shape[1]
     cols = pieces[0].shape[1]
     rows = pieces[0].shape[0] // blocks
@@ -193,17 +192,24 @@
             normed_ref[pl.ds(first, rows), col] = (
                 parts[index] * scale * gain_ref[:, col]
             ).astype(jnp.bfloat16)
+    mine = share_ref.shape[0]
+    first = pl.multiple_of((at_ref[2] * lax.axis_size("kv") + at_ref[3]) * mine, mine)
+    share_ref[...] = source_ref[pl.ds(first, mine), :]
 
 
 def norm_events(at, pieces, firsts, gain):
     length = pieces[0][0].shape[0]
     width = gain.shape[0]
-    shape = jax.ShapeDtypeStruct((length, width), jnp.bfloat16)
+    mine = length // (lax.axis_size("tp") * lax.axis_size("kv"))
     return pl.pallas_call(
         functools.partial(norm_kernel, [where for _, where in pieces], firsts),
-        out_shape=(shape, shape),
+        out_shape=(
+            jax.ShapeDtypeStruct((length, width), jnp.bfloat16),
+            jax.ShapeDtypeStruct((mine, width), jnp.bfloat16),
+        ),
         in_specs=[SM] + [VM] * (1 + len(pieces)),
         out_specs=(VM, VM),
+        scratch_shapes=[pltpu.VMEM((length, width), jnp.bfloat16)],
         compiler_params=params(),
         cost_estimate=cost(4),
         name="norm_events",
@@ -235,23 +241,30 @@
 
 
 def encoder_kernel(
-    firsts, ratio, at_ref, live_ref, normed_ref, history_ref, *refs
+    firsts, ratio, at_ref, live_ref, rows_ref, cache_ref, *refs
 ):
-    pieces, (out_ref, whole, projected, sems) = refs[:-4], refs[-4:]
-    length = normed_ref.shape[0]
+    pieces, (out_ref, whole, projected, normed_ref, history_ref, sems) = refs[:-6], refs[-6:]
+    length = rows_ref.shape[0]
     heads = out_ref.shape[1] // DH
     kv_heads = heads // ratio
     query_cols = heads * DH
     key_cols = kv_heads * DH
     past = history_ref.shape[1]
+    spare = sems.shape[0] - 2
+    early = pltpu.make_async_copy(rows_ref, normed_ref, sems.at[spare])
+    later = pltpu.make_async_copy(cache_ref, history_ref, sems.at[spare + 1])
+    early.start()
     copies = load_pieces(pieces, firsts, at_ref, 0, whole, slice(None), sems)
+    later.start()
     for copy in copies:
         copy.wait()
+    early.wait()
     tile = min(256, length)
     for row in range(0, length, tile):
         projected[row : row + tile, :] = jnp.dot(
             normed_ref[row : row + tile, :], whole[...], preferred_element_type=jnp.float32
         ).astype(jnp.bfloat16)
+    later.wait()
     live = live_ref[0] * BLK
     contract = (((1,), (1,)), ((), ()))
     for group in range(kv_heads):
@@ -304,12 +317,14 @@
             encoder_kernel, [places for _, places in pieces], query_cols // key_cols
         ),
         out_shape=jax.ShapeDtypeStruct((length, query_cols), jnp.bfloat16),
-        in_specs=[SM, SM, VM, VM] + [HB] * len(pieces),
+        in_specs=[SM, SM, HB, HB] + [HB] * len(pieces),
         out_specs=VM,
         scratch_shapes=[
             pltpu.VMEM((width, joined), jnp.bfloat16),
             pltpu.VMEM((length, joined), jnp.bfloat16),
-            pltpu.SemaphoreType.DMA((block_count(pieces),)),
+            pltpu.VMEM((length, width), jnp.bfloat16),
+            pltpu.VMEM(history.shape, jnp.bfloat16),
+            pltpu.SemaphoreType.DMA((block_count(pieces) + 2,)),
         ],
         compiler_params=params(),
         cost_estimate=cost(11),
@@ -366,69 +381,66 @@
     )
 
 
-def merge_kernel(count, at_ref, gain_ref, source_ref, *refs):
-    terms, (encoded_ref, crossed_ref) = refs[:count], refs[count:]
-    rows = encoded_ref.shape[0]
-    first = pl.multiple_of((at_ref[2] * lax.axis_size("kv") + at_ref[3]) * rows, rows)
-    total = source_ref[pl.ds(first, rows), :].astype(jnp.float32)
-    for term in terms:
-        total = total + term[...].astype(jnp.float32)
+def merge_kernel(first, gain_ref, source_ref, *refs):
+    near, (far, encoded_ref, crossed_ref) = refs[:-3], refs[-3:]
+    rows = slice(first, first + encoded_ref.shape[0])
+    total = source_ref[rows, :].astype(jnp.float32)
+    for term in near:
+        total = total + term[rows, :].astype(jnp.float32)
+    for term in range(far.shape[0]):
+        total = total + far[term].astype(jnp.float32)
     encoded_ref[...] = total.astype(jnp.bfloat16)
     square = jnp.mean(total * total, axis=-1, keepdims=True)
     crossed_ref[...] = (total * lax.rsqrt(square + eps) * gain_ref[...]).astype(jnp.bfloat16)
 
 
-def merge_terms(at, source, terms, gain):
-    shape = jax.ShapeDtypeStruct(terms[0].shape, jnp.bfloat16)
+def merge_terms(first, source, near, far, gain):
+    shape = jax.ShapeDtypeStruct(far.shape[1:], jnp.bfloat16)
     return pl.pallas_call(
-        functools.partial(merge_kernel, len(terms)),
+        functools.partial(merge_kernel, first),
         out_shape=(shape, shape),
-        in_specs=[SM] + [VM] * (2 + len(terms)),
+        in_specs=[VM] * (3 + len(near)),
         out_specs=(VM, VM),
         compiler_params=params(),
-        cost_estimate=cost(3),
-        name="merge_terms",
-    )(at, gain[None, :], source, *terms)
+        cost_estimate=cost(1),
+        name=f"merge_terms_{first}",
+    )(gain[None, :], source, *near, far)
 
 
 def cross_kernel(places, firsts, at_ref, *refs):
-    row_count, count = len(places), len(firsts)
-    rows_refs, pieces = refs[:row_count], refs[row_count : row_count + count]
-    out_ref, whole, sems = refs[row_count + count :]
-    copies = load_pieces(pieces, firsts, at_ref, 0, whole, slice(None), sems)
+    count = len(places)
+    pieces, (out_ref, source, whole, sems) = refs[:-4], refs[-4:]
+    copies = load_pieces(pieces[count:], firsts, at_ref, 0, whole, slice(None), sems)
+    copies += load_pieces(pieces[:count], places, at_ref, len(copies), source, slice(None), sems)
     for copy in copies:
         copy.wait()
-    rows = rows_refs[0].shape[0]
-    for index, rows_ref in enumerate(rows_refs):
-        first = pl.multiple_of(places[index](at_ref) * rows, rows)
-        out_ref[pl.ds(first, rows), :] = jnp.dot(
-            rows_ref[...], whole[...], preferred_element_type=jnp.float32
+    tile = min(256, out_ref.shape[0])
+    for row in range(0, out_ref.shape[0], tile):
+        out_ref[row : row + tile, :] = jnp.dot(
+            source[row : row + tile, :], whole[...], preferred_element_type=jnp.float32
         ).astype(jnp.bfloat16)
 
 
 def cross_project(at, row_pieces, pieces):
     width = row_pieces[0][0].shape[1]
-    rows = row_pieces[0][0].shape[0]
+    length = sum(rows.shape[0] for rows, _ in row_pieces)
     cols = pieces[0][0].shape[1]
     return pl.pallas_call(
         functools.partial(
-            cross_kernel, [where for _, where in row_pieces], [first for _, first in pieces]
+            cross_kernel, [places for _, places in row_pieces], [places for _, places in pieces]
         ),
-        out_shape=jax.ShapeDtypeStruct((rows * len(row_pieces), cols), jnp.bfloat16),
-        in_specs=[SM] + [VM] * len(row_pieces) + [HB] * len(pieces),
+        out_shape=jax.ShapeDtypeStruct((length, cols), jnp.bfloat16),
+        in_specs=[SM] + [HB] * (len(row_pieces) + len(pieces)),
         out_specs=VM,
         scratch_shapes=[
+            pltpu.VMEM((length, width), jnp.bfloat16),
             pltpu.VMEM((width, cols), jnp.bfloat16),
-            pltpu.SemaphoreType.DMA((block_count(pieces),)),
+            pltpu.SemaphoreType.DMA((block_count(row_pieces) + block_count(pieces),)),
         ],
         compiler_params=params(),
-        cost_estimate=cost(5),
+        cost_estimate=cost(2),
         name="cross_project",
-    )(
-        at,
-        *[rows for rows, _ in row_pieces],
-        *[piece for piece, _ in pieces],
-    )
+    )(at, *[rows for rows, _ in row_pieces], *[piece for piece, _ in pieces])
 
 
 def beam_kernel(
@@ -561,8 +573,8 @@
         joined, out, cross = map(Rows, (joined, out_weight, crossing))
         ways = [RING_WAYS[hop % len(RING_WAYS)] for hop in range(lax.axis_size("seq") - 1)]
         joined.hop(ways[0])
+        blocks[1], joined.last[1] = lax.optimization_barrier((blocks[1], joined.last[1]))
         mine = jnp.concatenate(blocks, axis=0)
-        mine, joined.last[1] = lax.optimization_barrier((mine, joined.last[1]))
         joined.fresh = [(joined.last[1], 1)]
         stage = [joined.last[1]]
         event_pieces = gather_heads(mine)
@@ -578,13 +590,9 @@
         out.start(*stage)
         normed, *_ = joined.held(normed, *out.last.values())
         joined_pieces = joined.pieces
-        far = [1 + hop // 2 if hop % 2 == 0 else -(1 + hop // 2) for hop in range(len(RING_WAYS), len(ways))]
         out.swap(normed)
         out.end()
-        out.keep()
-        for distance in far:
-            out.direct(distance, normed)
-        out_pieces = out.pieces
+        cross.start(normed)
     else:
         joined_pieces, out_pieces, cross_pieces = map(whole_rows, (joined, out_weight, crossing))
         normed, source = norm_events(at, gather_heads(blocks[0]), firsts, encoder_gain)
@@ -593,6 +601,10 @@
     attended = encoder_attention(
         at, normed, history_cache[:, 0], block_counts, joined_pieces
     )
+    if ringed:
+        out.swap(attended)
+        out_pieces = out.pieces
+        attended, *_ = lax.optimization_barrier((attended, *cross.last.values()))
     steps, beams = semantic_ids.shape
     codes = codes.reshape(steps, beams, codes.shape[1])
 
@@ -605,28 +617,39 @@
     arrived = [exchange(terms, "kv", e + 1) for e, terms in enumerate(sent)]
     late = []
     if ringed:
-        cross.start(*arrived)
-        for distance in far:
-            cross.direct(distance, *arrived)
-        late = list(cross.last.values())
-
-    def summed(d):
-        rows = slice(d * share, (d + 1) * share)
+        cross.swap(attended)
+        cross.end(attended)
+        late = [piece for piece, _ in cross.pieces[1:]] + list(cross.last.values())
+
+    parts = 2 if share % 32 == 0 else 1
+    part = share // parts
+
+    def summed(d, first):
+        rows = slice(d * share + first, d * share + first + part)
         return sum([a[rows].astype(jnp.float32) for a in arrived], kept[rows].astype(jnp.float32))
 
-    terms = [exchange(summed(d).astype(jnp.bfloat16), "tp", d) for d in range(1, tp)]
-    terms = [kept[:share]] + [a[:share] for a in arrived] + [after(t, *late) if late else t for t in terms]
-    encoded, crossed = merge_terms(at, source, terms, cross_gain)
-
-
-    def finish_cross():
-        cross.swap(crossed)
-        cross.end()
-        cross.keep()
-        return [piece for piece, _ in cross.pieces[1:]]
-
-    crossed_pieces = gather_heads(crossed, finish_cross if ringed else None)
-    keys_values = cross_project(at, crossed_pieces, cross.pieces if ringed else cross_pieces)
+    far = [
+        [exchange(summed(d, first).astype(jnp.bfloat16), "tp", d) for d in range(1, tp)]
+        for first in range(0, share, part)
+    ]
+    merged = [
+        merge_terms(index * part, source, [kept, *arrived], jnp.stack(terms), cross_gain)
+        for index, terms in enumerate(far)
+    ]
+    encoded = jnp.concatenate([encoded for encoded, _ in merged], axis=0)
+    if ringed:
+        cross.swap(merged[-1][1])
+        cross_pieces = cross.pieces
+    crossed_pieces = []
+    for index, (_, crossed) in enumerate(merged):
+        waits = late if index == 0 else []
+        if ringed and index == parts - 1:
+            waits = [*waits, cross_pieces[-1][0]]
+        for rows, where in gather_heads(crossed, waits):
+            crossed_pieces.append(
+                (rows, [functools.partial(lambda f, i, at: f(at) * share + i, where, index * part)])
+            )
+    keys_values = cross_project(at, crossed_pieces, cross_pieces)
 
     places = [functools.partial(place, 0, 0)]
     moves = []

time: 176 us -> 164 us (0.932)
  local copies, waits for them, and re-layouts: 11.8 us -> 5.78 us
  waiting for transfers between devices: 86.5 us -> 80.9 us
    ppermute x14 -> x12, waiting for transfers between devices: 55.3 us -> 29.2 us  [shift(): lax.ppermute(value, axis, [(i, (i + step) % size) for i in range(size)])]
    ppermute x17 -> x23, waiting for transfers between devices: 17.3 us -> 38.2 us  [exchange(): lax.ppermute(value, axis, [(i, partner(i, step, size)) for i in range(siz...]
    ppermute x17 -> x23, starting transfers between devices: 13 us -> 20.2 us  [exchange(): lax.ppermute(value, axis, [(i, partner(i, step, size)) for i in range(siz...]
    ppermute x14 -> x12, starting transfers between devices: 22.3 us -> 15.3 us  [shift(): lax.ppermute(value, axis, [(i, (i + step) % size) for i in range(size)])]
    unnamed x34 -> x30, local copies, waits for them, and re-layouts: 6.39 us -> 0.77 us
    pallas_call x2 -> x3, Pallas kernels: 3.78 us -> 2.83 us  [the longest x1 2.34 us: cross_project(): pl.pallas_call(functools.partial(cross_kernel, [places for _, places in r...]
  transfers between devices with their start and end apart: 43 -> 47, of which waited for: 22 -> 25; matrix products, arithmetic and copies ran while one was open for 6% -> 6% of each run, Pallas kernels for 6% -> 7%
where the time goes in v4:
time: 164 us
  waiting for transfers between devices  80.9 us (49%)
  starting transfers between devices  43 us (26%)
  Pallas kernels  24.5 us (15%)
  local copies, waits for them, and re-layouts  5.78 us (4%)
  other arithmetic  5.04 us (3%)
  matrix products  3.09 us (2%)
  between operations  1.71 us (1%)
    ppermute x23, waiting for transfers between devices, exchange(): lax.ppermute(value, axis, [(i, partner(i, step, size)) for i in range(siz...  38.2 us
    ppermute x12, waiting for transfers between devices, shift(): lax.ppermute(value, axis, [(i, (i + step) % size) for i in range(size)])  29.2 us
    ppermute x23, starting transfers between devices, exchange(): lax.ppermute(value, axis, [(i, partner(i, step, size)) for i in range(siz...  20.2 us
    ppermute x12, starting transfers between devices, shift(): lax.ppermute(value, axis, [(i, (i + step) % size) for i in range(size)])  15.3 us
    ppermute x12, waiting for transfers between devices, shards(): lax.ppermute(v, ('tp', 'kv'), move)  13.5 us
    pallas_call x1, Pallas kernels, encoder_attention(): pl.pallas_call(functools.partial(encoder_kernel, [places for _, places in...  8.64 us
    pallas_call x4, Pallas kernels, beam_step(): pl.pallas_call(functools.partial(beam_kernel, level, max(len(inputs) - 1,...  8.12 us
    ppermute x12, starting transfers between devices, shards(): lax.ppermute(v, ('tp', 'kv'), move)  7.59 us
  transfers between devices with their start and end apart: 47, of which 25 were waited for; matrix products, arithmetic and copies ran while one was open for 6% of the time, Pallas kernels for 7%

profile of v4, /device:TPU:0, one launch (start us, length us, event | category | flops | bytes accessed | tf_op | source)
XLA Modules:
  0.0 164.0 jit_solution(7319445277209826669)
XLA Ops:
  0.6 1.1 slice_bitcast_fusion.3
  1.8 1.2 pad_maximum_fusion.refs_0_
  3.0 3.1 %collective-permute-start.1 = (bf16[256,1024]{1,0:T(8,128)(2,1)S(1)}, bf16[256,1024]{1,0:T(8,128)(2,1)}, u32[]{:S(2)}, u32[]{:S(2)}) collective-permute-start(bf16[256,1024]{1,0:T(8,128)(2,1)S(1)} %constant_dynamic-slice_fusion.1), channel_id=1, source_target_pairs={{0,4},{4,8},{8,12},{12,0},{1,5},{5,9},{9,13},{13,1},{2,6},{6,10},{... | collective-permute-start | bytes 1572872 | tf_op jit(solution)/shard_map/ppermute | solution.py:53
  6.1 1.6 collective-permute-start
  7.8 2.2 %collective-permute-start.3 = (bf16[128,512]{1,0:T(8,128)(2,1)S(1)}, bf16[128,512]{1,0:T(8,128)(2,1)S(1)}, u32[]{:S(2)}, u32[]{:S(2)}) collective-permute-start(bf16[128,512]{1,0:T(8,128)(2,1)S(1)} %get-tuple-element.100), channel_id=1, source_target_pairs={{0,12},{4,0},{8,4},{12,8},{1,13},{5,1},{9,5},{13,9},{2,14},{6,2},{... | collective-permute-start | bytes 393224 | tf_op jit(solution)/shard_map/ppermute | solution.py:53
  10.0 0.8 collective-permute-start.2
  10.9 12.8 %collective-permute-done = bf16[128,512]{1,0:T(8,128)(2,1)S(1)} collective-permute-done((bf16[128,512]{1,0:T(8,128)(2,1)S(1)}, bf16[128,512]{1,0:T(8,128)(2,1)S(1)}, u32[]{:S(2)}, u32[]{:S(2)}) %collective-permute-start) | collective-permute-done | bytes 131104 | tf_op jit(solution)/shard_map/ppermute | solution.py:53
  23.7 1.8 %collective-permute-start.7 = (bf16[256,1024]{1,0:T(8,128)(2,1)}, bf16[256,1024]{1,0:T(8,128)(2,1)S(1)}, u32[]{:S(2)}, u32[]{:S(2)}) collective-permute-start(bf16[256,1024]{1,0:T(8,128)(2,1)} %collective-permute-done.1.refs_1_), channel_id=1, source_target_pairs={{0,16},{16,0},{1,17},{17,1},{2,18},{18,2},{3,19},{19,3},{4,20},{20... | collective-permute-start | bytes 1572872 | tf_op jit(solution)/shard_map/ppermute | solution.py:48
  25.7 5.6 %collective-permute-done.2 = bf16[128,512]{1,0:T(8,128)(2,1)S(1)} collective-permute-done((bf16[128,512]{1,0:T(8,128)(2,1)S(1)}, bf16[128,512]{1,0:T(8,128)(2,1)S(1)}, u32[]{:S(2)}, u32[]{:S(2)}) %collective-permute-start.2) | collective-permute-done | bytes 131104 | tf_op jit(solution)/shard_map/ppermute | solution.py:53
  31.3 0.8 pad_maximum_fusion.2.refs_0_
  32.1 1.5 collective-permute-start.4
  33.6 1.6 collective-permute-start.8
  35.3 3.1 %convolution_convert_fusion = bf16[64,2048]{1,0:T(8,128)(2,1)S(1)} fusion(bf16[64,1024]{1,0:T(8,128)(2,1)S(1)} %compare_convert_fusion, bf16[1024,2048]{1,0:T(8,128)(2,1)} %param.26), kind=kOutput, calls=%fused_computation | convolution fusion | flops 268566528 | bytes 4587520 | tf_op jit(solution)/shard_map/dot_general | solution.py:567
  39.0 7.3 %collective-permute-done.4.refs_1_ = bf16[512,512]{1,0:T(8,128)(2,1)} collective-permute-done((bf16[512,512]{1,0:T(8,128)(2,1)}, bf16[512,512]{1,0:T(8,128)(2,1)}, u32[]{:S(2)}, u32[]{:S(2)}) %collective-permute-start.4) | collective-permute-done | bytes 524320 | tf_op jit(solution)/shard_map/ppermute | solution.py:48
  46.3 1.0 collective-permute-done.8.refs_3_
  47.3 1.5 collective-permute-start.9
  48.9 0.6 collective-permute-start.12
  49.5 0.7 constant_dynamic-slice_fusion
  50.3 6.2 %collective-permute-done.12 = bf16[64,2048]{1,0:T(8,128)(2,1)S(1)} collective-permute-done((bf16[64,2048]{1,0:T(8,128)(2,1)S(1)}, bf16[64,2048]{1,0:T(8,128)(2,1)S(1)}, u32[]{:S(2)}, u32[]{:S(2)}) %collective-permute-start.12) | collective-permute-done | bytes 262176 | tf_op jit(solution)/shard_map/ppermute | solution.py:48
  56.5 0.7 copy-done.13
  57.3 2.9 %copy.17 = bf16[2048,512]{0,1:T(8,128)(2,1)S(1)} copy(bf16[2048,512]{1,0:T(8,128)(2,1)} %param.25) | data formatting | bytes 4194304 | tf_op jit(solution)/shard_map/optimization_barrier | solution.py:57
  60.2 1.2 add.87
  61.4 2.8 %norm_events.1 = (bf16[512,2048]{1,0:T(8,128)(2,1)S(1)}, bf16[128,2048]{1,0:T(8,128)(2,1)S(1)}) custom-call(s32[4]{0:T(128)S(1)} %pad_add_fusion.at_ref, f32[1,2048]{1,0:T(1,128)S(1)} %bitcast.44, bf16[512,512]{1,0:T(8,128)(2,1)} %pad_maximum_fusion.2.refs_0_, bf16[512,512]{1,0:T(8,128)(2,1)} %collective-permute-done.4.refs_1_, ...), custom_call_target="tpu_custom_call" | custom-call | bytes 12000000 | tf_op jit(solution)/shard_map/norm_events/pallas_call | solution.py:204
  64.2 1.6 collective-permute-done.10.refs_5_
  66.3 2.1 %collective-permute-start.15 = (bf16[256,512]{1,0:T(8,128)(2,1)}, bf16[256,512]{1,0:T(8,128)(2,1)S(1)}, u32[]{:S(2)}, u32[]{:S(2)}) collective-permute-start(bf16[256,512]{1,0:T(8,128)(2,1)} %constant_dynamic-slice_fusion), channel_id=1, source_target_pairs={{0,12},{4,0},{8,4},{12,8},{1,13},{5,1},{9,5},{13,9},{2,14},{6,2},{... | collective-permute-start | bytes 786440 | tf_op jit(solution)/shard_map/ppermute | solution.py:53
  69.0 2.0 %collective-permute-done.14.refs_1_ = bf16[256,512]{1,0:T(8,128)(2,1)S(1)} collective-permute-done((bf16[256,512]{1,0:T(8,128)(2,1)}, bf16[256,512]{1,0:T(8,128)(2,1)S(1)}, u32[]{:S(2)}, u32[]{:S(2)}) %collective-permute-start.14) | collective-permute-done | bytes 262176 | tf_op jit(solution)/shard_map/ppermute | solution.py:53
  71.0 6.1 %collective-permute-done.15.refs_3_ = bf16[256,512]{1,0:T(8,128)(2,1)S(1)} collective-permute-done((bf16[256,512]{1,0:T(8,128)(2,1)}, bf16[256,512]{1,0:T(8,128)(2,1)S(1)}, u32[]{:S(2)}, u32[]{:S(2)}) %collective-permute-start.15) | collective-permute-done | bytes 262176 | tf_op jit(solution)/shard_map/ppermute | solution.py:53
  77.7 3.3 %collective-permute-start.17 = (bf16[256,512]{1,0:T(8,128)(2,1)S(1)}, bf16[256,512]{1,0:T(8,128)(2,1)S(1)}, u32[]{:S(2)}, u32[]{:S(2)}) collective-permute-start(bf16[256,512]{1,0:T(8,128)(2,1)S(1)} %fusion), channel_id=1, source_target_pairs={{0,12},{4,0},{8,4},{12,8},{1,13},{5,1},{9,5},{13,9},{2,14},{6,2},{... | collective-permute-start | bytes 786440 | tf_op jit(solution)/shard_map/ppermute | solution.py:53
  80.9 1.4 collective-permute-start.18
  82.3 0.6 collective-permute-start.19
  83.0 8.6 %encoder_attention.1.attended_ref = bf16[512,512]{1,0:T(8,128)(2,1)S(1)} custom-call(s32[4]{0:T(128)S(1)} %pad_add_fusion.at_ref, s32[1]{0:T(128)S(6)} %copy.18.live_ref, bf16[512,2048]{1,0:T(8,128)(2,1)S(1)} %get-tuple-element.58.rows_ref, bf16[2,512,256]{2,1,0:T(8,128)(2,1)S(1)} %bitcast.35, bf16[512,1024]{1,0:T(8,128)(2,1)S(1)} %pad_maximum_fusion.refs_0_, ...), custom_call_target="tpu_custom_call" | custom-call | bytes 33000000 | tf_op jit(solution)/shard_map/encoder_attention/pallas_call | solution.py:315
  91.6 1.5 collective-permute-start.21
  93.2 4.8 %collective-permute-done.21.refs_6_ = bf16[256,512]{1,0:T(8,128)(2,1)S(1)} collective-permute-done((bf16[256,512]{1,0:T(8,128)(2,1)S(1)}, bf16[256,512]{1,0:T(8,128)(2,1)S(1)}, u32[]{:S(2)}, u32[]{:S(2)}) %collective-permute-start.21) | collective-permute-done | bytes 262176 | tf_op jit(solution)/shard_map/ppermute | solution.py:48
  98.1 2.1 %project_out.1 = (bf16[256,2048]{1,0:T(8,128)(2,1)S(1)}, bf16[256,2048]{1,0:T(8,128)(2,1)S(1)}) custom-call(s32[4]{0:T(128)S(1)} %pad_add_fusion.at_ref, bf16[512,512]{1,0:T(8,128)(2,1)S(1)} %encoder_attention.1.attended_ref, bf16[512,512]{1,0:T(8,128)(2,1)S(1)} %copy-done.2, bf16[256,512]{1,0:T(8,128)(2,1)S(1)} %collective-permute-done.14.refs_1_, ...), custom_call_target="tpu_custom_call" | custom-call | bytes 15000000 | tf_op jit(solution)/shard_map/project_out/pallas_call | solution.py:365
  100.3 2.6 %collective-permute-done.22.refs_1_ = bf16[256,2048]{1,0:T(8,128)(2,1)S(1)} collective-permute-done((bf16[256,2048]{1,0:T(8,128)(2,1)S(1)}, bf16[256,2048]{1,0:T(8,128)(2,1)S(1)}, u32[]{:S(2)}, u32[]{:S(2)}) %collective-permute-start.22) | collective-permute-done | bytes 1048608 | tf_op jit(solution)/shard_map/ppermute | solution.py:48
  103.0 2.9 %collective-permute-start.23 = (bf16[64,2048]{1,0:T(8,128)(2,1)S(1)}, bf16[64,2048]{1,0:T(8,128)(2,1)S(1)}, u32[]{:S(2)}, u32[]{:S(2)}) collective-permute-start(bf16[64,2048]{1,0:T(8,128)(2,1)S(1)} %get-tuple-element.94), channel_id=1, source_target_pairs={{0,2},{2,0},{1,3},{3,1},{4,6},{6,4},{5,7},{7,5},{8,10},{10,8},{9,1... | collective-permute-start | bytes 786440 | tf_op jit(solution)/shard_map/ppermute | solution.py:48
  106.5 1.6 collective-permute-start.27
  108.1 5.0 %collective-permute-done.23 = bf16[64,2048]{1,0:T(8,128)(2,1)S(1)} collective-permute-done((bf16[64,2048]{1,0:T(8,128)(2,1)S(1)}, bf16[64,2048]{1,0:T(8,128)(2,1)S(1)}, u32[]{:S(2)}, u32[]{:S(2)}) %collective-permute-start.23) | collective-permute-done | bytes 262176 | tf_op jit(solution)/shard_map/ppermute | solution.py:48
  113.3 2.1 %collective-permute-start.25 = (bf16[64,2048]{1,0:T(8,128)(2,1)S(1)}, bf16[64,2048]{1,0:T(8,128)(2,1)S(1)}, u32[]{:S(2)}, u32[]{:S(2)}) collective-permute-start(bf16[64,2048]{1,0:T(8,128)(2,1)S(1)} %get-tuple-element.76.refs_0_), channel_id=1, source_target_pairs={{0,2},{2,0},{1,3},{3,1},{4,6},{6,4},{5,7},{7,5},{8,10},{10,8},{9,1... | collective-permute-start | bytes 786440 | tf_op jit(solution)/shard_map/ppermute | solution.py:48
  115.5 3.2 %collective-permute-done.24 = bf16[64,2048]{1,0:T(8,128)(2,1)S(1)} collective-permute-done((bf16[64,2048]{1,0:T(8,128)(2,1)S(1)}, bf16[64,2048]{1,0:T(8,128)(2,1)S(1)}, u32[]{:S(2)}, u32[]{:S(2)}) %collective-permute-start.24) | collective-permute-done | bytes 262176 | tf_op jit(solution)/shard_map/ppermute | solution.py:48
  118.9 2.1 %collective-permute-start.31 = (bf16[64,2048]{1,0:T(8,128)(2,1)S(1)}, bf16[64,2048]{1,0:T(8,128)(2,1)S(1)}, u32[]{:S(2)}, u32[]{:S(2)}) collective-permute-start(bf16[64,2048]{1,0:T(8,128)(2,1)S(1)} %get-tuple-element.80.refs_4_), channel_id=1, source_target_pairs={{0,2},{2,0},{1,3},{3,1},{4,6},{6,4},{5,7},{7,5},{8,10},{10,8},{9,1... | collective-permute-start | bytes 786440 | tf_op jit(solution)/shard_map/ppermute | solution.py:48
  122.0 2.3 %collective-permute-done.25.refs_1_ = bf16[64,2048]{1,0:T(8,128)(2,1)S(1)} collective-permute-done((bf16[64,2048]{1,0:T(8,128)(2,1)S(1)}, bf16[64,2048]{1,0:T(8,128)(2,1)S(1)}, u32[]{:S(2)}, u32[]{:S(2)}) %collective-permute-start.25) | collective-permute-done | bytes 262176 | tf_op jit(solution)/shard_map/ppermute | solution.py:48
  124.3 5.1 %collective-permute-done.31.refs_5_ = bf16[64,2048]{1,0:T(8,128)(2,1)S(1)} collective-permute-done((bf16[64,2048]{1,0:T(8,128)(2,1)S(1)}, bf16[64,2048]{1,0:T(8,128)(2,1)S(1)}, u32[]{:S(2)}, u32[]{:S(2)}) %collective-permute-start.31) | collective-permute-done | bytes 262176 | tf_op jit(solution)/shard_map/ppermute | solution.py:48
  129.5 1.4 collective-permute-done.34.refs_7_
  131.0 2.3 %cross_project.1.cross_ref = bf16[512,512]{1,0:T(8,128)(2,1)S(1)} custom-call(s32[4]{0:T(128)S(1)} %pad_add_fusion.at_ref, bf16[64,2048]{1,0:T(8,128)(2,1)S(1)} %get-tuple-element.76.refs_0_, bf16[64,2048]{1,0:T(8,128)(2,1)S(1)} %collective-permute-done.25.refs_1_, bf16[64,2048]{1,0:T(8,128)(2,1)S(1)} %collective-permute-done.29.refs_2_, ...), custom_call_target="tpu_custom_call" | custom-call | bytes 6000000 | tf_op jit(solution)/shard_map/cross_project/pallas_call | solution.py:428
  133.4 1.9 %beam_step_0.1 = (f32[16,2048]{1,0:T(8,128)S(1)}, bf16[16,2048]{1,0:T(8,128)(2,1)S(1)}) custom-call(s32[4]{0:T(128)S(1)} %pad_add_fusion.at_ref, s32[1]{0:T(128)S(6)} %copy.18.live_ref, s32[3,16]{1,0:T(4,128)S(1)} %copy-done.7, f32[1,2048]{1,0:T(1,128)S(1)} %bitcast.38, bf16[2048,512]{1,0:T(8,128)(2,1)S(1)} %copy-done, bf16[512,2048]{1,0:T(8,128)(2,1)S(1)} %bitcast.31, ...), custom_call_target="tpu_custom_call" | custom-call | bytes 12000000 | tf_op jit(solution)/shard_map/beam_step_0/pallas_call | solution.py:523
  135.4 1.8 %collective-permute-start.36 = (bf16[16,2048]{1,0:T(8,128)(2,1)S(1)}, bf16[16,2048]{1,0:T(8,128)(2,1)S(1)}, u32[]{:S(2)}, u32[]{:S(2)}) collective-permute-start(bf16[16,2048]{1,0:T(8,128)(2,1)S(1)} %get-tuple-element.85.refs_1_), channel_id=1, source_target_pairs={{0,2},{1,3},{2,0},{3,1},{4,6},{5,7},{6,4},{7,5},{8,10},{9,11},{10,... | collective-permute-start | bytes 196616 | tf_op jit(solution)/shard_map/ppermute | solution.py:676
  137.2 2.6 %collective-permute-done.36.refs_3_ = bf16[16,2048]{1,0:T(8,128)(2,1)S(1)} collective-permute-done((bf16[16,2048]{1,0:T(8,128)(2,1)S(1)}, bf16[16,2048]{1,0:T(8,128)(2,1)S(1)}, u32[]{:S(2)}, u32[]{:S(2)}) %collective-permute-start.36) | collective-permute-done | bytes 65568 | tf_op jit(solution)/shard_map/ppermute | solution.py:676
  139.8 1.5 collective-permute-done.37.refs_4_
  141.4 2.1 %beam_step_1.1 = (f32[16,2048]{1,0:T(8,128)S(1)}, bf16[16,2048]{1,0:T(8,128)(2,1)S(1)}) custom-call(s32[4]{0:T(128)S(1)} %pad_add_fusion.at_ref, s32[1]{0:T(128)S(6)} %copy.18.live_ref, s32[3,16]{1,0:T(4,128)S(1)} %copy-done.7, f32[1,2048]{1,0:T(1,128)S(1)} %bitcast.39, bf16[2048,512]{1,0:T(8,128)(2,1)S(1)} %copy-done, bf16[512,2048]{1,0:T(8,128)(2,1)S(1)} %bitcast.32, ...), custom_call_target="tpu_custom_call" | custom-call | bytes 12000000 | tf_op jit(solution)/shard_map/beam_step_1/pallas_call | solution.py:523
  143.5 1.3 collective-permute-start.39
  145.3 2.8 %collective-permute-done.39.refs_3_ = bf16[16,2048]{1,0:T(8,128)(2,1)S(1)} collective-permute-done((bf16[16,2048]{1,0:T(8,128)(2,1)S(1)}, bf16[16,2048]{1,0:T(8,128)(2,1)S(1)}, u32[]{:S(2)}, u32[]{:S(2)}) %collective-permute-start.39) | collective-permute-done | bytes 65568 | tf_op jit(solution)/shard_map/ppermute | solution.py:676
  148.1 1.1 collective-permute-done.40.refs_4_
  149.2 2.1 %beam_step_2.1 = (f32[16,2048]{1,0:T(8,128)S(1)}, bf16[16,2048]{1,0:T(8,128)(2,1)S(1)}) custom-call(s32[4]{0:T(128)S(1)} %pad_add_fusion.at_ref, s32[1]{0:T(128)S(6)} %copy.18.live_ref, s32[3,16]{1,0:T(4,128)S(1)} %copy-done.7, f32[1,2048]{1,0:T(1,128)S(1)} %bitcast.40, bf16[2048,512]{1,0:T(8,128)(2,1)S(1)} %copy-done, bf16[512,2048]{1,0:T(8,128)(2,1)S(1)} %bitcast.33, ...), custom_call_target="tpu_custom_call" | custom-call | bytes 12000000 | tf_op jit(solution)/shard_map/beam_step_2/pallas_call | solution.py:523
  151.4 1.0 collective-permute-start.42
  152.4 0.7 collective-permute-start.43
  153.1 3.0 %collective-permute-done.42.refs_3_ = bf16[16,2048]{1,0:T(8,128)(2,1)S(1)} collective-permute-done((bf16[16,2048]{1,0:T(8,128)(2,1)S(1)}, bf16[16,2048]{1,0:T(8,128)(2,1)S(1)}, u32[]{:S(2)}, u32[]{:S(2)}) %collective-permute-start.42) | collective-permute-done | bytes 65568 | tf_op jit(solution)/shard_map/ppermute | solution.py:676
  156.1 0.7 collective-permute-done.43.refs_4_
  156.8 2.1 %beam_step_3.1 = (f32[16,512]{1,0:T(8,128)S(1)}, bf16[16,512]{1,0:T(8,128)(2,1)S(1)}, bf16[16,512]{1,0:T(8,128)(2,1)S(1)}, bf16[16,512]{1,0:T(8,128)(2,1)S(1)}) custom-call(s32[4]{0:T(128)S(1)} %pad_add_fusion.at_ref, s32[1]{0:T(128)S(6)} %copy.18.live_ref, s32[3,16]{1,0:T(4,128)S(1)} %copy-done.7, f32[1,2048]{1,0:T(1,128)S(1)} %bitcast.41, ...), custom_call_target="tpu_custom_call" | custom-call | bytes 12000000 | tf_op jit(solution)/shard_map/beam_step_3/pallas_call | solution.py:523
  158.9 0.8 collective-permute-start.46
  159.7 1.1 collective-permute-start.45
  160.8 0.8 maximum_bitcast_fusion
  162.1 1.3 collective-permute-done.45
  163.4 0.6 add_convert_fusion.2
  (91 shorter events, 6.0 us)
Async XLA Ops:
  0.6 5.5 %copy-start.11 = (bf16[4,128,512]{2,1,0:T(8,128)(2,1)S(1)}, bf16[4,128,512]{2,1,0:T(8,128)(2,1)}, u32[]{:S(2)}) copy-start(bf16[4,128,512]{2,1,0:T(8,128)(2,1)} %param.15) | copy-start | bytes 1572868
  1.8 9.0 %copy-start.14 = (s32[4,16]{1,0:T(4,128)S(1)}, s32[4,16]{1,0:T(4,128)}, u32[]{:S(2)}) copy-start(s32[4,16]{1,0:T(4,128)} %param.18) | copy-start | bytes 772
  3.0 20.7 %collective-permute-start.1 = (bf16[256,1024]{1,0:T(8,128)(2,1)S(1)}, bf16[256,1024]{1,0:T(8,128)(2,1)}, u32[]{:S(2)}, u32[]{:S(2)}) collective-permute-start(bf16[256,1024]{1,0:T(8,128)(2,1)S(1)} %constant_dynamic-slice_fusion.1), channel_id=1, source_target_pairs={{0,4},{4,8},{8,12},{12,0},{1,5},{5,9},{9,13},{13,1},{2,6},{6,10},{... | collective-permute-start | bytes 1572872 | tf_op jit(solution)/shard_map/ppermute | solution.py:53
  6.1 17.6 %collective-permute-start = (bf16[128,512]{1,0:T(8,128)(2,1)S(1)}, bf16[128,512]{1,0:T(8,128)(2,1)S(1)}, u32[]{:S(2)}, u32[]{:S(2)}) collective-permute-start(bf16[128,512]{1,0:T(8,128)(2,1)S(1)} %get-tuple-element.99), channel_id=1, source_target_pairs={{0,4},{4,8},{8,12},{12,0},{1,5},{5,9},{9,13},{13,1},{2,6},{6,10},{... | collective-permute-start | bytes 393224 | tf_op jit(solution)/shard_map/ppermute | solution.py:53
  7.8 17.9 %collective-permute-start.3 = (bf16[128,512]{1,0:T(8,128)(2,1)S(1)}, bf16[128,512]{1,0:T(8,128)(2,1)S(1)}, u32[]{:S(2)}, u32[]{:S(2)}) collective-permute-start(bf16[128,512]{1,0:T(8,128)(2,1)S(1)} %get-tuple-element.100), channel_id=1, source_target_pairs={{0,12},{4,0},{8,4},{12,8},{1,13},{5,1},{9,5},{13,9},{2,14},{6,2},{... | collective-permute-start | bytes 393224 | tf_op jit(solution)/shard_map/ppermute | solution.py:53
  10.0 21.3 %collective-permute-start.2 = (bf16[128,512]{1,0:T(8,128)(2,1)S(1)}, bf16[128,512]{1,0:T(8,128)(2,1)S(1)}, u32[]{:S(2)}, u32[]{:S(2)}) collective-permute-start(bf16[128,512]{1,0:T(8,128)(2,1)S(1)} %get-tuple-element.101), channel_id=1, source_target_pairs={{0,8},{4,12},{8,0},{12,4},{1,9},{5,13},{9,1},{13,5},{2,10},{6,14},... | collective-permute-start | bytes 393224 | tf_op jit(solution)/shard_map/ppermute | solution.py:53
  23.7 22.5 %collective-permute-start.7 = (bf16[256,1024]{1,0:T(8,128)(2,1)}, bf16[256,1024]{1,0:T(8,128)(2,1)S(1)}, u32[]{:S(2)}, u32[]{:S(2)}) collective-permute-start(bf16[256,1024]{1,0:T(8,128)(2,1)} %collective-permute-done.1.refs_1_), channel_id=1, source_target_pairs={{0,16},{16,0},{1,17},{17,1},{2,18},{18,2},{3,19},{19,3},{4,20},{20... | collective-permute-start | bytes 1572872 | tf_op jit(solution)/shard_map/ppermute | solution.py:48
  32.1 14.2 %collective-permute-start.4 = (bf16[512,512]{1,0:T(8,128)(2,1)}, bf16[512,512]{1,0:T(8,128)(2,1)}, u32[]{:S(2)}, u32[]{:S(2)}) collective-permute-start(bf16[512,512]{1,0:T(8,128)(2,1)} %pad_maximum_fusion.2.refs_0_), channel_id=1, source_target_pairs={{0,2},{2,0},{1,3},{3,1},{4,6},{6,4},{5,7},{7,5},{8,10},{10,8},{9,1... | collective-permute-start | bytes 1572872 | tf_op jit(solution)/shard_map/ppermute | solution.py:48
  33.6 13.7 %collective-permute-start.8 = (bf16[256,1024]{1,0:T(8,128)(2,1)S(1)}, bf16[256,1024]{1,0:T(8,128)(2,1)}, u32[]{:S(2)}, u32[]{:S(2)}) collective-permute-start(bf16[256,1024]{1,0:T(8,128)(2,1)S(1)} %constant_dynamic-slice_fusion.1), channel_id=1, source_target_pairs={{0,12},{4,0},{8,4},{12,8},{1,13},{5,1},{9,5},{13,9},{2,14},{6,2},{... | collective-permute-start | bytes 1572872 | tf_op jit(solution)/shard_map/ppermute | solution.py:53
  35.3 14.2 %copy-start.1 = (bf16[512,512]{1,0:T(8,128)(2,1)S(1)}, bf16[512,512]{1,0:T(8,128)(2,1)}, u32[]{:S(2)}) copy-start(bf16[512,512]{1,0:T(8,128)(2,1)} %refs_0_.1) | copy-start | bytes 1572868
  38.4 10.4 %collective-permute-start.11 = (bf16[64,2048]{1,0:T(8,128)(2,1)S(1)}, bf16[64,2048]{1,0:T(8,128)(2,1)S(1)}, u32[]{:S(2)}, u32[]{:S(2)}) collective-permute-start(bf16[64,2048]{1,0:T(8,128)(2,1)S(1)} %convolution_convert_fusion), channel_id=1, source_target_pairs={{0,1},{1,0},{2,3},{3,2},{4,5},{5,4},{6,7},{7,6},{8,9},{9,8},{10,11... | collective-permute-start | bytes 786440 | tf_op jit(solution)/shard_map/ppermute | solution.py:48
  38.5 22.9 %collective-permute-start.5 = (bf16[512,512]{1,0:T(8,128)(2,1)}, bf16[512,512]{1,0:T(8,128)(2,1)}, u32[]{:S(2)}, u32[]{:S(2)}) collective-permute-start(bf16[512,512]{1,0:T(8,128)(2,1)} %pad_maximum_fusion.2.refs_0_), channel_id=1, source_target_pairs={{0,1},{1,0},{2,3},{3,2},{4,5},{5,4},{6,7},{7,6},{8,9},{9,8},{10,11... | collective-permute-start | bytes 1572872 | tf_op jit(solution)/shard_map/ppermute | solution.py:48
  46.3 15.1 %collective-permute-start.6 = (bf16[512,512]{1,0:T(8,128)(2,1)}, bf16[512,512]{1,0:T(8,128)(2,1)}, u32[]{:S(2)}, u32[]{:S(2)}) collective-permute-start(bf16[512,512]{1,0:T(8,128)(2,1)} %collective-permute-done.4.refs_1_), channel_id=1, source_target_pairs={{0,1},{1,0},{2,3},{3,2},{4,5},{5,4},{6,7},{7,6},{8,9},{9,8},{10,11... | collective-permute-start | bytes 1572872 | tf_op jit(solution)/shard_map/ppermute | solution.py:48
  46.3 10.2 %copy-start.4 = (bf16[256,1024]{1,0:T(8,128)(2,1)}, bf16[256,1024]{1,0:T(8,128)(2,1)S(1)}, u32[]{:S(2)}) copy-start(bf16[256,1024]{1,0:T(8,128)(2,1)S(1)} %collective-permute-done.7.refs_2_) | copy-start | bytes 1572868
  47.3 16.9 %collective-permute-start.9 = (bf16[256,1024]{1,0:T(8,128)(2,1)}, bf16[256,1024]{1,0:T(8,128)(2,1)}, u32[]{:S(2)}, u32[]{:S(2)}) collective-permute-start(bf16[256,1024]{1,0:T(8,128)(2,1)} %collective-permute-done.8.refs_3_), channel_id=1, source_target_pairs={{0,16},{16,0},{1,17},{17,1},{2,18},{18,2},{3,19},{19,3},{4,20},{20... | collective-permute-start | bytes 1572872 | tf_op jit(solution)/shard_map/ppermute | solution.py:48
  48.8 17.0 %collective-permute-start.10 = (bf16[256,1024]{1,0:T(8,128)(2,1)}, bf16[256,1024]{1,0:T(8,128)(2,1)}, u32[]{:S(2)}, u32[]{:S(2)}) collective-permute-start(bf16[256,1024]{1,0:T(8,128)(2,1)} %collective-permute-done.1.refs_1_), channel_id=1, source_target_pairs={{0,4},{4,8},{8,12},{12,0},{1,5},{5,9},{9,13},{13,1},{2,6},{6,10},{... | collective-permute-start | bytes 1572872 | tf_op jit(solution)/shard_map/ppermute | solution.py:53
  48.9 7.6 %copy-start.10 = (bf16[64,2048]{1,0:T(8,128)(2,1)}, bf16[64,2048]{1,0:T(8,128)(2,1)S(1)}, u32[]{:S(2)}) copy-start(bf16[64,2048]{1,0:T(8,128)(2,1)S(1)} %add.86) | copy-start | bytes 786436
  48.9 7.6 %collective-permute-start.12 = (bf16[64,2048]{1,0:T(8,128)(2,1)S(1)}, bf16[64,2048]{1,0:T(8,128)(2,1)S(1)}, u32[]{:S(2)}, u32[]{:S(2)}) collective-permute-start(bf16[64,2048]{1,0:T(8,128)(2,1)S(1)} %add.86), channel_id=1, source_target_pairs={{0,2},{2,0},{1,3},{3,1},{4,6},{6,4},{5,7},{7,5},{8,10},{10,8},{9,1... | collective-permute-start | bytes 786440 | tf_op jit(solution)/shard_map/ppermute | solution.py:48
  56.5 0.7 copy-start.13
  56.5 14.5 %collective-permute-start.14 = (bf16[256,512]{1,0:T(8,128)(2,1)}, bf16[256,512]{1,0:T(8,128)(2,1)S(1)}, u32[]{:S(2)}, u32[]{:S(2)}) collective-permute-start(bf16[256,512]{1,0:T(8,128)(2,1)} %constant_dynamic-slice_fusion), channel_id=1, source_target_pairs={{0,4},{4,8},{8,12},{12,0},{1,5},{5,9},{9,13},{13,1},{2,6},{6,10},{... | collective-permute-start | bytes 786440 | tf_op jit(solution)/shard_map/ppermute | solution.py:53
  57.3 4.2 %copy-start.9 = (f32[2048]{0:T(1024)S(1)}, f32[2048]{0:T(1024)}, u32[]{:S(2)}) copy-start(f32[2048]{0:T(1024)} %param.27) | copy-start | bytes 24580
  60.2 10.8 %copy-start.12 = (bf16[2,512,256]{2,1,0:T(8,128)(2,1)S(1)}, bf16[2,512,256]{2,1,0:T(8,128)(2,1)}, u32[]{:S(2)}) copy-start(bf16[2,512,256]{2,1,0:T(8,128)(2,1)} %param.23) | copy-start | bytes 1572868
  61.4 21.6 %copy-start.3 = (bf16[2,1,512,256]{3,2,1,0:T(8,128)(2,1)S(1)}, bf16[2,1,512,256]{3,2,1,0:T(8,128)(2,1)}, u32[]{:S(2)}) copy-start(bf16[2,1,512,256]{3,2,1,0:T(8,128)(2,1)} %param.16) | copy-start | bytes 1572868
  61.4 21.6 %copy-start.5 = (bf16[256,1024]{1,0:T(8,128)(2,1)S(1)}, bf16[256,1024]{1,0:T(8,128)(2,1)}, u32[]{:S(2)}) copy-start(bf16[256,1024]{1,0:T(8,128)(2,1)} %copy-done.4) | copy-start | bytes 1572868
  65.8 11.3 %collective-permute-start.13 = (bf16[256,1024]{1,0:T(8,128)(2,1)}, bf16[256,1024]{1,0:T(8,128)(2,1)S(1)}, u32[]{:S(2)}, u32[]{:S(2)}) collective-permute-start(bf16[256,1024]{1,0:T(8,128)(2,1)} %collective-permute-done.10.refs_5_), channel_id=1, source_target_pairs={{0,16},{16,0},{1,17},{17,1},{2,18},{18,2},{3,19},{19,3},{4,20},{20... | collective-permute-start | bytes 1572872 | tf_op jit(solution)/shard_map/ppermute | solution.py:48
  66.3 10.8 %collective-permute-start.15 = (bf16[256,512]{1,0:T(8,128)(2,1)}, bf16[256,512]{1,0:T(8,128)(2,1)S(1)}, u32[]{:S(2)}, u32[]{:S(2)}) collective-permute-start(bf16[256,512]{1,0:T(8,128)(2,1)} %constant_dynamic-slice_fusion), channel_id=1, source_target_pairs={{0,12},{4,0},{8,4},{12,8},{1,13},{5,1},{9,5},{13,9},{2,14},{6,2},{... | collective-permute-start | bytes 786440 | tf_op jit(solution)/shard_map/ppermute | solution.py:53
  71.0 20.7 %collective-permute-start.20 = (bf16[256,512]{1,0:T(8,128)(2,1)S(1)}, bf16[256,512]{1,0:T(8,128)(2,1)S(1)}, u32[]{:S(2)}, u32[]{:S(2)}) collective-permute-start(bf16[256,512]{1,0:T(8,128)(2,1)S(1)} %collective-permute-done.14.refs_1_), channel_id=1, source_target_pairs={{0,4},{4,8},{8,12},{12,0},{1,5},{5,9},{9,13},{13,1},{2,6},{6,10},{... | collective-permute-start | bytes 786440 | tf_op jit(solution)/shard_map/ppermute | solution.py:53
  77.1 16.0 %collective-permute-start.16 = (bf16[256,512]{1,0:T(8,128)(2,1)S(1)}, bf16[256,512]{1,0:T(8,128)(2,1)S(1)}, u32[]{:S(2)}, u32[]{:S(2)}) collective-permute-start(bf16[256,512]{1,0:T(8,128)(2,1)S(1)} %fusion), channel_id=1, source_target_pairs={{0,4},{4,8},{8,12},{12,0},{1,5},{5,9},{9,13},{13,1},{2,6},{6,10},{... | collective-permute-start | bytes 786440 | tf_op jit(solution)/shard_map/ppermute | solution.py:53
  77.7 15.4 %collective-permute-start.17 = (bf16[256,512]{1,0:T(8,128)(2,1)S(1)}, bf16[256,512]{1,0:T(8,128)(2,1)S(1)}, u32[]{:S(2)}, u32[]{:S(2)}) collective-permute-start(bf16[256,512]{1,0:T(8,128)(2,1)S(1)} %fusion), channel_id=1, source_target_pairs={{0,12},{4,0},{8,4},{12,8},{1,13},{5,1},{9,5},{13,9},{2,14},{6,2},{... | collective-permute-start | bytes 786440 | tf_op jit(solution)/shard_map/ppermute | solution.py:53
  80.9 12.2 %collective-permute-start.18 = (bf16[256,512]{1,0:T(8,128)(2,1)S(1)}, bf16[256,512]{1,0:T(8,128)(2,1)S(1)}, u32[]{:S(2)}, u32[]{:S(2)}) collective-permute-start(bf16[256,512]{1,0:T(8,128)(2,1)S(1)} %collective-permute-done.14.refs_1_), channel_id=1, source_target_pairs={{0,16},{16,0},{1,17},{17,1},{2,18},{18,2},{3,19},{19,3},{4,20},{20... | collective-permute-start | bytes 786440 | tf_op jit(solution)/shard_map/ppermute | solution.py:48
  82.3 10.9 %collective-permute-start.19 = (bf16[256,512]{1,0:T(8,128)(2,1)S(1)}, bf16[256,512]{1,0:T(8,128)(2,1)S(1)}, u32[]{:S(2)}, u32[]{:S(2)}) collective-permute-start(bf16[256,512]{1,0:T(8,128)(2,1)S(1)} %collective-permute-done.15.refs_3_), channel_id=1, source_target_pairs={{0,16},{16,0},{1,17},{17,1},{2,18},{18,2},{3,19},{19,3},{4,20},{20... | collective-permute-start | bytes 786440 | tf_op jit(solution)/shard_map/ppermute | solution.py:48
  83.0 15.1 %copy-start.2 = (bf16[512,512]{1,0:T(8,128)(2,1)S(1)}, bf16[512,512]{1,0:T(8,128)(2,1)}, u32[]{:S(2)}) copy-start(bf16[512,512]{1,0:T(8,128)(2,1)} %refs_0_.1) | copy-start | bytes 1572868
  91.6 21.5 %copy-start.8 = (f32[2048]{0:T(1024)S(1)}, f32[2048]{0:T(1024)}, u32[]{:S(2)}) copy-start(f32[2048]{0:T(1024)} %param.28) | copy-start | bytes 24580
  91.6 6.4 %collective-permute-start.21 = (bf16[256,512]{1,0:T(8,128)(2,1)S(1)}, bf16[256,512]{1,0:T(8,128)(2,1)S(1)}, u32[]{:S(2)}, u32[]{:S(2)}) collective-permute-start(bf16[256,512]{1,0:T(8,128)(2,1)S(1)} %collective-permute-done.20.refs_5_), channel_id=1, source_target_pairs={{0,16},{16,0},{1,17},{17,1},{2,18},{18,2},{3,19},{19,3},{4,20},{20... | collective-permute-start | bytes 786440 | tf_op jit(solution)/shard_map/ppermute | solution.py:48
  100.2 2.7 %collective-permute-start.22 = (bf16[256,2048]{1,0:T(8,128)(2,1)S(1)}, bf16[256,2048]{1,0:T(8,128)(2,1)S(1)}, u32[]{:S(2)}, u32[]{:S(2)}) collective-permute-start(bf16[256,2048]{1,0:T(8,128)(2,1)S(1)} %get-tuple-element.72), channel_id=1, source_target_pairs={{0,1},{1,0},{2,3},{3,2},{4,5},{5,4},{6,7},{7,6},{8,9},{9,8},{10,11... | collective-permute-start | bytes 3145736 | tf_op jit(solution)/shard_map/ppermute | solution.py:48
  103.0 10.0 %collective-permute-start.23 = (bf16[64,2048]{1,0:T(8,128)(2,1)S(1)}, bf16[64,2048]{1,0:T(8,128)(2,1)S(1)}, u32[]{:S(2)}, u32[]{:S(2)}) collective-permute-start(bf16[64,2048]{1,0:T(8,128)(2,1)S(1)} %get-tuple-element.94), channel_id=1, source_target_pairs={{0,2},{2,0},{1,3},{3,1},{4,6},{6,4},{5,7},{7,5},{8,10},{10,8},{9,1... | collective-permute-start | bytes 786440 | tf_op jit(solution)/shard_map/ppermute | solution.py:48
  106.0 12.7 %collective-permute-start.24 = (bf16[64,2048]{1,0:T(8,128)(2,1)S(1)}, bf16[64,2048]{1,0:T(8,128)(2,1)S(1)}, u32[]{:S(2)}, u32[]{:S(2)}) collective-permute-start(bf16[64,2048]{1,0:T(8,128)(2,1)S(1)} %get-tuple-element.95), channel_id=1, source_target_pairs={{0,2},{2,0},{1,3},{3,1},{4,6},{6,4},{5,7},{7,5},{8,10},{10,8},{9,1... | collective-permute-start | bytes 786440 | tf_op jit(solution)/shard_map/ppermute | solution.py:48
  106.1 15.0 %collective-permute-start.28 = (bf16[256,512]{1,0:T(8,128)(2,1)S(1)}, bf16[256,512]{1,0:T(8,128)(2,1)S(1)}, u32[]{:S(2)}, u32[]{:S(2)}) collective-permute-start(bf16[256,512]{1,0:T(8,128)(2,1)S(1)} %collective-permute-done.16.refs_9_), channel_id=1, source_target_pairs={{0,4},{4,8},{8,12},{12,0},{1,5},{5,9},{9,13},{13,1},{2,6},{6,10},{... | collective-permute-start | bytes 786440 | tf_op jit(solution)/shard_map/ppermute | solution.py:53
  106.1 15.3 %collective-permute-start.26 = (bf16[256,512]{1,0:T(8,128)(2,1)S(1)}, bf16[256,512]{1,0:T(8,128)(2,1)S(1)}, u32[]{:S(2)}, u32[]{:S(2)}) collective-permute-start(bf16[256,512]{1,0:T(8,128)(2,1)S(1)} %collective-permute-done.16.refs_9_), channel_id=1, source_target_pairs={{0,16},{16,0},{1,17},{17,1},{2,18},{18,2},{3,19},{19,3},{4,20},{20... | collective-permute-start | bytes 786440 | tf_op jit(solution)/shard_map/ppermute | solution.py:48
  106.5 15.0 %collective-permute-start.27 = (bf16[256,512]{1,0:T(8,128)(2,1)S(1)}, bf16[256,512]{1,0:T(8,128)(2,1)S(1)}, u32[]{:S(2)}, u32[]{:S(2)}) collective-permute-start(bf16[256,512]{1,0:T(8,128)(2,1)S(1)} %collective-permute-done.17.refs_11_), channel_id=1, source_target_pairs={{0,16},{16,0},{1,17},{17,1},{2,18},{18,2},{3,19},{19,3},{4,20},{20... | collective-permute-start | bytes 786440 | tf_op jit(solution)/shard_map/ppermute | solution.py:48
  113.3 11.0 %collective-permute-start.25 = (bf16[64,2048]{1,0:T(8,128)(2,1)S(1)}, bf16[64,2048]{1,0:T(8,128)(2,1)S(1)}, u32[]{:S(2)}, u32[]{:S(2)}) collective-permute-start(bf16[64,2048]{1,0:T(8,128)(2,1)S(1)} %get-tuple-element.76.refs_0_), channel_id=1, source_target_pairs={{0,2},{2,0},{1,3},{3,1},{4,6},{6,4},{5,7},{7,5},{8,10},{10,8},{9,1... | collective-permute-start | bytes 786440 | tf_op jit(solution)/shard_map/ppermute | solution.py:48
  118.9 10.5 %collective-permute-start.31 = (bf16[64,2048]{1,0:T(8,128)(2,1)S(1)}, bf16[64,2048]{1,0:T(8,128)(2,1)S(1)}, u32[]{:S(2)}, u32[]{:S(2)}) collective-permute-start(bf16[64,2048]{1,0:T(8,128)(2,1)S(1)} %get-tuple-element.80.refs_4_), channel_id=1, source_target_pairs={{0,2},{2,0},{1,3},{3,1},{4,6},{6,4},{5,7},{7,5},{8,10},{10,8},{9,1... | collective-permute-start | bytes 786440 | tf_op jit(solution)/shard_map/ppermute | solution.py:48
  121.1 8.4 %collective-permute-start.32 = (bf16[256,512]{1,0:T(8,128)(2,1)S(1)}, bf16[256,512]{1,0:T(8,128)(2,1)S(1)}, u32[]{:S(2)}, u32[]{:S(2)}) collective-permute-start(bf16[256,512]{1,0:T(8,128)(2,1)S(1)} %collective-permute-done.28.refs_13_), channel_id=1, source_target_pairs={{0,16},{16,0},{1,17},{17,1},{2,18},{18,2},{3,19},{19,3},{4,20},{20... | collective-permute-start | bytes 786440 | tf_op jit(solution)/shard_map/ppermute | solution.py:48
  121.4 8.1 %collective-permute-start.29 = (bf16[64,2048]{1,0:T(8,128)(2,1)S(1)}, bf16[64,2048]{1,0:T(8,128)(2,1)S(1)}, u32[]{:S(2)}, u32[]{:S(2)}) collective-permute-start(bf16[64,2048]{1,0:T(8,128)(2,1)S(1)} %get-tuple-element.76.refs_0_), channel_id=1, source_target_pairs={{0,1},{1,0},{2,3},{3,2},{4,5},{5,4},{6,7},{7,6},{8,9},{9,8},{10,11... | collective-permute-start | bytes 786440 | tf_op jit(solution)/shard_map/ppermute | solution.py:48
  121.5 8.0 %collective-permute-start.33 = (bf16[64,2048]{1,0:T(8,128)(2,1)S(1)}, bf16[64,2048]{1,0:T(8,128)(2,1)S(1)}, u32[]{:S(2)}, u32[]{:S(2)}) collective-permute-start(bf16[64,2048]{1,0:T(8,128)(2,1)S(1)} %get-tuple-element.80.refs_4_), channel_id=1, source_target_pairs={{0,1},{1,0},{2,3},{3,2},{4,5},{5,4},{6,7},{7,6},{8,9},{9,8},{10,11... | collective-permute-start | bytes 786440 | tf_op jit(solution)/shard_map/ppermute | solution.py:48
  124.3 5.2 %collective-permute-start.30 = (bf16[64,2048]{1,0:T(8,128)(2,1)S(1)}, bf16[64,2048]{1,0:T(8,128)(2,1)S(1)}, u32[]{:S(2)}, u32[]{:S(2)}) collective-permute-start(bf16[64,2048]{1,0:T(8,128)(2,1)S(1)} %collective-permute-done.25.refs_1_), channel_id=1, source_target_pairs={{0,1},{1,0},{2,3},{3,2},{4,5},{5,4},{6,7},{7,6},{8,9},{9,8},{10,11... | collective-permute-start | bytes 786440 | tf_op jit(solution)/shard_map/ppermute | solution.py:48
  129.4 1.5 collective-permute-start.34
  129.5 3.9 %copy-start = (bf16[2048,512]{1,0:T(8,128)(2,1)S(1)}, bf16[2048,512]{1,0:T(8,128)(2,1)}, u32[]{:S(2)}) copy-start(bf16[2048,512]{1,0:T(8,128)(2,1)} %query_ref.7) | copy-start | bytes 6291460
  129.5 3.9 %copy-start.6 = (f32[2048]{0:T(1024)S(1)}, f32[2048]{0:T(1024)}, u32[]{:S(2)}) copy-start(f32[2048]{0:T(1024)} %param.29) | copy-start | bytes 24580
  129.5 3.9 %copy-start.7 = (s32[3,16]{1,0:T(4,128)S(1)}, s32[3,16]{1,0:T(4,128)}, u32[]{:S(2)}) copy-start(s32[3,16]{1,0:T(4,128)} %parent_ref.7) | copy-start | bytes 580
  135.3 1.9 %collective-permute-start.35 = (bf16[16,2048]{1,0:T(8,128)(2,1)S(1)}, bf16[16,2048]{1,0:T(8,128)(2,1)S(1)}, u32[]{:S(2)}, u32[]{:S(2)}) collective-permute-start(bf16[16,2048]{1,0:T(8,128)(2,1)S(1)} %get-tuple-element.85.refs_1_), channel_id=1, source_target_pairs={{0,1},{1,0},{2,3},{3,2},{4,5},{5,4},{6,7},{7,6},{8,9},{9,8},{10,11... | collective-permute-start | bytes 196616 | tf_op jit(solution)/shard_map/ppermute | solution.py:676
  135.4 4.4 %collective-permute-start.36 = (bf16[16,2048]{1,0:T(8,128)(2,1)S(1)}, bf16[16,2048]{1,0:T(8,128)(2,1)S(1)}, u32[]{:S(2)}, u32[]{:S(2)}) collective-permute-start(bf16[16,2048]{1,0:T(8,128)(2,1)S(1)} %get-tuple-element.85.refs_1_), channel_id=1, source_target_pairs={{0,2},{1,3},{2,0},{3,1},{4,6},{5,7},{6,4},{7,5},{8,10},{9,11},{10,... | collective-permute-start | bytes 196616 | tf_op jit(solution)/shard_map/ppermute | solution.py:676
  137.2 4.1 %collective-permute-start.37 = (bf16[16,2048]{1,0:T(8,128)(2,1)S(1)}, bf16[16,2048]{1,0:T(8,128)(2,1)S(1)}, u32[]{:S(2)}, u32[]{:S(2)}) collective-permute-start(bf16[16,2048]{1,0:T(8,128)(2,1)S(1)} %get-tuple-element.85.refs_1_), channel_id=1, source_target_pairs={{0,3},{1,2},{2,1},{3,0},{4,7},{5,6},{6,5},{7,4},{8,11},{9,10},{10,... | collective-permute-start | bytes 196616 | tf_op jit(solution)/shard_map/ppermute | solution.py:676
  143.4 1.9 %collective-permute-start.38 = (bf16[16,2048]{1,0:T(8,128)(2,1)S(1)}, bf16[16,2048]{1,0:T(8,128)(2,1)S(1)}, u32[]{:S(2)}, u32[]{:S(2)}) collective-permute-start(bf16[16,2048]{1,0:T(8,128)(2,1)S(1)} %get-tuple-element.87.refs_1_), channel_id=1, source_target_pairs={{0,1},{1,0},{2,3},{3,2},{4,5},{5,4},{6,7},{7,6},{8,9},{9,8},{10,11... | collective-permute-start | bytes 196616 | tf_op jit(solution)/shard_map/ppermute | solution.py:676
  143.5 4.5 %collective-permute-start.39 = (bf16[16,2048]{1,0:T(8,128)(2,1)S(1)}, bf16[16,2048]{1,0:T(8,128)(2,1)S(1)}, u32[]{:S(2)}, u32[]{:S(2)}) collective-permute-start(bf16[16,2048]{1,0:T(8,128)(2,1)S(1)} %get-tuple-element.87.refs_1_), channel_id=1, source_target_pairs={{0,2},{1,3},{2,0},{3,1},{4,6},{5,7},{6,4},{7,5},{8,10},{9,11},{10,... | collective-permute-start | bytes 196616 | tf_op jit(solution)/shard_map/ppermute | solution.py:676
  144.8 4.3 %collective-permute-start.40 = (bf16[16,2048]{1,0:T(8,128)(2,1)S(1)}, bf16[16,2048]{1,0:T(8,128)(2,1)S(1)}, u32[]{:S(2)}, u32[]{:S(2)}) collective-permute-start(bf16[16,2048]{1,0:T(8,128)(2,1)S(1)} %get-tuple-element.87.refs_1_), channel_id=1, source_target_pairs={{0,3},{1,2},{2,1},{3,0},{4,7},{5,6},{6,5},{7,4},{8,11},{9,10},{10,... | collective-permute-start | bytes 196616 | tf_op jit(solution)/shard_map/ppermute | solution.py:676
  151.3 1.9 %collective-permute-start.41 = (bf16[16,2048]{1,0:T(8,128)(2,1)S(1)}, bf16[16,2048]{1,0:T(8,128)(2,1)S(1)}, u32[]{:S(2)}, u32[]{:S(2)}) collective-permute-start(bf16[16,2048]{1,0:T(8,128)(2,1)S(1)} %get-tuple-element.89.refs_1_), channel_id=1, source_target_pairs={{0,1},{1,0},{2,3},{3,2},{4,5},{5,4},{6,7},{7,6},{8,9},{9,8},{10,11... | collective-permute-start | bytes 196616 | tf_op jit(solution)/shard_map/ppermute | solution.py:676
  151.4 4.8 %collective-permute-start.42 = (bf16[16,2048]{1,0:T(8,128)(2,1)S(1)}, bf16[16,2048]{1,0:T(8,128)(2,1)S(1)}, u32[]{:S(2)}, u32[]{:S(2)}) collective-permute-start(bf16[16,2048]{1,0:T(8,128)(2,1)S(1)} %get-tuple-element.89.refs_1_), channel_id=1, source_target_pairs={{0,2},{1,3},{2,0},{3,1},{4,6},{5,7},{6,4},{7,5},{8,10},{9,11},{10,... | collective-permute-start | bytes 196616 | tf_op jit(solution)/shard_map/ppermute | solution.py:676
  152.4 4.4 %collective-permute-start.43 = (bf16[16,2048]{1,0:T(8,128)(2,1)S(1)}, bf16[16,2048]{1,0:T(8,128)(2,1)S(1)}, u32[]{:S(2)}, u32[]{:S(2)}) collective-permute-start(bf16[16,2048]{1,0:T(8,128)(2,1)S(1)} %get-tuple-element.89.refs_1_), channel_id=1, source_target_pairs={{0,3},{1,2},{2,1},{3,0},{4,7},{5,6},{6,5},{7,4},{8,11},{9,10},{10,... | collective-permute-start | bytes 196616 | tf_op jit(solution)/shard_map/ppermute | solution.py:676
  158.9 3.2 %collective-permute-start.46 = (bf16[16,512]{1,0:T(8,128)(2,1)S(1)}, bf16[16,512]{1,0:T(8,128)(2,1)S(1)}, u32[]{:S(2)}, u32[]{:S(2)}) collective-permute-start(bf16[16,512]{1,0:T(8,128)(2,1)S(1)} %get-tuple-element.93), channel_id=1, source_target_pairs={{0,3},{1,2},{2,1},{3,0},{4,7},{5,6},{6,5},{7,4},{8,11},{9,10},{10,... | collective-permute-start | bytes 49160 | tf_op jit(solution)/shard_map/ppermute | solution.py:676
  159.7 3.8 %collective-permute-start.45 = (bf16[16,512]{1,0:T(8,128)(2,1)S(1)}, bf16[16,512]{1,0:T(8,128)(2,1)S(1)}, u32[]{:S(2)}, u32[]{:S(2)}) collective-permute-start(bf16[16,512]{1,0:T(8,128)(2,1)S(1)} %get-tuple-element.92), channel_id=1, source_target_pairs={{0,2},{1,3},{2,0},{3,1},{4,6},{5,7},{6,4},{7,5},{8,10},{9,11},{10,... | collective-permute-start | bytes 49160 | tf_op jit(solution)/shard_map/ppermute | solution.py:676
  160.8 2.6 %collective-permute-start.44 = (bf16[16,512]{1,0:T(8,128)(2,1)S(1)}, bf16[16,512]{1,0:T(8,128)(2,1)S(1)}, u32[]{:S(2)}, u32[]{:S(2)}) collective-permute-start(bf16[16,512]{1,0:T(8,128)(2,1)S(1)} %get-tuple-element.91), channel_id=1, source_target_pairs={{0,1},{1,0},{2,3},{3,2},{4,5},{5,4},{6,7},{7,6},{8,9},{9,8},{10,11... | collective-permute-start | bytes 49160 | tf_op jit(solution)/shard_map/ppermute | solution.py:676

commit v5 on v4

--- a/solution.py
+++ b/solution.py
@@ -87,16 +87,18 @@
 
 
 class Rows:
-    def __init__(self, value, *waits):
+    def __init__(self, columns):
+        columns = columns if isinstance(columns, list) else [columns]
+        value = jnp.concatenate(columns, axis=1)
         self.size = lax.axis_size("seq")
         self.rows = value.shape[0]
         self.shared = lax.axis_size("groups") == 2 and self.rows % 32 == 0
         self.pieces = [(value, [functools.partial(lambda r, at: at[0] * r, self.rows)])]
         half = self.rows // 2
         if self.shared:
-            value = lax.dynamic_slice_in_dim(value, lax.axis_index("groups") * half, half, 0)
-        if waits:
-            value = after(value, *waits)
+            first = lax.axis_index("groups") * half
+            columns = [lax.dynamic_slice_in_dim(column, first, half, 0) for column in columns]
+            value = jnp.concatenate(columns, axis=1)
         self.last = {1: value, -1: value}
         self.hops = {1: 0, -1: 0}
         self.fresh = []
@@ -338,55 +340,58 @@
     )
 
 
-def project_kernel(firsts, orders, at_ref, attended_ref, *refs):
+def project_kernel(firsts, orders, parts, at_ref, attended_ref, *refs):
     count = len(firsts)
     pieces, outs, (whole, sems) = refs[:count], refs[count:-2], refs[-2:]
     copies = load_pieces(pieces, firsts, at_ref, 0, whole, slice(None), sems)
-    share = outs[0].shape[0] // len(orders[0])
+    part = outs[0].shape[0] // len(orders[0])
     for copy in copies:
         copy.wait()
-    for index, out_ref in enumerate(outs):
-        parts = []
-        for where in orders[index]:
-            first = pl.multiple_of(where(at_ref) * share, share)
-            parts.append(attended_ref[pl.ds(first, share), :])
-        rows = jnp.concatenate(parts, axis=0)
-        out_ref[...] = lax.dot_general(
-            rows, whole[...], (((1,), (1,)), ((), ())), preferred_element_type=jnp.float32
+    for index, order in enumerate(orders):
+        rows = []
+        for step in range(parts):
+            for where in order:
+                first = pl.multiple_of((where(at_ref) * parts + step) * part, part)
+                rows.append(attended_ref[pl.ds(first, part), :])
+        terms = lax.dot_general(
+            jnp.concatenate(rows, axis=0),
+            whole[...],
+            (((1,), (1,)), ((), ())),
+            preferred_element_type=jnp.float32,
         ).astype(jnp.bfloat16)
-
-
-def project_out(at, attended, pieces, orders):
-    length, cols = attended.shape
-    groups = lax.axis_size("tp")
-    share = length // (groups * len(orders))
-    width = sum(piece.shape[0] for piece, _ in pieces)
-    shape = jax.ShapeDtypeStruct((groups * share, width), jnp.bfloat16)
-    return pl.pallas_call(
-        functools.partial(project_kernel, [first for _, first in pieces], orders),
-        out_shape=tuple([shape] * len(orders)),
+        size = part * len(order)
+        for step in range(parts):
+            outs[index * parts + step][...] = terms[step * size : (step + 1) * size, :]
+
+
+def project_out(at, attended, pieces, orders, part, parts):
+    cols = attended.shape[1]
+    width = pieces[0][0].shape[0] * lax.axis_size("seq")
+    if len(pieces) == 1:
+        width = pieces[0][0].shape[0]
+    shape = jax.ShapeDtypeStruct((len(orders[0]) * part, width), jnp.bfloat16)
+    outs = pl.pallas_call(
+        functools.partial(project_kernel, [places for _, places in pieces], orders, parts),
+        out_shape=tuple([shape] * len(orders) * parts),
         in_specs=[SM, VM] + [HB] * len(pieces),
-        out_specs=tuple([VM] * len(orders)),
+        out_specs=tuple([VM] * len(orders) * parts),
         scratch_shapes=[
             pltpu.VMEM((width, cols), jnp.bfloat16),
             pltpu.SemaphoreType.DMA((block_count(pieces),)),
         ],
         compiler_params=params(),
-        cost_estimate=cost(5),
+        cost_estimate=cost(2),
         name="project_out",
-    )(
-        at,
-        attended,
-        *[piece for piece, _ in pieces],
-    )
+    )(at, attended, *[piece for piece, _ in pieces])
+    return [outs[index * parts : (index + 1) * parts] for index in range(len(orders))]
 
 
 def merge_kernel(first, gain_ref, source_ref, *refs):
     near, (far, encoded_ref, crossed_ref) = refs[:-3], refs[-3:]
-    rows = slice(first, first + encoded_ref.shape[0])
-    total = source_ref[rows, :].astype(jnp.float32)
+    rows = encoded_ref.shape[0]
+    total = source_ref[first : first + rows, :].astype(jnp.float32)
     for term in near:
-        total = total + term[rows, :].astype(jnp.float32)
+        total = total + term[:rows, :].astype(jnp.float32)
     for term in range(far.shape[0]):
         total = total + far[term].astype(jnp.float32)
     encoded_ref[...] = total.astype(jnp.bfloat16)
@@ -554,7 +559,7 @@
     group, groups = my_tp * kv + my_kv, tp * kv
 
     at = position()
-    joined = jnp.concatenate([query_weight, keyval_weight[0], keyval_weight[1]], axis=1)
+    joined = [query_weight, keyval_weight[0], keyval_weight[1]]
     crossing = jnp.concatenate([cross_weight[0], cross_weight[1]], axis=1)
     ringed = lax.axis_size("seq") <= RING_LIMIT
     blocks, firsts = collect_events(events)
@@ -590,11 +595,13 @@
         out.start(*stage)
         normed, *_ = joined.held(normed, *out.last.values())
         joined_pieces = joined.pieces
-        out.swap(normed)
+        out.swap(*stage)
         out.end()
         cross.start(normed)
     else:
-        joined_pieces, out_pieces, cross_pieces = map(whole_rows, (joined, out_weight, crossing))
+        joined_pieces, out_pieces, cross_pieces = map(
+            whole_rows, (jnp.concatenate(joined, axis=1), out_weight, crossing)
+        )
         normed, source = norm_events(at, gather_heads(blocks[0]), firsts, encoder_gain)
         codes = look_up([])
         turned = decoder_out.T
@@ -612,29 +619,33 @@
         return partner(at[2], d, tp) * kv + partner(at[3], e, kv)
 
     orders = [[functools.partial(place, d, e) for d in range(tp)] for e in range(kv)]
-    kept, *sent = project_out(at, attended, out_pieces, orders)
     share = normed.shape[0] // groups
-    arrived = [exchange(terms, "kv", e + 1) for e, terms in enumerate(sent)]
+    parts = 2 if share % 32 == 0 else 1
+    part = share // parts
+    kept, *sent = project_out(at, attended, out_pieces, orders, part, parts)
+    arrived = [
+        [exchange(terms[step], "kv", e + 1) for e, terms in enumerate(sent)] for step in range(parts)
+    ]
     late = []
     if ringed:
         cross.swap(attended)
-        cross.end(attended)
+        cross.end(attended, cross.last[-1])
         late = [piece for piece, _ in cross.pieces[1:]] + list(cross.last.values())
 
-    parts = 2 if share % 32 == 0 else 1
-    part = share // parts
-
-    def summed(d, first):
-        rows = slice(d * share + first, d * share + first + part)
-        return sum([a[rows].astype(jnp.float32) for a in arrived], kept[rows].astype(jnp.float32))
-
-    far = [
-        [exchange(summed(d, first).astype(jnp.bfloat16), "tp", d) for d in range(1, tp)]
-        for first in range(0, share, part)
-    ]
+    def summed(d, step):
+        rows = slice(d * part, (d + 1) * part)
+        near = [kept[step], *arrived[step]]
+        return sum(terms[rows].astype(jnp.float32) for terms in near).astype(jnp.bfloat16)
+
     merged = [
-        merge_terms(index * part, source, [kept, *arrived], jnp.stack(terms), cross_gain)
-        for index, terms in enumerate(far)
+        merge_terms(
+            step * part,
+            source,
+            [kept[step], *arrived[step]],
+            jnp.stack([exchange(summed(d, step), "tp", d) for d in range(1, tp)]),
+            cross_gain,
+        )
+        for step in range(parts)
     ]
     encoded = jnp.concatenate([encoded for encoded, _ in merged], axis=0)
     if ringed:
@@ -671,10 +682,10 @@
             at, level, block_counts, beam_parents, places, decoder_gain, decoder_query, turned,
             keys_values, codes[level], inputs, last,
         )
-        if not last:
-            sent = sent * len(moves)
-        arrived = [lax.ppermute(v, ("tp", "kv"), move) for v, move in zip(sent, moves)]
-        inputs = [kept] + sent[:1] + arrived
+        if last:
+            arrived = [lax.ppermute(v, ("tp", "kv"), move) for v, move in zip(sent, moves)]
+        else:
+            inputs = [kept] + [terms for terms, _ in gather_heads(sent[0])]
     beam_out = sum([a.astype(jnp.float32) for a in arrived], kept).astype(jnp.bfloat16)
     return (encoded[None], beam_out)
 

time: 164 us -> 162 us (0.988)
  starting transfers between devices: 43 us -> 38 us
  waiting for transfers between devices: 80.9 us -> 83.9 us
    ppermute x23 -> x33, waiting for transfers between devices: 38.2 us -> 52 us  [exchange(): lax.ppermute(value, axis, [(i, partner(i, step, size)) for i in range(siz...]
    ppermute x12 -> x3, waiting for transfers between devices: 13.5 us -> 1.32 us  [shards(): lax.ppermute(v, ('tp', 'kv'), move)]
    ppermute x12 -> x3, starting transfers between devices: 7.59 us -> 1.93 us  [shards(): lax.ppermute(v, ('tp', 'kv'), move)]
    ppermute x12, starting transfers between devices: 15.3 us -> 17.1 us  [shift(): lax.ppermute(value, axis, [(i, (i + step) % size) for i in range(size)])]
    ppermute x23 -> x33, starting transfers between devices: 20.2 us -> 19 us  [exchange(): lax.ppermute(value, axis, [(i, partner(i, step, size)) for i in range(siz...]
  transfers between devices with their start and end apart: 47 -> 48, of which waited for: 25 -> 26; matrix products, arithmetic and copies ran while one was open for 6% -> 6% of each run, Pallas kernels for 7% -> 7%
where the time goes in v5:
time: 162 us
  waiting for transfers between devices  83.9 us (52%)
  starting transfers between devices  38 us (23%)
  Pallas kernels  24.1 us (15%)
  local copies, waits for them, and re-layouts  6.84 us (4%)
  other arithmetic  3.93 us (2%)
  matrix products  3.09 us (2%)
  between operations  1.76 us (1%)
    ppermute x33, waiting for transfers between devices, exchange(): lax.ppermute(value, axis, [(i, partner(i, step, size)) for i in range(siz...  52 us
    ppermute x12, waiting for transfers between devices, shift(): lax.ppermute(value, axis, [(i, (i + step) % size) for i in range(size)])  30.6 us
    ppermute x33, starting transfers between devices, exchange(): lax.ppermute(value, axis, [(i, partner(i, step, size)) for i in range(siz...  19 us
    ppermute x12, starting transfers between devices, shift(): lax.ppermute(value, axis, [(i, (i + step) % size) for i in range(size)])  17.1 us
    pallas_call x1, Pallas kernels, encoder_attention(): pl.pallas_call(functools.partial(encoder_kernel, [places for _, places in...  8.64 us
    pallas_call x4, Pallas kernels, beam_step(): pl.pallas_call(functools.partial(beam_kernel, level, max(len(inputs) - 1,...  8.12 us
  transfers between devices with their start and end apart: 48, of which 26 were waited for; matrix products, arithmetic and copies ran while one was open for 6% of the time, Pallas kernels for 7%

profile of v5, /device:TPU:0, one launch (start us, length us, event | category | flops | bytes accessed | tf_op | source)
XLA Modules:
  0.0 161.6 jit_solution(3101906763805936810)
XLA Ops:
  0.7 1.9 %slice_bitcast_fusion.3 = (bf16[512,256]{1,0:T(8,128)(2,1)}, bf16[512,256]{1,0:T(8,128)(2,1)}, bf16[1,512,256]{2,1,0:T(8,128)(2,1)S(1)}, bf16[1,512,256]{2,1,0:T(8,128)(2,1)S(1)}) fusion(bf16[2,512,256]{2,1,0:T(8,128)(2,1)} %param.21), kind=kLoop, calls=%fused_computation.26 | loop fusion | bytes 1572864 | tf_op jit(solution)/shard_map/squeeze | solution.py:562
  2.6 1.0 constant_dynamic-slice_fusion.1
  3.7 3.1 %collective-permute-start.1 = (bf16[256,1024]{1,0:T(8,128)(2,1)S(1)}, bf16[256,1024]{1,0:T(8,128)(2,1)}, u32[]{:S(2)}, u32[]{:S(2)}) collective-permute-start(bf16[256,1024]{1,0:T(8,128)(2,1)S(1)} %pad_maximum_fusion.2), channel_id=1, source_target_pairs={{0,4},{4,8},{8,12},{12,0},{1,5},{5,9},{9,13},{13,1},{2,6},{6,10},{... | collective-permute-start | bytes 1572872 | tf_op jit(solution)/shard_map/ppermute | solution.py:53
  6.8 1.6 %collective-permute-start = (bf16[128,512]{1,0:T(8,128)(2,1)S(1)}, bf16[128,512]{1,0:T(8,128)(2,1)S(1)}, u32[]{:S(2)}, u32[]{:S(2)}) collective-permute-start(bf16[128,512]{1,0:T(8,128)(2,1)S(1)} %get-tuple-element.113), channel_id=1, source_target_pairs={{0,4},{4,8},{8,12},{12,0},{1,5},{5,9},{9,13},{13,1},{2,6},{6,10},{... | collective-permute-start | bytes 393224 | tf_op jit(solution)/shard_map/ppermute | solution.py:53
  8.4 2.2 %collective-permute-start.3 = (bf16[128,512]{1,0:T(8,128)(2,1)S(1)}, bf16[128,512]{1,0:T(8,128)(2,1)S(1)}, u32[]{:S(2)}, u32[]{:S(2)}) collective-permute-start(bf16[128,512]{1,0:T(8,128)(2,1)S(1)} %get-tuple-element.114), channel_id=1, source_target_pairs={{0,12},{4,0},{8,4},{12,8},{1,13},{5,1},{9,5},{13,9},{2,14},{6,2},{... | collective-permute-start | bytes 393224 | tf_op jit(solution)/shard_map/ppermute | solution.py:53
  10.7 0.8 collective-permute-start.2
  11.5 12.8 %collective-permute-done = bf16[128,512]{1,0:T(8,128)(2,1)S(1)} collective-permute-done((bf16[128,512]{1,0:T(8,128)(2,1)S(1)}, bf16[128,512]{1,0:T(8,128)(2,1)S(1)}, u32[]{:S(2)}, u32[]{:S(2)}) %collective-permute-start) | collective-permute-done | bytes 131104 | tf_op jit(solution)/shard_map/ppermute | solution.py:53
  24.4 1.8 %collective-permute-start.7 = (bf16[256,1024]{1,0:T(8,128)(2,1)}, bf16[256,1024]{1,0:T(8,128)(2,1)S(1)}, u32[]{:S(2)}, u32[]{:S(2)}) collective-permute-start(bf16[256,1024]{1,0:T(8,128)(2,1)} %collective-permute-done.1.refs_1_), channel_id=1, source_target_pairs={{0,16},{16,0},{1,17},{17,1},{2,18},{18,2},{3,19},{19,3},{4,20},{20... | collective-permute-start | bytes 1572872 | tf_op jit(solution)/shard_map/ppermute | solution.py:48
  26.3 5.6 %collective-permute-done.2 = bf16[128,512]{1,0:T(8,128)(2,1)S(1)} collective-permute-done((bf16[128,512]{1,0:T(8,128)(2,1)S(1)}, bf16[128,512]{1,0:T(8,128)(2,1)S(1)}, u32[]{:S(2)}, u32[]{:S(2)}) %collective-permute-start.2) | collective-permute-done | bytes 131104 | tf_op jit(solution)/shard_map/ppermute | solution.py:53
  32.0 1.6 collective-permute-start.4
  33.5 1.6 %collective-permute-start.8 = (bf16[256,1024]{1,0:T(8,128)(2,1)S(1)}, bf16[256,1024]{1,0:T(8,128)(2,1)}, u32[]{:S(2)}, u32[]{:S(2)}) collective-permute-start(bf16[256,1024]{1,0:T(8,128)(2,1)S(1)} %pad_maximum_fusion.2), channel_id=1, source_target_pairs={{0,12},{4,0},{8,4},{12,8},{1,13},{5,1},{9,5},{13,9},{2,14},{6,2},{... | collective-permute-start | bytes 1572872 | tf_op jit(solution)/shard_map/ppermute | solution.py:53
  35.3 3.1 %convolution_convert_fusion = bf16[64,2048]{1,0:T(8,128)(2,1)S(1)} fusion(bf16[64,1024]{1,0:T(8,128)(2,1)S(1)} %compare_convert_fusion, bf16[1024,2048]{1,0:T(8,128)(2,1)} %param.26), kind=kOutput, calls=%fused_computation | convolution fusion | flops 268566528 | bytes 4587520 | tf_op jit(solution)/shard_map/dot_general | solution.py:572
  38.4 0.5 collective-permute-start.5
  38.9 6.9 %collective-permute-done.4.refs_1_ = bf16[512,512]{1,0:T(8,128)(2,1)S(1)} collective-permute-done((bf16[512,512]{1,0:T(8,128)(2,1)S(1)}, bf16[512,512]{1,0:T(8,128)(2,1)S(1)}, u32[]{:S(2)}, u32[]{:S(2)}) %collective-permute-start.4) | collective-permute-done | bytes 524320 | tf_op jit(solution)/shard_map/ppermute | solution.py:48
  45.9 1.3 collective-permute-done.8.refs_3_
  47.2 1.5 collective-permute-start.9
  48.7 0.8 add.88
  49.5 0.5 collective-permute-start.12
  50.1 0.7 slice_bitcast_fusion
  50.9 2.9 %copy.17 = bf16[2048,512]{0,1:T(8,128)(2,1)S(1)} copy(bf16[2048,512]{1,0:T(8,128)(2,1)} %param.25) | data formatting | bytes 4194304 | tf_op jit(solution)/shard_map/optimization_barrier | solution.py:57
  53.9 3.1 %collective-permute-done.12 = bf16[64,2048]{1,0:T(8,128)(2,1)} collective-permute-done((bf16[64,2048]{1,0:T(8,128)(2,1)}, bf16[64,2048]{1,0:T(8,128)(2,1)}, u32[]{:S(2)}, u32[]{:S(2)}) %collective-permute-start.12) | collective-permute-done | bytes 262176 | tf_op jit(solution)/shard_map/ppermute | solution.py:48
  57.0 1.1 add.89
  58.1 2.4 %norm_events.1 = (bf16[512,2048]{1,0:T(8,128)(2,1)S(1)}, bf16[128,2048]{1,0:T(8,128)(2,1)S(1)}) custom-call(s32[4]{0:T(128)S(1)} %pad_add_fusion.at_ref, f32[1,2048]{1,0:T(1,128)S(1)} %bitcast.48, bf16[512,512]{1,0:T(8,128)(2,1)S(1)} %pad_maximum_fusion.3.refs_0_, bf16[512,512]{1,0:T(8,128)(2,1)S(1)} %collective-permute-done.4.refs_1_, ...), custom_call_target="tpu_custom_call" | custom-call | bytes 12000000 | tf_op jit(solution)/shard_map/norm_events/pallas_call | solution.py:206
  60.6 3.0 %collective-permute-done.10.refs_5_ = bf16[256,1024]{1,0:T(8,128)(2,1)} collective-permute-done((bf16[256,1024]{1,0:T(8,128)(2,1)}, bf16[256,1024]{1,0:T(8,128)(2,1)}, u32[]{:S(2)}, u32[]{:S(2)}) %collective-permute-start.10) | collective-permute-done | bytes 524320 | tf_op jit(solution)/shard_map/ppermute | solution.py:53
  63.6 0.5 collective-permute-start.13
  64.3 3.8 %collective-permute-start.15 = (bf16[256,512]{1,0:T(8,128)(2,1)S(1)}, bf16[256,512]{1,0:T(8,128)(2,1)S(1)}, u32[]{:S(2)}, u32[]{:S(2)}) collective-permute-start(bf16[256,512]{1,0:T(8,128)(2,1)S(1)} %get-tuple-element.66), channel_id=1, source_target_pairs={{0,12},{4,0},{8,4},{12,8},{1,13},{5,1},{9,5},{13,9},{2,14},{6,2},{... | collective-permute-start | bytes 786440 | tf_op jit(solution)/shard_map/ppermute | solution.py:53
  68.1 7.3 %collective-permute-done.14.refs_1_ = bf16[256,512]{1,0:T(8,128)(2,1)S(1)} collective-permute-done((bf16[256,512]{1,0:T(8,128)(2,1)S(1)}, bf16[256,512]{1,0:T(8,128)(2,1)S(1)}, u32[]{:S(2)}, u32[]{:S(2)}) %collective-permute-start.14) | collective-permute-done | bytes 262176 | tf_op jit(solution)/shard_map/ppermute | solution.py:53
  76.2 1.6 collective-permute-start.18
  77.8 2.1 %collective-permute-start.19 = (bf16[256,512]{1,0:T(8,128)(2,1)S(1)}, bf16[256,512]{1,0:T(8,128)(2,1)S(1)}, u32[]{:S(2)}, u32[]{:S(2)}) collective-permute-start(bf16[256,512]{1,0:T(8,128)(2,1)S(1)} %collective-permute-done.15.refs_3_), channel_id=1, source_target_pairs={{0,16},{16,0},{1,17},{17,1},{2,18},{18,2},{3,19},{19,3},{4,20},{20... | collective-permute-start | bytes 786440 | tf_op jit(solution)/shard_map/ppermute | solution.py:48
  79.9 3.8 %collective-permute-start.17 = (bf16[256,512]{1,0:T(8,128)(2,1)S(1)}, bf16[256,512]{1,0:T(8,128)(2,1)S(1)}, u32[]{:S(2)}, u32[]{:S(2)}) collective-permute-start(bf16[256,512]{1,0:T(8,128)(2,1)S(1)} %get-tuple-element.75), channel_id=1, source_target_pairs={{0,12},{4,0},{8,4},{12,8},{1,13},{5,1},{9,5},{13,9},{2,14},{6,2},{... | collective-permute-start | bytes 786440 | tf_op jit(solution)/shard_map/ppermute | solution.py:53
  83.7 8.6 %encoder_attention.1.attended_ref = bf16[512,512]{1,0:T(8,128)(2,1)S(1)} custom-call(s32[4]{0:T(128)S(1)} %pad_add_fusion.at_ref, s32[1]{0:T(128)S(6)} %copy.18.live_ref, bf16[512,2048]{1,0:T(8,128)(2,1)S(1)} %get-tuple-element.67.rows_ref, bf16[2,512,256]{2,1,0:T(8,128)(2,1)S(1)} %bitcast.39, bf16[512,1024]{1,0:T(8,128)(2,1)S(1)} %pad_maximum_fusion.refs_0_, ...), custom_call_target="tpu_custom_call" | custom-call | bytes 33000000 | tf_op jit(solution)/shard_map/encoder_attention/pallas_call | solution.py:317
  92.8 6.0 %collective-permute-done.21.refs_6_ = bf16[256,512]{1,0:T(8,128)(2,1)S(1)} collective-permute-done((bf16[256,512]{1,0:T(8,128)(2,1)S(1)}, bf16[256,512]{1,0:T(8,128)(2,1)S(1)}, u32[]{:S(2)}, u32[]{:S(2)}) %collective-permute-start.21) | collective-permute-done | bytes 262176 | tf_op jit(solution)/shard_map/ppermute | solution.py:48
  98.8 2.1 %project_out.1 = (bf16[128,2048]{1,0:T(8,128)(2,1)S(1)}, bf16[128,2048]{1,0:T(8,128)(2,1)S(1)}, bf16[128,2048]{1,0:T(8,128)(2,1)S(1)}, bf16[128,2048]{1,0:T(8,128)(2,1)S(1)}) custom-call(s32[4]{0:T(128)S(1)} %pad_add_fusion.at_ref, bf16[512,512]{1,0:T(8,128)(2,1)S(1)} %encoder_attention.1.attended_ref, bf16[512,512]{1,0:T(8,128)(2,1)S(1)} %copy-done.1, ...), custom_call_target="tpu_custom_call" | custom-call | bytes 6000000 | tf_op jit(solution)/shard_map/project_out/pallas_call | solution.py:373
  101.0 0.5 collective-permute-start.24
  101.5 1.4 collective-permute-done.22.refs_1_
  103.0 0.6 collective-permute-start.23
  103.7 1.5 collective-permute-start.25
  105.7 1.5 collective-permute-start.28
  107.2 5.0 %collective-permute-done.23 = bf16[64,2048]{1,0:T(8,128)(2,1)S(1)} collective-permute-done((bf16[64,2048]{1,0:T(8,128)(2,1)S(1)}, bf16[64,2048]{1,0:T(8,128)(2,1)S(1)}, u32[]{:S(2)}, u32[]{:S(2)}) %collective-permute-start.23) | collective-permute-done | bytes 262176 | tf_op jit(solution)/shard_map/ppermute | solution.py:48
  112.4 0.6 collective-permute-start.26
  113.0 4.8 %collective-permute-done.25 = bf16[64,2048]{1,0:T(8,128)(2,1)S(1)} collective-permute-done((bf16[64,2048]{1,0:T(8,128)(2,1)S(1)}, bf16[64,2048]{1,0:T(8,128)(2,1)S(1)}, u32[]{:S(2)}, u32[]{:S(2)}) %collective-permute-start.25) | collective-permute-done | bytes 262176 | tf_op jit(solution)/shard_map/ppermute | solution.py:48
  118.1 0.6 collective-permute-start.32
  118.6 0.9 collective-permute-start.33
  120.1 3.3 %collective-permute-done.26.refs_1_ = bf16[64,2048]{1,0:T(8,128)(2,1)S(1)} collective-permute-done((bf16[64,2048]{1,0:T(8,128)(2,1)S(1)}, bf16[64,2048]{1,0:T(8,128)(2,1)S(1)}, u32[]{:S(2)}, u32[]{:S(2)}) %collective-permute-start.26) | collective-permute-done | bytes 262176 | tf_op jit(solution)/shard_map/ppermute | solution.py:48
  123.4 4.8 %collective-permute-done.32.refs_5_ = bf16[64,2048]{1,0:T(8,128)(2,1)S(1)} collective-permute-done((bf16[64,2048]{1,0:T(8,128)(2,1)S(1)}, bf16[64,2048]{1,0:T(8,128)(2,1)S(1)}, u32[]{:S(2)}, u32[]{:S(2)}) %collective-permute-start.32) | collective-permute-done | bytes 262176 | tf_op jit(solution)/shard_map/ppermute | solution.py:48
  128.3 1.4 collective-permute-done.35.refs_7_
  129.8 2.3 %cross_project.1.cross_ref = bf16[512,512]{1,0:T(8,128)(2,1)S(1)} custom-call(s32[4]{0:T(128)S(1)} %pad_add_fusion.at_ref, bf16[64,2048]{1,0:T(8,128)(2,1)S(1)} %get-tuple-element.87.refs_0_, bf16[64,2048]{1,0:T(8,128)(2,1)S(1)} %collective-permute-done.26.refs_1_, bf16[64,2048]{1,0:T(8,128)(2,1)S(1)} %collective-permute-done.30.refs_2_, ...), custom_call_target="tpu_custom_call" | custom-call | bytes 6000000 | tf_op jit(solution)/shard_map/cross_project/pallas_call | solution.py:433
  132.2 1.9 %beam_step_0.1 = (f32[16,2048]{1,0:T(8,128)S(1)}, bf16[16,2048]{1,0:T(8,128)(2,1)S(1)}) custom-call(s32[4]{0:T(128)S(1)} %pad_add_fusion.at_ref, s32[1]{0:T(128)S(6)} %copy.18.live_ref, s32[3,16]{1,0:T(4,128)S(1)} %copy-done.6, f32[1,2048]{1,0:T(1,128)S(1)} %bitcast.42, bf16[2048,512]{1,0:T(8,128)(2,1)S(1)} %copy-done, bf16[512,2048]{1,0:T(8,128)(2,1)S(1)} %bitcast.35, ...), custom_call_target="tpu_custom_call" | custom-call | bytes 12000000 | tf_op jit(solution)/shard_map/beam_step_0/pallas_call | solution.py:528
  134.1 0.5 collective-permute-start.36
  134.6 3.8 %collective-permute-done.36.refs_2_ = bf16[16,2048]{1,0:T(8,128)(2,1)S(1)} collective-permute-done((bf16[16,2048]{1,0:T(8,128)(2,1)S(1)}, bf16[16,2048]{1,0:T(8,128)(2,1)S(1)}, u32[]{:S(2)}, u32[]{:S(2)}) %collective-permute-start.36) | collective-permute-done | bytes 65568 | tf_op jit(solution)/shard_map/ppermute | solution.py:48
  138.4 1.2 collective-permute-done.38.refs_4_
  139.6 2.1 %beam_step_1.1 = (f32[16,2048]{1,0:T(8,128)S(1)}, bf16[16,2048]{1,0:T(8,128)(2,1)S(1)}) custom-call(s32[4]{0:T(128)S(1)} %pad_add_fusion.at_ref, s32[1]{0:T(128)S(6)} %copy.18.live_ref, s32[3,16]{1,0:T(4,128)S(1)} %copy-done.6, f32[1,2048]{1,0:T(1,128)S(1)} %bitcast.43, bf16[2048,512]{1,0:T(8,128)(2,1)S(1)} %copy-done, bf16[512,2048]{1,0:T(8,128)(2,1)S(1)} %bitcast.36, ...), custom_call_target="tpu_custom_call" | custom-call | bytes 12000000 | tf_op jit(solution)/shard_map/beam_step_1/pallas_call | solution.py:528
  141.7 0.5 collective-permute-start.39
  142.2 3.8 %collective-permute-done.39.refs_2_ = bf16[16,2048]{1,0:T(8,128)(2,1)S(1)} collective-permute-done((bf16[16,2048]{1,0:T(8,128)(2,1)S(1)}, bf16[16,2048]{1,0:T(8,128)(2,1)S(1)}, u32[]{:S(2)}, u32[]{:S(2)}) %collective-permute-start.39) | collective-permute-done | bytes 65568 | tf_op jit(solution)/shard_map/ppermute | solution.py:48
  146.0 1.2 collective-permute-done.41.refs_4_
  147.2 2.1 %beam_step_2.1 = (f32[16,2048]{1,0:T(8,128)S(1)}, bf16[16,2048]{1,0:T(8,128)(2,1)S(1)}) custom-call(s32[4]{0:T(128)S(1)} %pad_add_fusion.at_ref, s32[1]{0:T(128)S(6)} %copy.18.live_ref, s32[3,16]{1,0:T(4,128)S(1)} %copy-done.6, f32[1,2048]{1,0:T(1,128)S(1)} %bitcast.44, bf16[2048,512]{1,0:T(8,128)(2,1)S(1)} %copy-done, bf16[512,2048]{1,0:T(8,128)(2,1)S(1)} %bitcast.37, ...), custom_call_target="tpu_custom_call" | custom-call | bytes 12000000 | tf_op jit(solution)/shard_map/beam_step_2/pallas_call | solution.py:528
  149.3 0.5 collective-permute-start.42
  149.8 3.8 %collective-permute-done.42.refs_2_ = bf16[16,2048]{1,0:T(8,128)(2,1)S(1)} collective-permute-done((bf16[16,2048]{1,0:T(8,128)(2,1)S(1)}, bf16[16,2048]{1,0:T(8,128)(2,1)S(1)}, u32[]{:S(2)}, u32[]{:S(2)}) %collective-permute-start.42) | collective-permute-done | bytes 65568 | tf_op jit(solution)/shard_map/ppermute | solution.py:48
  153.6 1.2 collective-permute-done.44.refs_4_
  154.8 2.1 %beam_step_3.1 = (f32[16,512]{1,0:T(8,128)S(1)}, bf16[16,512]{1,0:T(8,128)(2,1)S(1)}, bf16[16,512]{1,0:T(8,128)(2,1)S(1)}, bf16[16,512]{1,0:T(8,128)(2,1)S(1)}) custom-call(s32[4]{0:T(128)S(1)} %pad_add_fusion.at_ref, s32[1]{0:T(128)S(6)} %copy.18.live_ref, s32[3,16]{1,0:T(4,128)S(1)} %copy-done.6, f32[1,2048]{1,0:T(1,128)S(1)} %bitcast.45, ...), custom_call_target="tpu_custom_call" | custom-call | bytes 12000000 | tf_op jit(solution)/shard_map/beam_step_3/pallas_call | solution.py:528
  157.2 1.5 collective-permute-start.46
  158.8 0.8 maximum_bitcast_fusion
  160.1 0.9 collective-permute-done.46
  161.0 0.6 add_convert_fusion.2
  (97 shorter events, 4.3 us)
Async XLA Ops:
  0.6 6.1 %copy-start.13 = (bf16[4,128,512]{2,1,0:T(8,128)(2,1)S(1)}, bf16[4,128,512]{2,1,0:T(8,128)(2,1)}, u32[]{:S(2)}) copy-start(bf16[4,128,512]{2,1,0:T(8,128)(2,1)} %param.15) | copy-start | bytes 1572868
  0.6 10.8 %copy-start.15 = (s32[4,16]{1,0:T(4,128)S(1)}, s32[4,16]{1,0:T(4,128)}, u32[]{:S(2)}) copy-start(s32[4,16]{1,0:T(4,128)} %param.18) | copy-start | bytes 772
  3.7 20.7 %collective-permute-start.1 = (bf16[256,1024]{1,0:T(8,128)(2,1)S(1)}, bf16[256,1024]{1,0:T(8,128)(2,1)}, u32[]{:S(2)}, u32[]{:S(2)}) collective-permute-start(bf16[256,1024]{1,0:T(8,128)(2,1)S(1)} %pad_maximum_fusion.2), channel_id=1, source_target_pairs={{0,4},{4,8},{8,12},{12,0},{1,5},{5,9},{9,13},{13,1},{2,6},{6,10},{... | collective-permute-start | bytes 1572872 | tf_op jit(solution)/shard_map/ppermute | solution.py:53
  6.8 17.6 %collective-permute-start = (bf16[128,512]{1,0:T(8,128)(2,1)S(1)}, bf16[128,512]{1,0:T(8,128)(2,1)S(1)}, u32[]{:S(2)}, u32[]{:S(2)}) collective-permute-start(bf16[128,512]{1,0:T(8,128)(2,1)S(1)} %get-tuple-element.113), channel_id=1, source_target_pairs={{0,4},{4,8},{8,12},{12,0},{1,5},{5,9},{9,13},{13,1},{2,6},{6,10},{... | collective-permute-start | bytes 393224 | tf_op jit(solution)/shard_map/ppermute | solution.py:53
  8.4 17.9 %collective-permute-start.3 = (bf16[128,512]{1,0:T(8,128)(2,1)S(1)}, bf16[128,512]{1,0:T(8,128)(2,1)S(1)}, u32[]{:S(2)}, u32[]{:S(2)}) collective-permute-start(bf16[128,512]{1,0:T(8,128)(2,1)S(1)} %get-tuple-element.114), channel_id=1, source_target_pairs={{0,12},{4,0},{8,4},{12,8},{1,13},{5,1},{9,5},{13,9},{2,14},{6,2},{... | collective-permute-start | bytes 393224 | tf_op jit(solution)/shard_map/ppermute | solution.py:53
  10.7 21.3 %collective-permute-start.2 = (bf16[128,512]{1,0:T(8,128)(2,1)S(1)}, bf16[128,512]{1,0:T(8,128)(2,1)S(1)}, u32[]{:S(2)}, u32[]{:S(2)}) collective-permute-start(bf16[128,512]{1,0:T(8,128)(2,1)S(1)} %get-tuple-element.115), channel_id=1, source_target_pairs={{0,8},{4,12},{8,0},{12,4},{1,9},{5,13},{9,1},{13,5},{2,10},{6,14},... | collective-permute-start | bytes 393224 | tf_op jit(solution)/shard_map/ppermute | solution.py:53
  24.4 21.5 %collective-permute-start.7 = (bf16[256,1024]{1,0:T(8,128)(2,1)}, bf16[256,1024]{1,0:T(8,128)(2,1)S(1)}, u32[]{:S(2)}, u32[]{:S(2)}) collective-permute-start(bf16[256,1024]{1,0:T(8,128)(2,1)} %collective-permute-done.1.refs_1_), channel_id=1, source_target_pairs={{0,16},{16,0},{1,17},{17,1},{2,18},{18,2},{3,19},{19,3},{4,20},{20... | collective-permute-start | bytes 1572872 | tf_op jit(solution)/shard_map/ppermute | solution.py:48
  32.0 13.9 %collective-permute-start.4 = (bf16[512,512]{1,0:T(8,128)(2,1)S(1)}, bf16[512,512]{1,0:T(8,128)(2,1)S(1)}, u32[]{:S(2)}, u32[]{:S(2)}) collective-permute-start(bf16[512,512]{1,0:T(8,128)(2,1)S(1)} %pad_maximum_fusion.3.refs_0_), channel_id=1, source_target_pairs={{0,2},{2,0},{1,3},{3,1},{4,6},{6,4},{5,7},{7,5},{8,10},{10,8},{9,1... | collective-permute-start | bytes 1572872 | tf_op jit(solution)/shard_map/ppermute | solution.py:48
  33.5 13.7 %collective-permute-start.8 = (bf16[256,1024]{1,0:T(8,128)(2,1)S(1)}, bf16[256,1024]{1,0:T(8,128)(2,1)}, u32[]{:S(2)}, u32[]{:S(2)}) collective-permute-start(bf16[256,1024]{1,0:T(8,128)(2,1)S(1)} %pad_maximum_fusion.2), channel_id=1, source_target_pairs={{0,12},{4,0},{8,4},{12,8},{1,13},{5,1},{9,5},{13,9},{2,14},{6,2},{... | collective-permute-start | bytes 1572872 | tf_op jit(solution)/shard_map/ppermute | solution.py:53
  35.2 14.9 %copy-start.14 = (bf16[2,512,256]{2,1,0:T(8,128)(2,1)S(1)}, bf16[2,512,256]{2,1,0:T(8,128)(2,1)}, u32[]{:S(2)}) copy-start(bf16[2,512,256]{2,1,0:T(8,128)(2,1)} %param.23) | copy-start | bytes 1572868
  38.4 10.4 %collective-permute-start.11 = (bf16[64,2048]{1,0:T(8,128)(2,1)S(1)}, bf16[64,2048]{1,0:T(8,128)(2,1)S(1)}, u32[]{:S(2)}, u32[]{:S(2)}) collective-permute-start(bf16[64,2048]{1,0:T(8,128)(2,1)S(1)} %convolution_convert_fusion), channel_id=1, source_target_pairs={{0,1},{1,0},{2,3},{3,2},{4,5},{5,4},{6,7},{7,6},{8,9},{9,8},{10,11... | collective-permute-start | bytes 786440 | tf_op jit(solution)/shard_map/ppermute | solution.py:48
  38.4 19.7 %collective-permute-start.5 = (bf16[512,512]{1,0:T(8,128)(2,1)S(1)}, bf16[512,512]{1,0:T(8,128)(2,1)}, u32[]{:S(2)}, u32[]{:S(2)}) collective-permute-start(bf16[512,512]{1,0:T(8,128)(2,1)S(1)} %pad_maximum_fusion.3.refs_0_), channel_id=1, source_target_pairs={{0,1},{1,0},{2,3},{3,2},{4,5},{5,4},{6,7},{7,6},{8,9},{9,8},{10,11... | collective-permute-start | bytes 1572872 | tf_op jit(solution)/shard_map/ppermute | solution.py:48
  45.9 12.2 %collective-permute-start.6 = (bf16[512,512]{1,0:T(8,128)(2,1)S(1)}, bf16[512,512]{1,0:T(8,128)(2,1)}, u32[]{:S(2)}, u32[]{:S(2)}) collective-permute-start(bf16[512,512]{1,0:T(8,128)(2,1)S(1)} %collective-permute-done.4.refs_1_), channel_id=1, source_target_pairs={{0,1},{1,0},{2,3},{3,2},{4,5},{5,4},{6,7},{7,6},{8,9},{9,8},{10,11... | collective-permute-start | bytes 1572872 | tf_op jit(solution)/shard_map/ppermute | solution.py:48
  45.9 4.2 %copy-start.3 = (bf16[256,1024]{1,0:T(8,128)(2,1)}, bf16[256,1024]{1,0:T(8,128)(2,1)S(1)}, u32[]{:S(2)}) copy-start(bf16[256,1024]{1,0:T(8,128)(2,1)S(1)} %collective-permute-done.7.refs_2_) | copy-start | bytes 1572868
  47.2 13.4 %collective-permute-start.9 = (bf16[256,1024]{1,0:T(8,128)(2,1)}, bf16[256,1024]{1,0:T(8,128)(2,1)}, u32[]{:S(2)}, u32[]{:S(2)}) collective-permute-start(bf16[256,1024]{1,0:T(8,128)(2,1)} %collective-permute-done.8.refs_3_), channel_id=1, source_target_pairs={{0,16},{16,0},{1,17},{17,1},{2,18},{18,2},{3,19},{19,3},{4,20},{20... | collective-permute-start | bytes 1572872 | tf_op jit(solution)/shard_map/ppermute | solution.py:48
  48.7 14.9 %collective-permute-start.10 = (bf16[256,1024]{1,0:T(8,128)(2,1)}, bf16[256,1024]{1,0:T(8,128)(2,1)}, u32[]{:S(2)}, u32[]{:S(2)}) collective-permute-start(bf16[256,1024]{1,0:T(8,128)(2,1)} %collective-permute-done.1.refs_1_), channel_id=1, source_target_pairs={{0,4},{4,8},{8,12},{12,0},{1,5},{5,9},{9,13},{13,1},{2,6},{6,10},{... | collective-permute-start | bytes 1572872 | tf_op jit(solution)/shard_map/ppermute | solution.py:53
  49.5 7.5 %collective-permute-start.12 = (bf16[64,2048]{1,0:T(8,128)(2,1)}, bf16[64,2048]{1,0:T(8,128)(2,1)}, u32[]{:S(2)}, u32[]{:S(2)}) collective-permute-start(bf16[64,2048]{1,0:T(8,128)(2,1)} %add.88), channel_id=1, source_target_pairs={{0,2},{2,0},{1,3},{3,1},{4,6},{6,4},{5,7},{7,5},{8,10},{10,8},{9,1... | collective-permute-start | bytes 786440 | tf_op jit(solution)/shard_map/ppermute | solution.py:48
  50.9 7.3 %copy-start.8 = (f32[2048]{0:T(1024)S(1)}, f32[2048]{0:T(1024)}, u32[]{:S(2)}) copy-start(f32[2048]{0:T(1024)} %param.27) | copy-start | bytes 24580
  53.8 10.3 %copy-start.1 = (bf16[512,512]{1,0:T(8,128)(2,1)S(1)}, bf16[512,512]{1,0:T(8,128)(2,1)}, u32[]{:S(2)}) copy-start(bf16[512,512]{1,0:T(8,128)(2,1)} %refs_0_.1) | copy-start | bytes 1572868
  53.8 10.3 %copy-start.9 = (bf16[512,256]{1,0:T(8,128)(2,1)S(1)}, bf16[512,256]{1,0:T(8,128)(2,1)}, u32[]{:S(2)}) copy-start(bf16[512,256]{1,0:T(8,128)(2,1)} %get-tuple-element.107) | copy-start | bytes 786436
  53.8 22.2 %copy-start.10 = (bf16[512,512]{1,0:T(8,128)(2,1)S(1)}, bf16[512,512]{1,0:T(8,128)(2,1)}, u32[]{:S(2)}) copy-start(bf16[512,512]{1,0:T(8,128)(2,1)} %param.20) | copy-start | bytes 1572868
  53.8 22.2 %copy-start.11 = (bf16[512,256]{1,0:T(8,128)(2,1)S(1)}, bf16[512,256]{1,0:T(8,128)(2,1)}, u32[]{:S(2)}) copy-start(bf16[512,256]{1,0:T(8,128)(2,1)} %get-tuple-element.108) | copy-start | bytes 786436
  53.9 22.2 %copy-start.12 = (bf16[512,256]{1,0:T(8,128)(2,1)S(1)}, bf16[512,256]{1,0:T(8,128)(2,1)}, u32[]{:S(2)}) copy-start(bf16[512,256]{1,0:T(8,128)(2,1)} %get-tuple-element.109) | copy-start | bytes 786436
  60.5 23.2 %copy-start.2 = (bf16[2,1,512,256]{3,2,1,0:T(8,128)(2,1)S(1)}, bf16[2,1,512,256]{3,2,1,0:T(8,128)(2,1)}, u32[]{:S(2)}) copy-start(bf16[2,1,512,256]{3,2,1,0:T(8,128)(2,1)} %param.16) | copy-start | bytes 1572868
  60.5 23.2 %copy-start.4 = (bf16[256,1024]{1,0:T(8,128)(2,1)S(1)}, bf16[256,1024]{1,0:T(8,128)(2,1)}, u32[]{:S(2)}) copy-start(bf16[256,1024]{1,0:T(8,128)(2,1)} %copy-done.3) | copy-start | bytes 1572868
  63.6 16.2 %collective-permute-start.13 = (bf16[256,1024]{1,0:T(8,128)(2,1)}, bf16[256,1024]{1,0:T(8,128)(2,1)S(1)}, u32[]{:S(2)}, u32[]{:S(2)}) collective-permute-start(bf16[256,1024]{1,0:T(8,128)(2,1)} %collective-permute-done.10.refs_5_), channel_id=1, source_target_pairs={{0,16},{16,0},{1,17},{17,1},{2,18},{18,2},{3,19},{19,3},{4,20},{20... | collective-permute-start | bytes 1572872 | tf_op jit(solution)/shard_map/ppermute | solution.py:48
  64.2 11.1 %collective-permute-start.14 = (bf16[256,512]{1,0:T(8,128)(2,1)S(1)}, bf16[256,512]{1,0:T(8,128)(2,1)S(1)}, u32[]{:S(2)}, u32[]{:S(2)}) collective-permute-start(bf16[256,512]{1,0:T(8,128)(2,1)S(1)} %get-tuple-element.66), channel_id=1, source_target_pairs={{0,4},{4,8},{8,12},{12,0},{1,5},{5,9},{9,13},{13,1},{2,6},{6,10},{... | collective-permute-start | bytes 786440 | tf_op jit(solution)/shard_map/ppermute | solution.py:53
  64.3 13.5 %collective-permute-start.15 = (bf16[256,512]{1,0:T(8,128)(2,1)S(1)}, bf16[256,512]{1,0:T(8,128)(2,1)S(1)}, u32[]{:S(2)}, u32[]{:S(2)}) collective-permute-start(bf16[256,512]{1,0:T(8,128)(2,1)S(1)} %get-tuple-element.66), channel_id=1, source_target_pairs={{0,12},{4,0},{8,4},{12,8},{1,13},{5,1},{9,5},{13,9},{2,14},{6,2},{... | collective-permute-start | bytes 786440 | tf_op jit(solution)/shard_map/ppermute | solution.py:53
  75.3 17.0 %collective-permute-start.20 = (bf16[256,512]{1,0:T(8,128)(2,1)S(1)}, bf16[256,512]{1,0:T(8,128)(2,1)S(1)}, u32[]{:S(2)}, u32[]{:S(2)}) collective-permute-start(bf16[256,512]{1,0:T(8,128)(2,1)S(1)} %collective-permute-done.14.refs_1_), channel_id=1, source_target_pairs={{0,4},{4,8},{8,12},{12,0},{1,5},{5,9},{9,13},{13,1},{2,6},{6,10},{... | collective-permute-start | bytes 786440 | tf_op jit(solution)/shard_map/ppermute | solution.py:53
  76.2 16.6 %collective-permute-start.18 = (bf16[256,512]{1,0:T(8,128)(2,1)S(1)}, bf16[256,512]{1,0:T(8,128)(2,1)S(1)}, u32[]{:S(2)}, u32[]{:S(2)}) collective-permute-start(bf16[256,512]{1,0:T(8,128)(2,1)S(1)} %collective-permute-done.14.refs_1_), channel_id=1, source_target_pairs={{0,16},{16,0},{1,17},{17,1},{2,18},{18,2},{3,19},{19,3},{4,20},{20... | collective-permute-start | bytes 786440 | tf_op jit(solution)/shard_map/ppermute | solution.py:48
  77.8 15.0 %collective-permute-start.19 = (bf16[256,512]{1,0:T(8,128)(2,1)S(1)}, bf16[256,512]{1,0:T(8,128)(2,1)S(1)}, u32[]{:S(2)}, u32[]{:S(2)}) collective-permute-start(bf16[256,512]{1,0:T(8,128)(2,1)S(1)} %collective-permute-done.15.refs_3_), channel_id=1, source_target_pairs={{0,16},{16,0},{1,17},{17,1},{2,18},{18,2},{3,19},{19,3},{4,20},{20... | collective-permute-start | bytes 786440 | tf_op jit(solution)/shard_map/ppermute | solution.py:48
  79.9 12.6 %collective-permute-start.16 = (bf16[256,512]{1,0:T(8,128)(2,1)S(1)}, bf16[256,512]{1,0:T(8,128)(2,1)S(1)}, u32[]{:S(2)}, u32[]{:S(2)}) collective-permute-start(bf16[256,512]{1,0:T(8,128)(2,1)S(1)} %get-tuple-element.75), channel_id=1, source_target_pairs={{0,4},{4,8},{8,12},{12,0},{1,5},{5,9},{9,13},{13,1},{2,6},{6,10},{... | collective-permute-start | bytes 786440 | tf_op jit(solution)/shard_map/ppermute | solution.py:53
  79.9 12.9 %collective-permute-start.17 = (bf16[256,512]{1,0:T(8,128)(2,1)S(1)}, bf16[256,512]{1,0:T(8,128)(2,1)S(1)}, u32[]{:S(2)}, u32[]{:S(2)}) collective-permute-start(bf16[256,512]{1,0:T(8,128)(2,1)S(1)} %get-tuple-element.75), channel_id=1, source_target_pairs={{0,12},{4,0},{8,4},{12,8},{1,13},{5,1},{9,5},{13,9},{2,14},{6,2},{... | collective-permute-start | bytes 786440 | tf_op jit(solution)/shard_map/ppermute | solution.py:53
  92.3 19.8 %copy-start.7 = (f32[2048]{0:T(1024)S(1)}, f32[2048]{0:T(1024)}, u32[]{:S(2)}) copy-start(f32[2048]{0:T(1024)} %param.28) | copy-start | bytes 24580
  92.4 6.4 %collective-permute-start.21 = (bf16[256,512]{1,0:T(8,128)(2,1)S(1)}, bf16[256,512]{1,0:T(8,128)(2,1)S(1)}, u32[]{:S(2)}, u32[]{:S(2)}) collective-permute-start(bf16[256,512]{1,0:T(8,128)(2,1)S(1)} %collective-permute-done.20.refs_5_), channel_id=1, source_target_pairs={{0,16},{16,0},{1,17},{17,1},{2,18},{18,2},{3,19},{19,3},{4,20},{20... | collective-permute-start | bytes 786440 | tf_op jit(solution)/shard_map/ppermute | solution.py:48
  100.9 2.0 %collective-permute-start.22 = (bf16[128,2048]{1,0:T(8,128)(2,1)S(1)}, bf16[128,2048]{1,0:T(8,128)(2,1)S(1)}, u32[]{:S(2)}, u32[]{:S(2)}) collective-permute-start(bf16[128,2048]{1,0:T(8,128)(2,1)S(1)} %get-tuple-element.81), channel_id=1, source_target_pairs={{0,1},{1,0},{2,3},{3,2},{4,5},{5,4},{6,7},{7,6},{8,9},{9,8},{10,11... | collective-permute-start | bytes 1572872 | tf_op jit(solution)/shard_map/ppermute | solution.py:48
  101.0 2.6 %collective-permute-start.24 = (bf16[128,2048]{1,0:T(8,128)(2,1)S(1)}, bf16[128,2048]{1,0:T(8,128)(2,1)S(1)}, u32[]{:S(2)}, u32[]{:S(2)}) collective-permute-start(bf16[128,2048]{1,0:T(8,128)(2,1)S(1)} %get-tuple-element.84), channel_id=1, source_target_pairs={{0,1},{1,0},{2,3},{3,2},{4,5},{5,4},{6,7},{7,6},{8,9},{9,8},{10,11... | collective-permute-start | bytes 1572872 | tf_op jit(solution)/shard_map/ppermute | solution.py:48
  103.0 9.2 %collective-permute-start.23 = (bf16[64,2048]{1,0:T(8,128)(2,1)S(1)}, bf16[64,2048]{1,0:T(8,128)(2,1)S(1)}, u32[]{:S(2)}, u32[]{:S(2)}) collective-permute-start(bf16[64,2048]{1,0:T(8,128)(2,1)S(1)} %add_convert_fusion.1), channel_id=1, source_target_pairs={{0,2},{2,0},{1,3},{3,1},{4,6},{6,4},{5,7},{7,5},{8,10},{10,8},{9,1... | collective-permute-start | bytes 786440 | tf_op jit(solution)/shard_map/ppermute | solution.py:48
  103.7 14.1 %collective-permute-start.25 = (bf16[64,2048]{1,0:T(8,128)(2,1)S(1)}, bf16[64,2048]{1,0:T(8,128)(2,1)S(1)}, u32[]{:S(2)}, u32[]{:S(2)}) collective-permute-start(bf16[64,2048]{1,0:T(8,128)(2,1)S(1)} %add_convert_fusion), channel_id=1, source_target_pairs={{0,2},{2,0},{1,3},{3,1},{4,6},{6,4},{5,7},{7,5},{8,10},{10,8},{9,1... | collective-permute-start | bytes 786440 | tf_op jit(solution)/shard_map/ppermute | solution.py:48
  105.2 13.4 %collective-permute-start.29 = (bf16[256,512]{1,0:T(8,128)(2,1)S(1)}, bf16[256,512]{1,0:T(8,128)(2,1)S(1)}, u32[]{:S(2)}, u32[]{:S(2)}) collective-permute-start(bf16[256,512]{1,0:T(8,128)(2,1)S(1)} %collective-permute-done.16.refs_9_), channel_id=1, source_target_pairs={{0,4},{4,8},{8,12},{12,0},{1,5},{5,9},{9,13},{13,1},{2,6},{6,10},{... | collective-permute-start | bytes 786440 | tf_op jit(solution)/shard_map/ppermute | solution.py:53
  105.2 14.3 %collective-permute-start.27 = (bf16[256,512]{1,0:T(8,128)(2,1)S(1)}, bf16[256,512]{1,0:T(8,128)(2,1)S(1)}, u32[]{:S(2)}, u32[]{:S(2)}) collective-permute-start(bf16[256,512]{1,0:T(8,128)(2,1)S(1)} %collective-permute-done.16.refs_9_), channel_id=1, source_target_pairs={{0,16},{16,0},{1,17},{17,1},{2,18},{18,2},{3,19},{19,3},{4,20},{20... | collective-permute-start | bytes 786440 | tf_op jit(solution)/shard_map/ppermute | solution.py:48
  105.7 14.0 %collective-permute-start.28 = (bf16[256,512]{1,0:T(8,128)(2,1)S(1)}, bf16[256,512]{1,0:T(8,128)(2,1)S(1)}, u32[]{:S(2)}, u32[]{:S(2)}) collective-permute-start(bf16[256,512]{1,0:T(8,128)(2,1)S(1)} %collective-permute-done.17.refs_11_), channel_id=1, source_target_pairs={{0,16},{16,0},{1,17},{17,1},{2,18},{18,2},{3,19},{19,3},{4,20},{20... | collective-permute-start | bytes 786440 | tf_op jit(solution)/shard_map/ppermute | solution.py:48
  112.4 11.0 %collective-permute-start.26 = (bf16[64,2048]{1,0:T(8,128)(2,1)S(1)}, bf16[64,2048]{1,0:T(8,128)(2,1)S(1)}, u32[]{:S(2)}, u32[]{:S(2)}) collective-permute-start(bf16[64,2048]{1,0:T(8,128)(2,1)S(1)} %get-tuple-element.87.refs_0_), channel_id=1, source_target_pairs={{0,2},{2,0},{1,3},{3,1},{4,6},{6,4},{5,7},{7,5},{8,10},{10,8},{9,1... | collective-permute-start | bytes 786440 | tf_op jit(solution)/shard_map/ppermute | solution.py:48
  118.1 10.2 %collective-permute-start.32 = (bf16[64,2048]{1,0:T(8,128)(2,1)S(1)}, bf16[64,2048]{1,0:T(8,128)(2,1)S(1)}, u32[]{:S(2)}, u32[]{:S(2)}) collective-permute-start(bf16[64,2048]{1,0:T(8,128)(2,1)S(1)} %get-tuple-element.92.refs_4_), channel_id=1, source_target_pairs={{0,2},{2,0},{1,3},{3,1},{4,6},{6,4},{5,7},{7,5},{8,10},{10,8},{9,1... | collective-permute-start | bytes 786440 | tf_op jit(solution)/shard_map/ppermute | solution.py:48
  118.6 9.6 %collective-permute-start.33 = (bf16[256,512]{1,0:T(8,128)(2,1)S(1)}, bf16[256,512]{1,0:T(8,128)(2,1)S(1)}, u32[]{:S(2)}, u32[]{:S(2)}) collective-permute-start(bf16[256,512]{1,0:T(8,128)(2,1)S(1)} %collective-permute-done.29.refs_13_), channel_id=1, source_target_pairs={{0,16},{16,0},{1,17},{17,1},{2,18},{18,2},{3,19},{19,3},{4,20},{20... | collective-permute-start | bytes 786440 | tf_op jit(solution)/shard_map/ppermute | solution.py:48
  119.6 8.7 %collective-permute-start.30 = (bf16[64,2048]{1,0:T(8,128)(2,1)S(1)}, bf16[64,2048]{1,0:T(8,128)(2,1)S(1)}, u32[]{:S(2)}, u32[]{:S(2)}) collective-permute-start(bf16[64,2048]{1,0:T(8,128)(2,1)S(1)} %get-tuple-element.87.refs_0_), channel_id=1, source_target_pairs={{0,1},{1,0},{2,3},{3,2},{4,5},{5,4},{6,7},{7,6},{8,9},{9,8},{10,11... | collective-permute-start | bytes 786440 | tf_op jit(solution)/shard_map/ppermute | solution.py:48
  119.6 8.7 %collective-permute-start.34 = (bf16[64,2048]{1,0:T(8,128)(2,1)S(1)}, bf16[64,2048]{1,0:T(8,128)(2,1)S(1)}, u32[]{:S(2)}, u32[]{:S(2)}) collective-permute-start(bf16[64,2048]{1,0:T(8,128)(2,1)S(1)} %get-tuple-element.92.refs_4_), channel_id=1, source_target_pairs={{0,1},{1,0},{2,3},{3,2},{4,5},{5,4},{6,7},{7,6},{8,9},{9,8},{10,11... | collective-permute-start | bytes 786440 | tf_op jit(solution)/shard_map/ppermute | solution.py:48
  123.4 4.9 %collective-permute-start.31 = (bf16[64,2048]{1,0:T(8,128)(2,1)S(1)}, bf16[64,2048]{1,0:T(8,128)(2,1)S(1)}, u32[]{:S(2)}, u32[]{:S(2)}) collective-permute-start(bf16[64,2048]{1,0:T(8,128)(2,1)S(1)} %collective-permute-done.26.refs_1_), channel_id=1, source_target_pairs={{0,1},{1,0},{2,3},{3,2},{4,5},{5,4},{6,7},{7,6},{8,9},{9,8},{10,11... | collective-permute-start | bytes 786440 | tf_op jit(solution)/shard_map/ppermute | solution.py:48
  128.2 1.5 collective-permute-start.35
  128.3 3.9 %copy-start = (bf16[2048,512]{1,0:T(8,128)(2,1)S(1)}, bf16[2048,512]{1,0:T(8,128)(2,1)}, u32[]{:S(2)}) copy-start(bf16[2048,512]{1,0:T(8,128)(2,1)} %query_ref.7) | copy-start | bytes 6291460
  128.3 3.9 %copy-start.5 = (f32[2048]{0:T(1024)S(1)}, f32[2048]{0:T(1024)}, u32[]{:S(2)}) copy-start(f32[2048]{0:T(1024)} %param.29) | copy-start | bytes 24580
  128.3 3.9 %copy-start.6 = (s32[3,16]{1,0:T(4,128)S(1)}, s32[3,16]{1,0:T(4,128)}, u32[]{:S(2)}) copy-start(s32[3,16]{1,0:T(4,128)} %parent_ref.7) | copy-start | bytes 580
  134.1 4.3 %collective-permute-start.36 = (bf16[16,2048]{1,0:T(8,128)(2,1)S(1)}, bf16[16,2048]{1,0:T(8,128)(2,1)S(1)}, u32[]{:S(2)}, u32[]{:S(2)}) collective-permute-start(bf16[16,2048]{1,0:T(8,128)(2,1)S(1)} %get-tuple-element.97.refs_1_), channel_id=1, source_target_pairs={{0,2},{2,0},{1,3},{3,1},{4,6},{6,4},{5,7},{7,5},{8,10},{10,8},{9,1... | collective-permute-start | bytes 196616 | tf_op jit(solution)/shard_map/ppermute | solution.py:48
  134.6 3.8 %collective-permute-start.37 = (bf16[16,2048]{1,0:T(8,128)(2,1)S(1)}, bf16[16,2048]{1,0:T(8,128)(2,1)S(1)}, u32[]{:S(2)}, u32[]{:S(2)}) collective-permute-start(bf16[16,2048]{1,0:T(8,128)(2,1)S(1)} %get-tuple-element.97.refs_1_), channel_id=1, source_target_pairs={{0,1},{1,0},{2,3},{3,2},{4,5},{5,4},{6,7},{7,6},{8,9},{9,8},{10,11... | collective-permute-start | bytes 196616 | tf_op jit(solution)/shard_map/ppermute | solution.py:48
  138.4 1.3 collective-permute-start.38
  141.7 4.3 %collective-permute-start.39 = (bf16[16,2048]{1,0:T(8,128)(2,1)S(1)}, bf16[16,2048]{1,0:T(8,128)(2,1)S(1)}, u32[]{:S(2)}, u32[]{:S(2)}) collective-permute-start(bf16[16,2048]{1,0:T(8,128)(2,1)S(1)} %get-tuple-element.99.refs_1_), channel_id=1, source_target_pairs={{0,2},{2,0},{1,3},{3,1},{4,6},{6,4},{5,7},{7,5},{8,10},{10,8},{9,1... | collective-permute-start | bytes 196616 | tf_op jit(solution)/shard_map/ppermute | solution.py:48
  142.2 3.8 %collective-permute-start.40 = (bf16[16,2048]{1,0:T(8,128)(2,1)S(1)}, bf16[16,2048]{1,0:T(8,128)(2,1)S(1)}, u32[]{:S(2)}, u32[]{:S(2)}) collective-permute-start(bf16[16,2048]{1,0:T(8,128)(2,1)S(1)} %get-tuple-element.99.refs_1_), channel_id=1, source_target_pairs={{0,1},{1,0},{2,3},{3,2},{4,5},{5,4},{6,7},{7,6},{8,9},{9,8},{10,11... | collective-permute-start | bytes 196616 | tf_op jit(solution)/shard_map/ppermute | solution.py:48
  146.0 1.3 collective-permute-start.41
  149.3 4.3 %collective-permute-start.42 = (bf16[16,2048]{1,0:T(8,128)(2,1)S(1)}, bf16[16,2048]{1,0:T(8,128)(2,1)S(1)}, u32[]{:S(2)}, u32[]{:S(2)}) collective-permute-start(bf16[16,2048]{1,0:T(8,128)(2,1)S(1)} %get-tuple-element.101.refs_1_), channel_id=1, source_target_pairs={{0,2},{2,0},{1,3},{3,1},{4,6},{6,4},{5,7},{7,5},{8,10},{10,8},{9,1... | collective-permute-start | bytes 196616 | tf_op jit(solution)/shard_map/ppermute | solution.py:48
  149.8 3.8 %collective-permute-start.43 = (bf16[16,2048]{1,0:T(8,128)(2,1)S(1)}, bf16[16,2048]{1,0:T(8,128)(2,1)S(1)}, u32[]{:S(2)}, u32[]{:S(2)}) collective-permute-start(bf16[16,2048]{1,0:T(8,128)(2,1)S(1)} %get-tuple-element.101.refs_1_), channel_id=1, source_target_pairs={{0,1},{1,0},{2,3},{3,2},{4,5},{5,4},{6,7},{7,6},{8,9},{9,8},{10,11... | collective-permute-start | bytes 196616 | tf_op jit(solution)/shard_map/ppermute | solution.py:48
  153.5 1.3 collective-permute-start.44
  156.9 3.2 %collective-permute-start.47 = (bf16[16,512]{1,0:T(8,128)(2,1)S(1)}, bf16[16,512]{1,0:T(8,128)(2,1)S(1)}, u32[]{:S(2)}, u32[]{:S(2)}) collective-permute-start(bf16[16,512]{1,0:T(8,128)(2,1)S(1)} %get-tuple-element.105), channel_id=1, source_target_pairs={{0,3},{1,2},{2,1},{3,0},{4,7},{5,6},{6,5},{7,4},{8,11},{9,10},{10,... | collective-permute-start | bytes 49160 | tf_op jit(solution)/shard_map/ppermute | solution.py:686
  157.2 3.8 %collective-permute-start.46 = (bf16[16,512]{1,0:T(8,128)(2,1)S(1)}, bf16[16,512]{1,0:T(8,128)(2,1)S(1)}, u32[]{:S(2)}, u32[]{:S(2)}) collective-permute-start(bf16[16,512]{1,0:T(8,128)(2,1)S(1)} %get-tuple-element.104), channel_id=1, source_target_pairs={{0,2},{1,3},{2,0},{3,1},{4,6},{5,7},{6,4},{7,5},{8,10},{9,11},{10,... | collective-permute-start | bytes 49160 | tf_op jit(solution)/shard_map/ppermute | solution.py:686
  158.7 2.2 %collective-permute-start.45 = (bf16[16,512]{1,0:T(8,128)(2,1)S(1)}, bf16[16,512]{1,0:T(8,128)(2,1)S(1)}, u32[]{:S(2)}, u32[]{:S(2)}) collective-permute-start(bf16[16,512]{1,0:T(8,128)(2,1)S(1)} %get-tuple-element.103), channel_id=1, source_target_pairs={{0,1},{1,0},{2,3},{3,2},{4,5},{5,4},{6,7},{7,6},{8,9},{9,8},{10,11... | collective-permute-start | bytes 49160 | tf_op jit(solution)/shard_map/ppermute | solution.py:686

commit v6 on v5

--- a/solution.py
+++ b/solution.py
@@ -275,38 +275,43 @@
         cached = slice(group * DH, (group + 1) * DH)
         for row in range(0, length, tile):
             reach = row + tile
-            for head in range(group * ratio, (group + 1) * ratio):
-                query = projected[row:reach, head * DH : (head + 1) * DH]
-                old = lax.dot_general(
-                    query, history_ref[0, :, cached], contract, preferred_element_type=jnp.float32
-                )
-                new = lax.dot_general(
-                    query, projected[:reach, keys], contract, preferred_element_type=jnp.float32
-                )
-                query_index = row + lax.broadcasted_iota(jnp.int32, (tile, reach), 0)
-                key_index = lax.broadcasted_iota(jnp.int32, (tile, reach), 1)
-                new = jnp.where((key_index <= query_index) & (key_index < live), new, -1e30)
-                top = jnp.maximum(
-                    jnp.max(old, axis=-1, keepdims=True), jnp.max(new, axis=-1, keepdims=True)
-                )
-                scale = DH ** (-0.5)
-                old = jnp.exp((old - top) * scale)
-                new = jnp.exp((new - top) * scale)
-                total_weight = jnp.sum(old, axis=-1, keepdims=True) + jnp.sum(
-                    new, axis=-1, keepdims=True
-                )
-                mixed = jnp.dot(
-                    old.astype(jnp.bfloat16),
-                    history_ref[1, :, cached],
-                    preferred_element_type=jnp.float32,
-                ) + jnp.dot(
-                    new.astype(jnp.bfloat16),
-                    projected[:reach, values],
-                    preferred_element_type=jnp.float32,
-                )
-                out_ref[row:reach, head * DH : (head + 1) * DH] = (mixed / total_weight).astype(
-                    jnp.bfloat16
-                )
+            heads_here = range(group * ratio, (group + 1) * ratio)
+            query = jnp.concatenate(
+                [projected[row:reach, head * DH : (head + 1) * DH] for head in heads_here], axis=0
+            )
+            old = lax.dot_general(
+                query, history_ref[0, :, cached], contract, preferred_element_type=jnp.float32
+            )
+            new = lax.dot_general(
+                query, projected[:reach, keys], contract, preferred_element_type=jnp.float32
+            )
+            query_index = row + lax.broadcasted_iota(jnp.int32, (tile, reach), 0)
+            key_index = lax.broadcasted_iota(jnp.int32, (tile, reach), 1)
+            visible = (key_index <= query_index) & (key_index < live)
+            new = jnp.where(jnp.concatenate([visible] * ratio, axis=0), new, -1e30)
+            top = jnp.maximum(
+                jnp.max(old, axis=-1, keepdims=True), jnp.max(new, axis=-1, keepdims=True)
+            )
+            scale = DH ** (-0.5)
+            old = jnp.exp((old - top) * scale)
+            new = jnp.exp((new - top) * scale)
+            total_weight = jnp.sum(old, axis=-1, keepdims=True) + jnp.sum(
+                new, axis=-1, keepdims=True
+            )
+            mixed = jnp.dot(
+                old.astype(jnp.bfloat16),
+                history_ref[1, :, cached],
+                preferred_element_type=jnp.float32,
+            ) + jnp.dot(
+                new.astype(jnp.bfloat16),
+                projected[:reach, values],
+                preferred_element_type=jnp.float32,
+            )
+            mixed = (mixed / total_weight).astype(jnp.bfloat16)
+            for index, head in enumerate(heads_here):
+                out_ref[row:reach, head * DH : (head + 1) * DH] = mixed[
+                    index * tile : (index + 1) * tile, :
+                ]
 
 
 def encoder_attention(at, normed, history, block_counts, pieces):

time: 162 us -> 161 us (level)
  no operation moved by 1% of the time
where the time goes in v6:
time: 161 us
  waiting for transfers between devices  83.9 us (52%)
  starting transfers between devices  38 us (24%)
  Pallas kernels  23.4 us (15%)
  local copies, waits for them, and re-layouts  6.84 us (4%)
  other arithmetic  3.93 us (2%)
  matrix products  3.09 us (2%)
  between operations  1.76 us (1%)
    ppermute x33, waiting for transfers between devices, exchange(): lax.ppermute(value, axis, [(i, partner(i, step, size)) for i in range(siz...  51.3 us
    ppermute x12, waiting for transfers between devices, shift(): lax.ppermute(value, axis, [(i, (i + step) % size) for i in range(size)])  31.2 us
    ppermute x33, starting transfers between devices, exchange(): lax.ppermute(value, axis, [(i, partner(i, step, size)) for i in range(siz...  19 us
    ppermute x12, starting transfers between devices, shift(): lax.ppermute(value, axis, [(i, (i + step) % size) for i in range(size)])  17.1 us
    pallas_call x4, Pallas kernels, beam_step(): pl.pallas_call(functools.partial(beam_kernel, level, max(len(inputs) - 1,...  8.12 us
    pallas_call x1, Pallas kernels, encoder_attention(): pl.pallas_call(functools.partial(encoder_kernel, [places for _, places in...  7.98 us
  transfers between devices with their start and end apart: 48, of which 26 were waited for; matrix products, arithmetic and copies ran while one was open for 6% of the time, Pallas kernels for 7%

profile of v6, /device:TPU:0, one launch (start us, length us, event | category | flops | bytes accessed | tf_op | source)
XLA Modules:
  0.0 160.9 jit_solution(7060418637770899698)
XLA Ops:
  0.7 1.9 %slice_bitcast_fusion.3 = (bf16[512,256]{1,0:T(8,128)(2,1)}, bf16[512,256]{1,0:T(8,128)(2,1)}, bf16[1,512,256]{2,1,0:T(8,128)(2,1)S(1)}, bf16[1,512,256]{2,1,0:T(8,128)(2,1)S(1)}) fusion(bf16[2,512,256]{2,1,0:T(8,128)(2,1)} %param.21), kind=kLoop, calls=%fused_computation.26 | loop fusion | bytes 1572864 | tf_op jit(solution)/shard_map/squeeze | solution.py:567
  2.6 1.0 constant_dynamic-slice_fusion.1
  3.7 3.1 %collective-permute-start.1 = (bf16[256,1024]{1,0:T(8,128)(2,1)S(1)}, bf16[256,1024]{1,0:T(8,128)(2,1)}, u32[]{:S(2)}, u32[]{:S(2)}) collective-permute-start(bf16[256,1024]{1,0:T(8,128)(2,1)S(1)} %pad_maximum_fusion.2), channel_id=1, source_target_pairs={{0,4},{4,8},{8,12},{12,0},{1,5},{5,9},{9,13},{13,1},{2,6},{6,10},{... | collective-permute-start | bytes 1572872 | tf_op jit(solution)/shard_map/ppermute | solution.py:53
  6.8 1.6 %collective-permute-start = (bf16[128,512]{1,0:T(8,128)(2,1)S(1)}, bf16[128,512]{1,0:T(8,128)(2,1)S(1)}, u32[]{:S(2)}, u32[]{:S(2)}) collective-permute-start(bf16[128,512]{1,0:T(8,128)(2,1)S(1)} %get-tuple-element.113), channel_id=1, source_target_pairs={{0,4},{4,8},{8,12},{12,0},{1,5},{5,9},{9,13},{13,1},{2,6},{6,10},{... | collective-permute-start | bytes 393224 | tf_op jit(solution)/shard_map/ppermute | solution.py:53
  8.4 2.2 %collective-permute-start.3 = (bf16[128,512]{1,0:T(8,128)(2,1)S(1)}, bf16[128,512]{1,0:T(8,128)(2,1)S(1)}, u32[]{:S(2)}, u32[]{:S(2)}) collective-permute-start(bf16[128,512]{1,0:T(8,128)(2,1)S(1)} %get-tuple-element.114), channel_id=1, source_target_pairs={{0,12},{4,0},{8,4},{12,8},{1,13},{5,1},{9,5},{13,9},{2,14},{6,2},{... | collective-permute-start | bytes 393224 | tf_op jit(solution)/shard_map/ppermute | solution.py:53
  10.7 0.8 collective-permute-start.2
  11.5 12.8 %collective-permute-done = bf16[128,512]{1,0:T(8,128)(2,1)S(1)} collective-permute-done((bf16[128,512]{1,0:T(8,128)(2,1)S(1)}, bf16[128,512]{1,0:T(8,128)(2,1)S(1)}, u32[]{:S(2)}, u32[]{:S(2)}) %collective-permute-start) | collective-permute-done | bytes 131104 | tf_op jit(solution)/shard_map/ppermute | solution.py:53
  24.4 1.8 %collective-permute-start.7 = (bf16[256,1024]{1,0:T(8,128)(2,1)}, bf16[256,1024]{1,0:T(8,128)(2,1)S(1)}, u32[]{:S(2)}, u32[]{:S(2)}) collective-permute-start(bf16[256,1024]{1,0:T(8,128)(2,1)} %collective-permute-done.1.refs_1_), channel_id=1, source_target_pairs={{0,16},{16,0},{1,17},{17,1},{2,18},{18,2},{3,19},{19,3},{4,20},{20... | collective-permute-start | bytes 1572872 | tf_op jit(solution)/shard_map/ppermute | solution.py:48
  26.3 5.6 %collective-permute-done.2 = bf16[128,512]{1,0:T(8,128)(2,1)S(1)} collective-permute-done((bf16[128,512]{1,0:T(8,128)(2,1)S(1)}, bf16[128,512]{1,0:T(8,128)(2,1)S(1)}, u32[]{:S(2)}, u32[]{:S(2)}) %collective-permute-start.2) | collective-permute-done | bytes 131104 | tf_op jit(solution)/shard_map/ppermute | solution.py:53
  32.0 1.6 collective-permute-start.4
  33.5 1.6 %collective-permute-start.8 = (bf16[256,1024]{1,0:T(8,128)(2,1)S(1)}, bf16[256,1024]{1,0:T(8,128)(2,1)}, u32[]{:S(2)}, u32[]{:S(2)}) collective-permute-start(bf16[256,1024]{1,0:T(8,128)(2,1)S(1)} %pad_maximum_fusion.2), channel_id=1, source_target_pairs={{0,12},{4,0},{8,4},{12,8},{1,13},{5,1},{9,5},{13,9},{2,14},{6,2},{... | collective-permute-start | bytes 1572872 | tf_op jit(solution)/shard_map/ppermute | solution.py:53
  35.3 3.1 %convolution_convert_fusion = bf16[64,2048]{1,0:T(8,128)(2,1)S(1)} fusion(bf16[64,1024]{1,0:T(8,128)(2,1)S(1)} %compare_convert_fusion, bf16[1024,2048]{1,0:T(8,128)(2,1)} %param.26), kind=kOutput, calls=%fused_computation | convolution fusion | flops 268566528 | bytes 4587520 | tf_op jit(solution)/shard_map/dot_general | solution.py:577
  38.4 0.5 collective-permute-start.5
  38.9 6.9 %collective-permute-done.4.refs_1_ = bf16[512,512]{1,0:T(8,128)(2,1)S(1)} collective-permute-done((bf16[512,512]{1,0:T(8,128)(2,1)S(1)}, bf16[512,512]{1,0:T(8,128)(2,1)S(1)}, u32[]{:S(2)}, u32[]{:S(2)}) %collective-permute-start.4) | collective-permute-done | bytes 524320 | tf_op jit(solution)/shard_map/ppermute | solution.py:48
  45.9 1.3 collective-permute-done.8.refs_3_
  47.2 1.5 collective-permute-start.9
  48.7 0.8 add.88
  49.5 0.5 collective-permute-start.12
  50.1 0.7 slice_bitcast_fusion
  50.9 2.9 %copy.17 = bf16[2048,512]{0,1:T(8,128)(2,1)S(1)} copy(bf16[2048,512]{1,0:T(8,128)(2,1)} %param.25) | data formatting | bytes 4194304 | tf_op jit(solution)/shard_map/optimization_barrier | solution.py:57
  53.9 3.1 %collective-permute-done.12 = bf16[64,2048]{1,0:T(8,128)(2,1)} collective-permute-done((bf16[64,2048]{1,0:T(8,128)(2,1)}, bf16[64,2048]{1,0:T(8,128)(2,1)}, u32[]{:S(2)}, u32[]{:S(2)}) %collective-permute-start.12) | collective-permute-done | bytes 262176 | tf_op jit(solution)/shard_map/ppermute | solution.py:48
  57.0 1.1 add.89
  58.1 2.4 %norm_events.1 = (bf16[512,2048]{1,0:T(8,128)(2,1)S(1)}, bf16[128,2048]{1,0:T(8,128)(2,1)S(1)}) custom-call(s32[4]{0:T(128)S(1)} %pad_add_fusion.at_ref, f32[1,2048]{1,0:T(1,128)S(1)} %bitcast.48, bf16[512,512]{1,0:T(8,128)(2,1)S(1)} %pad_maximum_fusion.3.refs_0_, bf16[512,512]{1,0:T(8,128)(2,1)S(1)} %collective-permute-done.4.refs_1_, ...), custom_call_target="tpu_custom_call" | custom-call | bytes 12000000 | tf_op jit(solution)/shard_map/norm_events/pallas_call | solution.py:206
  60.6 3.0 %collective-permute-done.10.refs_5_ = bf16[256,1024]{1,0:T(8,128)(2,1)} collective-permute-done((bf16[256,1024]{1,0:T(8,128)(2,1)}, bf16[256,1024]{1,0:T(8,128)(2,1)}, u32[]{:S(2)}, u32[]{:S(2)}) %collective-permute-start.10) | collective-permute-done | bytes 524320 | tf_op jit(solution)/shard_map/ppermute | solution.py:53
  63.6 0.5 collective-permute-start.13
  64.3 3.8 %collective-permute-start.15 = (bf16[256,512]{1,0:T(8,128)(2,1)S(1)}, bf16[256,512]{1,0:T(8,128)(2,1)S(1)}, u32[]{:S(2)}, u32[]{:S(2)}) collective-permute-start(bf16[256,512]{1,0:T(8,128)(2,1)S(1)} %get-tuple-element.66), channel_id=1, source_target_pairs={{0,12},{4,0},{8,4},{12,8},{1,13},{5,1},{9,5},{13,9},{2,14},{6,2},{... | collective-permute-start | bytes 786440 | tf_op jit(solution)/shard_map/ppermute | solution.py:53
  68.1 7.3 %collective-permute-done.14.refs_1_ = bf16[256,512]{1,0:T(8,128)(2,1)S(1)} collective-permute-done((bf16[256,512]{1,0:T(8,128)(2,1)S(1)}, bf16[256,512]{1,0:T(8,128)(2,1)S(1)}, u32[]{:S(2)}, u32[]{:S(2)}) %collective-permute-start.14) | collective-permute-done | bytes 262176 | tf_op jit(solution)/shard_map/ppermute | solution.py:53
  76.2 1.6 collective-permute-start.18
  77.8 2.1 %collective-permute-start.19 = (bf16[256,512]{1,0:T(8,128)(2,1)S(1)}, bf16[256,512]{1,0:T(8,128)(2,1)S(1)}, u32[]{:S(2)}, u32[]{:S(2)}) collective-permute-start(bf16[256,512]{1,0:T(8,128)(2,1)S(1)} %collective-permute-done.15.refs_3_), channel_id=1, source_target_pairs={{0,16},{16,0},{1,17},{17,1},{2,18},{18,2},{3,19},{19,3},{4,20},{20... | collective-permute-start | bytes 786440 | tf_op jit(solution)/shard_map/ppermute | solution.py:48
  79.9 3.8 %collective-permute-start.17 = (bf16[256,512]{1,0:T(8,128)(2,1)S(1)}, bf16[256,512]{1,0:T(8,128)(2,1)S(1)}, u32[]{:S(2)}, u32[]{:S(2)}) collective-permute-start(bf16[256,512]{1,0:T(8,128)(2,1)S(1)} %get-tuple-element.75), channel_id=1, source_target_pairs={{0,12},{4,0},{8,4},{12,8},{1,13},{5,1},{9,5},{13,9},{2,14},{6,2},{... | collective-permute-start | bytes 786440 | tf_op jit(solution)/shard_map/ppermute | solution.py:53
  83.7 8.0 %encoder_attention.1.attended_ref = bf16[512,512]{1,0:T(8,128)(2,1)S(1)} custom-call(s32[4]{0:T(128)S(1)} %pad_add_fusion.at_ref, s32[1]{0:T(128)S(6)} %copy.18.live_ref, bf16[512,2048]{1,0:T(8,128)(2,1)S(1)} %get-tuple-element.67.rows_ref, bf16[2,512,256]{2,1,0:T(8,128)(2,1)S(1)} %bitcast.39, bf16[512,1024]{1,0:T(8,128)(2,1)S(1)} %pad_maximum_fusion.refs_0_, ...), custom_call_target="tpu_custom_call" | custom-call | bytes 33000000 | tf_op jit(solution)/shard_map/encoder_attention/pallas_call | solution.py:322
  91.8 1.0 collective-permute-done.17.refs_11_
  92.8 5.3 %collective-permute-done.21.refs_6_ = bf16[256,512]{1,0:T(8,128)(2,1)S(1)} collective-permute-done((bf16[256,512]{1,0:T(8,128)(2,1)S(1)}, bf16[256,512]{1,0:T(8,128)(2,1)S(1)}, u32[]{:S(2)}, u32[]{:S(2)}) %collective-permute-start.21) | collective-permute-done | bytes 262176 | tf_op jit(solution)/shard_map/ppermute | solution.py:48
  98.1 2.1 %project_out.1 = (bf16[128,2048]{1,0:T(8,128)(2,1)S(1)}, bf16[128,2048]{1,0:T(8,128)(2,1)S(1)}, bf16[128,2048]{1,0:T(8,128)(2,1)S(1)}, bf16[128,2048]{1,0:T(8,128)(2,1)S(1)}) custom-call(s32[4]{0:T(128)S(1)} %pad_add_fusion.at_ref, bf16[512,512]{1,0:T(8,128)(2,1)S(1)} %encoder_attention.1.attended_ref, bf16[512,512]{1,0:T(8,128)(2,1)S(1)} %copy-done.1, ...), custom_call_target="tpu_custom_call" | custom-call | bytes 6000000 | tf_op jit(solution)/shard_map/project_out/pallas_call | solution.py:378
  100.8 1.4 collective-permute-done.22.refs_1_
  102.3 0.6 collective-permute-start.23
  103.0 1.5 collective-permute-start.25
  105.0 1.5 collective-permute-start.28
  106.6 5.0 %collective-permute-done.23 = bf16[64,2048]{1,0:T(8,128)(2,1)S(1)} collective-permute-done((bf16[64,2048]{1,0:T(8,128)(2,1)S(1)}, bf16[64,2048]{1,0:T(8,128)(2,1)S(1)}, u32[]{:S(2)}, u32[]{:S(2)}) %collective-permute-start.23) | collective-permute-done | bytes 262176 | tf_op jit(solution)/shard_map/ppermute | solution.py:48
  111.8 0.6 collective-permute-start.26
  112.3 4.8 %collective-permute-done.25 = bf16[64,2048]{1,0:T(8,128)(2,1)S(1)} collective-permute-done((bf16[64,2048]{1,0:T(8,128)(2,1)S(1)}, bf16[64,2048]{1,0:T(8,128)(2,1)S(1)}, u32[]{:S(2)}, u32[]{:S(2)}) %collective-permute-start.25) | collective-permute-done | bytes 262176 | tf_op jit(solution)/shard_map/ppermute | solution.py:48
  117.4 0.6 collective-permute-start.32
  118.0 0.9 collective-permute-start.33
  119.5 3.3 %collective-permute-done.26.refs_1_ = bf16[64,2048]{1,0:T(8,128)(2,1)S(1)} collective-permute-done((bf16[64,2048]{1,0:T(8,128)(2,1)S(1)}, bf16[64,2048]{1,0:T(8,128)(2,1)S(1)}, u32[]{:S(2)}, u32[]{:S(2)}) %collective-permute-start.26) | collective-permute-done | bytes 262176 | tf_op jit(solution)/shard_map/ppermute | solution.py:48
  122.8 4.8 %collective-permute-done.32.refs_5_ = bf16[64,2048]{1,0:T(8,128)(2,1)S(1)} collective-permute-done((bf16[64,2048]{1,0:T(8,128)(2,1)S(1)}, bf16[64,2048]{1,0:T(8,128)(2,1)S(1)}, u32[]{:S(2)}, u32[]{:S(2)}) %collective-permute-start.32) | collective-permute-done | bytes 262176 | tf_op jit(solution)/shard_map/ppermute | solution.py:48
  127.7 1.4 collective-permute-done.35.refs_7_
  129.1 2.3 %cross_project.1.cross_ref = bf16[512,512]{1,0:T(8,128)(2,1)S(1)} custom-call(s32[4]{0:T(128)S(1)} %pad_add_fusion.at_ref, bf16[64,2048]{1,0:T(8,128)(2,1)S(1)} %get-tuple-element.87.refs_0_, bf16[64,2048]{1,0:T(8,128)(2,1)S(1)} %collective-permute-done.26.refs_1_, bf16[64,2048]{1,0:T(8,128)(2,1)S(1)} %collective-permute-done.30.refs_2_, ...), custom_call_target="tpu_custom_call" | custom-call | bytes 6000000 | tf_op jit(solution)/shard_map/cross_project/pallas_call | solution.py:438
  131.5 1.9 %beam_step_0.1 = (f32[16,2048]{1,0:T(8,128)S(1)}, bf16[16,2048]{1,0:T(8,128)(2,1)S(1)}) custom-call(s32[4]{0:T(128)S(1)} %pad_add_fusion.at_ref, s32[1]{0:T(128)S(6)} %copy.18.live_ref, s32[3,16]{1,0:T(4,128)S(1)} %copy-done.6, f32[1,2048]{1,0:T(1,128)S(1)} %bitcast.42, bf16[2048,512]{1,0:T(8,128)(2,1)S(1)} %copy-done, bf16[512,2048]{1,0:T(8,128)(2,1)S(1)} %bitcast.35, ...), custom_call_target="tpu_custom_call" | custom-call | bytes 12000000 | tf_op jit(solution)/shard_map/beam_step_0/pallas_call | solution.py:533
  133.4 0.5 collective-permute-start.36
  133.9 3.8 %collective-permute-done.36.refs_2_ = bf16[16,2048]{1,0:T(8,128)(2,1)S(1)} collective-permute-done((bf16[16,2048]{1,0:T(8,128)(2,1)S(1)}, bf16[16,2048]{1,0:T(8,128)(2,1)S(1)}, u32[]{:S(2)}, u32[]{:S(2)}) %collective-permute-start.36) | collective-permute-done | bytes 65568 | tf_op jit(solution)/shard_map/ppermute | solution.py:48
  137.7 1.2 collective-permute-done.38.refs_4_
  138.9 2.1 %beam_step_1.1 = (f32[16,2048]{1,0:T(8,128)S(1)}, bf16[16,2048]{1,0:T(8,128)(2,1)S(1)}) custom-call(s32[4]{0:T(128)S(1)} %pad_add_fusion.at_ref, s32[1]{0:T(128)S(6)} %copy.18.live_ref, s32[3,16]{1,0:T(4,128)S(1)} %copy-done.6, f32[1,2048]{1,0:T(1,128)S(1)} %bitcast.43, bf16[2048,512]{1,0:T(8,128)(2,1)S(1)} %copy-done, bf16[512,2048]{1,0:T(8,128)(2,1)S(1)} %bitcast.36, ...), custom_call_target="tpu_custom_call" | custom-call | bytes 12000000 | tf_op jit(solution)/shard_map/beam_step_1/pallas_call | solution.py:533
  141.0 0.5 collective-permute-start.39
  141.5 3.8 %collective-permute-done.39.refs_2_ = bf16[16,2048]{1,0:T(8,128)(2,1)S(1)} collective-permute-done((bf16[16,2048]{1,0:T(8,128)(2,1)S(1)}, bf16[16,2048]{1,0:T(8,128)(2,1)S(1)}, u32[]{:S(2)}, u32[]{:S(2)}) %collective-permute-start.39) | collective-permute-done | bytes 65568 | tf_op jit(solution)/shard_map/ppermute | solution.py:48
  145.3 1.2 collective-permute-done.41.refs_4_
  146.5 2.1 %beam_step_2.1 = (f32[16,2048]{1,0:T(8,128)S(1)}, bf16[16,2048]{1,0:T(8,128)(2,1)S(1)}) custom-call(s32[4]{0:T(128)S(1)} %pad_add_fusion.at_ref, s32[1]{0:T(128)S(6)} %copy.18.live_ref, s32[3,16]{1,0:T(4,128)S(1)} %copy-done.6, f32[1,2048]{1,0:T(1,128)S(1)} %bitcast.44, bf16[2048,512]{1,0:T(8,128)(2,1)S(1)} %copy-done, bf16[512,2048]{1,0:T(8,128)(2,1)S(1)} %bitcast.37, ...), custom_call_target="tpu_custom_call" | custom-call | bytes 12000000 | tf_op jit(solution)/shard_map/beam_step_2/pallas_call | solution.py:533
  148.6 0.5 collective-permute-start.42
  149.1 3.8 %collective-permute-done.42.refs_2_ = bf16[16,2048]{1,0:T(8,128)(2,1)S(1)} collective-permute-done((bf16[16,2048]{1,0:T(8,128)(2,1)S(1)}, bf16[16,2048]{1,0:T(8,128)(2,1)S(1)}, u32[]{:S(2)}, u32[]{:S(2)}) %collective-permute-start.42) | collective-permute-done | bytes 65568 | tf_op jit(solution)/shard_map/ppermute | solution.py:48
  152.9 1.2 collective-permute-done.44.refs_4_
  154.1 2.1 %beam_step_3.1 = (f32[16,512]{1,0:T(8,128)S(1)}, bf16[16,512]{1,0:T(8,128)(2,1)S(1)}, bf16[16,512]{1,0:T(8,128)(2,1)S(1)}, bf16[16,512]{1,0:T(8,128)(2,1)S(1)}) custom-call(s32[4]{0:T(128)S(1)} %pad_add_fusion.at_ref, s32[1]{0:T(128)S(6)} %copy.18.live_ref, s32[3,16]{1,0:T(4,128)S(1)} %copy-done.6, f32[1,2048]{1,0:T(1,128)S(1)} %bitcast.45, ...), custom_call_target="tpu_custom_call" | custom-call | bytes 12000000 | tf_op jit(solution)/shard_map/beam_step_3/pallas_call | solution.py:533
  156.6 1.5 collective-permute-start.46
  158.1 0.8 maximum_bitcast_fusion
  159.4 0.9 collective-permute-done.46
  160.3 0.6 add_convert_fusion.2
  (97 shorter events, 4.5 us)
Async XLA Ops:
  0.6 6.1 %copy-start.13 = (bf16[4,128,512]{2,1,0:T(8,128)(2,1)S(1)}, bf16[4,128,512]{2,1,0:T(8,128)(2,1)}, u32[]{:S(2)}) copy-start(bf16[4,128,512]{2,1,0:T(8,128)(2,1)} %param.15) | copy-start | bytes 1572868
  0.6 10.8 %copy-start.15 = (s32[4,16]{1,0:T(4,128)S(1)}, s32[4,16]{1,0:T(4,128)}, u32[]{:S(2)}) copy-start(s32[4,16]{1,0:T(4,128)} %param.18) | copy-start | bytes 772
  3.7 20.7 %collective-permute-start.1 = (bf16[256,1024]{1,0:T(8,128)(2,1)S(1)}, bf16[256,1024]{1,0:T(8,128)(2,1)}, u32[]{:S(2)}, u32[]{:S(2)}) collective-permute-start(bf16[256,1024]{1,0:T(8,128)(2,1)S(1)} %pad_maximum_fusion.2), channel_id=1, source_target_pairs={{0,4},{4,8},{8,12},{12,0},{1,5},{5,9},{9,13},{13,1},{2,6},{6,10},{... | collective-permute-start | bytes 1572872 | tf_op jit(solution)/shard_map/ppermute | solution.py:53
  6.8 17.6 %collective-permute-start = (bf16[128,512]{1,0:T(8,128)(2,1)S(1)}, bf16[128,512]{1,0:T(8,128)(2,1)S(1)}, u32[]{:S(2)}, u32[]{:S(2)}) collective-permute-start(bf16[128,512]{1,0:T(8,128)(2,1)S(1)} %get-tuple-element.113), channel_id=1, source_target_pairs={{0,4},{4,8},{8,12},{12,0},{1,5},{5,9},{9,13},{13,1},{2,6},{6,10},{... | collective-permute-start | bytes 393224 | tf_op jit(solution)/shard_map/ppermute | solution.py:53
  8.4 17.9 %collective-permute-start.3 = (bf16[128,512]{1,0:T(8,128)(2,1)S(1)}, bf16[128,512]{1,0:T(8,128)(2,1)S(1)}, u32[]{:S(2)}, u32[]{:S(2)}) collective-permute-start(bf16[128,512]{1,0:T(8,128)(2,1)S(1)} %get-tuple-element.114), channel_id=1, source_target_pairs={{0,12},{4,0},{8,4},{12,8},{1,13},{5,1},{9,5},{13,9},{2,14},{6,2},{... | collective-permute-start | bytes 393224 | tf_op jit(solution)/shard_map/ppermute | solution.py:53
  10.7 21.3 %collective-permute-start.2 = (bf16[128,512]{1,0:T(8,128)(2,1)S(1)}, bf16[128,512]{1,0:T(8,128)(2,1)S(1)}, u32[]{:S(2)}, u32[]{:S(2)}) collective-permute-start(bf16[128,512]{1,0:T(8,128)(2,1)S(1)} %get-tuple-element.115), channel_id=1, source_target_pairs={{0,8},{4,12},{8,0},{12,4},{1,9},{5,13},{9,1},{13,5},{2,10},{6,14},... | collective-permute-start | bytes 393224 | tf_op jit(solution)/shard_map/ppermute | solution.py:53
  24.4 21.5 %collective-permute-start.7 = (bf16[256,1024]{1,0:T(8,128)(2,1)}, bf16[256,1024]{1,0:T(8,128)(2,1)S(1)}, u32[]{:S(2)}, u32[]{:S(2)}) collective-permute-start(bf16[256,1024]{1,0:T(8,128)(2,1)} %collective-permute-done.1.refs_1_), channel_id=1, source_target_pairs={{0,16},{16,0},{1,17},{17,1},{2,18},{18,2},{3,19},{19,3},{4,20},{20... | collective-permute-start | bytes 1572872 | tf_op jit(solution)/shard_map/ppermute | solution.py:48
  32.0 13.9 %collective-permute-start.4 = (bf16[512,512]{1,0:T(8,128)(2,1)S(1)}, bf16[512,512]{1,0:T(8,128)(2,1)S(1)}, u32[]{:S(2)}, u32[]{:S(2)}) collective-permute-start(bf16[512,512]{1,0:T(8,128)(2,1)S(1)} %pad_maximum_fusion.3.refs_0_), channel_id=1, source_target_pairs={{0,2},{2,0},{1,3},{3,1},{4,6},{6,4},{5,7},{7,5},{8,10},{10,8},{9,1... | collective-permute-start | bytes 1572872 | tf_op jit(solution)/shard_map/ppermute | solution.py:48
  33.5 13.7 %collective-permute-start.8 = (bf16[256,1024]{1,0:T(8,128)(2,1)S(1)}, bf16[256,1024]{1,0:T(8,128)(2,1)}, u32[]{:S(2)}, u32[]{:S(2)}) collective-permute-start(bf16[256,1024]{1,0:T(8,128)(2,1)S(1)} %pad_maximum_fusion.2), channel_id=1, source_target_pairs={{0,12},{4,0},{8,4},{12,8},{1,13},{5,1},{9,5},{13,9},{2,14},{6,2},{... | collective-permute-start | bytes 1572872 | tf_op jit(solution)/shard_map/ppermute | solution.py:53
  35.2 14.9 %copy-start.14 = (bf16[2,512,256]{2,1,0:T(8,128)(2,1)S(1)}, bf16[2,512,256]{2,1,0:T(8,128)(2,1)}, u32[]{:S(2)}) copy-start(bf16[2,512,256]{2,1,0:T(8,128)(2,1)} %param.23) | copy-start | bytes 1572868
  38.4 10.4 %collective-permute-start.11 = (bf16[64,2048]{1,0:T(8,128)(2,1)S(1)}, bf16[64,2048]{1,0:T(8,128)(2,1)S(1)}, u32[]{:S(2)}, u32[]{:S(2)}) collective-permute-start(bf16[64,2048]{1,0:T(8,128)(2,1)S(1)} %convolution_convert_fusion), channel_id=1, source_target_pairs={{0,1},{1,0},{2,3},{3,2},{4,5},{5,4},{6,7},{7,6},{8,9},{9,8},{10,11... | collective-permute-start | bytes 786440 | tf_op jit(solution)/shard_map/ppermute | solution.py:48
  38.4 19.7 %collective-permute-start.5 = (bf16[512,512]{1,0:T(8,128)(2,1)S(1)}, bf16[512,512]{1,0:T(8,128)(2,1)}, u32[]{:S(2)}, u32[]{:S(2)}) collective-permute-start(bf16[512,512]{1,0:T(8,128)(2,1)S(1)} %pad_maximum_fusion.3.refs_0_), channel_id=1, source_target_pairs={{0,1},{1,0},{2,3},{3,2},{4,5},{5,4},{6,7},{7,6},{8,9},{9,8},{10,11... | collective-permute-start | bytes 1572872 | tf_op jit(solution)/shard_map/ppermute | solution.py:48
  45.9 12.2 %collective-permute-start.6 = (bf16[512,512]{1,0:T(8,128)(2,1)S(1)}, bf16[512,512]{1,0:T(8,128)(2,1)}, u32[]{:S(2)}, u32[]{:S(2)}) collective-permute-start(bf16[512,512]{1,0:T(8,128)(2,1)S(1)} %collective-permute-done.4.refs_1_), channel_id=1, source_target_pairs={{0,1},{1,0},{2,3},{3,2},{4,5},{5,4},{6,7},{7,6},{8,9},{9,8},{10,11... | collective-permute-start | bytes 1572872 | tf_op jit(solution)/shard_map/ppermute | solution.py:48
  45.9 4.2 %copy-start.3 = (bf16[256,1024]{1,0:T(8,128)(2,1)}, bf16[256,1024]{1,0:T(8,128)(2,1)S(1)}, u32[]{:S(2)}) copy-start(bf16[256,1024]{1,0:T(8,128)(2,1)S(1)} %collective-permute-done.7.refs_2_) | copy-start | bytes 1572868
  47.2 13.4 %collective-permute-start.9 = (bf16[256,1024]{1,0:T(8,128)(2,1)}, bf16[256,1024]{1,0:T(8,128)(2,1)}, u32[]{:S(2)}, u32[]{:S(2)}) collective-permute-start(bf16[256,1024]{1,0:T(8,128)(2,1)} %collective-permute-done.8.refs_3_), channel_id=1, source_target_pairs={{0,16},{16,0},{1,17},{17,1},{2,18},{18,2},{3,19},{19,3},{4,20},{20... | collective-permute-start | bytes 1572872 | tf_op jit(solution)/shard_map/ppermute | solution.py:48
  48.7 14.9 %collective-permute-start.10 = (bf16[256,1024]{1,0:T(8,128)(2,1)}, bf16[256,1024]{1,0:T(8,128)(2,1)}, u32[]{:S(2)}, u32[]{:S(2)}) collective-permute-start(bf16[256,1024]{1,0:T(8,128)(2,1)} %collective-permute-done.1.refs_1_), channel_id=1, source_target_pairs={{0,4},{4,8},{8,12},{12,0},{1,5},{5,9},{9,13},{13,1},{2,6},{6,10},{... | collective-permute-start | bytes 1572872 | tf_op jit(solution)/shard_map/ppermute | solution.py:53
  49.5 7.5 %collective-permute-start.12 = (bf16[64,2048]{1,0:T(8,128)(2,1)}, bf16[64,2048]{1,0:T(8,128)(2,1)}, u32[]{:S(2)}, u32[]{:S(2)}) collective-permute-start(bf16[64,2048]{1,0:T(8,128)(2,1)} %add.88), channel_id=1, source_target_pairs={{0,2},{2,0},{1,3},{3,1},{4,6},{6,4},{5,7},{7,5},{8,10},{10,8},{9,1... | collective-permute-start | bytes 786440 | tf_op jit(solution)/shard_map/ppermute | solution.py:48
  50.9 7.3 %copy-start.8 = (f32[2048]{0:T(1024)S(1)}, f32[2048]{0:T(1024)}, u32[]{:S(2)}) copy-start(f32[2048]{0:T(1024)} %param.27) | copy-start | bytes 24580
  53.8 10.3 %copy-start.1 = (bf16[512,512]{1,0:T(8,128)(2,1)S(1)}, bf16[512,512]{1,0:T(8,128)(2,1)}, u32[]{:S(2)}) copy-start(bf16[512,512]{1,0:T(8,128)(2,1)} %refs_0_.1) | copy-start | bytes 1572868
  53.8 10.3 %copy-start.9 = (bf16[512,256]{1,0:T(8,128)(2,1)S(1)}, bf16[512,256]{1,0:T(8,128)(2,1)}, u32[]{:S(2)}) copy-start(bf16[512,256]{1,0:T(8,128)(2,1)} %get-tuple-element.107) | copy-start | bytes 786436
  53.8 22.2 %copy-start.10 = (bf16[512,512]{1,0:T(8,128)(2,1)S(1)}, bf16[512,512]{1,0:T(8,128)(2,1)}, u32[]{:S(2)}) copy-start(bf16[512,512]{1,0:T(8,128)(2,1)} %param.20) | copy-start | bytes 1572868
  53.8 22.2 %copy-start.11 = (bf16[512,256]{1,0:T(8,128)(2,1)S(1)}, bf16[512,256]{1,0:T(8,128)(2,1)}, u32[]{:S(2)}) copy-start(bf16[512,256]{1,0:T(8,128)(2,1)} %get-tuple-element.108) | copy-start | bytes 786436
  53.9 22.2 %copy-start.12 = (bf16[512,256]{1,0:T(8,128)(2,1)S(1)}, bf16[512,256]{1,0:T(8,128)(2,1)}, u32[]{:S(2)}) copy-start(bf16[512,256]{1,0:T(8,128)(2,1)} %get-tuple-element.109) | copy-start | bytes 786436
  60.5 23.2 %copy-start.2 = (bf16[2,1,512,256]{3,2,1,0:T(8,128)(2,1)S(1)}, bf16[2,1,512,256]{3,2,1,0:T(8,128)(2,1)}, u32[]{:S(2)}) copy-start(bf16[2,1,512,256]{3,2,1,0:T(8,128)(2,1)} %param.16) | copy-start | bytes 1572868
  60.5 23.2 %copy-start.4 = (bf16[256,1024]{1,0:T(8,128)(2,1)S(1)}, bf16[256,1024]{1,0:T(8,128)(2,1)}, u32[]{:S(2)}) copy-start(bf16[256,1024]{1,0:T(8,128)(2,1)} %copy-done.3) | copy-start | bytes 1572868
  63.6 16.2 %collective-permute-start.13 = (bf16[256,1024]{1,0:T(8,128)(2,1)}, bf16[256,1024]{1,0:T(8,128)(2,1)S(1)}, u32[]{:S(2)}, u32[]{:S(2)}) collective-permute-start(bf16[256,1024]{1,0:T(8,128)(2,1)} %collective-permute-done.10.refs_5_), channel_id=1, source_target_pairs={{0,16},{16,0},{1,17},{17,1},{2,18},{18,2},{3,19},{19,3},{4,20},{20... | collective-permute-start | bytes 1572872 | tf_op jit(solution)/shard_map/ppermute | solution.py:48
  64.2 11.1 %collective-permute-start.14 = (bf16[256,512]{1,0:T(8,128)(2,1)S(1)}, bf16[256,512]{1,0:T(8,128)(2,1)S(1)}, u32[]{:S(2)}, u32[]{:S(2)}) collective-permute-start(bf16[256,512]{1,0:T(8,128)(2,1)S(1)} %get-tuple-element.66), channel_id=1, source_target_pairs={{0,4},{4,8},{8,12},{12,0},{1,5},{5,9},{9,13},{13,1},{2,6},{6,10},{... | collective-permute-start | bytes 786440 | tf_op jit(solution)/shard_map/ppermute | solution.py:53
  64.3 13.5 %collective-permute-start.15 = (bf16[256,512]{1,0:T(8,128)(2,1)S(1)}, bf16[256,512]{1,0:T(8,128)(2,1)S(1)}, u32[]{:S(2)}, u32[]{:S(2)}) collective-permute-start(bf16[256,512]{1,0:T(8,128)(2,1)S(1)} %get-tuple-element.66), channel_id=1, source_target_pairs={{0,12},{4,0},{8,4},{12,8},{1,13},{5,1},{9,5},{13,9},{2,14},{6,2},{... | collective-permute-start | bytes 786440 | tf_op jit(solution)/shard_map/ppermute | solution.py:53
  75.3 16.3 %collective-permute-start.20 = (bf16[256,512]{1,0:T(8,128)(2,1)S(1)}, bf16[256,512]{1,0:T(8,128)(2,1)S(1)}, u32[]{:S(2)}, u32[]{:S(2)}) collective-permute-start(bf16[256,512]{1,0:T(8,128)(2,1)S(1)} %collective-permute-done.14.refs_1_), channel_id=1, source_target_pairs={{0,4},{4,8},{8,12},{12,0},{1,5},{5,9},{9,13},{13,1},{2,6},{6,10},{... | collective-permute-start | bytes 786440 | tf_op jit(solution)/shard_map/ppermute | solution.py:53
  76.2 16.6 %collective-permute-start.18 = (bf16[256,512]{1,0:T(8,128)(2,1)S(1)}, bf16[256,512]{1,0:T(8,128)(2,1)S(1)}, u32[]{:S(2)}, u32[]{:S(2)}) collective-permute-start(bf16[256,512]{1,0:T(8,128)(2,1)S(1)} %collective-permute-done.14.refs_1_), channel_id=1, source_target_pairs={{0,16},{16,0},{1,17},{17,1},{2,18},{18,2},{3,19},{19,3},{4,20},{20... | collective-permute-start | bytes 786440 | tf_op jit(solution)/shard_map/ppermute | solution.py:48
  77.8 15.0 %collective-permute-start.19 = (bf16[256,512]{1,0:T(8,128)(2,1)S(1)}, bf16[256,512]{1,0:T(8,128)(2,1)S(1)}, u32[]{:S(2)}, u32[]{:S(2)}) collective-permute-start(bf16[256,512]{1,0:T(8,128)(2,1)S(1)} %collective-permute-done.15.refs_3_), channel_id=1, source_target_pairs={{0,16},{16,0},{1,17},{17,1},{2,18},{18,2},{3,19},{19,3},{4,20},{20... | collective-permute-start | bytes 786440 | tf_op jit(solution)/shard_map/ppermute | solution.py:48
  79.9 11.9 %collective-permute-start.16 = (bf16[256,512]{1,0:T(8,128)(2,1)S(1)}, bf16[256,512]{1,0:T(8,128)(2,1)S(1)}, u32[]{:S(2)}, u32[]{:S(2)}) collective-permute-start(bf16[256,512]{1,0:T(8,128)(2,1)S(1)} %get-tuple-element.75), channel_id=1, source_target_pairs={{0,4},{4,8},{8,12},{12,0},{1,5},{5,9},{9,13},{13,1},{2,6},{6,10},{... | collective-permute-start | bytes 786440 | tf_op jit(solution)/shard_map/ppermute | solution.py:53
  79.9 12.9 %collective-permute-start.17 = (bf16[256,512]{1,0:T(8,128)(2,1)S(1)}, bf16[256,512]{1,0:T(8,128)(2,1)S(1)}, u32[]{:S(2)}, u32[]{:S(2)}) collective-permute-start(bf16[256,512]{1,0:T(8,128)(2,1)S(1)} %get-tuple-element.75), channel_id=1, source_target_pairs={{0,12},{4,0},{8,4},{12,8},{1,13},{5,1},{9,5},{13,9},{2,14},{6,2},{... | collective-permute-start | bytes 786440 | tf_op jit(solution)/shard_map/ppermute | solution.py:53
  91.7 19.8 %copy-start.7 = (f32[2048]{0:T(1024)S(1)}, f32[2048]{0:T(1024)}, u32[]{:S(2)}) copy-start(f32[2048]{0:T(1024)} %param.28) | copy-start | bytes 24580
  91.7 6.4 %collective-permute-start.21 = (bf16[256,512]{1,0:T(8,128)(2,1)S(1)}, bf16[256,512]{1,0:T(8,128)(2,1)S(1)}, u32[]{:S(2)}, u32[]{:S(2)}) collective-permute-start(bf16[256,512]{1,0:T(8,128)(2,1)S(1)} %collective-permute-done.20.refs_5_), channel_id=1, source_target_pairs={{0,16},{16,0},{1,17},{17,1},{2,18},{18,2},{3,19},{19,3},{4,20},{20... | collective-permute-start | bytes 786440 | tf_op jit(solution)/shard_map/ppermute | solution.py:48
  100.3 2.0 %collective-permute-start.22 = (bf16[128,2048]{1,0:T(8,128)(2,1)S(1)}, bf16[128,2048]{1,0:T(8,128)(2,1)S(1)}, u32[]{:S(2)}, u32[]{:S(2)}) collective-permute-start(bf16[128,2048]{1,0:T(8,128)(2,1)S(1)} %get-tuple-element.81), channel_id=1, source_target_pairs={{0,1},{1,0},{2,3},{3,2},{4,5},{5,4},{6,7},{7,6},{8,9},{9,8},{10,11... | collective-permute-start | bytes 1572872 | tf_op jit(solution)/shard_map/ppermute | solution.py:48
  100.3 2.6 %collective-permute-start.24 = (bf16[128,2048]{1,0:T(8,128)(2,1)S(1)}, bf16[128,2048]{1,0:T(8,128)(2,1)S(1)}, u32[]{:S(2)}, u32[]{:S(2)}) collective-permute-start(bf16[128,2048]{1,0:T(8,128)(2,1)S(1)} %get-tuple-element.84), channel_id=1, source_target_pairs={{0,1},{1,0},{2,3},{3,2},{4,5},{5,4},{6,7},{7,6},{8,9},{9,8},{10,11... | collective-permute-start | bytes 1572872 | tf_op jit(solution)/shard_map/ppermute | solution.py:48
  102.3 9.2 %collective-permute-start.23 = (bf16[64,2048]{1,0:T(8,128)(2,1)S(1)}, bf16[64,2048]{1,0:T(8,128)(2,1)S(1)}, u32[]{:S(2)}, u32[]{:S(2)}) collective-permute-start(bf16[64,2048]{1,0:T(8,128)(2,1)S(1)} %add_convert_fusion.1), channel_id=1, source_target_pairs={{0,2},{2,0},{1,3},{3,1},{4,6},{6,4},{5,7},{7,5},{8,10},{10,8},{9,1... | collective-permute-start | bytes 786440 | tf_op jit(solution)/shard_map/ppermute | solution.py:48
  103.0 14.1 %collective-permute-start.25 = (bf16[64,2048]{1,0:T(8,128)(2,1)S(1)}, bf16[64,2048]{1,0:T(8,128)(2,1)S(1)}, u32[]{:S(2)}, u32[]{:S(2)}) collective-permute-start(bf16[64,2048]{1,0:T(8,128)(2,1)S(1)} %add_convert_fusion), channel_id=1, source_target_pairs={{0,2},{2,0},{1,3},{3,1},{4,6},{6,4},{5,7},{7,5},{8,10},{10,8},{9,1... | collective-permute-start | bytes 786440 | tf_op jit(solution)/shard_map/ppermute | solution.py:48
  104.5 13.4 %collective-permute-start.29 = (bf16[256,512]{1,0:T(8,128)(2,1)S(1)}, bf16[256,512]{1,0:T(8,128)(2,1)S(1)}, u32[]{:S(2)}, u32[]{:S(2)}) collective-permute-start(bf16[256,512]{1,0:T(8,128)(2,1)S(1)} %collective-permute-done.16.refs_9_), channel_id=1, source_target_pairs={{0,4},{4,8},{8,12},{12,0},{1,5},{5,9},{9,13},{13,1},{2,6},{6,10},{... | collective-permute-start | bytes 786440 | tf_op jit(solution)/shard_map/ppermute | solution.py:53
  104.5 14.3 %collective-permute-start.27 = (bf16[256,512]{1,0:T(8,128)(2,1)S(1)}, bf16[256,512]{1,0:T(8,128)(2,1)S(1)}, u32[]{:S(2)}, u32[]{:S(2)}) collective-permute-start(bf16[256,512]{1,0:T(8,128)(2,1)S(1)} %collective-permute-done.16.refs_9_), channel_id=1, source_target_pairs={{0,16},{16,0},{1,17},{17,1},{2,18},{18,2},{3,19},{19,3},{4,20},{20... | collective-permute-start | bytes 786440 | tf_op jit(solution)/shard_map/ppermute | solution.py:48
  105.0 14.0 %collective-permute-start.28 = (bf16[256,512]{1,0:T(8,128)(2,1)S(1)}, bf16[256,512]{1,0:T(8,128)(2,1)S(1)}, u32[]{:S(2)}, u32[]{:S(2)}) collective-permute-start(bf16[256,512]{1,0:T(8,128)(2,1)S(1)} %collective-permute-done.17.refs_11_), channel_id=1, source_target_pairs={{0,16},{16,0},{1,17},{17,1},{2,18},{18,2},{3,19},{19,3},{4,20},{20... | collective-permute-start | bytes 786440 | tf_op jit(solution)/shard_map/ppermute | solution.py:48
  111.8 11.0 %collective-permute-start.26 = (bf16[64,2048]{1,0:T(8,128)(2,1)S(1)}, bf16[64,2048]{1,0:T(8,128)(2,1)S(1)}, u32[]{:S(2)}, u32[]{:S(2)}) collective-permute-start(bf16[64,2048]{1,0:T(8,128)(2,1)S(1)} %get-tuple-element.87.refs_0_), channel_id=1, source_target_pairs={{0,2},{2,0},{1,3},{3,1},{4,6},{6,4},{5,7},{7,5},{8,10},{10,8},{9,1... | collective-permute-start | bytes 786440 | tf_op jit(solution)/shard_map/ppermute | solution.py:48
  117.4 10.2 %collective-permute-start.32 = (bf16[64,2048]{1,0:T(8,128)(2,1)S(1)}, bf16[64,2048]{1,0:T(8,128)(2,1)S(1)}, u32[]{:S(2)}, u32[]{:S(2)}) collective-permute-start(bf16[64,2048]{1,0:T(8,128)(2,1)S(1)} %get-tuple-element.92.refs_4_), channel_id=1, source_target_pairs={{0,2},{2,0},{1,3},{3,1},{4,6},{6,4},{5,7},{7,5},{8,10},{10,8},{9,1... | collective-permute-start | bytes 786440 | tf_op jit(solution)/shard_map/ppermute | solution.py:48
  118.0 9.6 %collective-permute-start.33 = (bf16[256,512]{1,0:T(8,128)(2,1)S(1)}, bf16[256,512]{1,0:T(8,128)(2,1)S(1)}, u32[]{:S(2)}, u32[]{:S(2)}) collective-permute-start(bf16[256,512]{1,0:T(8,128)(2,1)S(1)} %collective-permute-done.29.refs_13_), channel_id=1, source_target_pairs={{0,16},{16,0},{1,17},{17,1},{2,18},{18,2},{3,19},{19,3},{4,20},{20... | collective-permute-start | bytes 786440 | tf_op jit(solution)/shard_map/ppermute | solution.py:48
  118.9 8.7 %collective-permute-start.30 = (bf16[64,2048]{1,0:T(8,128)(2,1)S(1)}, bf16[64,2048]{1,0:T(8,128)(2,1)S(1)}, u32[]{:S(2)}, u32[]{:S(2)}) collective-permute-start(bf16[64,2048]{1,0:T(8,128)(2,1)S(1)} %get-tuple-element.87.refs_0_), channel_id=1, source_target_pairs={{0,1},{1,0},{2,3},{3,2},{4,5},{5,4},{6,7},{7,6},{8,9},{9,8},{10,11... | collective-permute-start | bytes 786440 | tf_op jit(solution)/shard_map/ppermute | solution.py:48
  119.0 8.7 %collective-permute-start.34 = (bf16[64,2048]{1,0:T(8,128)(2,1)S(1)}, bf16[64,2048]{1,0:T(8,128)(2,1)S(1)}, u32[]{:S(2)}, u32[]{:S(2)}) collective-permute-start(bf16[64,2048]{1,0:T(8,128)(2,1)S(1)} %get-tuple-element.92.refs_4_), channel_id=1, source_target_pairs={{0,1},{1,0},{2,3},{3,2},{4,5},{5,4},{6,7},{7,6},{8,9},{9,8},{10,11... | collective-permute-start | bytes 786440 | tf_op jit(solution)/shard_map/ppermute | solution.py:48
  122.8 4.9 %collective-permute-start.31 = (bf16[64,2048]{1,0:T(8,128)(2,1)S(1)}, bf16[64,2048]{1,0:T(8,128)(2,1)S(1)}, u32[]{:S(2)}, u32[]{:S(2)}) collective-permute-start(bf16[64,2048]{1,0:T(8,128)(2,1)S(1)} %collective-permute-done.26.refs_1_), channel_id=1, source_target_pairs={{0,1},{1,0},{2,3},{3,2},{4,5},{5,4},{6,7},{7,6},{8,9},{9,8},{10,11... | collective-permute-start | bytes 786440 | tf_op jit(solution)/shard_map/ppermute | solution.py:48
  127.6 1.5 collective-permute-start.35
  127.6 3.9 %copy-start = (bf16[2048,512]{1,0:T(8,128)(2,1)S(1)}, bf16[2048,512]{1,0:T(8,128)(2,1)}, u32[]{:S(2)}) copy-start(bf16[2048,512]{1,0:T(8,128)(2,1)} %query_ref.7) | copy-start | bytes 6291460
  127.6 3.9 %copy-start.5 = (f32[2048]{0:T(1024)S(1)}, f32[2048]{0:T(1024)}, u32[]{:S(2)}) copy-start(f32[2048]{0:T(1024)} %param.29) | copy-start | bytes 24580
  127.6 3.9 %copy-start.6 = (s32[3,16]{1,0:T(4,128)S(1)}, s32[3,16]{1,0:T(4,128)}, u32[]{:S(2)}) copy-start(s32[3,16]{1,0:T(4,128)} %parent_ref.7) | copy-start | bytes 580
  133.4 4.3 %collective-permute-start.36 = (bf16[16,2048]{1,0:T(8,128)(2,1)S(1)}, bf16[16,2048]{1,0:T(8,128)(2,1)S(1)}, u32[]{:S(2)}, u32[]{:S(2)}) collective-permute-start(bf16[16,2048]{1,0:T(8,128)(2,1)S(1)} %get-tuple-element.97.refs_1_), channel_id=1, source_target_pairs={{0,2},{2,0},{1,3},{3,1},{4,6},{6,4},{5,7},{7,5},{8,10},{10,8},{9,1... | collective-permute-start | bytes 196616 | tf_op jit(solution)/shard_map/ppermute | solution.py:48
  133.9 3.8 %collective-permute-start.37 = (bf16[16,2048]{1,0:T(8,128)(2,1)S(1)}, bf16[16,2048]{1,0:T(8,128)(2,1)S(1)}, u32[]{:S(2)}, u32[]{:S(2)}) collective-permute-start(bf16[16,2048]{1,0:T(8,128)(2,1)S(1)} %get-tuple-element.97.refs_1_), channel_id=1, source_target_pairs={{0,1},{1,0},{2,3},{3,2},{4,5},{5,4},{6,7},{7,6},{8,9},{9,8},{10,11... | collective-permute-start | bytes 196616 | tf_op jit(solution)/shard_map/ppermute | solution.py:48
  137.7 1.3 collective-permute-start.38
  141.0 4.3 %collective-permute-start.39 = (bf16[16,2048]{1,0:T(8,128)(2,1)S(1)}, bf16[16,2048]{1,0:T(8,128)(2,1)S(1)}, u32[]{:S(2)}, u32[]{:S(2)}) collective-permute-start(bf16[16,2048]{1,0:T(8,128)(2,1)S(1)} %get-tuple-element.99.refs_1_), channel_id=1, source_target_pairs={{0,2},{2,0},{1,3},{3,1},{4,6},{6,4},{5,7},{7,5},{8,10},{10,8},{9,1... | collective-permute-start | bytes 196616 | tf_op jit(solution)/shard_map/ppermute | solution.py:48
  141.5 3.8 %collective-permute-start.40 = (bf16[16,2048]{1,0:T(8,128)(2,1)S(1)}, bf16[16,2048]{1,0:T(8,128)(2,1)S(1)}, u32[]{:S(2)}, u32[]{:S(2)}) collective-permute-start(bf16[16,2048]{1,0:T(8,128)(2,1)S(1)} %get-tuple-element.99.refs_1_), channel_id=1, source_target_pairs={{0,1},{1,0},{2,3},{3,2},{4,5},{5,4},{6,7},{7,6},{8,9},{9,8},{10,11... | collective-permute-start | bytes 196616 | tf_op jit(solution)/shard_map/ppermute | solution.py:48
  145.3 1.3 collective-permute-start.41
  148.6 4.3 %collective-permute-start.42 = (bf16[16,2048]{1,0:T(8,128)(2,1)S(1)}, bf16[16,2048]{1,0:T(8,128)(2,1)S(1)}, u32[]{:S(2)}, u32[]{:S(2)}) collective-permute-start(bf16[16,2048]{1,0:T(8,128)(2,1)S(1)} %get-tuple-element.101.refs_1_), channel_id=1, source_target_pairs={{0,2},{2,0},{1,3},{3,1},{4,6},{6,4},{5,7},{7,5},{8,10},{10,8},{9,1... | collective-permute-start | bytes 196616 | tf_op jit(solution)/shard_map/ppermute | solution.py:48
  149.1 3.8 %collective-permute-start.43 = (bf16[16,2048]{1,0:T(8,128)(2,1)S(1)}, bf16[16,2048]{1,0:T(8,128)(2,1)S(1)}, u32[]{:S(2)}, u32[]{:S(2)}) collective-permute-start(bf16[16,2048]{1,0:T(8,128)(2,1)S(1)} %get-tuple-element.101.refs_1_), channel_id=1, source_target_pairs={{0,1},{1,0},{2,3},{3,2},{4,5},{5,4},{6,7},{7,6},{8,9},{9,8},{10,11... | collective-permute-start | bytes 196616 | tf_op jit(solution)/shard_map/ppermute | solution.py:48
  152.9 1.3 collective-permute-start.44
  156.2 3.2 %collective-permute-start.47 = (bf16[16,512]{1,0:T(8,128)(2,1)S(1)}, bf16[16,512]{1,0:T(8,128)(2,1)S(1)}, u32[]{:S(2)}, u32[]{:S(2)}) collective-permute-start(bf16[16,512]{1,0:T(8,128)(2,1)S(1)} %get-tuple-element.105), channel_id=1, source_target_pairs={{0,3},{1,2},{2,1},{3,0},{4,7},{5,6},{6,5},{7,4},{8,11},{9,10},{10,... | collective-permute-start | bytes 49160 | tf_op jit(solution)/shard_map/ppermute | solution.py:691
  156.6 3.8 %collective-permute-start.46 = (bf16[16,512]{1,0:T(8,128)(2,1)S(1)}, bf16[16,512]{1,0:T(8,128)(2,1)S(1)}, u32[]{:S(2)}, u32[]{:S(2)}) collective-permute-start(bf16[16,512]{1,0:T(8,128)(2,1)S(1)} %get-tuple-element.104), channel_id=1, source_target_pairs={{0,2},{1,3},{2,0},{3,1},{4,6},{5,7},{6,4},{7,5},{8,10},{9,11},{10,... | collective-permute-start | bytes 49160 | tf_op jit(solution)/shard_map/ppermute | solution.py:691
  158.1 2.2 %collective-permute-start.45 = (bf16[16,512]{1,0:T(8,128)(2,1)S(1)}, bf16[16,512]{1,0:T(8,128)(2,1)S(1)}, u32[]{:S(2)}, u32[]{:S(2)}) collective-permute-start(bf16[16,512]{1,0:T(8,128)(2,1)S(1)} %get-tuple-element.103), channel_id=1, source_target_pairs={{0,1},{1,0},{2,3},{3,2},{4,5},{5,4},{6,7},{7,6},{8,9},{9,8},{10,11... | collective-permute-start | bytes 49160 | tf_op jit(solution)/shard_map/ppermute | solution.py:691

commit v7 on v6

--- a/solution.py
+++ b/solution.py
@@ -431,7 +431,7 @@
         ).astype(jnp.bfloat16)
 
 
-def cross_project(at, row_pieces, pieces):
+def cross_project(at, row_pieces, pieces, name):
     width = row_pieces[0][0].shape[1]
     length = sum(rows.shape[0] for rows, _ in row_pieces)
     cols = pieces[0][0].shape[1]
@@ -449,15 +449,16 @@
         ],
         compiler_params=params(),
         cost_estimate=cost(2),
-        name="cross_project",
+        name=name,
     )(at, *[rows for rows, _ in row_pieces], *[piece for piece, _ in pieces])
 
 
 def beam_kernel(
-    level, count, last, ratio, places,
-    at_ref, live_ref, parent_ref, gain_ref, query_ref, out_weight_ref, cross_ref, code_ref,
+    level, count, last, ratio, places, parts,
+    at_ref, live_ref, parent_ref, gain_ref, query_ref, out_weight_ref, code_ref,
     *refs,
 ):
+    crosses, refs = refs[:parts], refs[parts:]
     inputs, outs, moved = refs[: count + 1 if level else 0], refs[count + 1 if level else 0 : -1], refs[-1]
     beams = code_ref.shape[0]
     code = code_ref[...].astype(jnp.float32)
@@ -474,30 +475,39 @@
     normed = (hidden * lax.rsqrt(square + eps) * gain_ref[...]).astype(jnp.bfloat16)
     queries = jnp.dot(normed, query_ref[...], preferred_element_type=jnp.float32)
     queries = queries.astype(jnp.bfloat16)
-    key_cols = cross_ref.shape[1] // 2
-    events = cross_ref.shape[0]
+    key_cols = crosses[0].shape[1] // 2
     live = live_ref[0] * BLK
+    groups = lax.axis_size("tp") * lax.axis_size("kv")
+    part = crosses[0].shape[0] // groups
     attended = []
     for group in range(key_cols // DH):
         first = group * ratio
         stacked = jnp.concatenate(
             [queries[:, h * DH : (h + 1) * DH] for h in range(first, first + ratio)], axis=0
         )
-        scores = lax.dot_general(
-            stacked,
-            cross_ref[:, group * DH : (group + 1) * DH],
-            (((1,), (1,)), ((), ())),
-            preferred_element_type=jnp.float32,
+        scores = []
+        for index, cross_ref in enumerate(crosses):
+            part_scores = lax.dot_general(
+                stacked,
+                cross_ref[:, group * DH : (group + 1) * DH],
+                (((1,), (1,)), ((), ())),
+                preferred_element_type=jnp.float32,
+            )
+            row = lax.broadcasted_iota(jnp.int32, part_scores.shape, 1)
+            event = row // part * (part * parts) + index * part + row % part
+            scores.append(jnp.where(event < live, part_scores, -1e30))
+        top = functools.reduce(
+            jnp.maximum, [jnp.max(values, axis=-1, keepdims=True) for values in scores]
         )
-        index = lax.broadcasted_iota(jnp.int32, scores.shape, 1)
-        scores = jnp.where(index < live, scores, -1e30)
-        top = jnp.max(scores, axis=-1, keepdims=True)
-        raised = jnp.exp((scores - top) * DH ** (-0.5))
-        weight = jnp.sum(raised, axis=-1, keepdims=True)
-        mixed = jnp.dot(
-            raised.astype(jnp.bfloat16),
-            cross_ref[:, key_cols + group * DH : key_cols + (group + 1) * DH],
-            preferred_element_type=jnp.float32,
+        raised = [jnp.exp((values - top) * DH ** (-0.5)) for values in scores]
+        weight = sum(jnp.sum(values, axis=-1, keepdims=True) for values in raised)
+        mixed = sum(
+            jnp.dot(
+                values.astype(jnp.bfloat16),
+                cross_ref[:, key_cols + group * DH : key_cols + (group + 1) * DH],
+                preferred_element_type=jnp.float32,
+            )
+            for values, cross_ref in zip(raised, crosses)
         )
         mixed = (mixed / weight).astype(jnp.bfloat16)
         attended += [mixed[h * beams : (h + 1) * beams, :] for h in range(ratio)]
@@ -517,7 +527,9 @@
         outs[0][...] = moved[:, pl.ds(pl.multiple_of(places[0](at_ref) * cols, cols), cols)]
 
 
-def beam_step(at, level, live, parents, places, gain, query, out_weight, cross, code, inputs, last):
+def beam_step(
+    at, level, live, parents, places, gain, query, out_weight, crosses, code, inputs, last
+):
     beams, width = code.shape
     ratio = H // KVH
     if last:
@@ -531,15 +543,15 @@
             jax.ShapeDtypeStruct((beams, width), jnp.bfloat16),
         ]
     return pl.pallas_call(
-        functools.partial(beam_kernel, level, max(len(inputs) - 1, 0), last, ratio, places),
+        functools.partial(beam_kernel, level, max(len(inputs) - 1, 0), last, ratio, places, len(crosses)),
         out_shape=tuple(outs),
-        in_specs=[SM, SM, SM] + [VM] * (5 + len(inputs)),
+        in_specs=[SM, SM, SM] + [VM] * (4 + len(crosses) + len(inputs)),
         out_specs=tuple([VM] * len(outs)),
         scratch_shapes=[pltpu.VMEM((beams, width), jnp.float32)],
         compiler_params=params(),
         cost_estimate=cost(4),
         name=f"beam_step_{level}",
-    )(at, live, parents, gain[None, :], query, out_weight, cross, code, *inputs)
+    )(at, live, parents, gain[None, :], query, out_weight, code, *crosses, *inputs)
 
 
 def shards(
@@ -656,16 +668,16 @@
     if ringed:
         cross.swap(merged[-1][1])
         cross_pieces = cross.pieces
-    crossed_pieces = []
+    keys_values = []
     for index, (_, crossed) in enumerate(merged):
         waits = late if index == 0 else []
         if ringed and index == parts - 1:
             waits = [*waits, cross_pieces[-1][0]]
-        for rows, where in gather_heads(crossed, waits):
-            crossed_pieces.append(
-                (rows, [functools.partial(lambda f, i, at: f(at) * share + i, where, index * part)])
-            )
-    keys_values = cross_project(at, crossed_pieces, cross_pieces)
+        crossed_pieces = [
+            (rows, [functools.partial(lambda f, at: f(at) * part, where)])
+            for rows, where in gather_heads(crossed, waits)
+        ]
+        keys_values.append(cross_project(at, crossed_pieces, cross_pieces, f"cross_project_{index}"))
 
     places = [functools.partial(place, 0, 0)]
     moves = []

time: 161 us -> 161 us (level)
    pallas_call x1 -> x2, Pallas kernels: 2.34 us -> 3.33 us  [cross_project(): pl.pallas_call(functools.partial(cross_kernel, [places for _, places in r...]
  transfers between devices with their start and end apart: 48 -> 48, of which waited for: 26 -> 26; matrix products, arithmetic and copies ran while one was open for 6% -> 6% of each run, Pallas kernels for 7% -> 8%
where the time goes in v7:
time: 161 us
  waiting for transfers between devices  82.5 us (51%)
  starting transfers between devices  38.2 us (24%)
  Pallas kernels  24.4 us (15%)
  local copies, waits for them, and re-layouts  6.84 us (4%)
  other arithmetic  3.92 us (2%)
  matrix products  3.09 us (2%)
  between operations  1.79 us (1%)
    ppermute x33, waiting for transfers between devices, exchange(): lax.ppermute(value, axis, [(i, partner(i, step, size)) for i in range(siz...  49.9 us
    ppermute x12, waiting for transfers between devices, shift(): lax.ppermute(value, axis, [(i, (i + step) % size) for i in range(size)])  31.2 us
    ppermute x33, starting transfers between devices, exchange(): lax.ppermute(value, axis, [(i, partner(i, step, size)) for i in range(siz...  19.2 us
    ppermute x12, starting transfers between devices, shift(): lax.ppermute(value, axis, [(i, (i + step) % size) for i in range(size)])  17.1 us
    pallas_call x4, Pallas kernels, beam_step(): pl.pallas_call(functools.partial(beam_kernel, level, max(len(inputs) - 1,...  8.15 us
    pallas_call x1, Pallas kernels, encoder_attention(): pl.pallas_call(functools.partial(encoder_kernel, [places for _, places in...  7.98 us
    pallas_call x2, Pallas kernels, cross_project(): pl.pallas_call(functools.partial(cross_kernel, [places for _, places in r...  3.33 us
  transfers between devices with their start and end apart: 48, of which 26 were waited for; matrix products, arithmetic and copies ran while one was open for 6% of the time, Pallas kernels for 8%

profile of v7, /device:TPU:0, one launch (start us, length us, event | category | flops | bytes accessed | tf_op | source)
XLA Modules:
  0.0 160.7 jit_solution(10446362760227470717)
XLA Ops:
  0.7 1.9 %slice_bitcast_fusion.3 = (bf16[512,256]{1,0:T(8,128)(2,1)}, bf16[512,256]{1,0:T(8,128)(2,1)}, bf16[1,512,256]{2,1,0:T(8,128)(2,1)S(1)}, bf16[1,512,256]{2,1,0:T(8,128)(2,1)S(1)}) fusion(bf16[2,512,256]{2,1,0:T(8,128)(2,1)} %param.21), kind=kLoop, calls=%fused_computation.26 | loop fusion | bytes 1572864 | tf_op jit(solution)/shard_map/squeeze | solution.py:579
  2.6 1.0 constant_dynamic-slice_fusion.1
  3.7 3.1 %collective-permute-start.1 = (bf16[256,1024]{1,0:T(8,128)(2,1)S(1)}, bf16[256,1024]{1,0:T(8,128)(2,1)}, u32[]{:S(2)}, u32[]{:S(2)}) collective-permute-start(bf16[256,1024]{1,0:T(8,128)(2,1)S(1)} %pad_maximum_fusion.2), channel_id=1, source_target_pairs={{0,4},{4,8},{8,12},{12,0},{1,5},{5,9},{9,13},{13,1},{2,6},{6,10},{... | collective-permute-start | bytes 1572872 | tf_op jit(solution)/shard_map/ppermute | solution.py:53
  6.8 1.6 %collective-permute-start = (bf16[128,512]{1,0:T(8,128)(2,1)S(1)}, bf16[128,512]{1,0:T(8,128)(2,1)S(1)}, u32[]{:S(2)}, u32[]{:S(2)}) collective-permute-start(bf16[128,512]{1,0:T(8,128)(2,1)S(1)} %get-tuple-element.113), channel_id=1, source_target_pairs={{0,4},{4,8},{8,12},{12,0},{1,5},{5,9},{9,13},{13,1},{2,6},{6,10},{... | collective-permute-start | bytes 393224 | tf_op jit(solution)/shard_map/ppermute | solution.py:53
  8.4 2.2 %collective-permute-start.3 = (bf16[128,512]{1,0:T(8,128)(2,1)S(1)}, bf16[128,512]{1,0:T(8,128)(2,1)S(1)}, u32[]{:S(2)}, u32[]{:S(2)}) collective-permute-start(bf16[128,512]{1,0:T(8,128)(2,1)S(1)} %get-tuple-element.114), channel_id=1, source_target_pairs={{0,12},{4,0},{8,4},{12,8},{1,13},{5,1},{9,5},{13,9},{2,14},{6,2},{... | collective-permute-start | bytes 393224 | tf_op jit(solution)/shard_map/ppermute | solution.py:53
  10.7 0.8 collective-permute-start.2
  11.5 12.8 %collective-permute-done = bf16[128,512]{1,0:T(8,128)(2,1)S(1)} collective-permute-done((bf16[128,512]{1,0:T(8,128)(2,1)S(1)}, bf16[128,512]{1,0:T(8,128)(2,1)S(1)}, u32[]{:S(2)}, u32[]{:S(2)}) %collective-permute-start) | collective-permute-done | bytes 131104 | tf_op jit(solution)/shard_map/ppermute | solution.py:53
  24.4 1.8 %collective-permute-start.7 = (bf16[256,1024]{1,0:T(8,128)(2,1)}, bf16[256,1024]{1,0:T(8,128)(2,1)S(1)}, u32[]{:S(2)}, u32[]{:S(2)}) collective-permute-start(bf16[256,1024]{1,0:T(8,128)(2,1)} %collective-permute-done.1.refs_1_), channel_id=1, source_target_pairs={{0,16},{16,0},{1,17},{17,1},{2,18},{18,2},{3,19},{19,3},{4,20},{20... | collective-permute-start | bytes 1572872 | tf_op jit(solution)/shard_map/ppermute | solution.py:48
  26.3 5.6 %collective-permute-done.2 = bf16[128,512]{1,0:T(8,128)(2,1)S(1)} collective-permute-done((bf16[128,512]{1,0:T(8,128)(2,1)S(1)}, bf16[128,512]{1,0:T(8,128)(2,1)S(1)}, u32[]{:S(2)}, u32[]{:S(2)}) %collective-permute-start.2) | collective-permute-done | bytes 131104 | tf_op jit(solution)/shard_map/ppermute | solution.py:53
  32.0 1.6 collective-permute-start.4
  33.5 1.6 %collective-permute-start.8 = (bf16[256,1024]{1,0:T(8,128)(2,1)S(1)}, bf16[256,1024]{1,0:T(8,128)(2,1)}, u32[]{:S(2)}, u32[]{:S(2)}) collective-permute-start(bf16[256,1024]{1,0:T(8,128)(2,1)S(1)} %pad_maximum_fusion.2), channel_id=1, source_target_pairs={{0,12},{4,0},{8,4},{12,8},{1,13},{5,1},{9,5},{13,9},{2,14},{6,2},{... | collective-permute-start | bytes 1572872 | tf_op jit(solution)/shard_map/ppermute | solution.py:53
  35.3 3.1 %convolution_convert_fusion = bf16[64,2048]{1,0:T(8,128)(2,1)S(1)} fusion(bf16[64,1024]{1,0:T(8,128)(2,1)S(1)} %compare_convert_fusion, bf16[1024,2048]{1,0:T(8,128)(2,1)} %param.26), kind=kOutput, calls=%fused_computation | convolution fusion | flops 268566528 | bytes 4587520 | tf_op jit(solution)/shard_map/dot_general | solution.py:589
  38.4 0.5 collective-permute-start.5
  38.9 6.9 %collective-permute-done.4.refs_1_ = bf16[512,512]{1,0:T(8,128)(2,1)S(1)} collective-permute-done((bf16[512,512]{1,0:T(8,128)(2,1)S(1)}, bf16[512,512]{1,0:T(8,128)(2,1)S(1)}, u32[]{:S(2)}, u32[]{:S(2)}) %collective-permute-start.4) | collective-permute-done | bytes 524320 | tf_op jit(solution)/shard_map/ppermute | solution.py:48
  45.9 1.3 collective-permute-done.8.refs_3_
  47.2 1.5 collective-permute-start.9
  48.7 0.8 add.88
  49.5 0.5 collective-permute-start.12
  50.1 0.7 slice_bitcast_fusion
  50.9 2.9 %copy.17 = bf16[2048,512]{0,1:T(8,128)(2,1)S(1)} copy(bf16[2048,512]{1,0:T(8,128)(2,1)} %param.25) | data formatting | bytes 4194304 | tf_op jit(solution)/shard_map/optimization_barrier | solution.py:57
  53.9 3.1 %collective-permute-done.12 = bf16[64,2048]{1,0:T(8,128)(2,1)} collective-permute-done((bf16[64,2048]{1,0:T(8,128)(2,1)}, bf16[64,2048]{1,0:T(8,128)(2,1)}, u32[]{:S(2)}, u32[]{:S(2)}) %collective-permute-start.12) | collective-permute-done | bytes 262176 | tf_op jit(solution)/shard_map/ppermute | solution.py:48
  57.0 1.1 add.89
  58.1 2.4 %norm_events.1 = (bf16[512,2048]{1,0:T(8,128)(2,1)S(1)}, bf16[128,2048]{1,0:T(8,128)(2,1)S(1)}) custom-call(s32[4]{0:T(128)S(1)} %pad_add_fusion.at_ref, f32[1,2048]{1,0:T(1,128)S(1)} %bitcast.48, bf16[512,512]{1,0:T(8,128)(2,1)S(1)} %pad_maximum_fusion.3.refs_0_, bf16[512,512]{1,0:T(8,128)(2,1)S(1)} %collective-permute-done.4.refs_1_, ...), custom_call_target="tpu_custom_call" | custom-call | bytes 12000000 | tf_op jit(solution)/shard_map/norm_events/pallas_call | solution.py:206
  60.6 3.0 %collective-permute-done.10.refs_5_ = bf16[256,1024]{1,0:T(8,128)(2,1)} collective-permute-done((bf16[256,1024]{1,0:T(8,128)(2,1)}, bf16[256,1024]{1,0:T(8,128)(2,1)}, u32[]{:S(2)}, u32[]{:S(2)}) %collective-permute-start.10) | collective-permute-done | bytes 524320 | tf_op jit(solution)/shard_map/ppermute | solution.py:53
  63.6 0.5 collective-permute-start.13
  64.3 3.8 %collective-permute-start.15 = (bf16[256,512]{1,0:T(8,128)(2,1)S(1)}, bf16[256,512]{1,0:T(8,128)(2,1)S(1)}, u32[]{:S(2)}, u32[]{:S(2)}) collective-permute-start(bf16[256,512]{1,0:T(8,128)(2,1)S(1)} %get-tuple-element.66), channel_id=1, source_target_pairs={{0,12},{4,0},{8,4},{12,8},{1,13},{5,1},{9,5},{13,9},{2,14},{6,2},{... | collective-permute-start | bytes 786440 | tf_op jit(solution)/shard_map/ppermute | solution.py:53
  68.1 7.3 %collective-permute-done.14.refs_1_ = bf16[256,512]{1,0:T(8,128)(2,1)S(1)} collective-permute-done((bf16[256,512]{1,0:T(8,128)(2,1)S(1)}, bf16[256,512]{1,0:T(8,128)(2,1)S(1)}, u32[]{:S(2)}, u32[]{:S(2)}) %collective-permute-start.14) | collective-permute-done | bytes 262176 | tf_op jit(solution)/shard_map/ppermute | solution.py:53
  76.2 1.6 collective-permute-start.18
  77.8 2.1 %collective-permute-start.19 = (bf16[256,512]{1,0:T(8,128)(2,1)S(1)}, bf16[256,512]{1,0:T(8,128)(2,1)S(1)}, u32[]{:S(2)}, u32[]{:S(2)}) collective-permute-start(bf16[256,512]{1,0:T(8,128)(2,1)S(1)} %collective-permute-done.15.refs_3_), channel_id=1, source_target_pairs={{0,16},{16,0},{1,17},{17,1},{2,18},{18,2},{3,19},{19,3},{4,20},{20... | collective-permute-start | bytes 786440 | tf_op jit(solution)/shard_map/ppermute | solution.py:48
  79.9 3.8 %collective-permute-start.17 = (bf16[256,512]{1,0:T(8,128)(2,1)S(1)}, bf16[256,512]{1,0:T(8,128)(2,1)S(1)}, u32[]{:S(2)}, u32[]{:S(2)}) collective-permute-start(bf16[256,512]{1,0:T(8,128)(2,1)S(1)} %get-tuple-element.75), channel_id=1, source_target_pairs={{0,12},{4,0},{8,4},{12,8},{1,13},{5,1},{9,5},{13,9},{2,14},{6,2},{... | collective-permute-start | bytes 786440 | tf_op jit(solution)/shard_map/ppermute | solution.py:53
  83.7 8.0 %encoder_attention.1.attended_ref = bf16[512,512]{1,0:T(8,128)(2,1)S(1)} custom-call(s32[4]{0:T(128)S(1)} %pad_add_fusion.at_ref, s32[1]{0:T(128)S(6)} %copy.18.live_ref, bf16[512,2048]{1,0:T(8,128)(2,1)S(1)} %get-tuple-element.67.rows_ref, bf16[2,512,256]{2,1,0:T(8,128)(2,1)S(1)} %bitcast.39, bf16[512,1024]{1,0:T(8,128)(2,1)S(1)} %pad_maximum_fusion.refs_0_, ...), custom_call_target="tpu_custom_call" | custom-call | bytes 33000000 | tf_op jit(solution)/shard_map/encoder_attention/pallas_call | solution.py:322
  91.8 1.0 collective-permute-done.17.refs_7_
  92.8 5.3 %collective-permute-done.21.refs_6_ = bf16[256,512]{1,0:T(8,128)(2,1)S(1)} collective-permute-done((bf16[256,512]{1,0:T(8,128)(2,1)S(1)}, bf16[256,512]{1,0:T(8,128)(2,1)S(1)}, u32[]{:S(2)}, u32[]{:S(2)}) %collective-permute-start.21) | collective-permute-done | bytes 262176 | tf_op jit(solution)/shard_map/ppermute | solution.py:48
  98.1 2.1 %project_out.1 = (bf16[128,2048]{1,0:T(8,128)(2,1)S(1)}, bf16[128,2048]{1,0:T(8,128)(2,1)S(1)}, bf16[128,2048]{1,0:T(8,128)(2,1)S(1)}, bf16[128,2048]{1,0:T(8,128)(2,1)S(1)}) custom-call(s32[4]{0:T(128)S(1)} %pad_add_fusion.at_ref, bf16[512,512]{1,0:T(8,128)(2,1)S(1)} %encoder_attention.1.attended_ref, bf16[512,512]{1,0:T(8,128)(2,1)S(1)} %copy-done.1, ...), custom_call_target="tpu_custom_call" | custom-call | bytes 6000000 | tf_op jit(solution)/shard_map/project_out/pallas_call | solution.py:378
  100.8 1.4 collective-permute-done.22.refs_1_
  102.3 0.6 collective-permute-start.23
  103.0 1.5 collective-permute-start.25
  105.0 1.5 collective-permute-start.28
  106.6 5.0 %collective-permute-done.23 = bf16[64,2048]{1,0:T(8,128)(2,1)S(1)} collective-permute-done((bf16[64,2048]{1,0:T(8,128)(2,1)S(1)}, bf16[64,2048]{1,0:T(8,128)(2,1)S(1)}, u32[]{:S(2)}, u32[]{:S(2)}) %collective-permute-start.23) | collective-permute-done | bytes 262176 | tf_op jit(solution)/shard_map/ppermute | solution.py:48
  111.8 0.6 collective-permute-start.26
  112.3 4.8 %collective-permute-done.25 = bf16[64,2048]{1,0:T(8,128)(2,1)S(1)} collective-permute-done((bf16[64,2048]{1,0:T(8,128)(2,1)S(1)}, bf16[64,2048]{1,0:T(8,128)(2,1)S(1)}, u32[]{:S(2)}, u32[]{:S(2)}) %collective-permute-start.25) | collective-permute-done | bytes 262176 | tf_op jit(solution)/shard_map/ppermute | solution.py:48
  117.5 1.4 collective-permute-start.33
  119.5 3.3 %collective-permute-done.26.refs_1_ = bf16[64,2048]{1,0:T(8,128)(2,1)S(1)} collective-permute-done((bf16[64,2048]{1,0:T(8,128)(2,1)S(1)}, bf16[64,2048]{1,0:T(8,128)(2,1)S(1)}, u32[]{:S(2)}, u32[]{:S(2)}) %collective-permute-start.26) | collective-permute-done | bytes 262176 | tf_op jit(solution)/shard_map/ppermute | solution.py:48
  122.7 1.4 collective-permute-done.32.refs_10_
  124.2 3.4 %collective-permute-done.33.refs_1_ = bf16[64,2048]{1,0:T(8,128)(2,1)S(1)} collective-permute-done((bf16[64,2048]{1,0:T(8,128)(2,1)S(1)}, bf16[64,2048]{1,0:T(8,128)(2,1)S(1)}, u32[]{:S(2)}, u32[]{:S(2)}) %collective-permute-start.33) | collective-permute-done | bytes 262176 | tf_op jit(solution)/shard_map/ppermute | solution.py:48
  127.6 1.7 %cross_project_0.1.refs_0_ = bf16[256,512]{1,0:T(8,128)(2,1)S(1)} custom-call(s32[4]{0:T(128)S(1)} %pad_add_fusion.at_ref, bf16[64,2048]{1,0:T(8,128)(2,1)S(1)} %get-tuple-element.88.refs_0_, bf16[64,2048]{1,0:T(8,128)(2,1)S(1)} %collective-permute-done.26.refs_1_, bf16[64,2048]{1,0:T(8,128)(2,1)S(1)} %collective-permute-done.30.refs_2_, ...), custom_call_target="tpu_custom_call" | custom-call | bytes 6000000 | tf_op jit(solution)/shard_map/cross_project_0/pallas_call | solution.py:438
  129.3 1.7 %cross_project_1.1.refs_1_ = bf16[256,512]{1,0:T(8,128)(2,1)S(1)} custom-call(s32[4]{0:T(128)S(1)} %pad_add_fusion.at_ref, bf16[64,2048]{1,0:T(8,128)(2,1)S(1)} %get-tuple-element.93.refs_0_, bf16[64,2048]{1,0:T(8,128)(2,1)S(1)} %collective-permute-done.33.refs_1_, bf16[64,2048]{1,0:T(8,128)(2,1)S(1)} %collective-permute-done.34.refs_2_, ...), custom_call_target="tpu_custom_call" | custom-call | bytes 6000000 | tf_op jit(solution)/shard_map/cross_project_1/pallas_call | solution.py:438
  131.0 1.9 %beam_step_0.1 = (f32[16,2048]{1,0:T(8,128)S(1)}, bf16[16,2048]{1,0:T(8,128)(2,1)S(1)}) custom-call(s32[4]{0:T(128)S(1)} %pad_add_fusion.at_ref, s32[1]{0:T(128)S(6)} %copy.18.live_ref, s32[3,16]{1,0:T(4,128)S(1)} %copy-done.6, f32[1,2048]{1,0:T(1,128)S(1)} %bitcast.42, bf16[2048,512]{1,0:T(8,128)(2,1)S(1)} %copy-done, bf16[512,2048]{1,0:T(8,128)(2,1)S(1)} %bitcast.35, ...), custom_call_target="tpu_custom_call" | custom-call | bytes 12000000 | tf_op jit(solution)/shard_map/beam_step_0/pallas_call | solution.py:545
  133.0 0.5 collective-permute-start.36
  133.7 3.8 %collective-permute-done.36.refs_4_ = bf16[16,2048]{1,0:T(8,128)(2,1)S(1)} collective-permute-done((bf16[16,2048]{1,0:T(8,128)(2,1)S(1)}, bf16[16,2048]{1,0:T(8,128)(2,1)S(1)}, u32[]{:S(2)}, u32[]{:S(2)}) %collective-permute-start.36) | collective-permute-done | bytes 65568 | tf_op jit(solution)/shard_map/ppermute | solution.py:48
  137.5 1.2 collective-permute-done.38.refs_6_
  138.7 2.1 %beam_step_1.1 = (f32[16,2048]{1,0:T(8,128)S(1)}, bf16[16,2048]{1,0:T(8,128)(2,1)S(1)}) custom-call(s32[4]{0:T(128)S(1)} %pad_add_fusion.at_ref, s32[1]{0:T(128)S(6)} %copy.18.live_ref, s32[3,16]{1,0:T(4,128)S(1)} %copy-done.6, f32[1,2048]{1,0:T(1,128)S(1)} %bitcast.43, bf16[2048,512]{1,0:T(8,128)(2,1)S(1)} %copy-done, bf16[512,2048]{1,0:T(8,128)(2,1)S(1)} %bitcast.36, ...), custom_call_target="tpu_custom_call" | custom-call | bytes 12000000 | tf_op jit(solution)/shard_map/beam_step_1/pallas_call | solution.py:545
  140.8 0.5 collective-permute-start.39
  141.3 3.8 %collective-permute-done.39.refs_4_ = bf16[16,2048]{1,0:T(8,128)(2,1)S(1)} collective-permute-done((bf16[16,2048]{1,0:T(8,128)(2,1)S(1)}, bf16[16,2048]{1,0:T(8,128)(2,1)S(1)}, u32[]{:S(2)}, u32[]{:S(2)}) %collective-permute-start.39) | collective-permute-done | bytes 65568 | tf_op jit(solution)/shard_map/ppermute | solution.py:48
  145.1 1.2 collective-permute-done.41.refs_6_
  146.3 2.1 %beam_step_2.1 = (f32[16,2048]{1,0:T(8,128)S(1)}, bf16[16,2048]{1,0:T(8,128)(2,1)S(1)}) custom-call(s32[4]{0:T(128)S(1)} %pad_add_fusion.at_ref, s32[1]{0:T(128)S(6)} %copy.18.live_ref, s32[3,16]{1,0:T(4,128)S(1)} %copy-done.6, f32[1,2048]{1,0:T(1,128)S(1)} %bitcast.44, bf16[2048,512]{1,0:T(8,128)(2,1)S(1)} %copy-done, bf16[512,2048]{1,0:T(8,128)(2,1)S(1)} %bitcast.37, ...), custom_call_target="tpu_custom_call" | custom-call | bytes 12000000 | tf_op jit(solution)/shard_map/beam_step_2/pallas_call | solution.py:545
  148.4 0.5 collective-permute-start.42
  148.9 3.8 %collective-permute-done.42.refs_4_ = bf16[16,2048]{1,0:T(8,128)(2,1)S(1)} collective-permute-done((bf16[16,2048]{1,0:T(8,128)(2,1)S(1)}, bf16[16,2048]{1,0:T(8,128)(2,1)S(1)}, u32[]{:S(2)}, u32[]{:S(2)}) %collective-permute-start.42) | collective-permute-done | bytes 65568 | tf_op jit(solution)/shard_map/ppermute | solution.py:48
  152.7 1.2 collective-permute-done.44.refs_6_
  153.9 2.1 %beam_step_3.1 = (f32[16,512]{1,0:T(8,128)S(1)}, bf16[16,512]{1,0:T(8,128)(2,1)S(1)}, bf16[16,512]{1,0:T(8,128)(2,1)S(1)}, bf16[16,512]{1,0:T(8,128)(2,1)S(1)}) custom-call(s32[4]{0:T(128)S(1)} %pad_add_fusion.at_ref, s32[1]{0:T(128)S(6)} %copy.18.live_ref, s32[3,16]{1,0:T(4,128)S(1)} %copy-done.6, f32[1,2048]{1,0:T(1,128)S(1)} %bitcast.45, ...), custom_call_target="tpu_custom_call" | custom-call | bytes 12000000 | tf_op jit(solution)/shard_map/beam_step_3/pallas_call | solution.py:545
  156.4 1.5 collective-permute-start.46
  158.0 0.8 maximum_bitcast_fusion
  159.3 0.9 collective-permute-done.46
  160.1 0.6 add_convert_fusion.2
  (98 shorter events, 4.7 us)
Async XLA Ops:
  0.6 6.1 %copy-start.13 = (bf16[4,128,512]{2,1,0:T(8,128)(2,1)S(1)}, bf16[4,128,512]{2,1,0:T(8,128)(2,1)}, u32[]{:S(2)}) copy-start(bf16[4,128,512]{2,1,0:T(8,128)(2,1)} %param.15) | copy-start | bytes 1572868
  0.6 10.8 %copy-start.15 = (s32[4,16]{1,0:T(4,128)S(1)}, s32[4,16]{1,0:T(4,128)}, u32[]{:S(2)}) copy-start(s32[4,16]{1,0:T(4,128)} %param.18) | copy-start | bytes 772
  3.7 20.7 %collective-permute-start.1 = (bf16[256,1024]{1,0:T(8,128)(2,1)S(1)}, bf16[256,1024]{1,0:T(8,128)(2,1)}, u32[]{:S(2)}, u32[]{:S(2)}) collective-permute-start(bf16[256,1024]{1,0:T(8,128)(2,1)S(1)} %pad_maximum_fusion.2), channel_id=1, source_target_pairs={{0,4},{4,8},{8,12},{12,0},{1,5},{5,9},{9,13},{13,1},{2,6},{6,10},{... | collective-permute-start | bytes 1572872 | tf_op jit(solution)/shard_map/ppermute | solution.py:53
  6.8 17.6 %collective-permute-start = (bf16[128,512]{1,0:T(8,128)(2,1)S(1)}, bf16[128,512]{1,0:T(8,128)(2,1)S(1)}, u32[]{:S(2)}, u32[]{:S(2)}) collective-permute-start(bf16[128,512]{1,0:T(8,128)(2,1)S(1)} %get-tuple-element.113), channel_id=1, source_target_pairs={{0,4},{4,8},{8,12},{12,0},{1,5},{5,9},{9,13},{13,1},{2,6},{6,10},{... | collective-permute-start | bytes 393224 | tf_op jit(solution)/shard_map/ppermute | solution.py:53
  8.4 17.9 %collective-permute-start.3 = (bf16[128,512]{1,0:T(8,128)(2,1)S(1)}, bf16[128,512]{1,0:T(8,128)(2,1)S(1)}, u32[]{:S(2)}, u32[]{:S(2)}) collective-permute-start(bf16[128,512]{1,0:T(8,128)(2,1)S(1)} %get-tuple-element.114), channel_id=1, source_target_pairs={{0,12},{4,0},{8,4},{12,8},{1,13},{5,1},{9,5},{13,9},{2,14},{6,2},{... | collective-permute-start | bytes 393224 | tf_op jit(solution)/shard_map/ppermute | solution.py:53
  10.7 21.3 %collective-permute-start.2 = (bf16[128,512]{1,0:T(8,128)(2,1)S(1)}, bf16[128,512]{1,0:T(8,128)(2,1)S(1)}, u32[]{:S(2)}, u32[]{:S(2)}) collective-permute-start(bf16[128,512]{1,0:T(8,128)(2,1)S(1)} %get-tuple-element.115), channel_id=1, source_target_pairs={{0,8},{4,12},{8,0},{12,4},{1,9},{5,13},{9,1},{13,5},{2,10},{6,14},... | collective-permute-start | bytes 393224 | tf_op jit(solution)/shard_map/ppermute | solution.py:53
  24.4 21.5 %collective-permute-start.7 = (bf16[256,1024]{1,0:T(8,128)(2,1)}, bf16[256,1024]{1,0:T(8,128)(2,1)S(1)}, u32[]{:S(2)}, u32[]{:S(2)}) collective-permute-start(bf16[256,1024]{1,0:T(8,128)(2,1)} %collective-permute-done.1.refs_1_), channel_id=1, source_target_pairs={{0,16},{16,0},{1,17},{17,1},{2,18},{18,2},{3,19},{19,3},{4,20},{20... | collective-permute-start | bytes 1572872 | tf_op jit(solution)/shard_map/ppermute | solution.py:48
  32.0 13.9 %collective-permute-start.4 = (bf16[512,512]{1,0:T(8,128)(2,1)S(1)}, bf16[512,512]{1,0:T(8,128)(2,1)S(1)}, u32[]{:S(2)}, u32[]{:S(2)}) collective-permute-start(bf16[512,512]{1,0:T(8,128)(2,1)S(1)} %pad_maximum_fusion.3.refs_0_), channel_id=1, source_target_pairs={{0,2},{2,0},{1,3},{3,1},{4,6},{6,4},{5,7},{7,5},{8,10},{10,8},{9,1... | collective-permute-start | bytes 1572872 | tf_op jit(solution)/shard_map/ppermute | solution.py:48
  33.5 13.7 %collective-permute-start.8 = (bf16[256,1024]{1,0:T(8,128)(2,1)S(1)}, bf16[256,1024]{1,0:T(8,128)(2,1)}, u32[]{:S(2)}, u32[]{:S(2)}) collective-permute-start(bf16[256,1024]{1,0:T(8,128)(2,1)S(1)} %pad_maximum_fusion.2), channel_id=1, source_target_pairs={{0,12},{4,0},{8,4},{12,8},{1,13},{5,1},{9,5},{13,9},{2,14},{6,2},{... | collective-permute-start | bytes 1572872 | tf_op jit(solution)/shard_map/ppermute | solution.py:53
  35.2 14.9 %copy-start.14 = (bf16[2,512,256]{2,1,0:T(8,128)(2,1)S(1)}, bf16[2,512,256]{2,1,0:T(8,128)(2,1)}, u32[]{:S(2)}) copy-start(bf16[2,512,256]{2,1,0:T(8,128)(2,1)} %param.23) | copy-start | bytes 1572868
  38.4 10.4 %collective-permute-start.11 = (bf16[64,2048]{1,0:T(8,128)(2,1)S(1)}, bf16[64,2048]{1,0:T(8,128)(2,1)S(1)}, u32[]{:S(2)}, u32[]{:S(2)}) collective-permute-start(bf16[64,2048]{1,0:T(8,128)(2,1)S(1)} %convolution_convert_fusion), channel_id=1, source_target_pairs={{0,1},{1,0},{2,3},{3,2},{4,5},{5,4},{6,7},{7,6},{8,9},{9,8},{10,11... | collective-permute-start | bytes 786440 | tf_op jit(solution)/shard_map/ppermute | solution.py:48
  38.4 19.7 %collective-permute-start.5 = (bf16[512,512]{1,0:T(8,128)(2,1)S(1)}, bf16[512,512]{1,0:T(8,128)(2,1)}, u32[]{:S(2)}, u32[]{:S(2)}) collective-permute-start(bf16[512,512]{1,0:T(8,128)(2,1)S(1)} %pad_maximum_fusion.3.refs_0_), channel_id=1, source_target_pairs={{0,1},{1,0},{2,3},{3,2},{4,5},{5,4},{6,7},{7,6},{8,9},{9,8},{10,11... | collective-permute-start | bytes 1572872 | tf_op jit(solution)/shard_map/ppermute | solution.py:48
  45.9 12.2 %collective-permute-start.6 = (bf16[512,512]{1,0:T(8,128)(2,1)S(1)}, bf16[512,512]{1,0:T(8,128)(2,1)}, u32[]{:S(2)}, u32[]{:S(2)}) collective-permute-start(bf16[512,512]{1,0:T(8,128)(2,1)S(1)} %collective-permute-done.4.refs_1_), channel_id=1, source_target_pairs={{0,1},{1,0},{2,3},{3,2},{4,5},{5,4},{6,7},{7,6},{8,9},{9,8},{10,11... | collective-permute-start | bytes 1572872 | tf_op jit(solution)/shard_map/ppermute | solution.py:48
  45.9 4.2 %copy-start.3 = (bf16[256,1024]{1,0:T(8,128)(2,1)}, bf16[256,1024]{1,0:T(8,128)(2,1)S(1)}, u32[]{:S(2)}) copy-start(bf16[256,1024]{1,0:T(8,128)(2,1)S(1)} %collective-permute-done.7.refs_2_) | copy-start | bytes 1572868
  47.2 13.4 %collective-permute-start.9 = (bf16[256,1024]{1,0:T(8,128)(2,1)}, bf16[256,1024]{1,0:T(8,128)(2,1)}, u32[]{:S(2)}, u32[]{:S(2)}) collective-permute-start(bf16[256,1024]{1,0:T(8,128)(2,1)} %collective-permute-done.8.refs_3_), channel_id=1, source_target_pairs={{0,16},{16,0},{1,17},{17,1},{2,18},{18,2},{3,19},{19,3},{4,20},{20... | collective-permute-start | bytes 1572872 | tf_op jit(solution)/shard_map/ppermute | solution.py:48
  48.7 14.9 %collective-permute-start.10 = (bf16[256,1024]{1,0:T(8,128)(2,1)}, bf16[256,1024]{1,0:T(8,128)(2,1)}, u32[]{:S(2)}, u32[]{:S(2)}) collective-permute-start(bf16[256,1024]{1,0:T(8,128)(2,1)} %collective-permute-done.1.refs_1_), channel_id=1, source_target_pairs={{0,4},{4,8},{8,12},{12,0},{1,5},{5,9},{9,13},{13,1},{2,6},{6,10},{... | collective-permute-start | bytes 1572872 | tf_op jit(solution)/shard_map/ppermute | solution.py:53
  49.5 7.5 %collective-permute-start.12 = (bf16[64,2048]{1,0:T(8,128)(2,1)}, bf16[64,2048]{1,0:T(8,128)(2,1)}, u32[]{:S(2)}, u32[]{:S(2)}) collective-permute-start(bf16[64,2048]{1,0:T(8,128)(2,1)} %add.88), channel_id=1, source_target_pairs={{0,2},{2,0},{1,3},{3,1},{4,6},{6,4},{5,7},{7,5},{8,10},{10,8},{9,1... | collective-permute-start | bytes 786440 | tf_op jit(solution)/shard_map/ppermute | solution.py:48
  50.9 7.3 %copy-start.8 = (f32[2048]{0:T(1024)S(1)}, f32[2048]{0:T(1024)}, u32[]{:S(2)}) copy-start(f32[2048]{0:T(1024)} %param.27) | copy-start | bytes 24580
  53.8 10.3 %copy-start.1 = (bf16[512,512]{1,0:T(8,128)(2,1)S(1)}, bf16[512,512]{1,0:T(8,128)(2,1)}, u32[]{:S(2)}) copy-start(bf16[512,512]{1,0:T(8,128)(2,1)} %refs_0_.1) | copy-start | bytes 1572868
  53.8 10.3 %copy-start.9 = (bf16[512,256]{1,0:T(8,128)(2,1)S(1)}, bf16[512,256]{1,0:T(8,128)(2,1)}, u32[]{:S(2)}) copy-start(bf16[512,256]{1,0:T(8,128)(2,1)} %get-tuple-element.107) | copy-start | bytes 786436
  53.8 22.2 %copy-start.10 = (bf16[512,512]{1,0:T(8,128)(2,1)S(1)}, bf16[512,512]{1,0:T(8,128)(2,1)}, u32[]{:S(2)}) copy-start(bf16[512,512]{1,0:T(8,128)(2,1)} %param.20) | copy-start | bytes 1572868
  53.8 22.2 %copy-start.11 = (bf16[512,256]{1,0:T(8,128)(2,1)S(1)}, bf16[512,256]{1,0:T(8,128)(2,1)}, u32[]{:S(2)}) copy-start(bf16[512,256]{1,0:T(8,128)(2,1)} %get-tuple-element.108) | copy-start | bytes 786436
  53.9 22.2 %copy-start.12 = (bf16[512,256]{1,0:T(8,128)(2,1)S(1)}, bf16[512,256]{1,0:T(8,128)(2,1)}, u32[]{:S(2)}) copy-start(bf16[512,256]{1,0:T(8,128)(2,1)} %get-tuple-element.109) | copy-start | bytes 786436
  60.5 23.2 %copy-start.2 = (bf16[2,1,512,256]{3,2,1,0:T(8,128)(2,1)S(1)}, bf16[2,1,512,256]{3,2,1,0:T(8,128)(2,1)}, u32[]{:S(2)}) copy-start(bf16[2,1,512,256]{3,2,1,0:T(8,128)(2,1)} %param.16) | copy-start | bytes 1572868
  60.5 23.2 %copy-start.4 = (bf16[256,1024]{1,0:T(8,128)(2,1)S(1)}, bf16[256,1024]{1,0:T(8,128)(2,1)}, u32[]{:S(2)}) copy-start(bf16[256,1024]{1,0:T(8,128)(2,1)} %copy-done.3) | copy-start | bytes 1572868
  63.6 16.2 %collective-permute-start.13 = (bf16[256,1024]{1,0:T(8,128)(2,1)}, bf16[256,1024]{1,0:T(8,128)(2,1)S(1)}, u32[]{:S(2)}, u32[]{:S(2)}) collective-permute-start(bf16[256,1024]{1,0:T(8,128)(2,1)} %collective-permute-done.10.refs_5_), channel_id=1, source_target_pairs={{0,16},{16,0},{1,17},{17,1},{2,18},{18,2},{3,19},{19,3},{4,20},{20... | collective-permute-start | bytes 1572872 | tf_op jit(solution)/shard_map/ppermute | solution.py:48
  64.2 11.1 %collective-permute-start.14 = (bf16[256,512]{1,0:T(8,128)(2,1)S(1)}, bf16[256,512]{1,0:T(8,128)(2,1)S(1)}, u32[]{:S(2)}, u32[]{:S(2)}) collective-permute-start(bf16[256,512]{1,0:T(8,128)(2,1)S(1)} %get-tuple-element.66), channel_id=1, source_target_pairs={{0,4},{4,8},{8,12},{12,0},{1,5},{5,9},{9,13},{13,1},{2,6},{6,10},{... | collective-permute-start | bytes 786440 | tf_op jit(solution)/shard_map/ppermute | solution.py:53
  64.3 13.5 %collective-permute-start.15 = (bf16[256,512]{1,0:T(8,128)(2,1)S(1)}, bf16[256,512]{1,0:T(8,128)(2,1)S(1)}, u32[]{:S(2)}, u32[]{:S(2)}) collective-permute-start(bf16[256,512]{1,0:T(8,128)(2,1)S(1)} %get-tuple-element.66), channel_id=1, source_target_pairs={{0,12},{4,0},{8,4},{12,8},{1,13},{5,1},{9,5},{13,9},{2,14},{6,2},{... | collective-permute-start | bytes 786440 | tf_op jit(solution)/shard_map/ppermute | solution.py:53
  75.3 16.3 %collective-permute-start.20 = (bf16[256,512]{1,0:T(8,128)(2,1)S(1)}, bf16[256,512]{1,0:T(8,128)(2,1)S(1)}, u32[]{:S(2)}, u32[]{:S(2)}) collective-permute-start(bf16[256,512]{1,0:T(8,128)(2,1)S(1)} %collective-permute-done.14.refs_1_), channel_id=1, source_target_pairs={{0,4},{4,8},{8,12},{12,0},{1,5},{5,9},{9,13},{13,1},{2,6},{6,10},{... | collective-permute-start | bytes 786440 | tf_op jit(solution)/shard_map/ppermute | solution.py:53
  76.2 16.6 %collective-permute-start.18 = (bf16[256,512]{1,0:T(8,128)(2,1)S(1)}, bf16[256,512]{1,0:T(8,128)(2,1)S(1)}, u32[]{:S(2)}, u32[]{:S(2)}) collective-permute-start(bf16[256,512]{1,0:T(8,128)(2,1)S(1)} %collective-permute-done.14.refs_1_), channel_id=1, source_target_pairs={{0,16},{16,0},{1,17},{17,1},{2,18},{18,2},{3,19},{19,3},{4,20},{20... | collective-permute-start | bytes 786440 | tf_op jit(solution)/shard_map/ppermute | solution.py:48
  77.8 15.0 %collective-permute-start.19 = (bf16[256,512]{1,0:T(8,128)(2,1)S(1)}, bf16[256,512]{1,0:T(8,128)(2,1)S(1)}, u32[]{:S(2)}, u32[]{:S(2)}) collective-permute-start(bf16[256,512]{1,0:T(8,128)(2,1)S(1)} %collective-permute-done.15.refs_3_), channel_id=1, source_target_pairs={{0,16},{16,0},{1,17},{17,1},{2,18},{18,2},{3,19},{19,3},{4,20},{20... | collective-permute-start | bytes 786440 | tf_op jit(solution)/shard_map/ppermute | solution.py:48
  79.9 11.9 %collective-permute-start.16 = (bf16[256,512]{1,0:T(8,128)(2,1)S(1)}, bf16[256,512]{1,0:T(8,128)(2,1)S(1)}, u32[]{:S(2)}, u32[]{:S(2)}) collective-permute-start(bf16[256,512]{1,0:T(8,128)(2,1)S(1)} %get-tuple-element.75), channel_id=1, source_target_pairs={{0,4},{4,8},{8,12},{12,0},{1,5},{5,9},{9,13},{13,1},{2,6},{6,10},{... | collective-permute-start | bytes 786440 | tf_op jit(solution)/shard_map/ppermute | solution.py:53
  79.9 12.9 %collective-permute-start.17 = (bf16[256,512]{1,0:T(8,128)(2,1)S(1)}, bf16[256,512]{1,0:T(8,128)(2,1)S(1)}, u32[]{:S(2)}, u32[]{:S(2)}) collective-permute-start(bf16[256,512]{1,0:T(8,128)(2,1)S(1)} %get-tuple-element.75), channel_id=1, source_target_pairs={{0,12},{4,0},{8,4},{12,8},{1,13},{5,1},{9,5},{13,9},{2,14},{6,2},{... | collective-permute-start | bytes 786440 | tf_op jit(solution)/shard_map/ppermute | solution.py:53
  91.7 19.8 %copy-start.7 = (f32[2048]{0:T(1024)S(1)}, f32[2048]{0:T(1024)}, u32[]{:S(2)}) copy-start(f32[2048]{0:T(1024)} %param.28) | copy-start | bytes 24580
  91.7 6.4 %collective-permute-start.21 = (bf16[256,512]{1,0:T(8,128)(2,1)S(1)}, bf16[256,512]{1,0:T(8,128)(2,1)S(1)}, u32[]{:S(2)}, u32[]{:S(2)}) collective-permute-start(bf16[256,512]{1,0:T(8,128)(2,1)S(1)} %collective-permute-done.20.refs_5_), channel_id=1, source_target_pairs={{0,16},{16,0},{1,17},{17,1},{2,18},{18,2},{3,19},{19,3},{4,20},{20... | collective-permute-start | bytes 786440 | tf_op jit(solution)/shard_map/ppermute | solution.py:48
  100.3 2.0 %collective-permute-start.22 = (bf16[128,2048]{1,0:T(8,128)(2,1)S(1)}, bf16[128,2048]{1,0:T(8,128)(2,1)S(1)}, u32[]{:S(2)}, u32[]{:S(2)}) collective-permute-start(bf16[128,2048]{1,0:T(8,128)(2,1)S(1)} %get-tuple-element.81), channel_id=1, source_target_pairs={{0,1},{1,0},{2,3},{3,2},{4,5},{5,4},{6,7},{7,6},{8,9},{9,8},{10,11... | collective-permute-start | bytes 1572872 | tf_op jit(solution)/shard_map/ppermute | solution.py:48
  100.3 2.6 %collective-permute-start.24 = (bf16[128,2048]{1,0:T(8,128)(2,1)S(1)}, bf16[128,2048]{1,0:T(8,128)(2,1)S(1)}, u32[]{:S(2)}, u32[]{:S(2)}) collective-permute-start(bf16[128,2048]{1,0:T(8,128)(2,1)S(1)} %get-tuple-element.84), channel_id=1, source_target_pairs={{0,1},{1,0},{2,3},{3,2},{4,5},{5,4},{6,7},{7,6},{8,9},{9,8},{10,11... | collective-permute-start | bytes 1572872 | tf_op jit(solution)/shard_map/ppermute | solution.py:48
  102.3 9.2 %collective-permute-start.23 = (bf16[64,2048]{1,0:T(8,128)(2,1)S(1)}, bf16[64,2048]{1,0:T(8,128)(2,1)S(1)}, u32[]{:S(2)}, u32[]{:S(2)}) collective-permute-start(bf16[64,2048]{1,0:T(8,128)(2,1)S(1)} %add_convert_fusion.1), channel_id=1, source_target_pairs={{0,2},{2,0},{1,3},{3,1},{4,6},{6,4},{5,7},{7,5},{8,10},{10,8},{9,1... | collective-permute-start | bytes 786440 | tf_op jit(solution)/shard_map/ppermute | solution.py:48
  103.0 14.1 %collective-permute-start.25 = (bf16[64,2048]{1,0:T(8,128)(2,1)S(1)}, bf16[64,2048]{1,0:T(8,128)(2,1)S(1)}, u32[]{:S(2)}, u32[]{:S(2)}) collective-permute-start(bf16[64,2048]{1,0:T(8,128)(2,1)S(1)} %add_convert_fusion), channel_id=1, source_target_pairs={{0,2},{2,0},{1,3},{3,1},{4,6},{6,4},{5,7},{7,5},{8,10},{10,8},{9,1... | collective-permute-start | bytes 786440 | tf_op jit(solution)/shard_map/ppermute | solution.py:48
  104.5 12.9 %collective-permute-start.29 = (bf16[256,512]{1,0:T(8,128)(2,1)S(1)}, bf16[256,512]{1,0:T(8,128)(2,1)S(1)}, u32[]{:S(2)}, u32[]{:S(2)}) collective-permute-start(bf16[256,512]{1,0:T(8,128)(2,1)S(1)} %collective-permute-done.16.refs_5_), channel_id=1, source_target_pairs={{0,4},{4,8},{8,12},{12,0},{1,5},{5,9},{9,13},{13,1},{2,6},{6,10},{... | collective-permute-start | bytes 786440 | tf_op jit(solution)/shard_map/ppermute | solution.py:53
  104.5 14.4 %collective-permute-start.27 = (bf16[256,512]{1,0:T(8,128)(2,1)S(1)}, bf16[256,512]{1,0:T(8,128)(2,1)S(1)}, u32[]{:S(2)}, u32[]{:S(2)}) collective-permute-start(bf16[256,512]{1,0:T(8,128)(2,1)S(1)} %collective-permute-done.16.refs_5_), channel_id=1, source_target_pairs={{0,16},{16,0},{1,17},{17,1},{2,18},{18,2},{3,19},{19,3},{4,20},{20... | collective-permute-start | bytes 786440 | tf_op jit(solution)/shard_map/ppermute | solution.py:48
  105.0 14.0 %collective-permute-start.28 = (bf16[256,512]{1,0:T(8,128)(2,1)S(1)}, bf16[256,512]{1,0:T(8,128)(2,1)S(1)}, u32[]{:S(2)}, u32[]{:S(2)}) collective-permute-start(bf16[256,512]{1,0:T(8,128)(2,1)S(1)} %collective-permute-done.17.refs_7_), channel_id=1, source_target_pairs={{0,16},{16,0},{1,17},{17,1},{2,18},{18,2},{3,19},{19,3},{4,20},{20... | collective-permute-start | bytes 786440 | tf_op jit(solution)/shard_map/ppermute | solution.py:48
  111.8 11.0 %collective-permute-start.26 = (bf16[64,2048]{1,0:T(8,128)(2,1)S(1)}, bf16[64,2048]{1,0:T(8,128)(2,1)S(1)}, u32[]{:S(2)}, u32[]{:S(2)}) collective-permute-start(bf16[64,2048]{1,0:T(8,128)(2,1)S(1)} %get-tuple-element.88.refs_0_), channel_id=1, source_target_pairs={{0,2},{2,0},{1,3},{3,1},{4,6},{6,4},{5,7},{7,5},{8,10},{10,8},{9,1... | collective-permute-start | bytes 786440 | tf_op jit(solution)/shard_map/ppermute | solution.py:48
  117.4 6.8 %collective-permute-start.32 = (bf16[256,512]{1,0:T(8,128)(2,1)S(1)}, bf16[256,512]{1,0:T(8,128)(2,1)S(1)}, u32[]{:S(2)}, u32[]{:S(2)}) collective-permute-start(bf16[256,512]{1,0:T(8,128)(2,1)S(1)} %collective-permute-done.29.refs_9_), channel_id=1, source_target_pairs={{0,16},{16,0},{1,17},{17,1},{2,18},{18,2},{3,19},{19,3},{4,20},{20... | collective-permute-start | bytes 786440 | tf_op jit(solution)/shard_map/ppermute | solution.py:48
  117.5 10.1 %collective-permute-start.33 = (bf16[64,2048]{1,0:T(8,128)(2,1)S(1)}, bf16[64,2048]{1,0:T(8,128)(2,1)S(1)}, u32[]{:S(2)}, u32[]{:S(2)}) collective-permute-start(bf16[64,2048]{1,0:T(8,128)(2,1)S(1)} %get-tuple-element.93.refs_0_), channel_id=1, source_target_pairs={{0,2},{2,0},{1,3},{3,1},{4,6},{6,4},{5,7},{7,5},{8,10},{10,8},{9,1... | collective-permute-start | bytes 786440 | tf_op jit(solution)/shard_map/ppermute | solution.py:48
  118.9 8.7 %collective-permute-start.30 = (bf16[64,2048]{1,0:T(8,128)(2,1)S(1)}, bf16[64,2048]{1,0:T(8,128)(2,1)S(1)}, u32[]{:S(2)}, u32[]{:S(2)}) collective-permute-start(bf16[64,2048]{1,0:T(8,128)(2,1)S(1)} %get-tuple-element.88.refs_0_), channel_id=1, source_target_pairs={{0,1},{1,0},{2,3},{3,2},{4,5},{5,4},{6,7},{7,6},{8,9},{9,8},{10,11... | collective-permute-start | bytes 786440 | tf_op jit(solution)/shard_map/ppermute | solution.py:48
  119.0 10.3 %collective-permute-start.34 = (bf16[64,2048]{1,0:T(8,128)(2,1)S(1)}, bf16[64,2048]{1,0:T(8,128)(2,1)S(1)}, u32[]{:S(2)}, u32[]{:S(2)}) collective-permute-start(bf16[64,2048]{1,0:T(8,128)(2,1)S(1)} %get-tuple-element.93.refs_0_), channel_id=1, source_target_pairs={{0,1},{1,0},{2,3},{3,2},{4,5},{5,4},{6,7},{7,6},{8,9},{9,8},{10,11... | collective-permute-start | bytes 786440 | tf_op jit(solution)/shard_map/ppermute | solution.py:48
  122.7 4.9 %collective-permute-start.31 = (bf16[64,2048]{1,0:T(8,128)(2,1)S(1)}, bf16[64,2048]{1,0:T(8,128)(2,1)S(1)}, u32[]{:S(2)}, u32[]{:S(2)}) collective-permute-start(bf16[64,2048]{1,0:T(8,128)(2,1)S(1)} %collective-permute-done.26.refs_1_), channel_id=1, source_target_pairs={{0,1},{1,0},{2,3},{3,2},{4,5},{5,4},{6,7},{7,6},{8,9},{9,8},{10,11... | collective-permute-start | bytes 786440 | tf_op jit(solution)/shard_map/ppermute | solution.py:48
  127.6 1.8 %collective-permute-start.35 = (bf16[64,2048]{1,0:T(8,128)(2,1)S(1)}, bf16[64,2048]{1,0:T(8,128)(2,1)S(1)}, u32[]{:S(2)}, u32[]{:S(2)}) collective-permute-start(bf16[64,2048]{1,0:T(8,128)(2,1)S(1)} %collective-permute-done.33.refs_1_), channel_id=1, source_target_pairs={{0,1},{1,0},{2,3},{3,2},{4,5},{5,4},{6,7},{7,6},{8,9},{9,8},{10,11... | collective-permute-start | bytes 786440 | tf_op jit(solution)/shard_map/ppermute | solution.py:48
  129.3 1.7 %copy-start = (bf16[2048,512]{1,0:T(8,128)(2,1)S(1)}, bf16[2048,512]{1,0:T(8,128)(2,1)}, u32[]{:S(2)}) copy-start(bf16[2048,512]{1,0:T(8,128)(2,1)} %query_ref.7) | copy-start | bytes 6291460
  129.3 1.7 %copy-start.5 = (f32[2048]{0:T(1024)S(1)}, f32[2048]{0:T(1024)}, u32[]{:S(2)}) copy-start(f32[2048]{0:T(1024)} %param.29) | copy-start | bytes 24580
  129.3 1.7 %copy-start.6 = (s32[3,16]{1,0:T(4,128)S(1)}, s32[3,16]{1,0:T(4,128)}, u32[]{:S(2)}) copy-start(s32[3,16]{1,0:T(4,128)} %parent_ref.7) | copy-start | bytes 580
  133.0 4.5 %collective-permute-start.36 = (bf16[16,2048]{1,0:T(8,128)(2,1)S(1)}, bf16[16,2048]{1,0:T(8,128)(2,1)S(1)}, u32[]{:S(2)}, u32[]{:S(2)}) collective-permute-start(bf16[16,2048]{1,0:T(8,128)(2,1)S(1)} %get-tuple-element.97.refs_3_), channel_id=1, source_target_pairs={{0,2},{2,0},{1,3},{3,1},{4,6},{6,4},{5,7},{7,5},{8,10},{10,8},{9,1... | collective-permute-start | bytes 196616 | tf_op jit(solution)/shard_map/ppermute | solution.py:48
  133.5 4.0 %collective-permute-start.37 = (bf16[16,2048]{1,0:T(8,128)(2,1)S(1)}, bf16[16,2048]{1,0:T(8,128)(2,1)S(1)}, u32[]{:S(2)}, u32[]{:S(2)}) collective-permute-start(bf16[16,2048]{1,0:T(8,128)(2,1)S(1)} %get-tuple-element.97.refs_3_), channel_id=1, source_target_pairs={{0,1},{1,0},{2,3},{3,2},{4,5},{5,4},{6,7},{7,6},{8,9},{9,8},{10,11... | collective-permute-start | bytes 196616 | tf_op jit(solution)/shard_map/ppermute | solution.py:48
  137.5 1.3 collective-permute-start.38
  140.8 4.3 %collective-permute-start.39 = (bf16[16,2048]{1,0:T(8,128)(2,1)S(1)}, bf16[16,2048]{1,0:T(8,128)(2,1)S(1)}, u32[]{:S(2)}, u32[]{:S(2)}) collective-permute-start(bf16[16,2048]{1,0:T(8,128)(2,1)S(1)} %get-tuple-element.99.refs_3_), channel_id=1, source_target_pairs={{0,2},{2,0},{1,3},{3,1},{4,6},{6,4},{5,7},{7,5},{8,10},{10,8},{9,1... | collective-permute-start | bytes 196616 | tf_op jit(solution)/shard_map/ppermute | solution.py:48
  141.3 3.8 %collective-permute-start.40 = (bf16[16,2048]{1,0:T(8,128)(2,1)S(1)}, bf16[16,2048]{1,0:T(8,128)(2,1)S(1)}, u32[]{:S(2)}, u32[]{:S(2)}) collective-permute-start(bf16[16,2048]{1,0:T(8,128)(2,1)S(1)} %get-tuple-element.99.refs_3_), channel_id=1, source_target_pairs={{0,1},{1,0},{2,3},{3,2},{4,5},{5,4},{6,7},{7,6},{8,9},{9,8},{10,11... | collective-permute-start | bytes 196616 | tf_op jit(solution)/shard_map/ppermute | solution.py:48
  145.1 1.3 collective-permute-start.41
  148.4 4.3 %collective-permute-start.42 = (bf16[16,2048]{1,0:T(8,128)(2,1)S(1)}, bf16[16,2048]{1,0:T(8,128)(2,1)S(1)}, u32[]{:S(2)}, u32[]{:S(2)}) collective-permute-start(bf16[16,2048]{1,0:T(8,128)(2,1)S(1)} %get-tuple-element.101.refs_3_), channel_id=1, source_target_pairs={{0,2},{2,0},{1,3},{3,1},{4,6},{6,4},{5,7},{7,5},{8,10},{10,8},{9,1... | collective-permute-start | bytes 196616 | tf_op jit(solution)/shard_map/ppermute | solution.py:48
  148.9 3.8 %collective-permute-start.43 = (bf16[16,2048]{1,0:T(8,128)(2,1)S(1)}, bf16[16,2048]{1,0:T(8,128)(2,1)S(1)}, u32[]{:S(2)}, u32[]{:S(2)}) collective-permute-start(bf16[16,2048]{1,0:T(8,128)(2,1)S(1)} %get-tuple-element.101.refs_3_), channel_id=1, source_target_pairs={{0,1},{1,0},{2,3},{3,2},{4,5},{5,4},{6,7},{7,6},{8,9},{9,8},{10,11... | collective-permute-start | bytes 196616 | tf_op jit(solution)/shard_map/ppermute | solution.py:48
  152.7 1.3 collective-permute-start.44
  156.0 3.2 %collective-permute-start.47 = (bf16[16,512]{1,0:T(8,128)(2,1)S(1)}, bf16[16,512]{1,0:T(8,128)(2,1)S(1)}, u32[]{:S(2)}, u32[]{:S(2)}) collective-permute-start(bf16[16,512]{1,0:T(8,128)(2,1)S(1)} %get-tuple-element.105), channel_id=1, source_target_pairs={{0,3},{1,2},{2,1},{3,0},{4,7},{5,6},{6,5},{7,4},{8,11},{9,10},{10,... | collective-permute-start | bytes 49160 | tf_op jit(solution)/shard_map/ppermute | solution.py:703
  156.4 3.8 %collective-permute-start.46 = (bf16[16,512]{1,0:T(8,128)(2,1)S(1)}, bf16[16,512]{1,0:T(8,128)(2,1)S(1)}, u32[]{:S(2)}, u32[]{:S(2)}) collective-permute-start(bf16[16,512]{1,0:T(8,128)(2,1)S(1)} %get-tuple-element.104), channel_id=1, source_target_pairs={{0,2},{1,3},{2,0},{3,1},{4,6},{5,7},{6,4},{7,5},{8,10},{9,11},{10,... | collective-permute-start | bytes 49160 | tf_op jit(solution)/shard_map/ppermute | solution.py:703
  157.9 2.2 %collective-permute-start.45 = (bf16[16,512]{1,0:T(8,128)(2,1)S(1)}, bf16[16,512]{1,0:T(8,128)(2,1)S(1)}, u32[]{:S(2)}, u32[]{:S(2)}) collective-permute-start(bf16[16,512]{1,0:T(8,128)(2,1)S(1)} %get-tuple-element.103), channel_id=1, source_target_pairs={{0,1},{1,0},{2,3},{3,2},{4,5},{5,4},{6,7},{7,6},{8,9},{9,8},{10,11... | collective-permute-start | bytes 49160 | tf_op jit(solution)/shard_map/ppermute | solution.py:703

commit v8 on v7

--- a/solution.py
+++ b/solution.py
@@ -1,4 +1,5 @@
 import functools
+import math
 
 import jax
 import jax.numpy as jnp
@@ -292,9 +293,9 @@
             top = jnp.maximum(
                 jnp.max(old, axis=-1, keepdims=True), jnp.max(new, axis=-1, keepdims=True)
             )
-            scale = DH ** (-0.5)
-            old = jnp.exp((old - top) * scale)
-            new = jnp.exp((new - top) * scale)
+            scale = DH ** (-0.5) * math.log2(math.e)
+            old = jnp.exp2((old - top) * scale)
+            new = jnp.exp2((new - top) * scale)
             total_weight = jnp.sum(old, axis=-1, keepdims=True) + jnp.sum(
                 new, axis=-1, keepdims=True
             )
@@ -499,7 +500,7 @@
         top = functools.reduce(
             jnp.maximum, [jnp.max(values, axis=-1, keepdims=True) for values in scores]
         )
-        raised = [jnp.exp((values - top) * DH ** (-0.5)) for values in scores]
+        raised = [jnp.exp2((values - top) * (DH ** (-0.5) * math.log2(math.e))) for values in scores]
         weight = sum(jnp.sum(values, axis=-1, keepdims=True) for values in raised)
         mixed = sum(
             jnp.dot(

time: 161 us -> 161 us (level)
  transfers between devices with their start and end apart: 48 -> 48, of which waited for: 26 -> 27; matrix products, arithmetic and copies ran while one was open for 6% -> 6% of each run, Pallas kernels for 8% -> 8%
where the time goes in v8:
time: 161 us
  waiting for transfers between devices  82.5 us (51%)
  starting transfers between devices  38.2 us (24%)
  Pallas kernels  24.2 us (15%)
  local copies, waits for them, and re-layouts  6.84 us (4%)
  other arithmetic  3.92 us (2%)
  matrix products  3.09 us (2%)
  between operations  1.78 us (1%)
    ppermute x33, waiting for transfers between devices, exchange(): lax.ppermute(value, axis, [(i, partner(i, step, size)) for i in range(siz...  49.7 us
    ppermute x12, waiting for transfers between devices, shift(): lax.ppermute(value, axis, [(i, (i + step) % size) for i in range(size)])  31.5 us
    ppermute x33, starting transfers between devices, exchange(): lax.ppermute(value, axis, [(i, partner(i, step, size)) for i in range(siz...  19.2 us
    ppermute x12, starting transfers between devices, shift(): lax.ppermute(value, axis, [(i, (i + step) % size) for i in range(size)])  17.1 us
    pallas_call x4, Pallas kernels, beam_step(): pl.pallas_call(functools.partial(beam_kernel, level, max(len(inputs) - 1,...  8.13 us
    pallas_call x1, Pallas kernels, encoder_attention(): pl.pallas_call(functools.partial(encoder_kernel, [places for _, places in...  7.77 us
    pallas_call x2, Pallas kernels, cross_project(): pl.pallas_call(functools.partial(cross_kernel, [places for _, places in r...  3.33 us
  transfers between devices with their start and end apart: 48, of which 27 were waited for; matrix products, arithmetic and copies ran while one was open for 6% of the time, Pallas kernels for 8%

profile of v8, /device:TPU:0, one launch (start us, length us, event | category | flops | bytes accessed | tf_op | source)
XLA Modules:
  0.0 160.5 jit_solution(9074697135568889419)
XLA Ops:
  0.7 1.9 %slice_bitcast_fusion.3 = (bf16[512,256]{1,0:T(8,128)(2,1)}, bf16[512,256]{1,0:T(8,128)(2,1)}, bf16[1,512,256]{2,1,0:T(8,128)(2,1)S(1)}, bf16[1,512,256]{2,1,0:T(8,128)(2,1)S(1)}) fusion(bf16[2,512,256]{2,1,0:T(8,128)(2,1)} %param.21), kind=kLoop, calls=%fused_computation.26 | loop fusion | bytes 1572864 | tf_op jit(solution)/shard_map/squeeze | solution.py:580
  2.6 1.0 constant_dynamic-slice_fusion.1
  3.7 3.1 %collective-permute-start.1 = (bf16[256,1024]{1,0:T(8,128)(2,1)S(1)}, bf16[256,1024]{1,0:T(8,128)(2,1)}, u32[]{:S(2)}, u32[]{:S(2)}) collective-permute-start(bf16[256,1024]{1,0:T(8,128)(2,1)S(1)} %pad_maximum_fusion.2), channel_id=1, source_target_pairs={{0,4},{4,8},{8,12},{12,0},{1,5},{5,9},{9,13},{13,1},{2,6},{6,10},{... | collective-permute-start | bytes 1572872 | tf_op jit(solution)/shard_map/ppermute | solution.py:54
  6.8 1.6 %collective-permute-start = (bf16[128,512]{1,0:T(8,128)(2,1)S(1)}, bf16[128,512]{1,0:T(8,128)(2,1)S(1)}, u32[]{:S(2)}, u32[]{:S(2)}) collective-permute-start(bf16[128,512]{1,0:T(8,128)(2,1)S(1)} %get-tuple-element.113), channel_id=1, source_target_pairs={{0,4},{4,8},{8,12},{12,0},{1,5},{5,9},{9,13},{13,1},{2,6},{6,10},{... | collective-permute-start | bytes 393224 | tf_op jit(solution)/shard_map/ppermute | solution.py:54
  8.4 2.2 %collective-permute-start.3 = (bf16[128,512]{1,0:T(8,128)(2,1)S(1)}, bf16[128,512]{1,0:T(8,128)(2,1)S(1)}, u32[]{:S(2)}, u32[]{:S(2)}) collective-permute-start(bf16[128,512]{1,0:T(8,128)(2,1)S(1)} %get-tuple-element.114), channel_id=1, source_target_pairs={{0,12},{4,0},{8,4},{12,8},{1,13},{5,1},{9,5},{13,9},{2,14},{6,2},{... | collective-permute-start | bytes 393224 | tf_op jit(solution)/shard_map/ppermute | solution.py:54
  10.7 0.8 collective-permute-start.2
  11.5 12.8 %collective-permute-done = bf16[128,512]{1,0:T(8,128)(2,1)S(1)} collective-permute-done((bf16[128,512]{1,0:T(8,128)(2,1)S(1)}, bf16[128,512]{1,0:T(8,128)(2,1)S(1)}, u32[]{:S(2)}, u32[]{:S(2)}) %collective-permute-start) | collective-permute-done | bytes 131104 | tf_op jit(solution)/shard_map/ppermute | solution.py:54
  24.4 1.8 %collective-permute-start.7 = (bf16[256,1024]{1,0:T(8,128)(2,1)}, bf16[256,1024]{1,0:T(8,128)(2,1)S(1)}, u32[]{:S(2)}, u32[]{:S(2)}) collective-permute-start(bf16[256,1024]{1,0:T(8,128)(2,1)} %collective-permute-done.1.refs_1_), channel_id=1, source_target_pairs={{0,16},{16,0},{1,17},{17,1},{2,18},{18,2},{3,19},{19,3},{4,20},{20... | collective-permute-start | bytes 1572872 | tf_op jit(solution)/shard_map/ppermute | solution.py:49
  26.3 5.6 %collective-permute-done.2 = bf16[128,512]{1,0:T(8,128)(2,1)S(1)} collective-permute-done((bf16[128,512]{1,0:T(8,128)(2,1)S(1)}, bf16[128,512]{1,0:T(8,128)(2,1)S(1)}, u32[]{:S(2)}, u32[]{:S(2)}) %collective-permute-start.2) | collective-permute-done | bytes 131104 | tf_op jit(solution)/shard_map/ppermute | solution.py:54
  32.0 1.6 collective-permute-start.4
  33.5 1.6 %collective-permute-start.8 = (bf16[256,1024]{1,0:T(8,128)(2,1)S(1)}, bf16[256,1024]{1,0:T(8,128)(2,1)}, u32[]{:S(2)}, u32[]{:S(2)}) collective-permute-start(bf16[256,1024]{1,0:T(8,128)(2,1)S(1)} %pad_maximum_fusion.2), channel_id=1, source_target_pairs={{0,12},{4,0},{8,4},{12,8},{1,13},{5,1},{9,5},{13,9},{2,14},{6,2},{... | collective-permute-start | bytes 1572872 | tf_op jit(solution)/shard_map/ppermute | solution.py:54
  35.3 3.1 %convolution_convert_fusion = bf16[64,2048]{1,0:T(8,128)(2,1)S(1)} fusion(bf16[64,1024]{1,0:T(8,128)(2,1)S(1)} %compare_convert_fusion, bf16[1024,2048]{1,0:T(8,128)(2,1)} %param.26), kind=kOutput, calls=%fused_computation | convolution fusion | flops 268566528 | bytes 4587520 | tf_op jit(solution)/shard_map/dot_general | solution.py:590
  38.9 6.9 %collective-permute-done.4.refs_1_ = bf16[512,512]{1,0:T(8,128)(2,1)S(1)} collective-permute-done((bf16[512,512]{1,0:T(8,128)(2,1)S(1)}, bf16[512,512]{1,0:T(8,128)(2,1)S(1)}, u32[]{:S(2)}, u32[]{:S(2)}) %collective-permute-start.4) | collective-permute-done | bytes 524320 | tf_op jit(solution)/shard_map/ppermute | solution.py:49
  45.9 1.3 collective-permute-done.8.refs_3_
  47.2 1.5 collective-permute-start.9
  48.7 0.8 add.88
  49.5 0.5 collective-permute-start.12
  50.1 0.7 slice_bitcast_fusion
  50.9 2.9 %copy.17 = bf16[2048,512]{0,1:T(8,128)(2,1)S(1)} copy(bf16[2048,512]{1,0:T(8,128)(2,1)} %param.25) | data formatting | bytes 4194304 | tf_op jit(solution)/shard_map/optimization_barrier | solution.py:58
  53.9 3.1 %collective-permute-done.12 = bf16[64,2048]{1,0:T(8,128)(2,1)} collective-permute-done((bf16[64,2048]{1,0:T(8,128)(2,1)}, bf16[64,2048]{1,0:T(8,128)(2,1)}, u32[]{:S(2)}, u32[]{:S(2)}) %collective-permute-start.12) | collective-permute-done | bytes 262176 | tf_op jit(solution)/shard_map/ppermute | solution.py:49
  57.0 1.1 add.89
  58.1 2.4 %norm_events.1 = (bf16[512,2048]{1,0:T(8,128)(2,1)S(1)}, bf16[128,2048]{1,0:T(8,128)(2,1)S(1)}) custom-call(s32[4]{0:T(128)S(1)} %pad_add_fusion.at_ref, f32[1,2048]{1,0:T(1,128)S(1)} %bitcast.48, bf16[512,512]{1,0:T(8,128)(2,1)S(1)} %pad_maximum_fusion.3.refs_0_, bf16[512,512]{1,0:T(8,128)(2,1)S(1)} %collective-permute-done.4.refs_1_, ...), custom_call_target="tpu_custom_call" | custom-call | bytes 12000000 | tf_op jit(solution)/shard_map/norm_events/pallas_call | solution.py:207
  60.6 3.0 %collective-permute-done.10.refs_5_ = bf16[256,1024]{1,0:T(8,128)(2,1)} collective-permute-done((bf16[256,1024]{1,0:T(8,128)(2,1)}, bf16[256,1024]{1,0:T(8,128)(2,1)}, u32[]{:S(2)}, u32[]{:S(2)}) %collective-permute-start.10) | collective-permute-done | bytes 524320 | tf_op jit(solution)/shard_map/ppermute | solution.py:54
  63.6 0.5 collective-permute-start.13
  64.3 3.8 %collective-permute-start.15 = (bf16[256,512]{1,0:T(8,128)(2,1)S(1)}, bf16[256,512]{1,0:T(8,128)(2,1)S(1)}, u32[]{:S(2)}, u32[]{:S(2)}) collective-permute-start(bf16[256,512]{1,0:T(8,128)(2,1)S(1)} %get-tuple-element.66), channel_id=1, source_target_pairs={{0,12},{4,0},{8,4},{12,8},{1,13},{5,1},{9,5},{13,9},{2,14},{6,2},{... | collective-permute-start | bytes 786440 | tf_op jit(solution)/shard_map/ppermute | solution.py:54
  68.1 7.3 %collective-permute-done.14.refs_1_ = bf16[256,512]{1,0:T(8,128)(2,1)S(1)} collective-permute-done((bf16[256,512]{1,0:T(8,128)(2,1)S(1)}, bf16[256,512]{1,0:T(8,128)(2,1)S(1)}, u32[]{:S(2)}, u32[]{:S(2)}) %collective-permute-start.14) | collective-permute-done | bytes 262176 | tf_op jit(solution)/shard_map/ppermute | solution.py:54
  76.2 1.6 collective-permute-start.18
  77.8 2.1 %collective-permute-start.19 = (bf16[256,512]{1,0:T(8,128)(2,1)S(1)}, bf16[256,512]{1,0:T(8,128)(2,1)S(1)}, u32[]{:S(2)}, u32[]{:S(2)}) collective-permute-start(bf16[256,512]{1,0:T(8,128)(2,1)S(1)} %collective-permute-done.15.refs_3_), channel_id=1, source_target_pairs={{0,16},{16,0},{1,17},{17,1},{2,18},{18,2},{3,19},{19,3},{4,20},{20... | collective-permute-start | bytes 786440 | tf_op jit(solution)/shard_map/ppermute | solution.py:49
  79.9 3.8 %collective-permute-start.17 = (bf16[256,512]{1,0:T(8,128)(2,1)S(1)}, bf16[256,512]{1,0:T(8,128)(2,1)S(1)}, u32[]{:S(2)}, u32[]{:S(2)}) collective-permute-start(bf16[256,512]{1,0:T(8,128)(2,1)S(1)} %get-tuple-element.75), channel_id=1, source_target_pairs={{0,12},{4,0},{8,4},{12,8},{1,13},{5,1},{9,5},{13,9},{2,14},{6,2},{... | collective-permute-start | bytes 786440 | tf_op jit(solution)/shard_map/ppermute | solution.py:54
  83.7 7.8 %encoder_attention.1.attended_ref = bf16[512,512]{1,0:T(8,128)(2,1)S(1)} custom-call(s32[4]{0:T(128)S(1)} %pad_add_fusion.at_ref, s32[1]{0:T(128)S(6)} %copy.18.live_ref, bf16[512,2048]{1,0:T(8,128)(2,1)S(1)} %get-tuple-element.67.rows_ref, bf16[2,512,256]{2,1,0:T(8,128)(2,1)S(1)} %bitcast.39, bf16[512,1024]{1,0:T(8,128)(2,1)S(1)} %pad_maximum_fusion.refs_0_, ...), custom_call_target="tpu_custom_call" | custom-call | bytes 33000000 | tf_op jit(solution)/shard_map/encoder_attention/pallas_call | solution.py:323
  91.8 1.0 collective-permute-done.17.refs_7_
  92.8 5.1 %collective-permute-done.21.refs_6_ = bf16[256,512]{1,0:T(8,128)(2,1)S(1)} collective-permute-done((bf16[256,512]{1,0:T(8,128)(2,1)S(1)}, bf16[256,512]{1,0:T(8,128)(2,1)S(1)}, u32[]{:S(2)}, u32[]{:S(2)}) %collective-permute-start.21) | collective-permute-done | bytes 262176 | tf_op jit(solution)/shard_map/ppermute | solution.py:49
  97.9 2.1 %project_out.1 = (bf16[128,2048]{1,0:T(8,128)(2,1)S(1)}, bf16[128,2048]{1,0:T(8,128)(2,1)S(1)}, bf16[128,2048]{1,0:T(8,128)(2,1)S(1)}, bf16[128,2048]{1,0:T(8,128)(2,1)S(1)}) custom-call(s32[4]{0:T(128)S(1)} %pad_add_fusion.at_ref, bf16[512,512]{1,0:T(8,128)(2,1)S(1)} %encoder_attention.1.attended_ref, bf16[512,512]{1,0:T(8,128)(2,1)S(1)} %copy-done.1, ...), custom_call_target="tpu_custom_call" | custom-call | bytes 6000000 | tf_op jit(solution)/shard_map/project_out/pallas_call | solution.py:379
  100.1 0.5 collective-permute-start.24
  100.6 1.4 collective-permute-done.22.refs_1_
  102.1 0.6 collective-permute-start.23
  102.8 1.5 collective-permute-start.25
  104.8 1.5 collective-permute-start.28
  106.3 5.0 %collective-permute-done.23 = bf16[64,2048]{1,0:T(8,128)(2,1)S(1)} collective-permute-done((bf16[64,2048]{1,0:T(8,128)(2,1)S(1)}, bf16[64,2048]{1,0:T(8,128)(2,1)S(1)}, u32[]{:S(2)}, u32[]{:S(2)}) %collective-permute-start.23) | collective-permute-done | bytes 262176 | tf_op jit(solution)/shard_map/ppermute | solution.py:49
  111.6 0.6 collective-permute-start.26
  112.1 4.8 %collective-permute-done.25 = bf16[64,2048]{1,0:T(8,128)(2,1)S(1)} collective-permute-done((bf16[64,2048]{1,0:T(8,128)(2,1)S(1)}, bf16[64,2048]{1,0:T(8,128)(2,1)S(1)}, u32[]{:S(2)}, u32[]{:S(2)}) %collective-permute-start.25) | collective-permute-done | bytes 262176 | tf_op jit(solution)/shard_map/ppermute | solution.py:49
  117.3 1.4 collective-permute-start.33
  119.3 3.3 %collective-permute-done.26.refs_1_ = bf16[64,2048]{1,0:T(8,128)(2,1)S(1)} collective-permute-done((bf16[64,2048]{1,0:T(8,128)(2,1)S(1)}, bf16[64,2048]{1,0:T(8,128)(2,1)S(1)}, u32[]{:S(2)}, u32[]{:S(2)}) %collective-permute-start.26) | collective-permute-done | bytes 262176 | tf_op jit(solution)/shard_map/ppermute | solution.py:49
  122.5 1.4 collective-permute-done.32.refs_10_
  124.0 3.4 %collective-permute-done.33.refs_1_ = bf16[64,2048]{1,0:T(8,128)(2,1)S(1)} collective-permute-done((bf16[64,2048]{1,0:T(8,128)(2,1)S(1)}, bf16[64,2048]{1,0:T(8,128)(2,1)S(1)}, u32[]{:S(2)}, u32[]{:S(2)}) %collective-permute-start.33) | collective-permute-done | bytes 262176 | tf_op jit(solution)/shard_map/ppermute | solution.py:49
  127.4 1.7 %cross_project_0.1.refs_0_ = bf16[256,512]{1,0:T(8,128)(2,1)S(1)} custom-call(s32[4]{0:T(128)S(1)} %pad_add_fusion.at_ref, bf16[64,2048]{1,0:T(8,128)(2,1)S(1)} %get-tuple-element.88.refs_0_, bf16[64,2048]{1,0:T(8,128)(2,1)S(1)} %collective-permute-done.26.refs_1_, bf16[64,2048]{1,0:T(8,128)(2,1)S(1)} %collective-permute-done.30.refs_2_, ...), custom_call_target="tpu_custom_call" | custom-call | bytes 6000000 | tf_op jit(solution)/shard_map/cross_project_0/pallas_call | solution.py:439
  129.1 1.7 %cross_project_1.1.refs_1_ = bf16[256,512]{1,0:T(8,128)(2,1)S(1)} custom-call(s32[4]{0:T(128)S(1)} %pad_add_fusion.at_ref, bf16[64,2048]{1,0:T(8,128)(2,1)S(1)} %get-tuple-element.93.refs_0_, bf16[64,2048]{1,0:T(8,128)(2,1)S(1)} %collective-permute-done.33.refs_1_, bf16[64,2048]{1,0:T(8,128)(2,1)S(1)} %collective-permute-done.34.refs_2_, ...), custom_call_target="tpu_custom_call" | custom-call | bytes 6000000 | tf_op jit(solution)/shard_map/cross_project_1/pallas_call | solution.py:439
  130.8 1.9 %beam_step_0.1 = (f32[16,2048]{1,0:T(8,128)S(1)}, bf16[16,2048]{1,0:T(8,128)(2,1)S(1)}) custom-call(s32[4]{0:T(128)S(1)} %pad_add_fusion.at_ref, s32[1]{0:T(128)S(6)} %copy.18.live_ref, s32[3,16]{1,0:T(4,128)S(1)} %copy-done.6, f32[1,2048]{1,0:T(1,128)S(1)} %bitcast.42, bf16[2048,512]{1,0:T(8,128)(2,1)S(1)} %copy-done, bf16[512,2048]{1,0:T(8,128)(2,1)S(1)} %bitcast.35, ...), custom_call_target="tpu_custom_call" | custom-call | bytes 12000000 | tf_op jit(solution)/shard_map/beam_step_0/pallas_call | solution.py:546
  132.8 0.5 collective-permute-start.36
  133.5 3.8 %collective-permute-done.36.refs_4_ = bf16[16,2048]{1,0:T(8,128)(2,1)S(1)} collective-permute-done((bf16[16,2048]{1,0:T(8,128)(2,1)S(1)}, bf16[16,2048]{1,0:T(8,128)(2,1)S(1)}, u32[]{:S(2)}, u32[]{:S(2)}) %collective-permute-start.36) | collective-permute-done | bytes 65568 | tf_op jit(solution)/shard_map/ppermute | solution.py:49
  137.3 1.2 collective-permute-done.38.refs_6_
  138.5 2.1 %beam_step_1.1 = (f32[16,2048]{1,0:T(8,128)S(1)}, bf16[16,2048]{1,0:T(8,128)(2,1)S(1)}) custom-call(s32[4]{0:T(128)S(1)} %pad_add_fusion.at_ref, s32[1]{0:T(128)S(6)} %copy.18.live_ref, s32[3,16]{1,0:T(4,128)S(1)} %copy-done.6, f32[1,2048]{1,0:T(1,128)S(1)} %bitcast.43, bf16[2048,512]{1,0:T(8,128)(2,1)S(1)} %copy-done, bf16[512,2048]{1,0:T(8,128)(2,1)S(1)} %bitcast.36, ...), custom_call_target="tpu_custom_call" | custom-call | bytes 12000000 | tf_op jit(solution)/shard_map/beam_step_1/pallas_call | solution.py:546
  140.6 0.5 collective-permute-start.39
  141.1 3.8 %collective-permute-done.39.refs_4_ = bf16[16,2048]{1,0:T(8,128)(2,1)S(1)} collective-permute-done((bf16[16,2048]{1,0:T(8,128)(2,1)S(1)}, bf16[16,2048]{1,0:T(8,128)(2,1)S(1)}, u32[]{:S(2)}, u32[]{:S(2)}) %collective-permute-start.39) | collective-permute-done | bytes 65568 | tf_op jit(solution)/shard_map/ppermute | solution.py:49
  144.9 1.2 collective-permute-done.41.refs_6_
  146.1 2.1 %beam_step_2.1 = (f32[16,2048]{1,0:T(8,128)S(1)}, bf16[16,2048]{1,0:T(8,128)(2,1)S(1)}) custom-call(s32[4]{0:T(128)S(1)} %pad_add_fusion.at_ref, s32[1]{0:T(128)S(6)} %copy.18.live_ref, s32[3,16]{1,0:T(4,128)S(1)} %copy-done.6, f32[1,2048]{1,0:T(1,128)S(1)} %bitcast.44, bf16[2048,512]{1,0:T(8,128)(2,1)S(1)} %copy-done, bf16[512,2048]{1,0:T(8,128)(2,1)S(1)} %bitcast.37, ...), custom_call_target="tpu_custom_call" | custom-call | bytes 12000000 | tf_op jit(solution)/shard_map/beam_step_2/pallas_call | solution.py:546
  148.2 0.5 collective-permute-start.42
  148.7 3.8 %collective-permute-done.42.refs_4_ = bf16[16,2048]{1,0:T(8,128)(2,1)S(1)} collective-permute-done((bf16[16,2048]{1,0:T(8,128)(2,1)S(1)}, bf16[16,2048]{1,0:T(8,128)(2,1)S(1)}, u32[]{:S(2)}, u32[]{:S(2)}) %collective-permute-start.42) | collective-permute-done | bytes 65568 | tf_op jit(solution)/shard_map/ppermute | solution.py:49
  152.5 1.2 collective-permute-done.44.refs_6_
  153.7 2.1 %beam_step_3.1 = (f32[16,512]{1,0:T(8,128)S(1)}, bf16[16,512]{1,0:T(8,128)(2,1)S(1)}, bf16[16,512]{1,0:T(8,128)(2,1)S(1)}, bf16[16,512]{1,0:T(8,128)(2,1)S(1)}) custom-call(s32[4]{0:T(128)S(1)} %pad_add_fusion.at_ref, s32[1]{0:T(128)S(6)} %copy.18.live_ref, s32[3,16]{1,0:T(4,128)S(1)} %copy-done.6, f32[1,2048]{1,0:T(1,128)S(1)} %bitcast.45, ...), custom_call_target="tpu_custom_call" | custom-call | bytes 12000000 | tf_op jit(solution)/shard_map/beam_step_3/pallas_call | solution.py:546
  156.1 1.5 collective-permute-start.46
  157.7 0.8 maximum_bitcast_fusion
  159.0 0.9 collective-permute-done.46
  159.9 0.6 add_convert_fusion.2
  (98 shorter events, 5.0 us)
Async XLA Ops:
  0.6 6.1 %copy-start.13 = (bf16[4,128,512]{2,1,0:T(8,128)(2,1)S(1)}, bf16[4,128,512]{2,1,0:T(8,128)(2,1)}, u32[]{:S(2)}) copy-start(bf16[4,128,512]{2,1,0:T(8,128)(2,1)} %param.15) | copy-start | bytes 1572868
  0.6 10.8 %copy-start.15 = (s32[4,16]{1,0:T(4,128)S(1)}, s32[4,16]{1,0:T(4,128)}, u32[]{:S(2)}) copy-start(s32[4,16]{1,0:T(4,128)} %param.18) | copy-start | bytes 772
  3.7 20.7 %collective-permute-start.1 = (bf16[256,1024]{1,0:T(8,128)(2,1)S(1)}, bf16[256,1024]{1,0:T(8,128)(2,1)}, u32[]{:S(2)}, u32[]{:S(2)}) collective-permute-start(bf16[256,1024]{1,0:T(8,128)(2,1)S(1)} %pad_maximum_fusion.2), channel_id=1, source_target_pairs={{0,4},{4,8},{8,12},{12,0},{1,5},{5,9},{9,13},{13,1},{2,6},{6,10},{... | collective-permute-start | bytes 1572872 | tf_op jit(solution)/shard_map/ppermute | solution.py:54
  6.8 17.6 %collective-permute-start = (bf16[128,512]{1,0:T(8,128)(2,1)S(1)}, bf16[128,512]{1,0:T(8,128)(2,1)S(1)}, u32[]{:S(2)}, u32[]{:S(2)}) collective-permute-start(bf16[128,512]{1,0:T(8,128)(2,1)S(1)} %get-tuple-element.113), channel_id=1, source_target_pairs={{0,4},{4,8},{8,12},{12,0},{1,5},{5,9},{9,13},{13,1},{2,6},{6,10},{... | collective-permute-start | bytes 393224 | tf_op jit(solution)/shard_map/ppermute | solution.py:54
  8.4 17.9 %collective-permute-start.3 = (bf16[128,512]{1,0:T(8,128)(2,1)S(1)}, bf16[128,512]{1,0:T(8,128)(2,1)S(1)}, u32[]{:S(2)}, u32[]{:S(2)}) collective-permute-start(bf16[128,512]{1,0:T(8,128)(2,1)S(1)} %get-tuple-element.114), channel_id=1, source_target_pairs={{0,12},{4,0},{8,4},{12,8},{1,13},{5,1},{9,5},{13,9},{2,14},{6,2},{... | collective-permute-start | bytes 393224 | tf_op jit(solution)/shard_map/ppermute | solution.py:54
  10.7 21.3 %collective-permute-start.2 = (bf16[128,512]{1,0:T(8,128)(2,1)S(1)}, bf16[128,512]{1,0:T(8,128)(2,1)S(1)}, u32[]{:S(2)}, u32[]{:S(2)}) collective-permute-start(bf16[128,512]{1,0:T(8,128)(2,1)S(1)} %get-tuple-element.115), channel_id=1, source_target_pairs={{0,8},{4,12},{8,0},{12,4},{1,9},{5,13},{9,1},{13,5},{2,10},{6,14},... | collective-permute-start | bytes 393224 | tf_op jit(solution)/shard_map/ppermute | solution.py:54
  24.4 21.5 %collective-permute-start.7 = (bf16[256,1024]{1,0:T(8,128)(2,1)}, bf16[256,1024]{1,0:T(8,128)(2,1)S(1)}, u32[]{:S(2)}, u32[]{:S(2)}) collective-permute-start(bf16[256,1024]{1,0:T(8,128)(2,1)} %collective-permute-done.1.refs_1_), channel_id=1, source_target_pairs={{0,16},{16,0},{1,17},{17,1},{2,18},{18,2},{3,19},{19,3},{4,20},{20... | collective-permute-start | bytes 1572872 | tf_op jit(solution)/shard_map/ppermute | solution.py:49
  32.0 13.9 %collective-permute-start.4 = (bf16[512,512]{1,0:T(8,128)(2,1)S(1)}, bf16[512,512]{1,0:T(8,128)(2,1)S(1)}, u32[]{:S(2)}, u32[]{:S(2)}) collective-permute-start(bf16[512,512]{1,0:T(8,128)(2,1)S(1)} %pad_maximum_fusion.3.refs_0_), channel_id=1, source_target_pairs={{0,2},{2,0},{1,3},{3,1},{4,6},{6,4},{5,7},{7,5},{8,10},{10,8},{9,1... | collective-permute-start | bytes 1572872 | tf_op jit(solution)/shard_map/ppermute | solution.py:49
  33.5 13.7 %collective-permute-start.8 = (bf16[256,1024]{1,0:T(8,128)(2,1)S(1)}, bf16[256,1024]{1,0:T(8,128)(2,1)}, u32[]{:S(2)}, u32[]{:S(2)}) collective-permute-start(bf16[256,1024]{1,0:T(8,128)(2,1)S(1)} %pad_maximum_fusion.2), channel_id=1, source_target_pairs={{0,12},{4,0},{8,4},{12,8},{1,13},{5,1},{9,5},{13,9},{2,14},{6,2},{... | collective-permute-start | bytes 1572872 | tf_op jit(solution)/shard_map/ppermute | solution.py:54
  35.2 14.9 %copy-start.14 = (bf16[2,512,256]{2,1,0:T(8,128)(2,1)S(1)}, bf16[2,512,256]{2,1,0:T(8,128)(2,1)}, u32[]{:S(2)}) copy-start(bf16[2,512,256]{2,1,0:T(8,128)(2,1)} %param.23) | copy-start | bytes 1572868
  38.4 10.4 %collective-permute-start.11 = (bf16[64,2048]{1,0:T(8,128)(2,1)S(1)}, bf16[64,2048]{1,0:T(8,128)(2,1)S(1)}, u32[]{:S(2)}, u32[]{:S(2)}) collective-permute-start(bf16[64,2048]{1,0:T(8,128)(2,1)S(1)} %convolution_convert_fusion), channel_id=1, source_target_pairs={{0,1},{1,0},{2,3},{3,2},{4,5},{5,4},{6,7},{7,6},{8,9},{9,8},{10,11... | collective-permute-start | bytes 786440 | tf_op jit(solution)/shard_map/ppermute | solution.py:49
  38.4 19.7 %collective-permute-start.5 = (bf16[512,512]{1,0:T(8,128)(2,1)S(1)}, bf16[512,512]{1,0:T(8,128)(2,1)}, u32[]{:S(2)}, u32[]{:S(2)}) collective-permute-start(bf16[512,512]{1,0:T(8,128)(2,1)S(1)} %pad_maximum_fusion.3.refs_0_), channel_id=1, source_target_pairs={{0,1},{1,0},{2,3},{3,2},{4,5},{5,4},{6,7},{7,6},{8,9},{9,8},{10,11... | collective-permute-start | bytes 1572872 | tf_op jit(solution)/shard_map/ppermute | solution.py:49
  45.9 12.2 %collective-permute-start.6 = (bf16[512,512]{1,0:T(8,128)(2,1)S(1)}, bf16[512,512]{1,0:T(8,128)(2,1)}, u32[]{:S(2)}, u32[]{:S(2)}) collective-permute-start(bf16[512,512]{1,0:T(8,128)(2,1)S(1)} %collective-permute-done.4.refs_1_), channel_id=1, source_target_pairs={{0,1},{1,0},{2,3},{3,2},{4,5},{5,4},{6,7},{7,6},{8,9},{9,8},{10,11... | collective-permute-start | bytes 1572872 | tf_op jit(solution)/shard_map/ppermute | solution.py:49
  45.9 4.2 %copy-start.3 = (bf16[256,1024]{1,0:T(8,128)(2,1)}, bf16[256,1024]{1,0:T(8,128)(2,1)S(1)}, u32[]{:S(2)}) copy-start(bf16[256,1024]{1,0:T(8,128)(2,1)S(1)} %collective-permute-done.7.refs_2_) | copy-start | bytes 1572868
  47.2 13.4 %collective-permute-start.9 = (bf16[256,1024]{1,0:T(8,128)(2,1)}, bf16[256,1024]{1,0:T(8,128)(2,1)}, u32[]{:S(2)}, u32[]{:S(2)}) collective-permute-start(bf16[256,1024]{1,0:T(8,128)(2,1)} %collective-permute-done.8.refs_3_), channel_id=1, source_target_pairs={{0,16},{16,0},{1,17},{17,1},{2,18},{18,2},{3,19},{19,3},{4,20},{20... | collective-permute-start | bytes 1572872 | tf_op jit(solution)/shard_map/ppermute | solution.py:49
  48.7 14.9 %collective-permute-start.10 = (bf16[256,1024]{1,0:T(8,128)(2,1)}, bf16[256,1024]{1,0:T(8,128)(2,1)}, u32[]{:S(2)}, u32[]{:S(2)}) collective-permute-start(bf16[256,1024]{1,0:T(8,128)(2,1)} %collective-permute-done.1.refs_1_), channel_id=1, source_target_pairs={{0,4},{4,8},{8,12},{12,0},{1,5},{5,9},{9,13},{13,1},{2,6},{6,10},{... | collective-permute-start | bytes 1572872 | tf_op jit(solution)/shard_map/ppermute | solution.py:54
  49.5 7.5 %collective-permute-start.12 = (bf16[64,2048]{1,0:T(8,128)(2,1)}, bf16[64,2048]{1,0:T(8,128)(2,1)}, u32[]{:S(2)}, u32[]{:S(2)}) collective-permute-start(bf16[64,2048]{1,0:T(8,128)(2,1)} %add.88), channel_id=1, source_target_pairs={{0,2},{2,0},{1,3},{3,1},{4,6},{6,4},{5,7},{7,5},{8,10},{10,8},{9,1... | collective-permute-start | bytes 786440 | tf_op jit(solution)/shard_map/ppermute | solution.py:49
  50.9 7.3 %copy-start.8 = (f32[2048]{0:T(1024)S(1)}, f32[2048]{0:T(1024)}, u32[]{:S(2)}) copy-start(f32[2048]{0:T(1024)} %param.27) | copy-start | bytes 24580
  53.8 10.3 %copy-start.1 = (bf16[512,512]{1,0:T(8,128)(2,1)S(1)}, bf16[512,512]{1,0:T(8,128)(2,1)}, u32[]{:S(2)}) copy-start(bf16[512,512]{1,0:T(8,128)(2,1)} %refs_0_.1) | copy-start | bytes 1572868
  53.8 10.3 %copy-start.9 = (bf16[512,256]{1,0:T(8,128)(2,1)S(1)}, bf16[512,256]{1,0:T(8,128)(2,1)}, u32[]{:S(2)}) copy-start(bf16[512,256]{1,0:T(8,128)(2,1)} %get-tuple-element.107) | copy-start | bytes 786436
  53.8 22.2 %copy-start.10 = (bf16[512,512]{1,0:T(8,128)(2,1)S(1)}, bf16[512,512]{1,0:T(8,128)(2,1)}, u32[]{:S(2)}) copy-start(bf16[512,512]{1,0:T(8,128)(2,1)} %param.20) | copy-start | bytes 1572868
  53.8 22.2 %copy-start.11 = (bf16[512,256]{1,0:T(8,128)(2,1)S(1)}, bf16[512,256]{1,0:T(8,128)(2,1)}, u32[]{:S(2)}) copy-start(bf16[512,256]{1,0:T(8,128)(2,1)} %get-tuple-element.108) | copy-start | bytes 786436
  53.9 22.2 %copy-start.12 = (bf16[512,256]{1,0:T(8,128)(2,1)S(1)}, bf16[512,256]{1,0:T(8,128)(2,1)}, u32[]{:S(2)}) copy-start(bf16[512,256]{1,0:T(8,128)(2,1)} %get-tuple-element.109) | copy-start | bytes 786436
  60.5 23.2 %copy-start.2 = (bf16[2,1,512,256]{3,2,1,0:T(8,128)(2,1)S(1)}, bf16[2,1,512,256]{3,2,1,0:T(8,128)(2,1)}, u32[]{:S(2)}) copy-start(bf16[2,1,512,256]{3,2,1,0:T(8,128)(2,1)} %param.16) | copy-start | bytes 1572868
  60.5 23.2 %copy-start.4 = (bf16[256,1024]{1,0:T(8,128)(2,1)S(1)}, bf16[256,1024]{1,0:T(8,128)(2,1)}, u32[]{:S(2)}) copy-start(bf16[256,1024]{1,0:T(8,128)(2,1)} %copy-done.3) | copy-start | bytes 1572868
  63.6 16.2 %collective-permute-start.13 = (bf16[256,1024]{1,0:T(8,128)(2,1)}, bf16[256,1024]{1,0:T(8,128)(2,1)S(1)}, u32[]{:S(2)}, u32[]{:S(2)}) collective-permute-start(bf16[256,1024]{1,0:T(8,128)(2,1)} %collective-permute-done.10.refs_5_), channel_id=1, source_target_pairs={{0,16},{16,0},{1,17},{17,1},{2,18},{18,2},{3,19},{19,3},{4,20},{20... | collective-permute-start | bytes 1572872 | tf_op jit(solution)/shard_map/ppermute | solution.py:49
  64.2 11.1 %collective-permute-start.14 = (bf16[256,512]{1,0:T(8,128)(2,1)S(1)}, bf16[256,512]{1,0:T(8,128)(2,1)S(1)}, u32[]{:S(2)}, u32[]{:S(2)}) collective-permute-start(bf16[256,512]{1,0:T(8,128)(2,1)S(1)} %get-tuple-element.66), channel_id=1, source_target_pairs={{0,4},{4,8},{8,12},{12,0},{1,5},{5,9},{9,13},{13,1},{2,6},{6,10},{... | collective-permute-start | bytes 786440 | tf_op jit(solution)/shard_map/ppermute | solution.py:54
  64.3 13.5 %collective-permute-start.15 = (bf16[256,512]{1,0:T(8,128)(2,1)S(1)}, bf16[256,512]{1,0:T(8,128)(2,1)S(1)}, u32[]{:S(2)}, u32[]{:S(2)}) collective-permute-start(bf16[256,512]{1,0:T(8,128)(2,1)S(1)} %get-tuple-element.66), channel_id=1, source_target_pairs={{0,12},{4,0},{8,4},{12,8},{1,13},{5,1},{9,5},{13,9},{2,14},{6,2},{... | collective-permute-start | bytes 786440 | tf_op jit(solution)/shard_map/ppermute | solution.py:54
  75.3 16.1 %collective-permute-start.20 = (bf16[256,512]{1,0:T(8,128)(2,1)S(1)}, bf16[256,512]{1,0:T(8,128)(2,1)S(1)}, u32[]{:S(2)}, u32[]{:S(2)}) collective-permute-start(bf16[256,512]{1,0:T(8,128)(2,1)S(1)} %collective-permute-done.14.refs_1_), channel_id=1, source_target_pairs={{0,4},{4,8},{8,12},{12,0},{1,5},{5,9},{9,13},{13,1},{2,6},{6,10},{... | collective-permute-start | bytes 786440 | tf_op jit(solution)/shard_map/ppermute | solution.py:54
  76.2 16.6 %collective-permute-start.18 = (bf16[256,512]{1,0:T(8,128)(2,1)S(1)}, bf16[256,512]{1,0:T(8,128)(2,1)S(1)}, u32[]{:S(2)}, u32[]{:S(2)}) collective-permute-start(bf16[256,512]{1,0:T(8,128)(2,1)S(1)} %collective-permute-done.14.refs_1_), channel_id=1, source_target_pairs={{0,16},{16,0},{1,17},{17,1},{2,18},{18,2},{3,19},{19,3},{4,20},{20... | collective-permute-start | bytes 786440 | tf_op jit(solution)/shard_map/ppermute | solution.py:49
  77.8 15.0 %collective-permute-start.19 = (bf16[256,512]{1,0:T(8,128)(2,1)S(1)}, bf16[256,512]{1,0:T(8,128)(2,1)S(1)}, u32[]{:S(2)}, u32[]{:S(2)}) collective-permute-start(bf16[256,512]{1,0:T(8,128)(2,1)S(1)} %collective-permute-done.15.refs_3_), channel_id=1, source_target_pairs={{0,16},{16,0},{1,17},{17,1},{2,18},{18,2},{3,19},{19,3},{4,20},{20... | collective-permute-start | bytes 786440 | tf_op jit(solution)/shard_map/ppermute | solution.py:49
  79.9 11.9 %collective-permute-start.16 = (bf16[256,512]{1,0:T(8,128)(2,1)S(1)}, bf16[256,512]{1,0:T(8,128)(2,1)S(1)}, u32[]{:S(2)}, u32[]{:S(2)}) collective-permute-start(bf16[256,512]{1,0:T(8,128)(2,1)S(1)} %get-tuple-element.75), channel_id=1, source_target_pairs={{0,4},{4,8},{8,12},{12,0},{1,5},{5,9},{9,13},{13,1},{2,6},{6,10},{... | collective-permute-start | bytes 786440 | tf_op jit(solution)/shard_map/ppermute | solution.py:54
  79.9 12.9 %collective-permute-start.17 = (bf16[256,512]{1,0:T(8,128)(2,1)S(1)}, bf16[256,512]{1,0:T(8,128)(2,1)S(1)}, u32[]{:S(2)}, u32[]{:S(2)}) collective-permute-start(bf16[256,512]{1,0:T(8,128)(2,1)S(1)} %get-tuple-element.75), channel_id=1, source_target_pairs={{0,12},{4,0},{8,4},{12,8},{1,13},{5,1},{9,5},{13,9},{2,14},{6,2},{... | collective-permute-start | bytes 786440 | tf_op jit(solution)/shard_map/ppermute | solution.py:54
  91.5 19.8 %copy-start.7 = (f32[2048]{0:T(1024)S(1)}, f32[2048]{0:T(1024)}, u32[]{:S(2)}) copy-start(f32[2048]{0:T(1024)} %param.28) | copy-start | bytes 24580
  91.5 6.4 %collective-permute-start.21 = (bf16[256,512]{1,0:T(8,128)(2,1)S(1)}, bf16[256,512]{1,0:T(8,128)(2,1)S(1)}, u32[]{:S(2)}, u32[]{:S(2)}) collective-permute-start(bf16[256,512]{1,0:T(8,128)(2,1)S(1)} %collective-permute-done.20.refs_5_), channel_id=1, source_target_pairs={{0,16},{16,0},{1,17},{17,1},{2,18},{18,2},{3,19},{19,3},{4,20},{20... | collective-permute-start | bytes 786440 | tf_op jit(solution)/shard_map/ppermute | solution.py:49
  100.0 2.0 %collective-permute-start.22 = (bf16[128,2048]{1,0:T(8,128)(2,1)S(1)}, bf16[128,2048]{1,0:T(8,128)(2,1)S(1)}, u32[]{:S(2)}, u32[]{:S(2)}) collective-permute-start(bf16[128,2048]{1,0:T(8,128)(2,1)S(1)} %get-tuple-element.81), channel_id=1, source_target_pairs={{0,1},{1,0},{2,3},{3,2},{4,5},{5,4},{6,7},{7,6},{8,9},{9,8},{10,11... | collective-permute-start | bytes 1572872 | tf_op jit(solution)/shard_map/ppermute | solution.py:49
  100.1 2.6 %collective-permute-start.24 = (bf16[128,2048]{1,0:T(8,128)(2,1)S(1)}, bf16[128,2048]{1,0:T(8,128)(2,1)S(1)}, u32[]{:S(2)}, u32[]{:S(2)}) collective-permute-start(bf16[128,2048]{1,0:T(8,128)(2,1)S(1)} %get-tuple-element.84), channel_id=1, source_target_pairs={{0,1},{1,0},{2,3},{3,2},{4,5},{5,4},{6,7},{7,6},{8,9},{9,8},{10,11... | collective-permute-start | bytes 1572872 | tf_op jit(solution)/shard_map/ppermute | solution.py:49
  102.1 9.2 %collective-permute-start.23 = (bf16[64,2048]{1,0:T(8,128)(2,1)S(1)}, bf16[64,2048]{1,0:T(8,128)(2,1)S(1)}, u32[]{:S(2)}, u32[]{:S(2)}) collective-permute-start(bf16[64,2048]{1,0:T(8,128)(2,1)S(1)} %add_convert_fusion.1), channel_id=1, source_target_pairs={{0,2},{2,0},{1,3},{3,1},{4,6},{6,4},{5,7},{7,5},{8,10},{10,8},{9,1... | collective-permute-start | bytes 786440 | tf_op jit(solution)/shard_map/ppermute | solution.py:49
  102.8 14.1 %collective-permute-start.25 = (bf16[64,2048]{1,0:T(8,128)(2,1)S(1)}, bf16[64,2048]{1,0:T(8,128)(2,1)S(1)}, u32[]{:S(2)}, u32[]{:S(2)}) collective-permute-start(bf16[64,2048]{1,0:T(8,128)(2,1)S(1)} %add_convert_fusion), channel_id=1, source_target_pairs={{0,2},{2,0},{1,3},{3,1},{4,6},{6,4},{5,7},{7,5},{8,10},{10,8},{9,1... | collective-permute-start | bytes 786440 | tf_op jit(solution)/shard_map/ppermute | solution.py:49
  104.3 12.9 %collective-permute-start.29 = (bf16[256,512]{1,0:T(8,128)(2,1)S(1)}, bf16[256,512]{1,0:T(8,128)(2,1)S(1)}, u32[]{:S(2)}, u32[]{:S(2)}) collective-permute-start(bf16[256,512]{1,0:T(8,128)(2,1)S(1)} %collective-permute-done.16.refs_5_), channel_id=1, source_target_pairs={{0,4},{4,8},{8,12},{12,0},{1,5},{5,9},{9,13},{13,1},{2,6},{6,10},{... | collective-permute-start | bytes 786440 | tf_op jit(solution)/shard_map/ppermute | solution.py:54
  104.3 14.4 %collective-permute-start.27 = (bf16[256,512]{1,0:T(8,128)(2,1)S(1)}, bf16[256,512]{1,0:T(8,128)(2,1)S(1)}, u32[]{:S(2)}, u32[]{:S(2)}) collective-permute-start(bf16[256,512]{1,0:T(8,128)(2,1)S(1)} %collective-permute-done.16.refs_5_), channel_id=1, source_target_pairs={{0,16},{16,0},{1,17},{17,1},{2,18},{18,2},{3,19},{19,3},{4,20},{20... | collective-permute-start | bytes 786440 | tf_op jit(solution)/shard_map/ppermute | solution.py:49
  104.8 14.0 %collective-permute-start.28 = (bf16[256,512]{1,0:T(8,128)(2,1)S(1)}, bf16[256,512]{1,0:T(8,128)(2,1)S(1)}, u32[]{:S(2)}, u32[]{:S(2)}) collective-permute-start(bf16[256,512]{1,0:T(8,128)(2,1)S(1)} %collective-permute-done.17.refs_7_), channel_id=1, source_target_pairs={{0,16},{16,0},{1,17},{17,1},{2,18},{18,2},{3,19},{19,3},{4,20},{20... | collective-permute-start | bytes 786440 | tf_op jit(solution)/shard_map/ppermute | solution.py:49
  111.6 11.0 %collective-permute-start.26 = (bf16[64,2048]{1,0:T(8,128)(2,1)S(1)}, bf16[64,2048]{1,0:T(8,128)(2,1)S(1)}, u32[]{:S(2)}, u32[]{:S(2)}) collective-permute-start(bf16[64,2048]{1,0:T(8,128)(2,1)S(1)} %get-tuple-element.88.refs_0_), channel_id=1, source_target_pairs={{0,2},{2,0},{1,3},{3,1},{4,6},{6,4},{5,7},{7,5},{8,10},{10,8},{9,1... | collective-permute-start | bytes 786440 | tf_op jit(solution)/shard_map/ppermute | solution.py:49
  117.2 6.8 %collective-permute-start.32 = (bf16[256,512]{1,0:T(8,128)(2,1)S(1)}, bf16[256,512]{1,0:T(8,128)(2,1)S(1)}, u32[]{:S(2)}, u32[]{:S(2)}) collective-permute-start(bf16[256,512]{1,0:T(8,128)(2,1)S(1)} %collective-permute-done.29.refs_9_), channel_id=1, source_target_pairs={{0,16},{16,0},{1,17},{17,1},{2,18},{18,2},{3,19},{19,3},{4,20},{20... | collective-permute-start | bytes 786440 | tf_op jit(solution)/shard_map/ppermute | solution.py:49
  117.3 10.1 %collective-permute-start.33 = (bf16[64,2048]{1,0:T(8,128)(2,1)S(1)}, bf16[64,2048]{1,0:T(8,128)(2,1)S(1)}, u32[]{:S(2)}, u32[]{:S(2)}) collective-permute-start(bf16[64,2048]{1,0:T(8,128)(2,1)S(1)} %get-tuple-element.93.refs_0_), channel_id=1, source_target_pairs={{0,2},{2,0},{1,3},{3,1},{4,6},{6,4},{5,7},{7,5},{8,10},{10,8},{9,1... | collective-permute-start | bytes 786440 | tf_op jit(solution)/shard_map/ppermute | solution.py:49
  118.7 8.7 %collective-permute-start.30 = (bf16[64,2048]{1,0:T(8,128)(2,1)S(1)}, bf16[64,2048]{1,0:T(8,128)(2,1)S(1)}, u32[]{:S(2)}, u32[]{:S(2)}) collective-permute-start(bf16[64,2048]{1,0:T(8,128)(2,1)S(1)} %get-tuple-element.88.refs_0_), channel_id=1, source_target_pairs={{0,1},{1,0},{2,3},{3,2},{4,5},{5,4},{6,7},{7,6},{8,9},{9,8},{10,11... | collective-permute-start | bytes 786440 | tf_op jit(solution)/shard_map/ppermute | solution.py:49
  118.8 10.3 %collective-permute-start.34 = (bf16[64,2048]{1,0:T(8,128)(2,1)S(1)}, bf16[64,2048]{1,0:T(8,128)(2,1)S(1)}, u32[]{:S(2)}, u32[]{:S(2)}) collective-permute-start(bf16[64,2048]{1,0:T(8,128)(2,1)S(1)} %get-tuple-element.93.refs_0_), channel_id=1, source_target_pairs={{0,1},{1,0},{2,3},{3,2},{4,5},{5,4},{6,7},{7,6},{8,9},{9,8},{10,11... | collective-permute-start | bytes 786440 | tf_op jit(solution)/shard_map/ppermute | solution.py:49
  122.5 4.9 %collective-permute-start.31 = (bf16[64,2048]{1,0:T(8,128)(2,1)S(1)}, bf16[64,2048]{1,0:T(8,128)(2,1)S(1)}, u32[]{:S(2)}, u32[]{:S(2)}) collective-permute-start(bf16[64,2048]{1,0:T(8,128)(2,1)S(1)} %collective-permute-done.26.refs_1_), channel_id=1, source_target_pairs={{0,1},{1,0},{2,3},{3,2},{4,5},{5,4},{6,7},{7,6},{8,9},{9,8},{10,11... | collective-permute-start | bytes 786440 | tf_op jit(solution)/shard_map/ppermute | solution.py:49
  127.4 1.8 %collective-permute-start.35 = (bf16[64,2048]{1,0:T(8,128)(2,1)S(1)}, bf16[64,2048]{1,0:T(8,128)(2,1)S(1)}, u32[]{:S(2)}, u32[]{:S(2)}) collective-permute-start(bf16[64,2048]{1,0:T(8,128)(2,1)S(1)} %collective-permute-done.33.refs_1_), channel_id=1, source_target_pairs={{0,1},{1,0},{2,3},{3,2},{4,5},{5,4},{6,7},{7,6},{8,9},{9,8},{10,11... | collective-permute-start | bytes 786440 | tf_op jit(solution)/shard_map/ppermute | solution.py:49
  129.1 1.7 %copy-start = (bf16[2048,512]{1,0:T(8,128)(2,1)S(1)}, bf16[2048,512]{1,0:T(8,128)(2,1)}, u32[]{:S(2)}) copy-start(bf16[2048,512]{1,0:T(8,128)(2,1)} %query_ref.7) | copy-start | bytes 6291460
  129.1 1.7 %copy-start.5 = (f32[2048]{0:T(1024)S(1)}, f32[2048]{0:T(1024)}, u32[]{:S(2)}) copy-start(f32[2048]{0:T(1024)} %param.29) | copy-start | bytes 24580
  129.1 1.7 %copy-start.6 = (s32[3,16]{1,0:T(4,128)S(1)}, s32[3,16]{1,0:T(4,128)}, u32[]{:S(2)}) copy-start(s32[3,16]{1,0:T(4,128)} %parent_ref.7) | copy-start | bytes 580
  132.8 4.5 %collective-permute-start.36 = (bf16[16,2048]{1,0:T(8,128)(2,1)S(1)}, bf16[16,2048]{1,0:T(8,128)(2,1)S(1)}, u32[]{:S(2)}, u32[]{:S(2)}) collective-permute-start(bf16[16,2048]{1,0:T(8,128)(2,1)S(1)} %get-tuple-element.97.refs_3_), channel_id=1, source_target_pairs={{0,2},{2,0},{1,3},{3,1},{4,6},{6,4},{5,7},{7,5},{8,10},{10,8},{9,1... | collective-permute-start | bytes 196616 | tf_op jit(solution)/shard_map/ppermute | solution.py:49
  133.3 4.0 %collective-permute-start.37 = (bf16[16,2048]{1,0:T(8,128)(2,1)S(1)}, bf16[16,2048]{1,0:T(8,128)(2,1)S(1)}, u32[]{:S(2)}, u32[]{:S(2)}) collective-permute-start(bf16[16,2048]{1,0:T(8,128)(2,1)S(1)} %get-tuple-element.97.refs_3_), channel_id=1, source_target_pairs={{0,1},{1,0},{2,3},{3,2},{4,5},{5,4},{6,7},{7,6},{8,9},{9,8},{10,11... | collective-permute-start | bytes 196616 | tf_op jit(solution)/shard_map/ppermute | solution.py:49
  137.3 1.3 collective-permute-start.38
  140.6 4.3 %collective-permute-start.39 = (bf16[16,2048]{1,0:T(8,128)(2,1)S(1)}, bf16[16,2048]{1,0:T(8,128)(2,1)S(1)}, u32[]{:S(2)}, u32[]{:S(2)}) collective-permute-start(bf16[16,2048]{1,0:T(8,128)(2,1)S(1)} %get-tuple-element.99.refs_3_), channel_id=1, source_target_pairs={{0,2},{2,0},{1,3},{3,1},{4,6},{6,4},{5,7},{7,5},{8,10},{10,8},{9,1... | collective-permute-start | bytes 196616 | tf_op jit(solution)/shard_map/ppermute | solution.py:49
  141.1 3.8 %collective-permute-start.40 = (bf16[16,2048]{1,0:T(8,128)(2,1)S(1)}, bf16[16,2048]{1,0:T(8,128)(2,1)S(1)}, u32[]{:S(2)}, u32[]{:S(2)}) collective-permute-start(bf16[16,2048]{1,0:T(8,128)(2,1)S(1)} %get-tuple-element.99.refs_3_), channel_id=1, source_target_pairs={{0,1},{1,0},{2,3},{3,2},{4,5},{5,4},{6,7},{7,6},{8,9},{9,8},{10,11... | collective-permute-start | bytes 196616 | tf_op jit(solution)/shard_map/ppermute | solution.py:49
  144.9 1.3 collective-permute-start.41
  148.2 4.3 %collective-permute-start.42 = (bf16[16,2048]{1,0:T(8,128)(2,1)S(1)}, bf16[16,2048]{1,0:T(8,128)(2,1)S(1)}, u32[]{:S(2)}, u32[]{:S(2)}) collective-permute-start(bf16[16,2048]{1,0:T(8,128)(2,1)S(1)} %get-tuple-element.101.refs_3_), channel_id=1, source_target_pairs={{0,2},{2,0},{1,3},{3,1},{4,6},{6,4},{5,7},{7,5},{8,10},{10,8},{9,1... | collective-permute-start | bytes 196616 | tf_op jit(solution)/shard_map/ppermute | solution.py:49
  148.7 3.8 %collective-permute-start.43 = (bf16[16,2048]{1,0:T(8,128)(2,1)S(1)}, bf16[16,2048]{1,0:T(8,128)(2,1)S(1)}, u32[]{:S(2)}, u32[]{:S(2)}) collective-permute-start(bf16[16,2048]{1,0:T(8,128)(2,1)S(1)} %get-tuple-element.101.refs_3_), channel_id=1, source_target_pairs={{0,1},{1,0},{2,3},{3,2},{4,5},{5,4},{6,7},{7,6},{8,9},{9,8},{10,11... | collective-permute-start | bytes 196616 | tf_op jit(solution)/shard_map/ppermute | solution.py:49
  152.5 1.3 collective-permute-start.44
  155.8 3.2 %collective-permute-start.47 = (bf16[16,512]{1,0:T(8,128)(2,1)S(1)}, bf16[16,512]{1,0:T(8,128)(2,1)S(1)}, u32[]{:S(2)}, u32[]{:S(2)}) collective-permute-start(bf16[16,512]{1,0:T(8,128)(2,1)S(1)} %get-tuple-element.105), channel_id=1, source_target_pairs={{0,3},{1,2},{2,1},{3,0},{4,7},{5,6},{6,5},{7,4},{8,11},{9,10},{10,... | collective-permute-start | bytes 49160 | tf_op jit(solution)/shard_map/ppermute | solution.py:704
  156.1 3.8 %collective-permute-start.46 = (bf16[16,512]{1,0:T(8,128)(2,1)S(1)}, bf16[16,512]{1,0:T(8,128)(2,1)S(1)}, u32[]{:S(2)}, u32[]{:S(2)}) collective-permute-start(bf16[16,512]{1,0:T(8,128)(2,1)S(1)} %get-tuple-element.104), channel_id=1, source_target_pairs={{0,2},{1,3},{2,0},{3,1},{4,6},{5,7},{6,4},{7,5},{8,10},{9,11},{10,... | collective-permute-start | bytes 49160 | tf_op jit(solution)/shard_map/ppermute | solution.py:704
  157.7 2.2 %collective-permute-start.45 = (bf16[16,512]{1,0:T(8,128)(2,1)S(1)}, bf16[16,512]{1,0:T(8,128)(2,1)S(1)}, u32[]{:S(2)}, u32[]{:S(2)}) collective-permute-start(bf16[16,512]{1,0:T(8,128)(2,1)S(1)} %get-tuple-element.103), channel_id=1, source_target_pairs={{0,1},{1,0},{2,3},{3,2},{4,5},{5,4},{6,7},{7,6},{8,9},{9,8},{10,11... | collective-permute-start | bytes 49160 | tf_op jit(solution)/shard_map/ppermute | solution.py:704
